TPU v7x, 32 devices: a whole 2x2x4 slice. The times are simulated.
32 devices in a mesh: seq: 8 (over z, y), tensor: 4 (over x, core).
Axes of the slice: x: 2, y: 2, z: 4, core: 2. Of those that a mesh axis runs over, the one named last changes fastest.
Arguments:
- inputs: bfloat16 [6144, 2560], P(('seq', 'tensor')), may hold values from -6 to 6
- segments: int32 [6144], replicated, may hold values from 0 to 31, as said below
- positions: int32 [6144], P('seq'), may hold values from 0 to 4046, as said below
- gain_attn: float32 [2560], P('seq'), may hold values from 0.5 to 1.5
- query_weight: float32 [2560, 2560], P('seq', 'tensor'), may hold values from -0.125 to 0.125
- key_weight: float32 [2560, 640], P('seq', 'tensor'), may hold values from -0.125 to 0.125
- value_weight: float32 [2560, 640], P('seq', 'tensor'), may hold values from -0.125 to 0.125
- out_weight: float32 [2560, 2560], P('tensor', 'seq'), may hold values from -2 to 2
- gain_mlp: float32 [2560], P('seq'), may hold values from 0.5 to 1.5
- gate_weight: float32 [2560, 6912], P('seq', 'tensor'), may hold values from -0.125 to 0.125
- up_weight: float32 [2560, 6912], P('seq', 'tensor'), may hold values from -0.125 to 0.125
- down_weight: float32 [6912, 2560], P('tensor', 'seq'), may hold values from -0.078125 to 0.078125
- cotangent: bfloat16 [6144, 2560], P(('seq', 'tensor')), may hold values from -6 to 6
Outputs:
- output: bfloat16 [6144, 2560], P(('seq', 'tensor'))
- input_grad: bfloat16 [6144, 2560], P(('seq', 'tensor'))
- gain_attn_grad: float32 [2560], P('seq')
- query_weight_grad: float32 [2560, 2560], P('seq', 'tensor')
- key_weight_grad: float32 [2560, 640], P('seq', 'tensor')
- value_weight_grad: float32 [2560, 640], P('seq', 'tensor')
- out_weight_grad: float32 [2560, 2560], P('tensor', 'seq')
- gain_mlp_grad: float32 [2560], P('seq')
- gate_weight_grad: float32 [2560, 6912], P('seq', 'tensor')
- up_weight_grad: float32 [2560, 6912], P('seq', 'tensor')
- down_weight_grad: float32 [6912, 2560], P('tensor', 'seq')
Inputs may be any that keep to these rules, and one draw needn't show every extreme that they name: `segments`: tokens k * 3072 to (k + 1) * 3072 - 1 form packed sequence k. Each sequence is cut into documents of consecutive tokens; within a sequence document numbers rise by one from each document to the next, and every number of a sequence is larger than every number of an earlier one; the first sequence starts at 0 and the last document of the last sequence carries the largest number. No document crosses a sequence's end. A document holds 200 to 2000 tokens, except the last one of a sequence, which may hold fewer; the first document of the first sequence holds exactly 2000. `positions`: A token's position is its index within its document plus an offset of 0 to 2047 shared by the whole document; the first document of the first sequence has offset 2047.
All inputs are finite; a program needn't handle non-finite values.
Results may differ from a plain program's by a relative error of at most 0.023.
Values may be sent and summed in bfloat16 or wider, within the bound.
No kernel may reach another device: no remote copies, remote signals or barrier semaphores. Data moves between devices by JAX's collectives and lax.ppermute only.
A program may use at most 256 MiB of HBM per device.

v0:
```python
import jax
import jax.numpy as jnp
from jax import lax
from jax.sharding import PartitionSpec as P

HEADS = 32
KV = 8
HD = 80
DOC_MOST = 2000


eps = 1e-05
rope_base = 10000.0


def passed_along(block, axis, distance):
    devices = range(lax.axis_size(axis))
    route = [(i - distance, i) for i in devices if i - distance in devices]
    return lax.ppermute(block, axis, route)


def rope_tables(positions, width):
    half_width = width // 2
    frequency = rope_base ** (-(jnp.arange(half_width, dtype=jnp.float32) * 2.0 / width))
    angles = positions.astype(jnp.float32)[:, None] * frequency[None, :]
    return (jnp.cos(angles)[:, None, :], jnp.sin(angles)[:, None, :])


def rotate(values, cos_tab, sine_tab):
    half_width = values.shape[-1] // 2
    front_half = values[..., :half_width]
    back_half = values[..., half_width:]
    return jnp.concatenate(
        [front_half * cos_tab - back_half * sine_tab, back_half * cos_tab + front_half * sine_tab],
        axis=-1,
    )


def unrotate(gradient, cos_tab, sine_tab):
    half_width = gradient.shape[-1] // 2
    front_half = gradient[..., :half_width]
    back_half = gradient[..., half_width:]
    return jnp.concatenate(
        [front_half * cos_tab + back_half * sine_tab, back_half * cos_tab - front_half * sine_tab],
        axis=-1,
    )


def gather_rows(values):
    return lax.all_gather(values, "tensor", axis=0, tiled=True)


def sum_rows(term_fn, own_rows):
    return lax.psum_scatter(
        term_fn(jnp.int32(0), lax.axis_size("tensor") * own_rows).astype(jnp.bfloat16),
        "tensor",
        scatter_dimension=0,
        tiled=True,
    ).astype(jnp.float32)


def contract_rows(left_side, right_side):
    return lax.dot_general(
        left_side, right_side, (((0,), (0,)), ((), ())), preferred_element_type=jnp.float32
    )


def contract_cols(left_side, right_side):
    return lax.dot_general(
        left_side, right_side, (((1,), (1,)), ((), ())), preferred_element_type=jnp.float32
    )


def norm_back(gradient, normed, inverse, gain_vec):
    scaled = gradient * gain_vec
    return inverse * (scaled - normed * jnp.mean(scaled * normed, axis=-1, keepdims=True))


def per_device(
    inputs,
    segments,
    positions,
    gain_attn,
    query_weight,
    key_weight,
    value_weight,
    out_weight,
    gain_mlp,
    gate_weight,
    up_weight,
    down_weight,
    cotangent,
):
    tok_seq = positions.shape[0]
    own_rows = inputs.shape[0]
    kv_local = key_weight.shape[1] // HD
    group_size = HEADS // KV
    reach_devs = (DOC_MOST - 2) // tok_seq + 1
    score_scale = HD ** (-0.5)
    seq_index = lax.axis_index("seq")
    wide = jnp.bfloat16
    gain_one, weight_q, weight_k, weight_v, weight_o, gain_two, weight_g, weight_u, weight_d = (
        lax.all_gather(gain_attn.astype(wide), "seq", axis=0, tiled=True),
        lax.all_gather(query_weight.astype(wide), "seq", axis=0, tiled=True),
        lax.all_gather(key_weight.astype(wide), "seq", axis=0, tiled=True),
        lax.all_gather(value_weight.astype(wide), "seq", axis=0, tiled=True),
        lax.all_gather(out_weight.astype(wide), "seq", axis=1, tiled=True),
        lax.all_gather(gain_mlp.astype(wide), "seq", axis=0, tiled=True),
        lax.all_gather(gate_weight.astype(wide), "seq", axis=0, tiled=True),
        lax.all_gather(up_weight.astype(wide), "seq", axis=0, tiled=True),
        lax.all_gather(down_weight.astype(wide), "seq", axis=1, tiled=True),
    )
    gain_first = gain_one.astype(jnp.float32)
    gain_second = gain_two.astype(jnp.float32)
    input_f32 = inputs.astype(jnp.float32)
    inverse_one = lax.rsqrt(jnp.mean(input_f32 * input_f32, axis=-1, keepdims=True) + eps)
    normed_one = input_f32 * inverse_one
    h_one = gather_rows((normed_one * gain_first).astype(wide))
    cos_tab, sine_tab = rope_tables(positions, HD)
    q_pre = jnp.dot(h_one, weight_q, preferred_element_type=jnp.float32).reshape(tok_seq, -1, HD)
    k_pre = jnp.dot(h_one, weight_k, preferred_element_type=jnp.float32).reshape(tok_seq, -1, HD)
    queries = rotate(q_pre, cos_tab, sine_tab).reshape(tok_seq, -1).astype(wide)
    keys_rot = rotate(k_pre, cos_tab, sine_tab).reshape(tok_seq, -1).astype(wide)
    values_own = jnp.dot(h_one, weight_v, preferred_element_type=jnp.float32).astype(wide)
    key_list = []
    value_list = []
    for distance in range(reach_devs, 0, -1):
        far_keys, far_values = passed_along((keys_rot, values_own), "seq", distance)
        key_list.append(far_keys)
        value_list.append(far_values)
    key_span = (reach_devs + 1) * tok_seq
    key_heads = jnp.concatenate(key_list + [keys_rot], axis=0).reshape(key_span, kv_local, HD)
    value_heads = jnp.concatenate(value_list + [values_own], axis=0).reshape(key_span, kv_local, HD)
    padded_segs = jnp.concatenate([jnp.full((reach_devs * tok_seq,), -1, jnp.int32), segments])
    key_segs = lax.dynamic_slice_in_dim(padded_segs, seq_index * tok_seq, key_span, 0)
    query_segs = lax.dynamic_slice_in_dim(segments, seq_index * tok_seq, tok_seq, 0)
    key_places = (seq_index - reach_devs) * tok_seq + jnp.arange(key_span, dtype=jnp.int32)
    query_places = seq_index * tok_seq + jnp.arange(tok_seq, dtype=jnp.int32)
    block_rows = min(tok_seq, 256)
    blocks = tok_seq // block_rows
    numbers = jnp.arange(blocks, dtype=jnp.int32)

    def scores_of(number):
        first_row = number * block_rows
        query_blk = lax.dynamic_slice_in_dim(queries, first_row, block_rows, 0).reshape(
            block_rows, kv_local, group_size, HD
        )
        seg_blk = lax.dynamic_slice_in_dim(query_segs, first_row, block_rows, 0)
        place_blk = lax.dynamic_slice_in_dim(query_places, first_row, block_rows, 0)
        allowed = (seg_blk[:, None] == key_segs[None, :]) & (
            key_places[None, :] <= place_blk[:, None]
        )
        scores = (
            jnp.einsum("qcgd,kcd->cgqk", query_blk, key_heads, preferred_element_type=jnp.float32)
            * score_scale
        )
        return (query_blk, jnp.where(allowed, scores, -1e30))

    def forward_block(number):
        query_blk, scores = scores_of(number)
        row_max = jnp.max(scores, axis=-1, keepdims=True)
        exp_terms = jnp.exp(scores - row_max)
        row_total = jnp.sum(exp_terms, axis=-1, keepdims=True)
        attn_probs = (exp_terms / row_total).astype(wide)
        out_blk = jnp.einsum(
            "cgqk,kcd->qcgd", attn_probs, value_heads, preferred_element_type=jnp.float32
        )
        return (
            out_blk.reshape(block_rows, -1).astype(wide),
            (row_max + jnp.log(row_total))[..., 0],
        )

    attended, log_totals = lax.map(forward_block, numbers)
    attended = attended.reshape(tok_seq, -1)

    def attn_term(first_row, row_count):
        return jnp.dot(attended, weight_o, preferred_element_type=jnp.float32)

    x_mid = input_f32 + sum_rows(attn_term, own_rows)
    inverse_two = lax.rsqrt(jnp.mean(x_mid * x_mid, axis=-1, keepdims=True) + eps)
    normed_two = x_mid * inverse_two
    h_two = gather_rows((normed_two * gain_second).astype(wide))
    gate_pre = jnp.dot(h_two, weight_g, preferred_element_type=jnp.float32)
    up_pre = jnp.dot(h_two, weight_u, preferred_element_type=jnp.float32)
    sigmoid_gate = jax.nn.sigmoid(gate_pre)
    hidden = (gate_pre * sigmoid_gate * up_pre).astype(wide)

    def mlp_term(first_row, row_count):
        return jnp.dot(hidden, weight_d, preferred_element_type=jnp.float32)

    output = (x_mid + sum_rows(mlp_term, own_rows)).astype(wide)
    gain_one, weight_q, weight_k, weight_v, weight_o, gain_two, weight_g, weight_u, weight_d = (
        lax.all_gather(gain_attn.astype(wide), "seq", axis=0, tiled=True),
        lax.all_gather(query_weight.astype(wide), "seq", axis=0, tiled=True),
        lax.all_gather(key_weight.astype(wide), "seq", axis=0, tiled=True),
        lax.all_gather(value_weight.astype(wide), "seq", axis=0, tiled=True),
        lax.all_gather(out_weight.astype(wide), "seq", axis=1, tiled=True),
        lax.all_gather(gain_mlp.astype(wide), "seq", axis=0, tiled=True),
        lax.all_gather(gate_weight.astype(wide), "seq", axis=0, tiled=True),
        lax.all_gather(up_weight.astype(wide), "seq", axis=0, tiled=True),
        lax.all_gather(down_weight.astype(wide), "seq", axis=1, tiled=True),
    )
    gain_first = gain_one.astype(jnp.float32)
    gain_second = gain_two.astype(jnp.float32)
    grad_mix = gather_rows(cotangent)
    grad_hidden = contract_cols(grad_mix, weight_d)
    grad_gate = (
        grad_hidden * up_pre * sigmoid_gate * (1.0 + gate_pre * (1.0 - sigmoid_gate))
    ).astype(wide)
    grad_up = (grad_hidden * gate_pre * sigmoid_gate).astype(wide)
    down_grad = contract_rows(hidden, grad_mix)
    gate_grad = contract_rows(h_two, grad_gate)
    up_grad = contract_rows(h_two, grad_up)

    def mlp_back(first_row, row_count):
        return contract_cols(grad_gate, weight_g) + contract_cols(grad_up, weight_u)

    grad_h_two = sum_rows(mlp_back, own_rows)
    gain_two_part = jnp.sum(grad_h_two * normed_two, axis=0)
    grad_mid = cotangent.astype(jnp.float32) + norm_back(
        grad_h_two, normed_two, inverse_two, gain_second
    )
    grad_branch = gather_rows(grad_mid.astype(wide))
    out_grad = contract_rows(attended, grad_branch)
    grad_attended = contract_cols(grad_branch, weight_o).astype(wide)

    def backward_block(running, number):
        query_blk, scores = scores_of(number)
        log_blk = lax.dynamic_index_in_dim(log_totals, number, 0, keepdims=False)
        attn_probs = jnp.exp(scores - log_blk[..., None])
        grad_blk = lax.dynamic_slice_in_dim(
            grad_attended, number * block_rows, block_rows, 0
        ).reshape(block_rows, kv_local, group_size, HD)
        grad_probs = jnp.einsum(
            "qcgd,kcd->cgqk", grad_blk, value_heads, preferred_element_type=jnp.float32
        )
        grad_scores = (
            attn_probs * (grad_probs - jnp.sum(attn_probs * grad_probs, axis=-1, keepdims=True))
        ).astype(wide)
        grad_query_blk = (
            jnp.einsum("cgqk,kcd->qcgd", grad_scores, key_heads, preferred_element_type=jnp.float32)
            * score_scale
        )
        key_acc = (
            running[0]
            + jnp.einsum(
                "cgqk,qcgd->kcd", grad_scores, query_blk, preferred_element_type=jnp.float32
            )
            * score_scale
        )
        value_acc = running[1] + jnp.einsum(
            "cgqk,qcgd->kcd", attn_probs.astype(wide), grad_blk, preferred_element_type=jnp.float32
        )
        return ((key_acc, value_acc), grad_query_blk.reshape(block_rows, -1))

    zero_acc = jnp.zeros((key_span, kv_local, HD), jnp.float32)
    (key_acc, value_acc), grad_query_all = lax.scan(backward_block, (zero_acc, zero_acc), numbers)
    key_acc = key_acc.reshape(key_span, -1)
    value_acc = value_acc.reshape(key_span, -1)
    grad_keys = key_acc[reach_devs * tok_seq :]
    grad_values = value_acc[reach_devs * tok_seq :]
    for distance in range(1, reach_devs + 1):
        row_from = (reach_devs - distance) * tok_seq
        back_keys, back_values = (
            passed_along(
                key_acc[row_from : row_from + tok_seq].astype(jnp.bfloat16), "seq", -distance
            ).astype(jnp.float32),
            passed_along(
                value_acc[row_from : row_from + tok_seq].astype(jnp.bfloat16), "seq", -distance
            ).astype(jnp.float32),
        )
        grad_keys = grad_keys + back_keys
        grad_values = grad_values + back_values
    grad_q_pre = (
        unrotate(grad_query_all.reshape(tok_seq, -1, HD), cos_tab, sine_tab)
        .reshape(tok_seq, -1)
        .astype(wide)
    )
    grad_k_pre = (
        unrotate(grad_keys.reshape(tok_seq, -1, HD), cos_tab, sine_tab)
        .reshape(tok_seq, -1)
        .astype(wide)
    )
    grad_v_pre = grad_values.astype(wide)
    query_grad = contract_rows(h_one, grad_q_pre)
    key_grad = contract_rows(h_one, grad_k_pre)
    value_grad = contract_rows(h_one, grad_v_pre)

    def attn_back(first_row, row_count):
        return (
            contract_cols(grad_q_pre, weight_q)
            + contract_cols(grad_k_pre, weight_k)
            + contract_cols(grad_v_pre, weight_v)
        )

    grad_h_one = sum_rows(attn_back, own_rows)
    gain_one_part = jnp.sum(grad_h_one * normed_one, axis=0)
    input_grad = (grad_mid + norm_back(grad_h_one, normed_one, inverse_one, gain_first)).astype(
        wide
    )
    gain_one_sum, gain_two_sum = lax.psum((gain_one_part, gain_two_part), "tensor")
    reduced = (
        lax.psum_scatter(
            gain_one_sum.astype(jnp.bfloat16), "seq", scatter_dimension=0, tiled=True
        ).astype(jnp.float32),
        lax.psum_scatter(
            query_grad.astype(jnp.bfloat16), "seq", scatter_dimension=0, tiled=True
        ).astype(jnp.float32),
        lax.psum_scatter(
            key_grad.astype(jnp.bfloat16), "seq", scatter_dimension=0, tiled=True
        ).astype(jnp.float32),
        lax.psum_scatter(
            value_grad.astype(jnp.bfloat16), "seq", scatter_dimension=0, tiled=True
        ).astype(jnp.float32),
        lax.psum_scatter(
            out_grad.astype(jnp.bfloat16), "seq", scatter_dimension=1, tiled=True
        ).astype(jnp.float32),
        lax.psum_scatter(
            gain_two_sum.astype(jnp.bfloat16), "seq", scatter_dimension=0, tiled=True
        ).astype(jnp.float32),
        lax.psum_scatter(
            gate_grad.astype(jnp.bfloat16), "seq", scatter_dimension=0, tiled=True
        ).astype(jnp.float32),
        lax.psum_scatter(
            up_grad.astype(jnp.bfloat16), "seq", scatter_dimension=0, tiled=True
        ).astype(jnp.float32),
        lax.psum_scatter(
            down_grad.astype(jnp.bfloat16), "seq", scatter_dimension=1, tiled=True
        ).astype(jnp.float32),
    )
    return (
        output,
        input_grad,
        reduced[0],
        reduced[1],
        reduced[2],
        reduced[3],
        reduced[4],
        reduced[5],
        reduced[6],
        reduced[7],
        reduced[8],
    )


def solution(mesh):
    in_specs = (
        P(("seq", "tensor"), None),
        P(),
        P("seq"),
        P("seq"),
        P("seq", "tensor"),
        P("seq", "tensor"),
        P("seq", "tensor"),
        P("tensor", "seq"),
        P("seq"),
        P("seq", "tensor"),
        P("seq", "tensor"),
        P("tensor", "seq"),
        P(("seq", "tensor"), None),
    )
    out_specs = (
        P(("seq", "tensor"), None),
        P(("seq", "tensor"), None),
        P("seq"),
        P("seq", "tensor"),
        P("seq", "tensor"),
        P("seq", "tensor"),
        P("tensor", "seq"),
        P("seq"),
        P("seq", "tensor"),
        P("seq", "tensor"),
        P("tensor", "seq"),
    )
    return jax.shard_map(
        per_device, mesh=mesh, in_specs=in_specs, out_specs=out_specs, check_vma=False
    )
```

profile of v0, /device:TPU:0, one launch (start us, length us, event | category | flops | bytes accessed | tf_op | source)
XLA Modules:
  0.0 2189.4 jit_solution(14719038451576452837)
XLA Ops:
  12.8 38.8 %all-reduce.7 = (bf16[2560]{0:T(1024)(128)(2,1)S(1)}, bf16[2560]{0:T(1024)(128)(2,1)}) all-reduce(bf16[2560]{0:T(1024)(128)(2,1)S(1)} %dynamic-update-slice, bf16[2560]{0:T(1024)(128)(2,1)S(1)} %dynamic-update-slice.1), channel_id=1, replica_groups=mesh['seq'=8,'tensor'=4] {'seq'}, use_global_device_ids=true, to_apply=%add.1 | all-reduce | flops 5120 | bytes 20480
  56.3 32.7 %all-gather.1 = bf16[8,320,160]{1,2,0:T(8,128)(2,1)S(1)} all-gather(bf16[1,320,160]{1,2,0:T(8,128)(2,1)S(1)} %convert_bitcast_fusion), channel_id=1, replica_groups=mesh['seq'=8,'tensor'=4] {'seq'}, dimensions={0}, use_global_device_ids=true | all-gather | bytes 921600 | tf_op jit(solution)/shard_map/all_gather | solution.py:106
  90.0 34.9 %all-gather = bf16[8,320,160]{1,2,0:T(8,128)(2,1)S(1)} all-gather(bf16[1,320,160]{1,2,0:T(8,128)(2,1)S(1)} %convert_bitcast_fusion.1), channel_id=1, replica_groups=mesh['seq'=8,'tensor'=4] {'seq'}, dimensions={0}, use_global_device_ids=true | all-gather | bytes 921600 | tf_op jit(solution)/shard_map/all_gather | solution.py:105
  188.7 114.8 %while.28 = (s32[]{:T(128)}, bf16[3,256,640]{2,1,0:T(8,128)(2,1)}, f32[3,2,4,256]{3,2,1,0:T(4,128)S(1)}, s32[3]{0:T(128)S(1)}, s32[768]{0:T(1024)S(1)}, /*index=...) while((s32[]{:T(128)}, bf16[3,256,640]{2,1,0:T(8,128)(2,1)}, ...), condition=%wide.region_4.5_spmd.clone, body=%wide.region_1.4_spmd.clone.sunk | while | flops 2091287552 | bytes 83339488 | solution.py:173
  314.4 49.6 %reduce-scatter.16.cloned.1.call-done = bf16[192,2560]{1,0:T(8,128)(2,1)} async-done(((bf16[768,2560]{1,0:T(8,128)(2,1)}), bf16[192,2560]{1,0:T(8,128)(2,1)}) %reduce-scatter.16.cloned.1.call-update) | async-done | bytes 983056 | tf_op jit(solution)/shard_map/reduce_scatter | solution.py:54
  375.0 126.7 %all-gather.22.cloned.1.call-done = bf16[2560,1728]{1,0:T(8,128)(2,1)} async-done(((bf16[320,1728]{1,0:T(8,128)(2,1)}), bf16[2560,1728]{1,0:T(8,128)(2,1)}) %all-gather.22.cloned.1.call-update) | async-done | bytes 8847376 | tf_op jit(solution)/shard_map/all_gather | solution.py:110
  501.7 32.7 %all-gather.18.cloned.1.call-done = bf16[768,2560]{1,0:T(8,128)(2,1)} async-done(((bf16[192,2560]{1,0:T(8,128)(2,1)}), bf16[768,2560]{1,0:T(8,128)(2,1)}) %all-gather.18.cloned.1.call-update) | async-done | bytes 3932176 | tf_op jit(solution)/shard_map/all_gather | solution.py:50
  547.2 125.1 %all-gather.20.cloned.1.call-done = bf16[2560,1728]{1,0:T(8,128)(2,1)} async-done(((bf16[320,1728]{1,0:T(8,128)(2,1)}), bf16[2560,1728]{1,0:T(8,128)(2,1)}) %all-gather.20.cloned.1.call-update) | async-done | bytes 8847376 | tf_op jit(solution)/shard_map/all_gather | solution.py:109
  684.9 20.2 all-gather.26.cloned.1.call-done
  705.2 137.9 %all-gather.24.cloned.1.call-done = bf16[1728,2560]{0,1:T(8,128)(2,1)} async-done(((bf16[1728,320]{0,1:T(8,128)(2,1)}), bf16[1728,2560]{0,1:T(8,128)(2,1)}) %all-gather.24.cloned.1.call-update) | async-done | bytes 8847376 | tf_op jit(solution)/shard_map/all_gather | solution.py:111
  843.1 16.9 multiply_convert_fusion
  882.4 41.2 %reduce-scatter.20.cloned.1.call-done = bf16[192,2560]{1,0:T(8,128)(2,1)} async-done(((bf16[768,2560]{1,0:T(8,128)(2,1)}), bf16[192,2560]{1,0:T(8,128)(2,1)}) %reduce-scatter.20.cloned.1.call-update) | async-done | bytes 983056 | tf_op jit(solution)/shard_map/reduce_scatter | solution.py:54
  930.3 33.0 %all-gather.28.cloned.1.call-done = bf16[768,2560]{1,0:T(8,128)(2,1)} async-done(((bf16[192,2560]{1,0:T(8,128)(2,1)}), bf16[768,2560]{1,0:T(8,128)(2,1)}) %all-gather.28.cloned.1.call-update) | async-done | bytes 3932176 | tf_op jit(solution)/shard_map/all_gather | solution.py:50
  970.6 303.3 %while.29 = (s32[]{:T(128)}, f32[3072,2,80]{0,2,1:T(8,128)}, f32[3072,2,80]{0,2,1:T(8,128)}, f32[3,256,640]{1,0,2:T(4,128)}, s32[3]{0:T(128)S(1)}, /*index=5*/bf...) while((s32[]{:T(128)}, f32[3072,2,80]{0,2,1:T(8,128)}, ...), condition=%wide.region_12.13_spmd.clone, body=%wide.region_10.12_spmd.clone.sunk | while | flops 5132518400 | bytes 209357104 | solution.py:257
  1000.5 16.9 fusion.153
  1017.4 21.4 fusion.154
  1056.3 14.9 dynamic_update_slice.22
  1101.2 16.9 fusion.153
  1118.1 21.4 fusion.154
  1157.5 14.9 dynamic_update_slice.22
  1202.5 16.9 fusion.153
  1219.4 21.4 fusion.154
  1258.8 14.9 dynamic_update_slice.22
  1318.7 17.8 collective-permute-done.7
  1419.9 17.5 reduce-scatter.34.cloned.1.call-done
  1439.2 160.6 %reduce-scatter.32.cloned.1.call-done = bf16[1728,320]{0,1:T(8,128)(2,1)} async-done(((bf16[1728,2560]{0,1:T(8,128)(2,1)}), bf16[1728,320]{0,1:T(8,128)(2,1)}) %reduce-scatter.32.cloned.1.call-update) | async-done | bytes 1105936 | tf_op jit(solution)/shard_map/reduce_scatter | solution.py:327
  1602.6 160.0 %reduce-scatter.30.cloned.1.call-done = bf16[320,1728]{1,0:T(8,128)(2,1)} async-done(((bf16[2560,1728]{1,0:T(8,128)(2,1)}), bf16[320,1728]{1,0:T(8,128)(2,1)}) %reduce-scatter.30.cloned.1.call-update) | async-done | bytes 1105936 | tf_op jit(solution)/shard_map/reduce_scatter | solution.py:324
  1765.4 159.7 %reduce-scatter.28.cloned.1.call-done = bf16[320,1728]{1,0:T(8,128)(2,1)} async-done(((bf16[2560,1728]{1,0:T(8,128)(2,1)}), bf16[320,1728]{1,0:T(8,128)(2,1)}) %reduce-scatter.28.cloned.1.call-update) | async-done | bytes 1105936 | tf_op jit(solution)/shard_map/reduce_scatter | solution.py:321
  1927.8 76.4 %reduce-scatter.26.cloned.1.call-done = bf16[640,320]{0,1:T(8,128)(2,1)} async-done(((bf16[640,2560]{0,1:T(8,128)(2,1)}), bf16[640,320]{0,1:T(8,128)(2,1)}) %reduce-scatter.26.cloned.1.call-update) | async-done | bytes 409616 | tf_op jit(solution)/shard_map/reduce_scatter | solution.py:315
  2006.1 76.6 %reduce-scatter.24.cloned.1.call-done = bf16[320,640]{1,0:T(8,128)(2,1)} async-done(((bf16[2560,640]{1,0:T(8,128)(2,1)}), bf16[320,640]{1,0:T(8,128)(2,1)}) %reduce-scatter.24.cloned.1.call-update) | async-done | bytes 409616 | tf_op jit(solution)/shard_map/reduce_scatter | solution.py:306
  2084.7 42.7 %reduce-scatter.22.cloned.1.call-done = bf16[192,2560]{1,0:T(8,128)(2,1)} async-done(((bf16[768,2560]{1,0:T(8,128)(2,1)}), bf16[192,2560]{1,0:T(8,128)(2,1)}) %reduce-scatter.22.cloned.1.call-update) | async-done | bytes 983056 | tf_op jit(solution)/shard_map/reduce_scatter | solution.py:54
  2139.6 37.2 %all-reduce.6 = (bf16[2560]{0:T(1024)(128)(2,1)S(1)}, bf16[2560]{0:T(1024)(128)(2,1)S(1)}) all-reduce(bf16[2560]{0:T(1024)(128)(2,1)S(1)} %get-tuple-element.317, bf16[2560]{0:T(1024)(128)(2,1)S(1)} %get-tuple-element.318), channel_id=6, replica_groups=mesh['seq'=8,'tensor'=4] {'seq'}, use_global_device_ids=true, to_apply=%region_17.18.clone | all-reduce | flops 5120 | bytes 20480
  (327 shorter events, 564.0 us)
Async XLA Ops:
  7.2 119.2 %all-gather.12.cloned.1.call-start = ((), (), s32[]{:S(2)}) async-start(), calls=%async_computation.11 | async-start | bytes 4915200 | tf_op jit(solution)/shard_map/all_gather | solution.py:50
  54.1 105.3 %all-gather.14.cloned.1.call-start = ((), (), s32[]{:S(2)}) async-start(), calls=%async_computation.12 | async-start | bytes 3686400 | tf_op jit(solution)/shard_map/all_gather | solution.py:104
  55.0 248.5 %all-gather.16.cloned.1.call-start = ((), (), s32[]{:S(2)}) async-start(), calls=%async_computation.13 | async-start | bytes 3686400 | tf_op jit(solution)/shard_map/all_gather | solution.py:107
  55.9 308.1 %reduce-scatter.16.cloned.1.call-start = ((), (), s32[]{:S(2)}) async-start(), calls=%async_computation.14 | async-start | bytes 4915200 | tf_op jit(solution)/shard_map/reduce_scatter | solution.py:54
  130.2 36.5 %collective-permute-start.5 = (bf16[768,160]{0,1:T(8,128)(2,1)S(1)}, bf16[768,160]{0,1:T(8,128)(2,1)S(1)}, u32[]{:S(2)}, u32[]{:S(2)}) collective-permute-start(bf16[768,160]{0,1:T(8,128)(2,1)S(1)} %convolution_convert_fusion.10), channel_id=1, source_target_pairs={{0,4},{4,8},{8,12},{12,16},{16,20},{20,24},{24,28},{1,5},{5,9},{9,... | collective-permute-start | bytes 737288 | tf_op jit(solution)/shard_map/ppermute | solution.py:19
  131.5 45.7 %collective-permute-start.4 = (bf16[768,160]{0,1:T(8,128)(2,1)S(1)}, bf16[768,160]{0,1:T(8,128)(2,1)S(1)}, u32[]{:S(2)}, u32[]{:S(2)}) collective-permute-start(bf16[768,160]{0,1:T(8,128)(2,1)S(1)} %convolution_convert_fusion.10), channel_id=1, source_target_pairs={{0,8},{4,12},{8,16},{12,20},{16,24},{20,28},{1,9},{5,13},{9,17},{1... | collective-permute-start | bytes 737288 | tf_op jit(solution)/shard_map/ppermute | solution.py:19
  132.8 45.1 %collective-permute-start.3 = (bf16[768,160]{0,1:T(8,128)(2,1)S(1)}, bf16[768,160]{0,1:T(8,128)(2,1)}, u32[]{:S(2)}, u32[]{:S(2)}) collective-permute-start(bf16[768,160]{0,1:T(8,128)(2,1)S(1)} %convolution_convert_fusion.10), channel_id=1, source_target_pairs={{0,12},{4,16},{8,20},{12,24},{16,28},{1,13},{5,17},{9,21},{13,25},... | collective-permute-start | bytes 737288 | tf_op jit(solution)/shard_map/ppermute | solution.py:19
  143.4 35.7 %collective-permute-start.2 = (bf16[768,160]{0,1:T(8,128)(2,1)S(1)}, bf16[768,160]{0,1:T(8,128)(2,1)S(1)}, u32[]{:S(2)}, u32[]{:S(2)}) collective-permute-start(bf16[768,160]{0,1:T(8,128)(2,1)S(1)} %bitcast.270), channel_id=1, source_target_pairs={{0,4},{4,8},{8,12},{12,16},{16,20},{20,24},{24,28},{1,5},{5,9},{9,... | collective-permute-start | bytes 737288 | tf_op jit(solution)/shard_map/ppermute | solution.py:19
  145.4 33.7 %collective-permute-start.1 = (bf16[768,160]{0,1:T(8,128)(2,1)S(1)}, bf16[768,160]{0,1:T(8,128)(2,1)S(1)}, u32[]{:S(2)}, u32[]{:S(2)}) collective-permute-start(bf16[768,160]{0,1:T(8,128)(2,1)S(1)} %bitcast.271), channel_id=1, source_target_pairs={{0,8},{4,12},{8,16},{12,20},{16,24},{20,28},{1,9},{5,13},{9,17},{1... | collective-permute-start | bytes 737288 | tf_op jit(solution)/shard_map/ppermute | solution.py:19
  166.7 21.0 collective-permute-start
  311.4 190.3 %all-gather.22.cloned.1.call-start = ((), (), s32[]{:S(2)}) async-start(), calls=%async_computation.17 | async-start | bytes 10321920 | tf_op jit(solution)/shard_map/all_gather | solution.py:110
  314.3 220.1 %all-gather.18.cloned.1.call-start = ((), (), s32[]{:S(2)}) async-start(), calls=%async_computation.15 | async-start | bytes 4915200 | tf_op jit(solution)/shard_map/all_gather | solution.py:50
  368.2 304.2 %all-gather.20.cloned.1.call-start = ((), (), s32[]{:S(2)}) async-start(), calls=%async_computation.16 | async-start | bytes 10321920 | tf_op jit(solution)/shard_map/all_gather | solution.py:109
  371.0 334.2 %all-gather.26.cloned.1.call-start = ((), (), s32[]{:S(2)}) async-start(), calls=%async_computation.20 | async-start | bytes 4915200 | tf_op jit(solution)/shard_map/all_gather | solution.py:50
  371.7 471.3 %all-gather.24.cloned.1.call-start = ((), (), s32[]{:S(2)}) async-start(), calls=%async_computation.18 | async-start | bytes 10321920 | tf_op jit(solution)/shard_map/all_gather | solution.py:111
  374.6 549.0 %reduce-scatter.20.cloned.1.call-start = ((), (), s32[]{:S(2)}) async-start(), calls=%async_computation.21 | async-start | bytes 4915200 | tf_op jit(solution)/shard_map/reduce_scatter | solution.py:54
  882.4 81.0 %all-gather.28.cloned.1.call-start = ((), (), s32[]{:S(2)}) async-start(), calls=%async_computation.22 | async-start | bytes 4915200 | tf_op jit(solution)/shard_map/all_gather | solution.py:50
  930.2 488.0 %reduce-scatter.36.cloned.1.call-start = ((), (), s32[]{:S(2)}) async-start(), calls=%async_computation.30 | async-start | bytes 1474560
  1275.8 11.6 collective-permute-start.11
  1277.1 14.9 collective-permute-start.9
  1278.4 19.7 collective-permute-start.10
  1300.5 136.9 %reduce-scatter.34.cloned.1.call-start = ((), (), s32[]{:S(2)}) async-start(), calls=%async_computation.29 | async-start | bytes 1474560
  1300.8 11.0 collective-permute-start.8
  1302.3 16.4 collective-permute-start.6
  1303.6 32.9 %collective-permute-start.7 = (bf16[768,160]{0,1:T(8,128)(2,1)S(1)}, bf16[768,160]{0,1:T(8,128)(2,1)S(1)}, u32[]{:S(2)}, u32[]{:S(2)}) collective-permute-start(bf16[768,160]{0,1:T(8,128)(2,1)S(1)} %bitcast.276), channel_id=1, source_target_pairs={{8,0},{12,4},{16,8},{20,12},{24,16},{28,20},{9,1},{13,5},{17,9},{2... | collective-permute-start | bytes 737288 | tf_op jit(solution)/shard_map/ppermute | solution.py:19
  1339.1 260.7 %reduce-scatter.32.cloned.1.call-start = ((), (), s32[]{:S(2)}) async-start(), calls=%async_computation.28 | async-start | bytes 10321920 | tf_op jit(solution)/shard_map/reduce_scatter | solution.py:327
  1351.2 411.3 %reduce-scatter.30.cloned.1.call-start = ((), (), s32[]{:S(2)}) async-start(), calls=%async_computation.27 | async-start | bytes 10321920 | tf_op jit(solution)/shard_map/reduce_scatter | solution.py:324
  1363.3 561.7 %reduce-scatter.28.cloned.1.call-start = ((), (), s32[]{:S(2)}) async-start(), calls=%async_computation.26 | async-start | bytes 10321920 | tf_op jit(solution)/shard_map/reduce_scatter | solution.py:321
  1375.8 628.3 %reduce-scatter.26.cloned.1.call-start = ((), (), s32[]{:S(2)}) async-start(), calls=%async_computation.25 | async-start | bytes 3686400 | tf_op jit(solution)/shard_map/reduce_scatter | solution.py:315
  1384.2 698.5 %reduce-scatter.24.cloned.1.call-start = ((), (), s32[]{:S(2)}) async-start(), calls=%async_computation.24 | async-start | bytes 3686400 | tf_op jit(solution)/shard_map/reduce_scatter | solution.py:306
  1394.5 732.8 %reduce-scatter.22.cloned.1.call-start = ((), (), s32[]{:S(2)}) async-start(), calls=%async_computation.23 | async-start | bytes 4915200 | tf_op jit(solution)/shard_map/reduce_scatter | solution.py:54
  1404.5 773.0 %reduce-scatter.18.cloned.1.call-start = ((), (), s32[]{:S(2)}) async-start(), calls=%async_computation.19 | async-start | bytes 4915200 | tf_op jit(solution)/shard_map/reduce_scatter | solution.py:54
  (42 other events, 6037.0 us)
Sparse Core Ops, SparseCore 0:
  54.3 30.2 all-gather.11
  87.3 72.0 all-gather.13
  162.2 74.5 all-gather.15
  311.5 52.3 reduce-scatter.15
  366.8 134.8 all-gather.21
  503.2 31.1 all-gather.17
  537.4 134.8 all-gather.19
  674.0 31.1 all-gather.25
  708.2 134.8 all-gather.23
  882.5 41.0 reduce-scatter.19
  930.3 32.9 all-gather.27
  1300.6 69.3 reduce-scatter.35
  1374.0 63.3 reduce-scatter.33
  1440.9 158.7 reduce-scatter.31
  1603.7 158.7 reduce-scatter.29
  1766.1 158.9 reduce-scatter.27
  1928.9 75.2 reduce-scatter.25
  2007.6 75.0 reduce-scatter.23
  2085.4 41.8 reduce-scatter.21
  2129.7 42.8 reduce-scatter.17
where the time goes:
time: 2200 us; the launch traced here: 2190 us
  waiting for transfers between devices  1330 us (60%)
  matrix products  402 us (18%)
  other arithmetic  158 us (7%)
  blocking collectives  154 us (7%)
  local copies, waits for them, and re-layouts  83.2 us (4%)
  starting transfers between devices  35.6 us (2%)
    reduce_scatter x1, waiting for transfers between devices, per_device(): lax.psum_scatter(down_grad.astype(jnp.bfloat16), 'seq', scatter_dimension...  161 us
    reduce_scatter x1, waiting for transfers between devices, per_device(): lax.psum_scatter(up_grad.astype(jnp.bfloat16), 'seq', scatter_dimension=0...  160 us
    reduce_scatter x1, waiting for transfers between devices, per_device(): lax.psum_scatter(gate_grad.astype(jnp.bfloat16), 'seq', scatter_dimension...  160 us
    all_gather x1, waiting for transfers between devices, per_device(): lax.all_gather(down_weight.astype(wide), 'seq', axis=1, tiled=True)  138 us
    reduce_scatter x4, waiting for transfers between devices, sum_rows(): lax.psum_scatter(term_fn(jnp.int32(0), lax.axis_size('tensor') * own_rows...  133 us
    all_gather x1, waiting for transfers between devices, per_device(): lax.all_gather(up_weight.astype(wide), 'seq', axis=0, tiled=True)  127 us
    all_gather x1, waiting for transfers between devices, per_device(): lax.all_gather(gate_weight.astype(wide), 'seq', axis=0, tiled=True)  125 us
    all_gather x4, waiting for transfers between devices, gather_rows(): return lax.all_gather(values, 'tensor', axis=0, tiled=True)  86 us
  transfers between devices with their start and end apart: 32, of which 23 were waited for; matrix products, arithmetic and copies ran while one was open for 12% of the time, Pallas kernels for 0%

commit v1 on v0

v1 whole, which is shorter than its diff:
```python
import functools

import jax
import jax.numpy as jnp
from jax import lax
from jax.experimental import pallas as pl
from jax.experimental.pallas import tpu as pltpu
from jax.sharding import Mesh
from jax.sharding import PartitionSpec as P

HEADS = 32
KV = 8
HD = 80
SEQS = 2
DOC_MOST = 2000
GROUP = HEADS // KV

eps = 1e-05
rope_base = 10000.0
LOG2E = 1.4426950408889634
SCORE_LOG2 = HD ** (-0.5) * LOG2E
SCORE_SCALE = HD ** (-0.5)
LOW = -1e30
BQ = 256
KB = 256
WIDE = jnp.bfloat16
F32 = jnp.float32
VMEM_BYTES = 48 * 1024 * 1024

SWAP = [(0, 1), (1, 0)]


def dot(a, b, ca, cb):
    return lax.dot_general(a, b, (((ca,), (cb,)), ((), ())), preferred_element_type=F32)


def turn_kernel(rotary, heads, index_ref, rows_ref, cos_ref, sin_ref, out_ref):
    own = rows_ref.shape[0] // 8
    half = HD // 2
    for pair in range(4):
        parts = [
            rows_ref[pl.ds(pl.multiple_of(index_ref[2 * pair + k] * own, own), own), :].astype(F32)
            for k in range(2)
        ]
        turned = jnp.concatenate(parts, axis=0).T
        lanes = slice(pair * 2 * own, (pair + 1) * 2 * own)
        cos_tab, sin_tab = cos_ref[:, lanes], sin_ref[:, lanes]
        for h in range(heads):
            front, back = turned[h * HD : h * HD + half], turned[h * HD + half : (h + 1) * HD]
            if h < rotary:
                front, back = front * cos_tab - back * sin_tab, back * cos_tab + front * sin_tab
            out_ref[h * HD : (h + 1) * HD, lanes] = jnp.concatenate([front, back], axis=0).astype(
                out_ref.dtype
            )


def to_columns(rows, index, cos_tab, sin_tab, rotary, heads):
    count = rows.shape[0]
    full = lambda shape: pl.BlockSpec(shape, lambda i, s: (0, 0))
    return pl.pallas_call(
        functools.partial(turn_kernel, rotary, heads),
        grid_spec=pltpu.PrefetchScalarGridSpec(
            num_scalar_prefetch=1,
            grid=(1,),
            in_specs=[full(rows.shape), full(cos_tab.shape), full(sin_tab.shape)],
            out_specs=full((heads * HD, count)),
        ),
        out_shape=jax.ShapeDtypeStruct((heads * HD, count), WIDE),
        compiler_params=pltpu.CompilerParams(vmem_limit_bytes=VMEM_BYTES),
    )(index, rows, cos_tab, sin_tab)


def back_kernel(rotary, heads, index_ref, cols_ref, cos_ref, sin_ref, out_ref):
    own = cols_ref.shape[1] // 8
    half = HD // 2
    width = out_ref.shape[1]
    for pair in range(4):
        lanes = slice(pair * 2 * own, (pair + 1) * 2 * own)
        cos_tab, sin_tab = cos_ref[:, lanes], sin_ref[:, lanes]
        parts = []
        for h in range(heads):
            front = cols_ref[h * HD : h * HD + half, lanes].astype(F32)
            back = cols_ref[h * HD + half : (h + 1) * HD, lanes].astype(F32)
            if h < rotary:
                front, back = front * cos_tab + back * sin_tab, back * cos_tab - front * sin_tab
            parts += [front, back]
        if width > heads * HD:
            parts.append(jnp.zeros((width - heads * HD, 2 * own), F32))
        rows = jnp.concatenate(parts, axis=0).T.astype(out_ref.dtype)
        for k in range(2):
            first = pl.multiple_of(index_ref[2 * pair + k] * own, own)
            out_ref[pl.ds(first, own), :] = rows[k * own : (k + 1) * own]


def to_rows(cols, index, cos_tab, sin_tab, rotary, heads, width):
    count = cols.shape[1]
    full = lambda shape: pl.BlockSpec(shape, lambda i, s: (0, 0))
    return pl.pallas_call(
        functools.partial(back_kernel, rotary, heads),
        grid_spec=pltpu.PrefetchScalarGridSpec(
            num_scalar_prefetch=1,
            grid=(1,),
            in_specs=[full(cols.shape), full(cos_tab.shape), full(sin_tab.shape)],
            out_specs=full((count, width)),
        ),
        out_shape=jax.ShapeDtypeStruct((count, width), WIDE),
        compiler_params=pltpu.CompilerParams(vmem_limit_bytes=VMEM_BYTES),
    )(index, cols, cos_tab, sin_tab)


def allowed_mask(block, starts, own_places):
    places = block * KB + lax.broadcasted_iota(jnp.int32, (KB, 1), 0)
    return (places >= starts) & (places <= own_places)


def attend_kernel(span_before, bounds_ref, q_ref, kv_ref, start_ref, out_ref, log_ref, k_rows, acc):
    step = pl.program_id(0)
    span = kv_ref.shape[1]

    @pl.when(step == 0)
    def _():
        for j in range(span // KB):
            k_rows[j * KB : (j + 1) * KB, :] = (
                kv_ref[0:HD, j * KB : (j + 1) * KB].astype(F32).T.astype(WIDE)
            )

    starts = start_ref[0:1, :]
    own_places = span_before + step * BQ + lax.broadcasted_iota(jnp.int32, (1, BQ), 1)
    acc[...] = jnp.zeros_like(acc)

    def one(masked, block, carry):
        first = pl.multiple_of(block * KB, KB)
        keys = k_rows[pl.ds(first, KB), :]
        values = kv_ref[HD : 2 * HD, pl.ds(first, KB)]
        if masked:
            mask = allowed_mask(block, starts, own_places)
        fresh = []
        for h in range(GROUP):
            top, total = carry[2 * h], carry[2 * h + 1]
            scores = dot(keys, q_ref[h * HD : (h + 1) * HD, :], 1, 0) * SCORE_LOG2
            if masked:
                scores = jnp.where(mask, scores, LOW)
            new_top = jnp.maximum(top, jnp.max(scores, axis=0, keepdims=True))
            probs = jnp.exp2(scores - new_top)
            fade = jnp.exp2(top - new_top)
            total = fade * total + jnp.sum(probs, axis=0, keepdims=True)
            acc[h] = fade * acc[h] + dot(values, probs.astype(WIDE), 1, 0)
            fresh += [new_top, total]
        return tuple(fresh)

    carry = (jnp.full((1, BQ), LOW, F32), jnp.zeros((1, BQ), F32)) * GROUP
    lo, full_lo, full_hi, hi = [bounds_ref[k, step] for k in range(4)]
    carry = lax.fori_loop(lo, full_lo, functools.partial(one, True), carry)
    carry = lax.fori_loop(full_lo, full_hi, functools.partial(one, False), carry)
    carry = lax.fori_loop(full_hi, hi, functools.partial(one, True), carry)
    for h in range(GROUP):
        top, total = carry[2 * h], carry[2 * h + 1]
        out_ref[h * HD : (h + 1) * HD, :] = (acc[h] / total).astype(WIDE)
        log_ref[h : h + 1, :] = top + jnp.log2(total)


def attend(q_cols, kv_cols, starts, bounds):
    count, span = q_cols.shape[1], kv_cols.shape[1]
    return pl.pallas_call(
        functools.partial(attend_kernel, span - count),
        grid_spec=pltpu.PrefetchScalarGridSpec(
            num_scalar_prefetch=1,
            grid=(count // BQ,),
            in_specs=[
                pl.BlockSpec((GROUP * HD, BQ), lambda i, s: (0, i)),
                pl.BlockSpec((2 * HD, span), lambda i, s: (0, 0)),
                pl.BlockSpec((1, BQ), lambda i, s: (0, i)),
            ],
            out_specs=[
                pl.BlockSpec((GROUP * HD, BQ), lambda i, s: (0, i)),
                pl.BlockSpec((8, BQ), lambda i, s: (0, i)),
            ],
            scratch_shapes=[pltpu.VMEM((span, HD), WIDE), pltpu.VMEM((GROUP, HD, BQ), F32)],
        ),
        out_shape=[
            jax.ShapeDtypeStruct((GROUP * HD, count), WIDE),
            jax.ShapeDtypeStruct((8, count), F32),
        ],
        compiler_params=pltpu.CompilerParams(vmem_limit_bytes=VMEM_BYTES),
    )(bounds, q_cols, kv_cols, starts)


def attend_back_kernel(
    span_before,
    bounds_ref,
    q_ref,
    kv_ref,
    start_ref,
    out_ref,
    log_ref,
    grad_ref,
    dq_ref,
    dkv_ref,
    k_rows,
    v_rows,
    q_rows,
    g_rows,
    dk,
    dv,
    probs_all,
    grads_all,
    dq,
):
    step = pl.program_id(0)
    span = kv_ref.shape[1]

    @pl.when(step == 0)
    def _():
        for j in range(span // KB):
            lanes = slice(j * KB, (j + 1) * KB)
            k_rows[lanes, :] = kv_ref[0:HD, lanes].astype(F32).T.astype(WIDE)
            v_rows[lanes, :] = kv_ref[HD : 2 * HD, lanes].astype(F32).T.astype(WIDE)
        dk[...] = jnp.zeros_like(dk)
        dv[...] = jnp.zeros_like(dv)

    starts = start_ref[0:1, :]
    own_places = span_before + step * BQ + lax.broadcasted_iota(jnp.int32, (1, BQ), 1)
    dq[...] = jnp.zeros_like(dq)
    deltas = []
    for h in range(GROUP):
        part = slice(h * HD, (h + 1) * HD)
        q_f32, g_f32 = q_ref[part, :].astype(F32), grad_ref[part, :].astype(F32)
        q_rows[h * BQ : (h + 1) * BQ, :] = q_f32.T.astype(WIDE)
        g_rows[h * BQ : (h + 1) * BQ, :] = g_f32.T.astype(WIDE)
        deltas.append(jnp.sum(g_f32 * out_ref[part, :].astype(F32), axis=0, keepdims=True))

    def one(masked, block, carry):
        first = pl.multiple_of(block * KB, KB)
        rows = pl.ds(first, KB)
        keys, values = k_rows[rows, :], v_rows[rows, :]
        key_cols = kv_ref[0:HD, rows]
        if masked:
            mask = allowed_mask(block, starts, own_places)
        for h in range(GROUP):
            part = slice(h * HD, (h + 1) * HD)
            lanes = slice(h * BQ, (h + 1) * BQ)
            scores = dot(keys, q_ref[part, :], 1, 0) * SCORE_LOG2 - log_ref[h : h + 1, :]
            if masked:
                scores = jnp.where(mask, scores, LOW)
            probs = jnp.exp2(scores)
            grad_probs = dot(values, grad_ref[part, :], 1, 0)
            grad_scores = (probs * (grad_probs - deltas[h])).astype(WIDE)
            probs_all[:, lanes] = probs.astype(WIDE)
            grads_all[:, lanes] = grad_scores
            dq[h] += dot(key_cols, grad_scores, 1, 0)
        dv[rows, :] += dot(probs_all[...], g_rows[...], 1, 0)
        dk[rows, :] += dot(grads_all[...], q_rows[...], 1, 0)
        return carry

    lo, full_lo, full_hi, hi = [bounds_ref[k, step] for k in range(4)]
    lax.fori_loop(lo, full_lo, functools.partial(one, True), 0)
    lax.fori_loop(full_lo, full_hi, functools.partial(one, False), 0)
    lax.fori_loop(full_hi, hi, functools.partial(one, True), 0)
    for h in range(GROUP):
        dq_ref[h * HD : (h + 1) * HD, :] = dq[h] * SCORE_SCALE

    @pl.when(step == pl.num_programs(0) - 1)
    def _():
        for j in range(span // KB):
            lanes = slice(j * KB, (j + 1) * KB)
            dkv_ref[0:HD, lanes] = dk[lanes, :].T * SCORE_SCALE
            dkv_ref[HD : 2 * HD, lanes] = dv[lanes, :].T


def attend_back(q_cols, kv_cols, starts, bounds, out_cols, logs, grad_cols):
    count, span = q_cols.shape[1], kv_cols.shape[1]
    wide_block = pl.BlockSpec((GROUP * HD, BQ), lambda i, s: (0, i))
    return pl.pallas_call(
        functools.partial(attend_back_kernel, span - count),
        grid_spec=pltpu.PrefetchScalarGridSpec(
            num_scalar_prefetch=1,
            grid=(count // BQ,),
            in_specs=[
                wide_block,
                pl.BlockSpec((2 * HD, span), lambda i, s: (0, 0)),
                pl.BlockSpec((1, BQ), lambda i, s: (0, i)),
                wide_block,
                pl.BlockSpec((8, BQ), lambda i, s: (0, i)),
                wide_block,
            ],
            out_specs=[wide_block, pl.BlockSpec((2 * HD, span), lambda i, s: (0, 0))],
            scratch_shapes=[
                pltpu.VMEM((span, HD), WIDE),
                pltpu.VMEM((span, HD), WIDE),
                pltpu.VMEM((GROUP * BQ, HD), WIDE),
                pltpu.VMEM((GROUP * BQ, HD), WIDE),
                pltpu.VMEM((span, HD), F32),
                pltpu.VMEM((span, HD), F32),
                pltpu.VMEM((KB, GROUP * BQ), WIDE),
                pltpu.VMEM((KB, GROUP * BQ), WIDE),
                pltpu.VMEM((GROUP, HD, BQ), F32),
            ],
        ),
        out_shape=[
            jax.ShapeDtypeStruct((GROUP * HD, count), F32),
            jax.ShapeDtypeStruct((2 * HD, span), F32),
        ],
        compiler_params=pltpu.CompilerParams(vmem_limit_bytes=VMEM_BYTES),
    )(bounds, q_cols, kv_cols, starts, out_cols, logs, grad_cols)


def shifted(block, distance):
    count = lax.axis_size("z")
    route = [(i - distance, i) for i in range(count) if 0 <= i - distance < count]
    return lax.ppermute(block, "z", route)


def gather_plane(block):
    half = block.shape[0] // 2
    over_x = lax.ppermute(block, "x", SWAP)
    over_y = lax.ppermute(block, "y", SWAP)
    far_top = lax.ppermute(over_y[:half], "x", SWAP)
    far_low = lax.ppermute(over_x[half:], "y", SWAP)
    mine = [block, over_x, over_y, far_top, far_low]
    other = [lax.ppermute(part, "c", SWAP) for part in mine]
    return jnp.concatenate(mine + other, axis=0)


def sum_plane(term):
    own = term.shape[0] // 8
    half = own // 2
    low = term.astype(WIDE)
    got = lax.ppermute(low[4 * own :], "c", SWAP)
    total = low[: 4 * own].astype(F32) + got.astype(F32)
    far = total[3 * own :].astype(WIDE)
    top = lax.ppermute(far[:half], "x", SWAP)
    bottom = lax.ppermute(far[half:], "y", SWAP)
    to_x = jnp.concatenate(
        [total[own : own + half], total[own + half : 2 * own] + bottom.astype(F32)], axis=0
    ).astype(WIDE)
    to_y = jnp.concatenate(
        [total[2 * own : 2 * own + half] + top.astype(F32), total[2 * own + half : 3 * own]],
        axis=0,
    ).astype(WIDE)
    over_x = lax.ppermute(to_x, "x", SWAP)
    over_y = lax.ppermute(to_y, "y", SWAP)
    return total[:own] + over_x.astype(F32) + over_y.astype(F32)


def share_columns(block, first_y):
    half = block.shape[1] // 2
    keep = jnp.where(first_y, block[:, :half], block[:, half:])
    give = jnp.where(first_y, block[:, half:], block[:, :half])
    got = lax.ppermute(give, "y", SWAP)
    return jnp.concatenate([jnp.where(first_y, keep, got), jnp.where(first_y, got, keep)], axis=0)


def unshare_columns(block, first_y):
    half = block.shape[0] // 2
    keep = jnp.where(first_y, block[:half], block[half:])
    give = jnp.where(first_y, block[half:], block[:half])
    got = lax.ppermute(give, "y", SWAP)
    return jnp.where(first_y, keep, got), jnp.where(first_y, got, keep)


def gather_z(block):
    return lax.all_gather(block, "z", axis=0, tiled=True)


def sum_z(block):
    return lax.psum_scatter(block.astype(WIDE), "z", scatter_dimension=0, tiled=True)


def padded(block, multiple=128):
    extra = -block.shape[1] % multiple
    return jnp.pad(block, ((0, 0), (0, extra))) if extra else block


def norm_back(gradient, normed, inverse, gain_vec):
    scaled = gradient * gain_vec
    return inverse * (scaled - normed * jnp.mean(scaled * normed, axis=-1, keepdims=True))


def per_device(
    inputs,
    segments,
    positions,
    gain_attn,
    query_weight,
    key_weight,
    value_weight,
    out_weight,
    gain_mlp,
    gate_weight,
    up_weight,
    down_weight,
    cotangent,
):
    own = inputs.shape[0]
    count = 8 * own
    length = segments.shape[0] // SEQS
    reach = (DOC_MOST - 2) // count + 1
    if length % count == 0:
        reach = min(reach, length // count - 1)
    span = (reach + 1) * count
    z, y = lax.axis_index("z"), lax.axis_index("y")
    x, c = lax.axis_index("x"), lax.axis_index("c")
    first_y = y == 0

    w_q, w_k, w_v, w_g, w_u = [
        w.astype(WIDE) for w in (query_weight, key_weight, value_weight, gate_weight, up_weight)
    ]
    w_o, w_d = out_weight.T.astype(WIDE), down_weight.T.astype(WIDE)
    nq, nk, nf = w_q.shape[1] // 2, w_k.shape[1] // 2, w_g.shape[1] // 2
    rows_w = w_q.shape[0]
    gains = gather_z(
        lax.all_gather(jnp.stack([gain_attn, gain_mlp], 1).astype(WIDE), "y", axis=0, tiled=True)
    ).astype(F32)
    gain_first, gain_second = gains[:, 0], gains[:, 1]
    halves = lambda w: (w[:, : w.shape[1] // 2], w[:, w.shape[1] // 2 :])
    interleave = lambda *ws: jnp.concatenate(
        [padded(jnp.concatenate([halves(w)[i] for w in ws], axis=1)) for i in range(2)], axis=1
    )
    full_a = gather_z(share_columns(interleave(w_q, w_k, w_v), first_y))
    full_o = gather_z(share_columns(w_o, first_y))
    full_g = gather_z(share_columns(interleave(w_g), first_y))
    full_u = gather_z(share_columns(interleave(w_u), first_y))
    full_d = gather_z(share_columns(interleave(w_d), first_y))

    other_positions = lax.ppermute(positions, "y", SWAP)
    token_positions = jnp.where(
        first_y,
        jnp.concatenate([positions, other_positions]),
        jnp.concatenate([other_positions, positions]),
    )
    frequency = rope_base ** (-(jnp.arange(HD // 2, dtype=F32) * 2.0 / HD))
    angles = frequency[:, None] * token_positions.astype(F32)[None, :]
    cos_tab, sin_tab = jnp.cos(angles), jnp.sin(angles)
    places = jnp.arange(8, dtype=jnp.int32)
    flips = places ^ (y * 4 + x * 2 + c).astype(jnp.int32)
    index = (flips % 2) * 4 + flips // 2
    padded_segs = jnp.concatenate([jnp.full((reach * count,), -1, jnp.int32), segments])
    key_segs = lax.dynamic_slice_in_dim(padded_segs, z * count, span, 0)
    query_segs = lax.dynamic_slice_in_dim(segments, z * count, count, 0)
    starts = jnp.sum((key_segs[:, None] < query_segs[None, :]).astype(jnp.int32), axis=0)
    first_rows = jnp.arange(count // BQ, dtype=jnp.int32) * BQ
    lo = starts[first_rows] // KB
    hi = (reach * count + first_rows + BQ + KB - 1) // KB
    full_lo = jnp.clip((starts[first_rows + BQ - 1] + KB - 1) // KB, lo, hi)
    full_hi = jnp.clip((reach * count + first_rows + 1) // KB, full_lo, hi)
    bounds = jnp.stack([lo, full_lo, full_hi, hi])
    starts = starts[None, :]

    x_all = gather_plane(inputs).astype(F32)
    inverse_all = lax.rsqrt(jnp.mean(x_all * x_all, axis=-1, keepdims=True) + eps)
    h_one = (x_all * inverse_all * gain_first).astype(WIDE)
    qkv = dot(h_one, full_a, 1, 0)
    turned = to_columns(qkv, index, cos_tab, sin_tab, GROUP + 1, GROUP + 2)
    q_cols, kv_own = turned[: GROUP * HD], turned[GROUP * HD :]
    kv_cols = jnp.concatenate(
        [shifted(kv_own, distance) for distance in range(reach, 0, -1)] + [kv_own], axis=1
    )
    out_cols, logs = attend(q_cols, kv_cols, starts, bounds)
    attended = to_rows(out_cols, index, cos_tab, sin_tab, 0, GROUP, GROUP * HD)
    input_f32 = inputs.astype(F32)
    inverse_one = lax.rsqrt(jnp.mean(input_f32 * input_f32, axis=-1, keepdims=True) + eps)
    normed_one = input_f32 * inverse_one
    x_mid = input_f32 + sum_plane(dot(attended, full_o, 1, 1))

    inverse_two = lax.rsqrt(jnp.mean(x_mid * x_mid, axis=-1, keepdims=True) + eps)
    normed_two = x_mid * inverse_two
    h_two = gather_plane((normed_two * gain_second).astype(WIDE))
    grad_mix = gather_plane(cotangent)
    gate_pre = dot(h_two, full_g, 1, 0)
    up_pre = dot(h_two, full_u, 1, 0)
    sigmoid_gate = jax.nn.sigmoid(gate_pre)
    hidden = (gate_pre * sigmoid_gate * up_pre).astype(WIDE)
    output = (x_mid + sum_plane(dot(hidden, full_d, 1, 1))).astype(WIDE)

    grad_hidden = dot(grad_mix, full_d, 1, 0)
    grad_gate = (
        grad_hidden * up_pre * sigmoid_gate * (1.0 + gate_pre * (1.0 - sigmoid_gate))
    ).astype(WIDE)
    grad_up = (grad_hidden * gate_pre * sigmoid_gate).astype(WIDE)
    grad_h_two = sum_plane(dot(grad_gate, full_g, 1, 1) + dot(grad_up, full_u, 1, 1))
    down_grad = sum_z(dot(grad_mix, hidden, 0, 0))
    gate_grad = sum_z(dot(h_two, grad_gate, 0, 0))
    up_grad = sum_z(dot(h_two, grad_up, 0, 0))
    grad_mid = cotangent.astype(F32) + norm_back(grad_h_two, normed_two, inverse_two, gain_second)
    grad_branch = gather_plane(grad_mid.astype(WIDE))

    grad_attended = dot(grad_branch, full_o, 1, 0).astype(WIDE)
    out_grad = sum_z(dot(grad_branch, attended, 0, 0))
    grad_cols = to_columns(grad_attended, index, cos_tab, sin_tab, 0, GROUP)
    dq_cols, dkv_cols = attend_back(q_cols, kv_cols, starts, bounds, out_cols, logs, grad_cols)
    dkv_own = dkv_cols[:, reach * count :]
    for distance in range(1, reach + 1):
        first = (reach - distance) * count
        dkv_own = dkv_own + shifted(
            dkv_cols[:, first : first + count].astype(WIDE), -distance
        ).astype(F32)
    grad_qkv = to_rows(
        jnp.concatenate([dq_cols, dkv_own], axis=0),
        index,
        cos_tab,
        sin_tab,
        GROUP + 1,
        GROUP + 2,
        full_a.shape[1],
    )
    grad_h_one = sum_plane(dot(grad_qkv, full_a, 1, 1))
    qkv_grad = sum_z(dot(h_one, grad_qkv, 0, 0))
    input_grad = (grad_mid + norm_back(grad_h_one, normed_one, inverse_one, gain_first)).astype(
        WIDE
    )

    def columns(summed, width):
        one, two = unshare_columns(summed, first_y)
        return jnp.concatenate([one[:, :width], two[:, :width]], axis=1).astype(F32)

    down_out = columns(down_grad, nf).T
    gate_out = columns(gate_grad, nf)
    up_out = columns(up_grad, nf)
    o_out = columns(out_grad, nq).T
    one, two = unshare_columns(qkv_grad, first_y)
    pick = lambda a, b: jnp.concatenate([one[:, a:b], two[:, a:b]], axis=1).astype(F32)
    q_out, k_out, v_out = pick(0, nq), pick(nq, nq + nk), pick(nq + nk, nq + 2 * nk)

    def row_sums(weight, grad):
        return jnp.sum(weight.astype(F32) * grad, axis=1)

    gain_sums = jnp.stack(
        [
            row_sums(w_q, q_out) + row_sums(w_k, k_out) + row_sums(w_v, v_out),
            row_sums(w_g, gate_out) + row_sums(w_u, up_out),
        ]
    )
    gain_sums = gain_sums + lax.ppermute(gain_sums, "x", SWAP)
    gain_sums = gain_sums + lax.ppermute(gain_sums, "c", SWAP)
    gain_one_out = gain_sums[0] / gain_attn.astype(WIDE).astype(F32)
    gain_two_out = gain_sums[1] / gain_mlp.astype(WIDE).astype(F32)
    return (
        output,
        input_grad,
        gain_one_out,
        q_out,
        k_out,
        v_out,
        o_out,
        gain_two_out,
        gate_out,
        up_out,
        down_out,
    )


def solution(mesh):
    seq, tensor = mesh.shape["seq"], mesh.shape["tensor"]
    grid = Mesh(
        mesh.devices.reshape(seq // 2, 2, tensor // 2, 2), ("z", "y", "x", "c")
    )
    rows, cols = ("z", "y"), ("x", "c")
    tokens, weight, weight_t = P(rows + cols, None), P(rows, cols), P(cols, rows)
    in_specs = (
        tokens,
        P(),
        P(rows),
        P(rows),
        weight,
        weight,
        weight,
        weight_t,
        P(rows),
        weight,
        weight,
        weight_t,
        tokens,
    )
    out_specs = (
        tokens,
        tokens,
        P(rows),
        weight,
        weight,
        weight,
        weight_t,
        P(rows),
        weight,
        weight,
        weight_t,
    )
    return jax.shard_map(
        per_device, mesh=grid, in_specs=in_specs, out_specs=out_specs, check_vma=False
    )
```

time: 2200 us -> 964 us (0.44)
  waiting for transfers between devices: 1330 us -> 446 us
  matrix products: 402 us -> 148 us
  blocking collectives: 154 us -> 35.8 us
  Pallas kernels: 0 us -> 63.5 us
  other arithmetic: 158 us -> 101 us
  starting transfers between devices: 35.6 us -> 64.6 us
    reduce_scatter x9 -> x5, waiting for transfers between devices: 767 us -> 114 us  [sum_z(): lax.psum_scatter(block.astype(WIDE), 'z', scatter_dimension=0, tiled=True)]
    all_gather x9 -> x5, waiting for transfers between devices: 488 us -> 87.9 us  [gather_z(): return lax.all_gather(block, 'z', axis=0, tiled=True)]
    dot_general x42 -> x15, matrix products: 402 us -> 148 us  [dot(): lax.dot_general(a, b, (((ca,), (cb,)), ((), ())), preferred_element_type=...]
    ppermute x12 -> x71, waiting for transfers between devices: 56.8 us -> 244 us  [the longest x4 58 us: gather_plane(): over_y = lax.ppermute(block, 'y', SWAP)]
    convert_element_type x25 -> x8, other arithmetic: 98.8 us -> 6.32 us  [the longest x2 3.02 us: per_device(): w.astype(WIDE)]
    unnamed x2 -> x0, blocking collectives: 76 us -> none
    pallas_call x0 -> x6, Pallas kernels: none -> 63.5 us  [the longest x1 31.7 us: attend_back(): pl.pallas_call(functools.partial(attend_back_kernel, span - count), grid_...]
    dynamic_update_slice x12 -> x0, local copies, waits for them, and re-layouts: 49.7 us -> none  [the longest x6 46.8 us: per_device(): lax.scan(backward_block, (zero_acc, zero_acc), numbers)]
  transfers between devices with their start and end apart: 32 -> 81, of which waited for: 23 -> 36; matrix products, arithmetic and copies ran while one was open for 12% -> 26% of each run, Pallas kernels for 0% -> 7%
where the time goes in v1:
time: 964 us; the launch traced here: 957 us
  waiting for transfers between devices  446 us (46%)
  matrix products  148 us (15%)
  other arithmetic  101 us (10%)
  local copies, waits for them, and re-layouts  82 us (9%)
  starting transfers between devices  64.6 us (7%)
  Pallas kernels  63.5 us (7%)
  blocking collectives  35.8 us (4%)
  between operations  15.9 us (2%)
    dot_general x15, matrix products, dot(): lax.dot_general(a, b, (((ca,), (cb,)), ((), ())), preferred_element_type=...  148 us
    reduce_scatter x5, waiting for transfers between devices, sum_z(): lax.psum_scatter(block.astype(WIDE), 'z', scatter_dimension=0, tiled=True)  114 us
    all_gather x5, waiting for transfers between devices, gather_z(): return lax.all_gather(block, 'z', axis=0, tiled=True)  87.9 us
    ppermute x4, waiting for transfers between devices, gather_plane(): over_y = lax.ppermute(block, 'y', SWAP)  58 us
    unnamed x214, local copies, waits for them, and re-layouts  55.2 us
    ppermute x4, waiting for transfers between devices, sum_plane(): over_y = lax.ppermute(to_y, 'y', SWAP)  41.3 us
    ppermute x5, waiting for transfers between devices, unshare_columns(): got = lax.ppermute(give, 'y', SWAP)  40.2 us
    pallas_call x1, Pallas kernels, attend_back(): pl.pallas_call(functools.partial(attend_back_kernel, span - count), grid_...  31.7 us
  transfers between devices with their start and end apart: 81, of which 36 were waited for; matrix products, arithmetic and copies ran while one was open for 26% of the time, Pallas kernels for 7%

profile of v1, /device:TPU:0, one launch (start us, length us, event | category | flops | bytes accessed | tf_op | source)
XLA Modules:
  0.0 957.0 jit_solution(4319526240826010110)
XLA Ops:
  26.6 22.1 %all-gather = bf16[2,320,2]{1,2,0:T(2,128)(2,1)S(1)} all-gather(bf16[1,320,2]{1,2,0:T(2,128)(2,1)S(1)} %maximum_bitcast_fusion), channel_id=1, replica_groups=mesh['z'=4,'y'=2,'x'=2,'c'=2] {'y'}, dimensions={0}, use_global_device_ids=true | all-gather | bytes 3840 | tf_op jit(solution)/shard_map/all_gather | solution.py:412
  48.7 13.7 %all_gather.22 = bf16[2560,2]{0,1:T(2,128)(2,1)S(1)} all-gather(bf16[640,2]{0,1:T(2,128)(2,1)S(1)} %reshape.405), channel_id=1, replica_groups=mesh['z'=4,'y'=2,'x'=2,'c'=2] {'z'}, dimensions={0}, use_global_device_ids=true | all-gather | bytes 12800 | tf_op jit(solution)/shard_map/all_gather | solution.py:362
  106.9 7.7 fusion.6.rows_ref
  133.8 27.3 %shard_map.213 = (bf16[320,1536]{1,0:T(8,128)(2,1)S(1)}, f32[8,1536]{1,0:T(8,128)S(1)}) custom-call(s32[4,6]{1,0:T(4,128)S(1)} %pad_add_fusion.bounds_ref, bf16[320,1536]{1,0:T(8,128)(2,1)S(1)} %slice.405.q_ref, bf16[160,3072]{1,0:T(8,128)(2,1)S(1)} %pad_maximum_fusion.4.kv_ref, s32[1,1536]{1,0:T(1,128)S(1)} %broadcast_in_dim.2.start_ref), custom_call_target="tpu_custom_call" | custom-call | tf_op jit(solution)/shard_map/pallas_call | solution.py:164
  174.6 20.2 %collective-permute-done.36 = bf16[192,2560]{1,0:T(8,128)(2,1)S(1)} collective-permute-done((bf16[192,2560]{1,0:T(8,128)(2,1)}, bf16[192,2560]{1,0:T(8,128)(2,1)S(1)}, u32[]{:S(2)}, u32[]{:S(2)}) %collective-permute-start.36) | collective-permute-done | bytes 983072 | tf_op jit(solution)/shard_map/ppermute | solution.py:316
  199.2 7.8 collective-permute-done.29
  207.4 6.8 convert_add_fusion.3
  221.3 6.8 collective-permute-done.16
  240.0 15.4 %collective-permute-done.17 = bf16[192,2560]{1,0:T(8,128)(2,1)S(1)} collective-permute-done((bf16[192,2560]{1,0:T(8,128)(2,1)S(1)}, bf16[192,2560]{1,0:T(8,128)(2,1)S(1)}, u32[]{:S(2)}, u32[]{:S(2)}) %collective-permute-start.17) | collective-permute-done | bytes 983072 | tf_op jit(solution)/shard_map/ppermute | solution.py:341
  265.5 17.1 %collective-permute-done.19 = bf16[192,2560]{1,0:T(8,128)(2,1)S(1)} collective-permute-done((bf16[192,2560]{1,0:T(8,128)(2,1)S(1)}, bf16[192,2560]{1,0:T(8,128)(2,1)S(1)}, u32[]{:S(2)}, u32[]{:S(2)}) %collective-permute-start.19) | collective-permute-done | bytes 983072 | tf_op jit(solution)/shard_map/ppermute | solution.py:316
  302.9 13.5 %fusion.59 = f32[1536,896]{1,0:T(8,128)} fusion(bf16[1536,2560]{1,0:T(8,128)(2,1)} %constant_dynamic-update-slice_fusion.10, bf16[2560,896]{1,0:T(8,128)(2,1)} %all-gather.11.cloned.1.call-done), kind=kOutput, calls=%fused_computation.265 | convolution fusion | flops 7046430720 | bytes 17956864 | tf_op jit(solution)/shard_map/dot_general | solution.py:34
  316.4 14.5 %multiply_convert_fusion = (bf16[1536,896]{1,0:T(8,128)(2,1)S(1)}, f32[1536,896]{1,0:T(8,128)}) fusion(f32[1536,896]{1,0:T(8,128)} %fusion.59, bf16[1536,2560]{1,0:T(8,128)(2,1)} %constant_dynamic-update-slice_fusion.20, bf16[2560,896]{1,0:T(8,128)(2,1)} %all-gather.15.cloned.1.call-done), kind=kOutput, calls=%fused_computation.16 | convolution fusion | flops 7054688256 | bytes 26214400 | tf_op jit(solution)/shard_map/dot_general | solution.py:34
  332.5 12.1 %convolution_convert_fusion.4 = bf16[2560,896]{1,0:T(8,128)(2,1)} fusion(bf16[1536,2560]{1,0:T(8,128)(2,1)} %constant_dynamic-update-slice_fusion.10, bf16[1536,896]{1,0:T(8,128)(2,1)S(1)} %get-tuple-element.182), kind=kOutput, calls=%fused_computation.21 | convolution fusion | flops 7048724480 | bytes 15204352 | tf_op jit(solution)/shard_map/dot_general | solution.py:34
  345.1 91.5 %reduce-scatter.12.cloned.1.call-done = bf16[640,896]{1,0:T(8,128)(2,1)} async-done(((bf16[2560,896]{1,0:T(8,128)(2,1)}), bf16[640,896]{1,0:T(8,128)(2,1)}) %reduce-scatter.12.cloned.1.call-update) | async-done | bytes 1146896 | tf_op jit(solution)/shard_map/reduce_scatter | solution.py:366
  439.5 13.3 %collective-permute-done.66 = bf16[320,896]{1,0:T(8,128)(2,1)S(1)} collective-permute-done((bf16[320,896]{1,0:T(8,128)(2,1)S(1)}, bf16[320,896]{1,0:T(8,128)(2,1)S(1)}, u32[]{:S(2)}, u32[]{:S(2)}) %collective-permute-start.66) | collective-permute-done | bytes 573472 | tf_op jit(solution)/shard_map/ppermute | solution.py:357
  457.4 12.4 %collective-permute-done.28 = bf16[320,896]{1,0:T(8,128)(2,1)S(1)} collective-permute-done((bf16[320,896]{1,0:T(8,128)(2,1)S(1)}, bf16[320,896]{1,0:T(8,128)(2,1)S(1)}, u32[]{:S(2)}, u32[]{:S(2)}) %collective-permute-start.28) | collective-permute-done | bytes 573472 | tf_op jit(solution)/shard_map/ppermute | solution.py:349
  471.4 87.8 %all-gather.13.cloned.1.call-done = bf16[2560,896]{1,0:T(8,128)(2,1)} async-done(((bf16[640,896]{1,0:T(8,128)(2,1)}), bf16[2560,896]{1,0:T(8,128)(2,1)}) %all-gather.13.cloned.1.call-update) | async-done | bytes 4587536 | tf_op jit(solution)/shard_map/all_gather | solution.py:362
  559.2 17.0 %multiply_convert_fusion.1 = (bf16[1536,896]{1,0:T(8,128)(2,1)}, bf16[1536,896]{1,0:T(8,128)(2,1)S(1)}) fusion(f32[1536,896]{1,0:T(8,128)} %fusion.59, f32[1536,896]{1,0:T(8,128)} %get-tuple-element.183, bf16[1536,2560]{1,0:T(8,128)(2,1)} %constant_dynamic-update-slice_fusion.10, bf16[2560,896]{1,0:T(8,128)(2,1)} %all-gather.13.cloned.1.call-done), kind=kOutput, calls=%fused_computation.17 | convolution fusion | flops 7064322048 | bytes 28966912 | tf_op jit(solution)/shard_map/dot_general | solution.py:34
  577.7 8.8 convolution_convert_fusion.1
  590.3 11.0 %fusion.60 = f32[1536,2560]{1,0:T(8,128)} fusion(bf16[1536,896]{1,0:T(8,128)(2,1)S(1)} %copy-done.76, bf16[2560,896]{1,0:T(8,128)(2,1)S(1)} %copy-done.71), kind=kOutput, calls=%fused_computation.266 | convolution fusion | flops 7046430720 | bytes 23068672 | tf_op jit(solution)/shard_map/dot_general | solution.py:34
  601.3 12.6 %add_convert_fusion = bf16[1536,2560]{1,0:T(8,128)(2,1)S(1)} fusion(f32[1536,2560]{1,0:T(8,128)} %fusion.60, bf16[1536,896]{1,0:T(8,128)(2,1)} %get-tuple-element.113, bf16[2560,896]{1,0:T(8,128)(2,1)S(1)} %bitcast.72), kind=kOutput, calls=%fused_computation.8 | convolution fusion | flops 7054295040 | bytes 30932992 | tf_op jit(solution)/shard_map/dot_general | solution.py:34
  620.3 12.3 %convolution_convert_fusion.5 = bf16[2560,896]{1,0:T(8,128)(2,1)} fusion(bf16[1536,2560]{1,0:T(8,128)(2,1)} %constant_dynamic-update-slice_fusion.10, bf16[1536,896]{1,0:T(8,128)(2,1)S(1)} %copy-done.74), kind=kOutput, calls=%fused_computation.22 | convolution fusion | flops 7048724480 | bytes 15204352 | tf_op jit(solution)/shard_map/dot_general | solution.py:34
  641.7 6.8 convert_add_fusion.1
  670.6 10.2 %convolution_convert_fusion.3 = bf16[2560,896]{1,0:T(8,128)(2,1)} fusion(bf16[1536,2560]{1,0:T(8,128)(2,1)S(1)} %bitcast.70, bf16[1536,896]{1,0:T(8,128)(2,1)S(1)} %copy-done.78), kind=kOutput, calls=%fused_computation.20 | convolution fusion | flops 7048724480 | bytes 15204352 | tf_op jit(solution)/shard_map/dot_general | solution.py:34
  687.4 19.8 %collective-permute-done.48 = bf16[192,2560]{1,0:T(8,128)(2,1)S(1)} collective-permute-done((bf16[192,2560]{1,0:T(8,128)(2,1)}, bf16[192,2560]{1,0:T(8,128)(2,1)S(1)}, u32[]{:S(2)}, u32[]{:S(2)}) %collective-permute-start.48) | collective-permute-done | bytes 983072 | tf_op jit(solution)/shard_map/ppermute | solution.py:341
  718.5 20.7 %collective-permute-done.50 = bf16[192,2560]{1,0:T(8,128)(2,1)S(1)} collective-permute-done((bf16[192,2560]{1,0:T(8,128)(2,1)S(1)}, bf16[192,2560]{1,0:T(8,128)(2,1)S(1)}, u32[]{:S(2)}, u32[]{:S(2)}) %collective-permute-start.50) | collective-permute-done | bytes 983072 | tf_op jit(solution)/shard_map/ppermute | solution.py:316
  742.1 8.9 collective-permute-done.51
  765.3 31.7 %shard_map.216 = (f32[320,1536]{1,0:T(8,128)S(1)}, f32[160,3072]{1,0:T(8,128)}) custom-call(s32[4,6]{1,0:T(4,128)S(1)} %copy-done.16, bf16[320,1536]{1,0:T(8,128)(2,1)S(1)} %copy-done.1, bf16[160,3072]{1,0:T(8,128)(2,1)S(1)} %copy-done.3, s32[1,1536]{1,0:T(1,128)S(1)} %copy-done.14, bf16[320,1536]{1,0:T(8,128)(2,1)S(1)} %copy-done.10, ...), custom_call_target="tpu_custom_call" | custom-call | tf_op jit(solution)/shard_map/pallas_call | solution.py:273
  799.7 20.1 %collective-permute-done.58 = bf16[160,1536]{1,0:T(8,128)(2,1)S(1)} collective-permute-done((bf16[160,1536]{1,0:T(8,128)(2,1)S(1)}, bf16[160,1536]{1,0:T(8,128)(2,1)S(1)}, u32[]{:S(2)}, u32[]{:S(2)}) %collective-permute-start.58) | collective-permute-done | bytes 491552 | tf_op jit(solution)/shard_map/ppermute | solution.py:310
  839.5 10.5 %convolution_convert_fusion.6 = bf16[2560,512]{1,0:T(8,128)(2,1)} fusion(bf16[1536,512]{1,0:T(8,128)(2,1)S(1)} %shard_map.217, bf16[1536,2560]{1,0:T(8,128)(2,1)} %constant_dynamic-update-slice_fusion, f32[2560]{0:T(1024)S(1)} %copy-done.53, f32[1536]{0:T(1024)S(1)} %copy-done.64), kind=kOutput, calls=%fused_computation.23 | convolution fusion | flops 4043571200 | bytes 12075008 | tf_op jit(solution)/shard_map/dot_general | solution.py:34
  885.2 21.6 %collective-permute-done.69 = bf16[320,320]{1,0:T(8,128)(2,1)S(1)} collective-permute-done((bf16[320,320]{1,0:T(8,128)(2,1)S(1)}, bf16[320,320]{1,0:T(8,128)(2,1)S(1)}, u32[]{:S(2)}, u32[]{:S(2)}) %collective-permute-start.69) | collective-permute-done | bytes 204832 | tf_op jit(solution)/shard_map/ppermute | solution.py:357
  907.9 22.9 %reduce-scatter.8.cloned.1.call-done = bf16[640,512]{1,0:T(8,128)(2,1)} async-done(((bf16[2560,512]{1,0:T(8,128)(2,1)}), bf16[640,512]{1,0:T(8,128)(2,1)}) %reduce-scatter.8.cloned.1.call-update) | async-done | bytes 655376 | tf_op jit(solution)/shard_map/reduce_scatter | solution.py:366
  (516 shorter events, 316.2 us)
Async XLA Ops:
  7.2 99.6 %all-gather.7.cloned.1.call-start = ((), (), s32[]{:S(2)}) async-start(), calls=%async_computation.5 | async-start | bytes 3276800 | tf_op jit(solution)/shard_map/all_gather | solution.py:362
  14.4 64.4 %collective-permute-start.1 = (bf16[192,2560]{1,0:T(8,128)(2,1)S(1)}, bf16[192,2560]{1,0:T(8,128)(2,1)}, u32[]{:S(2)}, u32[]{:S(2)}) collective-permute-start(bf16[192,2560]{1,0:T(8,128)(2,1)S(1)} %copy-done.24), channel_id=1, source_target_pairs={{0,4},{4,0},{1,5},{5,1},{2,6},{6,2},{3,7},{7,3},{8,12},{12,8},{9,1... | collective-permute-start | bytes 2949128 | tf_op jit(solution)/shard_map/ppermute | solution.py:316
  14.5 66.9 %collective-permute-start = (bf16[192,2560]{1,0:T(8,128)(2,1)S(1)}, bf16[192,2560]{1,0:T(8,128)(2,1)}, u32[]{:S(2)}, u32[]{:S(2)}) collective-permute-start(bf16[192,2560]{1,0:T(8,128)(2,1)S(1)} %copy-done.24), channel_id=1, source_target_pairs={{0,2},{2,0},{1,3},{3,1},{4,6},{6,4},{5,7},{7,5},{8,10},{10,8},{9,1... | collective-permute-start | bytes 2949128 | tf_op jit(solution)/shard_map/ppermute | solution.py:315
  16.4 79.1 %collective-permute-start.4 = (bf16[192,2560]{1,0:T(8,128)(2,1)S(1)}, bf16[192,2560]{1,0:T(8,128)(2,1)}, u32[]{:S(2)}, u32[]{:S(2)}) collective-permute-start(bf16[192,2560]{1,0:T(8,128)(2,1)S(1)} %copy-done.24), channel_id=1, source_target_pairs={{0,1},{1,0},{2,3},{3,2},{4,5},{5,4},{6,7},{7,6},{8,9},{9,8},{10,11... | collective-permute-start | bytes 2949128 | tf_op jit(solution)/shard_map/ppermute | solution.py:320
  16.4 56.4 %collective-permute-start.10 = (s32[768]{0:T(1024)S(1)}, s32[768]{0:T(1024)}, u32[]{:S(2)}, u32[]{:S(2)}) collective-permute-start(s32[768]{0:T(1024)S(1)} %copy-done.66), channel_id=1, source_target_pairs={{0,4},{4,0},{1,5},{5,1},{2,6},{6,2},{3,7},{7,3},{8,12},{12,8},{9,1... | collective-permute-start | bytes 9224 | tf_op jit(solution)/shard_map/ppermute | solution.py:425
  24.2 138.9 %all-gather.9.cloned.1.call-start = ((), (), s32[]{:S(2)}) async-start(), calls=%async_computation.6 | async-start | bytes 2457600 | tf_op jit(solution)/shard_map/all_gather | solution.py:362
  24.4 51.8 %collective-permute-start.12 = (bf16[320,320]{1,0:T(8,128)(2,1)S(1)}, bf16[320,320]{1,0:T(8,128)(2,1)}, u32[]{:S(2)}, u32[]{:S(2)}) collective-permute-start(bf16[320,320]{1,0:T(8,128)(2,1)S(1)} %broadcast_select_fusion.38), channel_id=1, source_target_pairs={{0,4},{4,0},{1,5},{5,1},{2,6},{6,2},{3,7},{7,3},{8,12},{12,8},{9,1... | collective-permute-start | bytes 614408 | tf_op jit(solution)/shard_map/ppermute | solution.py:349
  72.8 49.2 %collective-permute-start.27 = (bf16[320,896]{1,0:T(8,128)(2,1)}, bf16[320,896]{1,0:T(8,128)(2,1)}, u32[]{:S(2)}, u32[]{:S(2)}) collective-permute-start(bf16[320,896]{1,0:T(8,128)(2,1)} %broadcast_select_fusion.22), channel_id=1, source_target_pairs={{0,4},{4,0},{1,5},{5,1},{2,6},{6,2},{3,7},{7,3},{8,12},{12,8},{9,1... | collective-permute-start | bytes 1720328 | tf_op jit(solution)/shard_map/ppermute | solution.py:349
  78.3 224.7 %all-gather.11.cloned.1.call-start = ((), (), s32[]{:S(2)}) async-start(), calls=%async_computation.7 | async-start | bytes 5734400 | tf_op jit(solution)/shard_map/all_gather | solution.py:362
  125.7 190.7 %all-gather.15.cloned.1.call-start = ((), (), s32[]{:S(2)}) async-start(), calls=%async_computation.9 | async-start | bytes 5734400 | tf_op jit(solution)/shard_map/all_gather | solution.py:362
  169.8 37.5 %collective-permute-start.13 = (bf16[768,2560]{1,0:T(8,128)(2,1)S(1)}, bf16[768,2560]{1,0:T(8,128)(2,1)}, u32[]{:S(2)}, u32[]{:S(2)}) collective-permute-start(bf16[768,2560]{1,0:T(8,128)(2,1)S(1)} %slice.410), channel_id=1, source_target_pairs={{0,1},{1,0},{2,3},{3,2},{4,5},{5,4},{6,7},{7,6},{8,9},{9,8},{10,11... | collective-permute-start | bytes 11796488 | tf_op jit(solution)/shard_map/ppermute | solution.py:328
  172.6 63.5 %collective-permute-start.39 = (bf16[192,2560]{1,0:T(8,128)(2,1)}, bf16[192,2560]{1,0:T(8,128)(2,1)}, u32[]{:S(2)}, u32[]{:S(2)}) collective-permute-start(bf16[192,2560]{1,0:T(8,128)(2,1)} %param.25), channel_id=1, source_target_pairs={{0,1},{1,0},{2,3},{3,2},{4,5},{5,4},{6,7},{7,6},{8,9},{9,8},{10,11... | collective-permute-start | bytes 2949128 | tf_op jit(solution)/shard_map/ppermute | solution.py:320
  173.9 33.1 %collective-permute-start.29 = (bf16[320,896]{1,0:T(8,128)(2,1)S(1)}, bf16[320,896]{1,0:T(8,128)(2,1)S(1)}, u32[]{:S(2)}, u32[]{:S(2)}) collective-permute-start(bf16[320,896]{1,0:T(8,128)(2,1)S(1)} %copy-done.47), channel_id=1, source_target_pairs={{0,4},{4,0},{1,5},{5,1},{2,6},{6,2},{3,7},{7,3},{8,12},{12,8},{9,1... | collective-permute-start | bytes 1720328 | tf_op jit(solution)/shard_map/ppermute | solution.py:349
  197.6 36.0 %collective-permute-start.38 = (bf16[96,2560]{1,0:T(8,128)(2,1)}, bf16[96,2560]{1,0:T(8,128)(2,1)}, u32[]{:S(2)}, u32[]{:S(2)}) collective-permute-start(bf16[96,2560]{1,0:T(8,128)(2,1)} %slice.437), channel_id=1, source_target_pairs={{0,4},{4,0},{1,5},{5,1},{2,6},{6,2},{3,7},{7,3},{8,12},{12,8},{9,1... | collective-permute-start | bytes 1474568 | tf_op jit(solution)/shard_map/ppermute | solution.py:318
  219.1 217.5 %reduce-scatter.12.cloned.1.call-start = ((), (), s32[]{:S(2)}) async-start(), calls=%async_computation.12 | async-start | bytes 5734400 | tf_op jit(solution)/shard_map/reduce_scatter | solution.py:366
  219.4 43.4 %collective-permute-start.41 = (bf16[192,2560]{1,0:T(8,128)(2,1)S(1)}, bf16[192,2560]{1,0:T(8,128)(2,1)S(1)}, u32[]{:S(2)}, u32[]{:S(2)}) collective-permute-start(bf16[192,2560]{1,0:T(8,128)(2,1)S(1)} %collective-permute-done.36), channel_id=1, source_target_pairs={{0,1},{1,0},{2,3},{3,2},{4,5},{5,4},{6,7},{7,6},{8,9},{9,8},{10,11... | collective-permute-start | bytes 2949128 | tf_op jit(solution)/shard_map/ppermute | solution.py:320
  236.1 27.7 %collective-permute-start.42 = (bf16[96,2560]{1,0:T(8,128)(2,1)}, bf16[96,2560]{1,0:T(8,128)(2,1)S(1)}, u32[]{:S(2)}, u32[]{:S(2)}) collective-permute-start(bf16[96,2560]{1,0:T(8,128)(2,1)} %collective-permute-done.37), channel_id=1, source_target_pairs={{0,1},{1,0},{2,3},{3,2},{4,5},{5,4},{6,7},{7,6},{8,9},{9,8},{10,11... | collective-permute-start | bytes 1474568 | tf_op jit(solution)/shard_map/ppermute | solution.py:320
  238.4 26.3 %collective-permute-start.43 = (bf16[96,2560]{1,0:T(8,128)(2,1)}, bf16[96,2560]{1,0:T(8,128)(2,1)S(1)}, u32[]{:S(2)}, u32[]{:S(2)}) collective-permute-start(bf16[96,2560]{1,0:T(8,128)(2,1)} %collective-permute-done.38), channel_id=1, source_target_pairs={{0,1},{1,0},{2,3},{3,2},{4,5},{5,4},{6,7},{7,6},{8,9},{9,8},{10,11... | collective-permute-start | bytes 1474568 | tf_op jit(solution)/shard_map/ppermute | solution.py:320
  265.5 32.7 %collective-permute-start.22 = (bf16[192,2560]{1,0:T(8,128)(2,1)S(1)}, bf16[192,2560]{1,0:T(8,128)(2,1)S(1)}, u32[]{:S(2)}, u32[]{:S(2)}) collective-permute-start(bf16[192,2560]{1,0:T(8,128)(2,1)S(1)} %get-tuple-element.100), channel_id=1, source_target_pairs={{0,1},{1,0},{2,3},{3,2},{4,5},{5,4},{6,7},{7,6},{8,9},{9,8},{10,11... | collective-permute-start | bytes 2949128 | tf_op jit(solution)/shard_map/ppermute | solution.py:320
  344.7 214.6 %all-gather.13.cloned.1.call-start = ((), (), s32[]{:S(2)}) async-start(), calls=%async_computation.8 | async-start | bytes 5734400 | tf_op jit(solution)/shard_map/all_gather | solution.py:362
  471.3 366.0 %reduce-scatter.10.cloned.1.call-start = ((), (), s32[]{:S(2)}) async-start(), calls=%async_computation.11 | async-start | bytes 5734400 | tf_op jit(solution)/shard_map/reduce_scatter | solution.py:366
  588.7 44.0 %collective-permute-start.30 = (bf16[768,2560]{1,0:T(8,128)(2,1)}, bf16[768,2560]{1,0:T(8,128)(2,1)}, u32[]{:S(2)}, u32[]{:S(2)}) collective-permute-start(bf16[768,2560]{1,0:T(8,128)(2,1)} %slice.428), channel_id=1, source_target_pairs={{0,1},{1,0},{2,3},{3,2},{4,5},{5,4},{6,7},{7,6},{8,9},{9,8},{10,11... | collective-permute-start | bytes 11796488 | tf_op jit(solution)/shard_map/ppermute | solution.py:328
  632.6 217.4 %reduce-scatter.14.cloned.1.call-start = ((), (), s32[]{:S(2)}) async-start(), calls=%async_computation.13 | async-start | bytes 5734400 | tf_op jit(solution)/shard_map/reduce_scatter | solution.py:366
  656.3 31.1 %collective-permute-start.34 = (bf16[192,2560]{1,0:T(8,128)(2,1)}, bf16[192,2560]{1,0:T(8,128)(2,1)}, u32[]{:S(2)}, u32[]{:S(2)}) collective-permute-start(bf16[192,2560]{1,0:T(8,128)(2,1)} %pad_maximum_fusion.8), channel_id=1, source_target_pairs={{0,4},{4,0},{1,5},{5,1},{2,6},{6,2},{3,7},{7,3},{8,12},{12,8},{9,1... | collective-permute-start | bytes 2949128 | tf_op jit(solution)/shard_map/ppermute | solution.py:341
  658.4 29.1 %collective-permute-start.32 = (bf16[192,2560]{1,0:T(8,128)(2,1)}, bf16[192,2560]{1,0:T(8,128)(2,1)}, u32[]{:S(2)}, u32[]{:S(2)}) collective-permute-start(bf16[192,2560]{1,0:T(8,128)(2,1)} %pad_maximum_fusion.7), channel_id=1, source_target_pairs={{0,2},{2,0},{1,3},{3,1},{4,6},{6,4},{5,7},{7,5},{8,10},{10,8},{9,1... | collective-permute-start | bytes 2949128 | tf_op jit(solution)/shard_map/ppermute | solution.py:340
  667.5 39.7 %collective-permute-start.48 = (bf16[192,2560]{1,0:T(8,128)(2,1)}, bf16[192,2560]{1,0:T(8,128)(2,1)S(1)}, u32[]{:S(2)}, u32[]{:S(2)}) collective-permute-start(bf16[192,2560]{1,0:T(8,128)(2,1)} %pad_maximum_fusion.10), channel_id=1, source_target_pairs={{0,4},{4,0},{1,5},{5,1},{2,6},{6,2},{3,7},{7,3},{8,12},{12,8},{9,1... | collective-permute-start | bytes 2949128 | tf_op jit(solution)/shard_map/ppermute | solution.py:341
  670.1 37.1 %collective-permute-start.46 = (bf16[192,2560]{1,0:T(8,128)(2,1)}, bf16[192,2560]{1,0:T(8,128)(2,1)}, u32[]{:S(2)}, u32[]{:S(2)}) collective-permute-start(bf16[192,2560]{1,0:T(8,128)(2,1)} %pad_maximum_fusion.9), channel_id=1, source_target_pairs={{0,2},{2,0},{1,3},{3,1},{4,6},{6,4},{5,7},{7,5},{8,10},{10,8},{9,1... | collective-permute-start | bytes 2949128 | tf_op jit(solution)/shard_map/ppermute | solution.py:340
  680.8 200.3 %reduce-scatter.16.cloned.1.call-start = ((), (), s32[]{:S(2)}) async-start(), calls=%async_computation.14 | async-start | bytes 2457600 | tf_op jit(solution)/shard_map/reduce_scatter | solution.py:366
  718.5 33.2 %collective-permute-start.53 = (bf16[192,2560]{1,0:T(8,128)(2,1)S(1)}, bf16[192,2560]{1,0:T(8,128)(2,1)S(1)}, u32[]{:S(2)}, u32[]{:S(2)}) collective-permute-start(bf16[192,2560]{1,0:T(8,128)(2,1)S(1)} %get-tuple-element.97), channel_id=1, source_target_pairs={{0,1},{1,0},{2,3},{3,2},{4,5},{5,4},{6,7},{7,6},{8,9},{9,8},{10,11... | collective-permute-start | bytes 2949128 | tf_op jit(solution)/shard_map/ppermute | solution.py:320
  837.2 93.5 %reduce-scatter.8.cloned.1.call-start = ((), (), s32[]{:S(2)}) async-start(), calls=%async_computation.10 | async-start | bytes 3276800 | tf_op jit(solution)/shard_map/reduce_scatter | solution.py:366
  878.3 55.1 %collective-permute-start.63 = (bf16[192,2560]{1,0:T(8,128)(2,1)}, bf16[192,2560]{1,0:T(8,128)(2,1)}, u32[]{:S(2)}, u32[]{:S(2)}) collective-permute-start(bf16[192,2560]{1,0:T(8,128)(2,1)} %pad_maximum_fusion.12), channel_id=1, source_target_pairs={{0,4},{4,0},{1,5},{5,1},{2,6},{6,2},{3,7},{7,3},{8,12},{12,8},{9,1... | collective-permute-start | bytes 2949128 | tf_op jit(solution)/shard_map/ppermute | solution.py:341
  880.5 52.9 %collective-permute-start.61 = (bf16[192,2560]{1,0:T(8,128)(2,1)}, bf16[192,2560]{1,0:T(8,128)(2,1)}, u32[]{:S(2)}, u32[]{:S(2)}) collective-permute-start(bf16[192,2560]{1,0:T(8,128)(2,1)} %pad_maximum_fusion.11), channel_id=1, source_target_pairs={{0,2},{2,0},{1,3},{3,1},{4,6},{6,4},{5,7},{7,5},{8,10},{10,8},{9,1... | collective-permute-start | bytes 2949128 | tf_op jit(solution)/shard_map/ppermute | solution.py:340
  (136 other events, 2156.4 us)
Sparse Core Ops, SparseCore 0:
  24.3 56.7 all-gather.6
  82.6 42.3 all-gather.8
  126.6 87.1 all-gather.10
  219.2 95.4 all-gather.14
  344.8 91.7 reduce-scatter.11
  471.5 87.7 all-gather.12
  632.7 81.6 reduce-scatter.9
  716.7 85.3 reduce-scatter.13
  837.4 39.8 reduce-scatter.15
  879.4 51.3 reduce-scatter.7

commit v2 on v1

--- a/solution.py
+++ b/solution.py
@@ -22,6 +22,7 @@
 SCORE_SCALE = HD ** (-0.5)
 LOW = -1e30
 BQ = 256
+CHUNK = 384
 KB = 256
 WIDE = jnp.bfloat16
 F32 = jnp.float32
@@ -67,6 +68,7 @@
         ),
         out_shape=jax.ShapeDtypeStruct((heads * HD, count), WIDE),
         compiler_params=pltpu.CompilerParams(vmem_limit_bytes=VMEM_BYTES),
+        cost_estimate=pl.CostEstimate(flops=10**6, bytes_accessed=10**5, transcendentals=0),
     )(index, rows, cos_tab, sin_tab)
 
 
@@ -105,6 +107,7 @@
         ),
         out_shape=jax.ShapeDtypeStruct((count, width), WIDE),
         compiler_params=pltpu.CompilerParams(vmem_limit_bytes=VMEM_BYTES),
+        cost_estimate=pl.CostEstimate(flops=10**6, bytes_accessed=10**5, transcendentals=0),
     )(index, cols, cos_tab, sin_tab)
 
 
@@ -182,6 +185,7 @@
             jax.ShapeDtypeStruct((8, count), F32),
         ],
         compiler_params=pltpu.CompilerParams(vmem_limit_bytes=VMEM_BYTES),
+        cost_estimate=pl.CostEstimate(flops=10**6, bytes_accessed=10**5, transcendentals=0),
     )(bounds, q_cols, kv_cols, starts)
 
 
@@ -301,60 +305,241 @@
             jax.ShapeDtypeStruct((2 * HD, span), F32),
         ],
         compiler_params=pltpu.CompilerParams(vmem_limit_bytes=VMEM_BYTES),
+        cost_estimate=pl.CostEstimate(flops=10**6, bytes_accessed=10**5, transcendentals=0),
     )(bounds, q_cols, kv_cols, starts, out_cols, logs, grad_cols)
 
 
-def shifted(block, distance):
+def project_kernel(x_ref, gain_ref, weight_ref, h_ref, out_ref):
+    x = x_ref[...].astype(F32)
+    inverse = lax.rsqrt(jnp.mean(x * x, axis=-1, keepdims=True) + eps)
+    h = (x * inverse * gain_ref[...]).astype(WIDE)
+    h_ref[...] = h
+    out_ref[...] = dot(h, weight_ref[...], 1, 0)
+
+
+def project(x_all, gain_row, weights, rows=256):
+    count, model = x_all.shape
+    width = weights.shape[1]
+    return pl.pallas_call(
+        project_kernel,
+        grid=(count // rows,),
+        in_specs=[
+            pl.BlockSpec((rows, model), lambda i: (i, 0)),
+            pl.BlockSpec((1, model), lambda i: (0, 0)),
+            pl.BlockSpec(weights.shape, lambda i: (0, 0), pipeline_mode=pl.Buffered(1)),
+        ],
+        out_specs=[
+            pl.BlockSpec((rows, model), lambda i: (i, 0)),
+            pl.BlockSpec((rows, width), lambda i: (i, 0)),
+        ],
+        out_shape=[
+            jax.ShapeDtypeStruct((count, model), WIDE),
+            jax.ShapeDtypeStruct((count, width), F32),
+        ],
+        compiler_params=pltpu.CompilerParams(vmem_limit_bytes=VMEM_BYTES),
+        cost_estimate=pl.CostEstimate(flops=10**6, bytes_accessed=10**5, transcendentals=0),
+    )(x_all, gain_row, weights)
+
+
+def hidden_kernel(h_ref, cot_ref, weight_ref, out_ref):
+    width = weight_ref.shape[1] // 3
+    gate = dot(h_ref[...], weight_ref[:, width : 2 * width], 1, 0)
+    up = dot(h_ref[...], weight_ref[:, 2 * width :], 1, 0)
+    grad = dot(cot_ref[...], weight_ref[:, :width], 1, 0)
+    sigma = 1.0 / (1.0 + jnp.exp(-gate))
+    silu = gate * sigma
+    out_ref[:, :width] = (silu * up).astype(WIDE)
+    out_ref[:, width : 2 * width] = (grad * up * sigma * (1.0 + gate * (1.0 - sigma))).astype(WIDE)
+    out_ref[:, 2 * width :] = (grad * silu).astype(WIDE)
+
+
+def hidden_units(h_two, cot, weights, rows=256):
+    count, model = h_two.shape
+    return pl.pallas_call(
+        hidden_kernel,
+        grid=(count // rows,),
+        in_specs=[
+            pl.BlockSpec((rows, model), lambda i: (i, 0)),
+            pl.BlockSpec((rows, model), lambda i: (i, 0)),
+            pl.BlockSpec(weights.shape, lambda i: (0, 0), pipeline_mode=pl.Buffered(1)),
+        ],
+        out_specs=pl.BlockSpec((rows, weights.shape[1]), lambda i: (i, 0)),
+        out_shape=jax.ShapeDtypeStruct((count, weights.shape[1]), WIDE),
+        compiler_params=pltpu.CompilerParams(vmem_limit_bytes=VMEM_BYTES),
+        cost_estimate=pl.CostEstimate(flops=10**6, bytes_accessed=10**5, transcendentals=0),
+    )(h_two, cot, weights)
+
+
+def rows_kernel(spans, has_prior, *refs):
+    out_ref = refs[-1]
+    total = refs[-2][...].astype(F32) if has_prior else None
+    for k, (lo, hi) in enumerate(spans):
+        part = dot(refs[2 * k][:, lo:hi], refs[2 * k + 1][:, lo:hi], 1, 1)
+        total = part if total is None else total + part
+    out_ref[...] = total.astype(out_ref.dtype)
+
+
+def row_products(pairs, spans, first, count, prior=None, rows=256):
+    model = pairs[0][1].shape[0]
+    at = first // rows
+    operands, specs = [], []
+    for a, b in pairs:
+        operands += [a, b]
+        specs += [
+            pl.BlockSpec((rows, a.shape[1]), lambda i: (i + at, 0)),
+            pl.BlockSpec(b.shape, lambda i: (0, 0), pipeline_mode=pl.Buffered(1)),
+        ]
+    if prior is not None:
+        operands.append(prior)
+        specs.append(pl.BlockSpec((rows, model), lambda i: (i, 0)))
+    return pl.pallas_call(
+        functools.partial(rows_kernel, spans, prior is not None),
+        grid=(count // rows,),
+        in_specs=specs,
+        out_specs=pl.BlockSpec((rows, model), lambda i: (i, 0)),
+        out_shape=jax.ShapeDtypeStruct((count, model), WIDE),
+        compiler_params=pltpu.CompilerParams(vmem_limit_bytes=VMEM_BYTES),
+        cost_estimate=pl.CostEstimate(flops=10**6, bytes_accessed=10**5, transcendentals=0),
+    )(*operands)
+
+
+def grads_kernel(spans, *refs):
+    out_ref = refs[-1]
+    for k, (lo, hi, at) in enumerate(spans):
+        out_ref[:, at : at + hi - lo] = dot(refs[2 * k][...], refs[2 * k + 1][:, lo:hi], 0, 0).astype(
+            WIDE
+        )
+    end = max(at + hi - lo for lo, hi, at in spans)
+    if end < out_ref.shape[1]:
+        out_ref[:, end:] = jnp.zeros((out_ref.shape[0], out_ref.shape[1] - end), WIDE)
+
+
+def column_products(pairs, spans, width, rows=256):
+    count, model = pairs[0][0].shape
+    operands, specs = [], []
+    for a, b in pairs:
+        operands += [a, b]
+        specs += [
+            pl.BlockSpec((count, rows), lambda i: (0, i)),
+            pl.BlockSpec(b.shape, lambda i: (0, 0), pipeline_mode=pl.Buffered(1)),
+        ]
+    return pl.pallas_call(
+        functools.partial(grads_kernel, spans),
+        grid=(model // rows,),
+        in_specs=specs,
+        out_specs=pl.BlockSpec((rows, width), lambda i: (i, 0)),
+        out_shape=jax.ShapeDtypeStruct((model, width), WIDE),
+        compiler_params=pltpu.CompilerParams(vmem_limit_bytes=VMEM_BYTES),
+        cost_estimate=pl.CostEstimate(flops=10**6, bytes_accessed=10**5, transcendentals=0),
+    )(*operands)
+
+
+def hidden_grads(h_two, cot, acts):
+    width = acts.shape[1] // 3
+    return column_products(
+        [(cot, acts), (h_two, acts)],
+        [(0, width, 0), (width, 3 * width, width)],
+        3 * width,
+    )
+
+
+def tied(value, *others):
+    return lax.optimization_barrier((value, *others))[0]
+
+
+def together(*values):
+    return lax.optimization_barrier(values)
+
+
+def shifted(block, distance, period):
     count = lax.axis_size("z")
-    route = [(i - distance, i) for i in range(count) if 0 <= i - distance < count]
+    route = [
+        (i - distance, i)
+        for i in range(count)
+        if 0 <= i - distance < count and (i - distance) // period == i // period
+    ]
     return lax.ppermute(block, "z", route)
 
 
-def gather_plane(block):
-    half = block.shape[0] // 2
-    over_x = lax.ppermute(block, "x", SWAP)
-    over_y = lax.ppermute(block, "y", SWAP)
-    far_top = lax.ppermute(over_y[:half], "x", SWAP)
-    far_low = lax.ppermute(over_x[half:], "y", SWAP)
-    mine = [block, over_x, over_y, far_top, far_low]
-    other = [lax.ppermute(part, "c", SWAP) for part in mine]
-    return jnp.concatenate(mine + other, axis=0)
-
-
-def sum_plane(term):
-    own = term.shape[0] // 8
+def over(block, axis):
+    return lax.ppermute(block, axis, SWAP)
+
+
+def across(block):
+    return lax.ppermute(block, ("y", "x"), [(i, 3 - i) for i in range(4)])
+
+
+def plane_step_one(block):
+    return over(block, "x"), over(block, "y")
+
+
+def plane_step_two(over_x, over_y):
+    half = over_x.shape[0] // 2
+    return over(over_y[:half], "x"), over(over_x[half:], "y")
+
+
+def plane_join(*mine):
+    return jnp.concatenate(list(mine) + [over(part, "c") for part in mine], axis=0)
+
+
+def core_sum(own, term, prior=None):
+    half = 4 * own
+    got = over(term(half, half).astype(WIDE), "c")
+    mine = term(0, half)
+    return (mine.astype(F32) + got.astype(F32)).astype(WIDE)
+
+
+def product(a, b):
+    return lambda first, count: dot(a[first : first + count], b, 1, 1)
+
+
+def plane_sum_one(total):
+    own = total.shape[0] // 4
     half = own // 2
-    low = term.astype(WIDE)
-    got = lax.ppermute(low[4 * own :], "c", SWAP)
-    total = low[: 4 * own].astype(F32) + got.astype(F32)
-    far = total[3 * own :].astype(WIDE)
-    top = lax.ppermute(far[:half], "x", SWAP)
-    bottom = lax.ppermute(far[half:], "y", SWAP)
+    return over(total[3 * own : 3 * own + half], "x"), over(total[3 * own + half :], "y")
+
+
+def plane_sum_two(total, top, bottom):
+    own = total.shape[0] // 4
+    half = own // 2
+    wide = lambda a, b: (a.astype(F32) + b.astype(F32)).astype(WIDE)
     to_x = jnp.concatenate(
-        [total[own : own + half], total[own + half : 2 * own] + bottom.astype(F32)], axis=0
-    ).astype(WIDE)
+        [total[own : own + half], wide(total[own + half : 2 * own], bottom)], axis=0
+    )
     to_y = jnp.concatenate(
-        [total[2 * own : 2 * own + half] + top.astype(F32), total[2 * own + half : 3 * own]],
-        axis=0,
-    ).astype(WIDE)
-    over_x = lax.ppermute(to_x, "x", SWAP)
-    over_y = lax.ppermute(to_y, "y", SWAP)
-    return total[:own] + over_x.astype(F32) + over_y.astype(F32)
-
-
-def share_columns(block, first_y):
+        [wide(total[2 * own : 2 * own + half], top), total[2 * own + half : 3 * own]], axis=0
+    )
+    return over(to_x, "x"), over(to_y, "y")
+
+
+def added(total, *parts):
+    own = total.shape[0] // 4
+    return sum((part.astype(F32) for part in parts), total[:own].astype(F32))
+
+
+def kept_columns(block, first_y):
     half = block.shape[1] // 2
     keep = jnp.where(first_y, block[:, :half], block[:, half:])
     give = jnp.where(first_y, block[:, half:], block[:, :half])
-    got = lax.ppermute(give, "y", SWAP)
+    return keep, give
+
+
+def both_rows(keep, got, first_y):
     return jnp.concatenate([jnp.where(first_y, keep, got), jnp.where(first_y, got, keep)], axis=0)
+
+
+def share_columns(block, first_y, *after):
+    keep, give = kept_columns(block, first_y)
+    if after:
+        give = tied(give, *after)
+    return both_rows(keep, over(give, "y"), first_y)
 
 
 def unshare_columns(block, first_y):
     half = block.shape[0] // 2
     keep = jnp.where(first_y, block[:half], block[half:])
     give = jnp.where(first_y, block[half:], block[:half])
-    got = lax.ppermute(give, "y", SWAP)
+    got = over(give, "y")
     return jnp.where(first_y, keep, got), jnp.where(first_y, got, keep)
 
 
@@ -395,8 +580,10 @@
     count = 8 * own
     length = segments.shape[0] // SEQS
     reach = (DOC_MOST - 2) // count + 1
+    period = lax.axis_size("z")
     if length % count == 0:
-        reach = min(reach, length // count - 1)
+        period = length // count
+        reach = min(reach, period - 1)
     span = (reach + 1) * count
     z, y = lax.axis_index("z"), lax.axis_index("y")
     x, c = lax.axis_index("x"), lax.axis_index("c")
@@ -408,19 +595,33 @@
     w_o, w_d = out_weight.T.astype(WIDE), down_weight.T.astype(WIDE)
     nq, nk, nf = w_q.shape[1] // 2, w_k.shape[1] // 2, w_g.shape[1] // 2
     rows_w = w_q.shape[0]
-    gains = gather_z(
-        lax.all_gather(jnp.stack([gain_attn, gain_mlp], 1).astype(WIDE), "y", axis=0, tiled=True)
-    ).astype(F32)
+    halves = lambda w: (w[:, : w.shape[1] // 2], w[:, w.shape[1] // 2 :])
+    gain_pair = jnp.stack([gain_attn, gain_mlp] * 2, 1).astype(WIDE)
+    near_a = share_columns(
+        jnp.concatenate(
+            [
+                padded(jnp.concatenate([halves(w)[i] for w in (w_q, w_k, w_v, gain_pair)], axis=1))
+                for i in range(2)
+            ],
+            axis=1,
+        ),
+        first_y,
+    )
+    chunks = (slice(0, CHUNK), slice(CHUNK, nf))
+    triple = lambda cut: jnp.concatenate(
+        [padded(halves(w)[i][:, cut]) for i in range(2) for w in (w_d, w_g, w_u)], axis=1
+    )
+    x_parts = over(inputs, "x"), over(tied(inputs, near_a), "y")
+    x_parts += plane_step_two(*x_parts)
+    x_all = plane_join(inputs, *x_parts)
+    cot_parts = plane_step_one(tied(cotangent, *x_parts))
+    near_o = share_columns(w_o, first_y, *x_parts)
+    near_c = [share_columns(triple(cut), first_y, *x_parts) for cut in chunks]
+    full_a, full_o = gather_z(near_a), gather_z(near_o)
+    full_c = [gather_z(near) for near in near_c]
+    first_gain = nq + 2 * nk
+    gains = full_a[:, first_gain : first_gain + 2].astype(F32)
     gain_first, gain_second = gains[:, 0], gains[:, 1]
-    halves = lambda w: (w[:, : w.shape[1] // 2], w[:, w.shape[1] // 2 :])
-    interleave = lambda *ws: jnp.concatenate(
-        [padded(jnp.concatenate([halves(w)[i] for w in ws], axis=1)) for i in range(2)], axis=1
-    )
-    full_a = gather_z(share_columns(interleave(w_q, w_k, w_v), first_y))
-    full_o = gather_z(share_columns(w_o, first_y))
-    full_g = gather_z(share_columns(interleave(w_g), first_y))
-    full_u = gather_z(share_columns(interleave(w_u), first_y))
-    full_d = gather_z(share_columns(interleave(w_d), first_y))
 
     other_positions = lax.ppermute(positions, "y", SWAP)
     token_positions = jnp.where(
@@ -446,53 +647,83 @@
     bounds = jnp.stack([lo, full_lo, full_hi, hi])
     starts = starts[None, :]
 
-    x_all = gather_plane(inputs).astype(F32)
-    inverse_all = lax.rsqrt(jnp.mean(x_all * x_all, axis=-1, keepdims=True) + eps)
-    h_one = (x_all * inverse_all * gain_first).astype(WIDE)
-    qkv = dot(h_one, full_a, 1, 0)
+    h_one, qkv = project(x_all, gain_first[None, :], full_a)
     turned = to_columns(qkv, index, cos_tab, sin_tab, GROUP + 1, GROUP + 2)
     q_cols, kv_own = turned[: GROUP * HD], turned[GROUP * HD :]
-    kv_cols = jnp.concatenate(
-        [shifted(kv_own, distance) for distance in range(reach, 0, -1)] + [kv_own], axis=1
-    )
+    far_kv = [shifted(kv_own, distance, period) for distance in range(reach, 0, -1)]
+    kv_cols = jnp.concatenate(far_kv + [kv_own], axis=1)
+    kv_cols, full_o, *near_all = together(kv_cols, full_o, *near_c, *cot_parts)
+    cot_parts = near_all[len(near_c) :]
+    cot_far = plane_step_two(*cot_parts)
     out_cols, logs = attend(q_cols, kv_cols, starts, bounds)
+    out_cols, *cot_far = together(out_cols, *cot_far)
     attended = to_rows(out_cols, index, cos_tab, sin_tab, 0, GROUP, GROUP * HD)
+    grad_mix = plane_join(cotangent, *cot_parts, *cot_far)
     input_f32 = inputs.astype(F32)
     inverse_one = lax.rsqrt(jnp.mean(input_f32 * input_f32, axis=-1, keepdims=True) + eps)
     normed_one = input_f32 * inverse_one
-    x_mid = input_f32 + sum_plane(dot(attended, full_o, 1, 1))
+    mid_total = core_sum(own, product(attended, full_o))
+    mid_far = plane_sum_one(mid_total)
+    mid_near = plane_sum_two(mid_total, *mid_far)
+    x_mid = input_f32 + added(mid_total, *mid_near)
 
     inverse_two = lax.rsqrt(jnp.mean(x_mid * x_mid, axis=-1, keepdims=True) + eps)
     normed_two = x_mid * inverse_two
-    h_two = gather_plane((normed_two * gain_second).astype(WIDE))
-    grad_mix = gather_plane(cotangent)
-    gate_pre = dot(h_two, full_g, 1, 0)
-    up_pre = dot(h_two, full_u, 1, 0)
-    sigmoid_gate = jax.nn.sigmoid(gate_pre)
-    hidden = (gate_pre * sigmoid_gate * up_pre).astype(WIDE)
-    output = (x_mid + sum_plane(dot(hidden, full_d, 1, 1))).astype(WIDE)
-
-    grad_hidden = dot(grad_mix, full_d, 1, 0)
-    grad_gate = (
-        grad_hidden * up_pre * sigmoid_gate * (1.0 + gate_pre * (1.0 - sigmoid_gate))
-    ).astype(WIDE)
-    grad_up = (grad_hidden * gate_pre * sigmoid_gate).astype(WIDE)
-    grad_h_two = sum_plane(dot(grad_gate, full_g, 1, 1) + dot(grad_up, full_u, 1, 1))
-    down_grad = sum_z(dot(grad_mix, hidden, 0, 0))
-    gate_grad = sum_z(dot(h_two, grad_gate, 0, 0))
-    up_grad = sum_z(dot(h_two, grad_up, 0, 0))
+    h_own = (normed_two * gain_second).astype(WIDE)
+    h_parts = plane_step_one(h_own)
+    h_parts += plane_step_two(*h_parts)
+    h_two, grad_mix = together(plane_join(h_own, *h_parts), grad_mix)
+    half = 4 * own
+    acts = [hidden_units(h_two, grad_mix, full_c[0])]
+    width = [full.shape[1] // 3 for full in full_c]
+    later = lambda k: (width[k], 3 * width[k])
+    back_other = row_products([(acts[0], full_c[0])], [later(0)], half, half)
+    back_mine = row_products([(acts[0], full_c[0])], [later(0)], 0, half)
+    grads = [hidden_grads(h_two, grad_mix, acts[0])]
+    full_c[1], back_mine, back_other, *grads = together(full_c[1], back_mine, back_other, *grads)
+    sums = [sum_z(grads[0])]
+    acts.append(hidden_units(h_two, grad_mix, full_c[1]))
+    back_other = row_products([(acts[1], full_c[1])], [later(1)], half, half, back_other)
+    got = over(back_other, "c")
+    back_mine = row_products([(acts[1], full_c[1])], [later(1)], 0, half, back_mine)
+    back_total = (back_mine.astype(F32) + got.astype(F32)).astype(WIDE)
+    back_far = plane_sum_one(back_total)
+    grads.append(hidden_grads(h_two, grad_mix, acts[1]))
+    back_near = plane_sum_two(back_total, *back_far)
+    *back_near, grads[1] = together(*back_near, grads[1])
+    sums.append(sum_z(grads[1]))
+    grad_h_two = added(back_total, *back_near)
     grad_mid = cotangent.astype(F32) + norm_back(grad_h_two, normed_two, inverse_two, gain_second)
-    grad_branch = gather_plane(grad_mid.astype(WIDE))
+    branch_own = grad_mid.astype(WIDE)
+    branch_parts = plane_step_one(branch_own)
+    acts_later = [tied(part, branch_own) for part in acts]
+    hidden_pairs = list(zip(acts_later, full_c))
+    out_other = row_products(hidden_pairs, [(0, w) for w in width], half, half)
+    *branch_parts, out_other = together(*branch_parts, out_other)
+    out_got = over(out_other, "c")
+    branch_far = plane_step_two(*branch_parts)
+    hidden_pairs = [(tied(part, *branch_parts), full) for part, full in zip(acts, full_c)]
+    out_mine = row_products(hidden_pairs, [(0, w) for w in width], 0, half)
+    *branch_far, out_mine, out_got = together(*branch_far, out_mine, out_got)
+    out_total = (out_mine.astype(F32) + out_got.astype(F32)).astype(WIDE)
+    grad_branch = plane_join(branch_own, *branch_parts, *branch_far)
+    grad_branch, out_total, sums[0] = together(grad_branch, out_total, sums[0])
 
     grad_attended = dot(grad_branch, full_o, 1, 0).astype(WIDE)
-    out_grad = sum_z(dot(grad_branch, attended, 0, 0))
     grad_cols = to_columns(grad_attended, index, cos_tab, sin_tab, 0, GROUP)
+    out_total, sums[0] = together(out_total, sums[0], grad_cols)[:2]
+    out_sends = [
+        over(out_total[own : 2 * own], "x"),
+        over(out_total[2 * own : 3 * own], "y"),
+        across(out_total[3 * own :]),
+    ]
+    owned = [unshare_columns(sums[0], first_y)]
     dq_cols, dkv_cols = attend_back(q_cols, kv_cols, starts, bounds, out_cols, logs, grad_cols)
     dkv_own = dkv_cols[:, reach * count :]
     for distance in range(1, reach + 1):
         first = (reach - distance) * count
         dkv_own = dkv_own + shifted(
-            dkv_cols[:, first : first + count].astype(WIDE), -distance
+            dkv_cols[:, first : first + count].astype(WIDE), -distance, period
         ).astype(F32)
     grad_qkv = to_rows(
         jnp.concatenate([dq_cols, dkv_own], axis=0),
@@ -503,23 +734,42 @@
         GROUP + 2,
         full_a.shape[1],
     )
-    grad_h_one = sum_plane(dot(grad_qkv, full_a, 1, 1))
-    qkv_grad = sum_z(dot(h_one, grad_qkv, 0, 0))
+    qkv_part = column_products([(h_one, grad_qkv)], [(0, full_a.shape[1], 0)], full_a.shape[1])
+    grad_qkv, qkv_part = together(grad_qkv, qkv_part)
+    one_total = core_sum(own, product(grad_qkv, full_a))
+    one_total, qkv_part, sums[1] = together(one_total, qkv_part, sums[1])
+    qkv_grad = sum_z(qkv_part)
+    one_far = plane_sum_one(one_total)
+    out_part = column_products([(grad_branch, tied(attended, qkv_part))], [(0, nq, 0)], nq)
+    *one_far, to_x, to_y, to_xy = together(*one_far, *out_sends)
+    out_sends = to_x, to_y, to_xy
+    output = (x_mid + added(out_total, *out_sends)).astype(WIDE)
+    one_near = plane_sum_two(one_total, *one_far)
+    *one_near, qkv_grad, out_part = together(*one_near, qkv_grad, out_part)
+    out_grad = sum_z(out_part)
+    grad_h_one = added(one_total, *one_near)
     input_grad = (grad_mid + norm_back(grad_h_one, normed_one, inverse_one, gain_first)).astype(
         WIDE
     )
 
-    def columns(summed, width):
-        one, two = unshare_columns(summed, first_y)
-        return jnp.concatenate([one[:, :width], two[:, :width]], axis=1).astype(F32)
-
-    down_out = columns(down_grad, nf).T
-    gate_out = columns(gate_grad, nf)
-    up_out = columns(up_grad, nf)
-    o_out = columns(out_grad, nq).T
+    owned.append(unshare_columns(sums[1], first_y))
+    kept = [CHUNK, nf - CHUNK]
+
+    def unit_columns(k):
+        return jnp.concatenate(
+            [
+                owned[j][i][:, k * width[j] : k * width[j] + kept[j]]
+                for i in range(2)
+                for j in range(2)
+            ],
+            axis=1,
+        ).astype(F32)
+
+    down_out, gate_out, up_out = unit_columns(0).T, unit_columns(1), unit_columns(2)
     one, two = unshare_columns(qkv_grad, first_y)
     pick = lambda a, b: jnp.concatenate([one[:, a:b], two[:, a:b]], axis=1).astype(F32)
     q_out, k_out, v_out = pick(0, nq), pick(nq, nq + nk), pick(nq + nk, nq + 2 * nk)
+    o_out = jnp.concatenate(unshare_columns(out_grad, first_y), axis=1).T.astype(F32)
 
     def row_sums(weight, grad):
         return jnp.sum(weight.astype(F32) * grad, axis=1)

time: 964 us -> 812 us (0.84)
  Pallas kernels: 63.5 us -> 218 us
  matrix products: 148 us -> 24.6 us
  waiting for transfers between devices: 446 us -> 334 us
  blocking collectives: 35.8 us -> 0 us
  other arithmetic: 101 us -> 75 us
    pallas_call x0 -> x13, Pallas kernels: none -> 154 us  [the longest x4 55.5 us: column_products(): pl.pallas_call(functools.partial(grads_kernel, spans), grid=(model // row...]
    dot_general x15 -> x5, matrix products: 148 us -> 24.6 us  [dot(): lax.dot_general(a, b, (((ca,), (cb,)), ((), ())), preferred_element_type=...]
    reduce_scatter x5 -> x4, waiting for transfers between devices: 114 us -> 19.8 us  [sum_z(): lax.psum_scatter(block.astype(WIDE), 'z', scatter_dimension=0, tiled=True)]
    all_gather x5 -> x4, waiting for transfers between devices: 87.9 us -> 47.9 us  [gather_z(): return lax.all_gather(block, 'z', axis=0, tiled=True)]
    all_gather x2 -> x0, blocking collectives: 35.8 us -> none  [the longest x1 22.1 us: per_device(): lax.all_gather(jnp.stack([gain_attn, gain_mlp], 1).astype(WIDE), 'y', axi...]
    add x3 -> x0, other arithmetic: 18.4 us -> none  [sum_plane(): total = low[:4 * own].astype(F32) + got.astype(F32)]
    convert_element_type x1 -> x8, other arithmetic: 0.01 us -> 16.7 us  [the longest x1 4.97 us: per_device(): out_total = (out_mine.astype(F32) + out_got.astype(F32)).astype(WIDE)]
    ppermute x2, waiting for transfers between devices: 26.5 us -> 42.6 us  [shifted(): return lax.ppermute(block, 'z', route)]
  transfers between devices with their start and end apart: 81 -> 76, of which waited for: 36 -> 32; matrix products, arithmetic and copies ran while one was open for 26% -> 20% of each run, Pallas kernels for 7% -> 27%
where the time goes in v2:
time: 812 us; the launch traced here: 805 us
  waiting for transfers between devices  334 us (41%)
  Pallas kernels  218 us (27%)
  local copies, waits for them, and re-layouts  76.3 us (9%)
  other arithmetic  75 us (9%)
  starting transfers between devices  61.2 us (8%)
  matrix products  24.6 us (3%)
  between operations  16 us (2%)
    ppermute x62, waiting for transfers between devices, over(): return lax.ppermute(block, axis, SWAP)  222 us
    pallas_call x4, Pallas kernels, column_products(): pl.pallas_call(functools.partial(grads_kernel, spans), grid=(model // row...  55.5 us
    pallas_call x6, Pallas kernels, row_products(): pl.pallas_call(functools.partial(rows_kernel, spans, prior is not None),...  54.4 us
    ppermute x62, starting transfers between devices, over(): return lax.ppermute(block, axis, SWAP)  49.8 us
    all_gather x4, waiting for transfers between devices, gather_z(): return lax.all_gather(block, 'z', axis=0, tiled=True)  47.9 us
    ppermute x2, waiting for transfers between devices, shifted(): return lax.ppermute(block, 'z', route)  42.6 us
    unnamed x180, local copies, waits for them, and re-layouts  41.6 us
    pallas_call x2, Pallas kernels, hidden_units(): pl.pallas_call(hidden_kernel, grid=(count // rows,), in_specs=[pl.BlockSp...  34.8 us
  transfers between devices with their start and end apart: 76, of which 32 were waited for; matrix products, arithmetic and copies ran while one was open for 20% of the time, Pallas kernels for 27%

profile of v2, /device:TPU:0, one launch (start us, length us, event | category | flops | bytes accessed | tf_op | source)
XLA Modules:
  0.0 805.3 jit_solution(11509456242642950170)
XLA Ops:
  16.2 7.7 collective-permute-done.1
  37.1 11.0 %collective-permute-done = bf16[192,2560]{1,0:T(8,128)(2,1)} collective-permute-done((bf16[192,2560]{1,0:T(8,128)(2,1)S(1)}, bf16[192,2560]{1,0:T(8,128)(2,1)}, u32[]{:S(2)}, u32[]{:S(2)}) %collective-permute-start) | collective-permute-done | bytes 983072 | tf_op jit(solution)/shard_map/ppermute | solution.py:465
  59.7 8.0 collective-permute-done.4
  82.0 14.2 %collective-permute-done.13 = bf16[320,1152]{1,0:T(8,128)(2,1)} collective-permute-done((bf16[320,1152]{1,0:T(8,128)(2,1)}, bf16[320,1152]{1,0:T(8,128)(2,1)}, u32[]{:S(2)}, u32[]{:S(2)}) %collective-permute-start.13) | collective-permute-done | bytes 737312 | tf_op jit(solution)/shard_map/ppermute | solution.py:465
  118.5 9.2 %shard_map.212 = (bf16[1536,2560]{1,0:T(8,128)(2,1)}, f32[1536,512]{1,0:T(8,128)S(1)}) custom-call(bf16[1536,2560]{1,0:T(8,128)(2,1)} %constant_dynamic-update-slice_fusion.x_ref, f32[1,2560]{1,0:T(1,128)S(1)} %broadcast_in_dim_squeeze.2.gain_ref, bf16[2560,512]{1,0:T(8,128)(2,1)S(1)} %copy-done.12), custom_call_target="tpu_custom_call" | custom-call | flops 1000000 | bytes 100000 | tf_op jit(solution)/shard_map/pallas_call | solution.py:323
  133.9 17.2 %collective-permute-done.14 = bf16[320,1536]{1,0:T(8,128)(2,1)} collective-permute-done((bf16[320,1536]{1,0:T(8,128)(2,1)}, bf16[320,1536]{1,0:T(8,128)(2,1)}, u32[]{:S(2)}, u32[]{:S(2)}) %collective-permute-start.14) | collective-permute-done | bytes 983072 | tf_op jit(solution)/shard_map/ppermute | solution.py:465
  161.7 27.3 %shard_map.214 = (bf16[320,1536]{1,0:T(8,128)(2,1)S(1)}, f32[8,1536]{1,0:T(8,128)S(1)}) custom-call(s32[4,6]{1,0:T(4,128)S(1)} %pad_add_fusion.bounds_ref, bf16[320,1536]{1,0:T(8,128)(2,1)S(1)} %slice.433.q_ref, bf16[160,3072]{1,0:T(8,128)(2,1)S(1)} %pad_maximum_fusion.3.kv_ref, s32[1,1536]{1,0:T(1,128)S(1)} %broadcast_in_dim.2.start_ref), custom_call_target="tpu_custom_call" | custom-call | flops 1000000 | bytes 100000 | tf_op jit(solution)/shard_map/pallas_call | solution.py:167
  212.2 7.7 collective-permute-done.22
  224.7 19.7 %collective-permute-done.23 = bf16[192,2560]{1,0:T(8,128)(2,1)S(1)} collective-permute-done((bf16[192,2560]{1,0:T(8,128)(2,1)S(1)}, bf16[192,2560]{1,0:T(8,128)(2,1)S(1)}, u32[]{:S(2)}, u32[]{:S(2)}) %collective-permute-start.23) | collective-permute-done | bytes 983072 | tf_op jit(solution)/shard_map/ppermute | solution.py:465
  250.1 20.2 %collective-permute-done.25 = bf16[192,2560]{1,0:T(8,128)(2,1)S(1)} collective-permute-done((bf16[192,2560]{1,0:T(8,128)(2,1)S(1)}, bf16[192,2560]{1,0:T(8,128)(2,1)S(1)}, u32[]{:S(2)}, u32[]{:S(2)}) %collective-permute-start.25) | collective-permute-done | bytes 983072 | tf_op jit(solution)/shard_map/ppermute | solution.py:465
  287.9 17.1 %shard_map.216.refs_0_.refs_1_.refs_3_ = bf16[1536,1152]{1,0:T(8,128)(2,1)S(1)} custom-call(bf16[1536,2560]{1,0:T(8,128)(2,1)} %constant_dynamic-update-slice_fusion.10.h_ref.refs_2_, bf16[1536,2560]{1,0:T(8,128)(2,1)} %copy-done.18, bf16[2560,1152]{1,0:T(8,128)(2,1)} %all-gather.11.cloned.1.call-done.weight_ref.refs_1_), custom_call_target="tpu_custom_call" | custom-call | flops 1000000 | bytes 100000 | tf_op jit(solution)/shard_map/pallas_call | solution.py:358
  305.0 16.2 %shard_map.219 = bf16[2560,1152]{1,0:T(8,128)(2,1)} custom-call(bf16[1536,2560]{1,0:T(8,128)(2,1)} %copy-done.18, bf16[1536,1152]{1,0:T(8,128)(2,1)S(1)} %shard_map.216.refs_0_.refs_1_.refs_3_, bf16[1536,2560]{1,0:T(8,128)(2,1)} %constant_dynamic-update-slice_fusion.10.h_ref.refs_2_, bf16[1536,1152]{1,0:T(8,128)(2,1)S(1)} %shard_map.216.refs_0_.refs_1_.refs_3_), custom_call_target="tpu_custom_call" | custom-call | flops 1000000 | bytes 100000 | tf_op jit(solution)/shard_map/pallas_call | solution.py:426
  321.2 7.5 shard_map.218.refs_2_
  328.7 7.4 shard_map.217.refs_2_
  336.1 47.9 %all-gather.9.cloned.1.call-done.weight_ref.refs_1_.refs_3_ = bf16[2560,1536]{1,0:T(8,128)(2,1)} async-done(((bf16[640,1536]{1,0:T(8,128)(2,1)}), bf16[2560,1536]{1,0:T(8,128)(2,1)}) %all-gather.9.cloned.1.call-update) | async-done | bytes 7864336 | tf_op jit(solution)/shard_map/all_gather | solution.py:547
  384.3 17.8 %shard_map.220.refs_0_.refs_1_.refs_3_.refs_2_ = bf16[1536,1536]{1,0:T(8,128)(2,1)S(1)} custom-call(bf16[1536,2560]{1,0:T(8,128)(2,1)} %constant_dynamic-update-slice_fusion.10.h_ref.refs_2_, bf16[1536,2560]{1,0:T(8,128)(2,1)} %copy-done.18, bf16[2560,1536]{1,0:T(8,128)(2,1)} %all-gather.9.cloned.1.call-done.weight_ref.refs_1_.refs_3_), custom_call_target="tpu_custom_call" | custom-call | flops 1000000 | bytes 100000 | tf_op jit(solution)/shard_map/pallas_call | solution.py:358
  404.2 8.7 %shard_map.222 = bf16[768,2560]{1,0:T(8,128)(2,1)S(1)} custom-call(bf16[1536,1536]{1,0:T(8,128)(2,1)} %copy-done, bf16[2560,1536]{1,0:T(8,128)(2,1)} %all-gather.9.cloned.1.call-done.weight_ref.refs_1_.refs_3_, bf16[768,2560]{1,0:T(8,128)(2,1)} %shard_map.218.refs_2_), custom_call_target="tpu_custom_call" | custom-call | flops 1000000 | bytes 100000 | tf_op jit(solution)/shard_map/pallas_call | solution.py:395
  412.9 8.7 %shard_map.221 = bf16[768,2560]{1,0:T(8,128)(2,1)S(1)} custom-call(bf16[1536,1536]{1,0:T(8,128)(2,1)} %copy-done, bf16[2560,1536]{1,0:T(8,128)(2,1)} %all-gather.9.cloned.1.call-done.weight_ref.refs_1_.refs_3_, bf16[768,2560]{1,0:T(8,128)(2,1)} %shard_map.217.refs_2_), custom_call_target="tpu_custom_call" | custom-call | flops 1000000 | bytes 100000 | tf_op jit(solution)/shard_map/pallas_call | solution.py:395
  428.2 10.6 %collective-permute-done.41 = bf16[96,2560]{1,0:T(8,128)(2,1)S(1)} collective-permute-done((bf16[96,2560]{1,0:T(8,128)(2,1)S(1)}, bf16[96,2560]{1,0:T(8,128)(2,1)S(1)}, u32[]{:S(2)}, u32[]{:S(2)}) %collective-permute-start.41) | collective-permute-done | bytes 491552 | tf_op jit(solution)/shard_map/ppermute | solution.py:465
  444.3 17.7 %shard_map.223 = bf16[2560,1536]{1,0:T(8,128)(2,1)} custom-call(bf16[1536,2560]{1,0:T(8,128)(2,1)} %copy-done.18, bf16[1536,1536]{1,0:T(8,128)(2,1)S(1)} %bitcast.41, bf16[1536,2560]{1,0:T(8,128)(2,1)} %constant_dynamic-update-slice_fusion.10.h_ref.refs_2_, bf16[1536,1536]{1,0:T(8,128)(2,1)S(1)} %bitcast.41), custom_call_target="tpu_custom_call" | custom-call | flops 1000000 | bytes 100000 | tf_op jit(solution)/shard_map/pallas_call | solution.py:426
  478.0 11.2 %shard_map.224 = bf16[768,2560]{1,0:T(8,128)(2,1)} custom-call(bf16[1536,1152]{1,0:T(8,128)(2,1)S(1)} %shard_map.216.refs_0_.refs_1_.refs_3_, bf16[2560,1152]{1,0:T(8,128)(2,1)} %all-gather.11.cloned.1.call-done.weight_ref.refs_1_, bf16[1536,1536]{1,0:T(8,128)(2,1)} %copy-done, bf16[2560,1536]{1,0:T(8,128)(2,1)} %all-gather.9.cloned.1.call-done.weight_ref.refs_1_.refs_3_), custom_call_target="tpu_custom_call" | custom-call | flops 1000000 | bytes 100000 | tf_op jit(solution)/shard_map/pallas_call | solution.py:395
  489.1 8.0 collective-permute-done.44
  502.0 11.0 %shard_map.225 = bf16[768,2560]{1,0:T(8,128)(2,1)} custom-call(bf16[1536,1152]{1,0:T(8,128)(2,1)S(1)} %shard_map.216.refs_0_.refs_1_.refs_3_, bf16[2560,1152]{1,0:T(8,128)(2,1)} %all-gather.11.cloned.1.call-done.weight_ref.refs_1_, bf16[1536,1536]{1,0:T(8,128)(2,1)} %copy-done, bf16[2560,1536]{1,0:T(8,128)(2,1)} %all-gather.9.cloned.1.call-done.weight_ref.refs_1_.refs_3_), custom_call_target="tpu_custom_call" | custom-call | flops 1000000 | bytes 100000 | tf_op jit(solution)/shard_map/pallas_call | solution.py:395
  526.0 7.5 convolution_convert_fusion.2
  538.5 32.0 %shard_map.227 = (f32[320,1536]{1,0:T(8,128)S(1)}, f32[160,3072]{1,0:T(8,128)}) custom-call(s32[4,6]{1,0:T(4,128)S(1)} %pad_add_fusion.bounds_ref, bf16[320,1536]{1,0:T(8,128)(2,1)S(1)} %copy-done.4, bf16[160,3072]{1,0:T(8,128)(2,1)S(1)} %copy-done.2, s32[1,1536]{1,0:T(1,128)S(1)} %broadcast_in_dim.2.start_ref, bf16[320,1536]{1,0:T(8,128)(2,1)S(1)} %copy-done.15, ...), custom_call_target="tpu_custom_call" | custom-call | flops 1000000 | bytes 100000 | tf_op jit(solution)/shard_map/pallas_call | solution.py:277
  573.1 42.6 %collective-permute-done.53 = bf16[160,1536]{1,0:T(8,128)(2,1)S(1)} collective-permute-done((bf16[160,1536]{1,0:T(8,128)(2,1)S(1)}, bf16[160,1536]{1,0:T(8,128)(2,1)S(1)}, u32[]{:S(2)}, u32[]{:S(2)}) %collective-permute-start.53) | collective-permute-done | bytes 491552 | tf_op jit(solution)/shard_map/ppermute | solution.py:461
  618.4 10.7 %shard_map.229 = bf16[2560,512]{1,0:T(8,128)(2,1)} custom-call(bf16[1536,2560]{1,0:T(8,128)(2,1)} %get-tuple-element.109.refs_0_, bf16[1536,512]{1,0:T(8,128)(2,1)S(1)} %shard_map.228.refs_1_), custom_call_target="tpu_custom_call" | custom-call | flops 1000000 | bytes 100000 | tf_op jit(solution)/shard_map/pallas_call | solution.py:426
  640.3 33.8 %collective-permute-done.63 = bf16[320,1152]{1,0:T(8,128)(2,1)S(1)} collective-permute-done((bf16[320,1152]{1,0:T(8,128)(2,1)S(1)}, bf16[320,1152]{1,0:T(8,128)(2,1)S(1)}, u32[]{:S(2)}, u32[]{:S(2)}) %collective-permute-start.63) | collective-permute-done | bytes 737312 | tf_op jit(solution)/shard_map/ppermute | solution.py:465
  686.8 10.9 %shard_map.230 = bf16[2560,320]{1,0:T(8,128)(2,1)} custom-call(bf16[1536,2560]{1,0:T(8,128)(2,1)} %constant_dynamic-update-slice_fusion.30.refs_0_, bf16[1536,320]{1,0:T(8,128)(2,1)S(1)} %copy-done.11), custom_call_target="tpu_custom_call" | custom-call | flops 1000000 | bytes 100000 | tf_op jit(solution)/shard_map/pallas_call | solution.py:426
  698.5 7.3 collective-permute-done.56
  716.3 10.5 %collective-permute-done.64 = bf16[320,1536]{1,0:T(8,128)(2,1)S(1)} collective-permute-done((bf16[320,1536]{1,0:T(8,128)(2,1)S(1)}, bf16[320,1536]{1,0:T(8,128)(2,1)S(1)}, u32[]{:S(2)}, u32[]{:S(2)}) %collective-permute-start.64) | collective-permute-done | bytes 983072 | tf_op jit(solution)/shard_map/ppermute | solution.py:465
  767.3 19.8 %reduce-scatter.11.cloned.1.call-done = bf16[640,320]{1,0:T(8,128)(2,1)} async-done(((bf16[2560,320]{1,0:T(8,128)(2,1)}), bf16[640,320]{1,0:T(8,128)(2,1)}) %reduce-scatter.11.cloned.1.call-update) | async-done | bytes 409616 | tf_op jit(solution)/shard_map/reduce_scatter | solution.py:551
  (464 shorter events, 282.4 us)
Async XLA Ops:
  7.2 108.7 %all-gather.5.cloned.1.call-start = ((), (), s32[]{:S(2)}) async-start(), calls=%async_computation.4 | async-start | bytes 3276800 | tf_op jit(solution)/shard_map/all_gather | solution.py:547
  24.9 130.5 %all-gather.7.cloned.1.call-start = ((), (), s32[]{:S(2)}) async-start(), calls=%async_computation.5 | async-start | bytes 2457600 | tf_op jit(solution)/shard_map/all_gather | solution.py:547
  26.8 81.1 %collective-permute-start.5 = (bf16[192,2560]{1,0:T(8,128)(2,1)S(1)}, bf16[192,2560]{1,0:T(8,128)(2,1)}, u32[]{:S(2)}, u32[]{:S(2)}) collective-permute-start(bf16[192,2560]{1,0:T(8,128)(2,1)S(1)} %copy-done.23), channel_id=1, source_target_pairs={{0,1},{1,0},{2,3},{3,2},{4,5},{5,4},{6,7},{7,6},{8,9},{9,8},{10,11... | collective-permute-start | bytes 2949128 | tf_op jit(solution)/shard_map/ppermute | solution.py:465
  26.8 55.2 %collective-permute-start.10 = (s32[768]{0:T(1024)S(1)}, s32[768]{0:T(1024)S(1)}, u32[]{:S(2)}, u32[]{:S(2)}) collective-permute-start(s32[768]{0:T(1024)S(1)} %copy-done.65), channel_id=1, source_target_pairs={{0,4},{4,0},{1,5},{5,1},{2,6},{6,2},{3,7},{7,3},{8,12},{12,8},{9,1... | collective-permute-start | bytes 9224 | tf_op jit(solution)/shard_map/ppermute | solution.py:626
  33.3 24.7 %collective-permute-start.2 = (bf16[192,2560]{1,0:T(8,128)(2,1)S(1)}, bf16[192,2560]{1,0:T(8,128)(2,1)S(1)}, u32[]{:S(2)}, u32[]{:S(2)}) collective-permute-start(bf16[192,2560]{1,0:T(8,128)(2,1)S(1)} %copy-done.23), channel_id=1, source_target_pairs={{0,4},{4,0},{1,5},{5,1},{2,6},{6,2},{3,7},{7,3},{8,12},{12,8},{9,1... | collective-permute-start | bytes 2949128 | tf_op jit(solution)/shard_map/ppermute | solution.py:465
  77.2 210.7 %all-gather.11.cloned.1.call-start = ((), (), s32[]{:S(2)}) async-start(), calls=%async_computation.7 | async-start | bytes 7372800 | tf_op jit(solution)/shard_map/all_gather | solution.py:547
  99.3 284.7 %all-gather.9.cloned.1.call-start = ((), (), s32[]{:S(2)}) async-start(), calls=%async_computation.6 | async-start | bytes 9830400 | tf_op jit(solution)/shard_map/all_gather | solution.py:547
  105.7 49.7 %collective-permute-start.16 = (bf16[192,2560]{1,0:T(8,128)(2,1)}, bf16[192,2560]{1,0:T(8,128)(2,1)}, u32[]{:S(2)}, u32[]{:S(2)}) collective-permute-start(bf16[192,2560]{1,0:T(8,128)(2,1)} %param.25), channel_id=1, source_target_pairs={{0,4},{4,0},{1,5},{5,1},{2,6},{6,2},{3,7},{7,3},{8,12},{12,8},{9,1... | collective-permute-start | bytes 2949128 | tf_op jit(solution)/shard_map/ppermute | solution.py:465
  107.9 47.5 %collective-permute-start.15 = (bf16[192,2560]{1,0:T(8,128)(2,1)}, bf16[192,2560]{1,0:T(8,128)(2,1)}, u32[]{:S(2)}, u32[]{:S(2)}) collective-permute-start(bf16[192,2560]{1,0:T(8,128)(2,1)} %param.25), channel_id=1, source_target_pairs={{0,2},{2,0},{1,3},{3,1},{4,6},{6,4},{5,7},{7,5},{8,10},{10,8},{9,1... | collective-permute-start | bytes 2949128 | tf_op jit(solution)/shard_map/ppermute | solution.py:465
  111.4 39.7 %collective-permute-start.14 = (bf16[320,1536]{1,0:T(8,128)(2,1)}, bf16[320,1536]{1,0:T(8,128)(2,1)}, u32[]{:S(2)}, u32[]{:S(2)}) collective-permute-start(bf16[320,1536]{1,0:T(8,128)(2,1)} %broadcast_select_fusion.6), channel_id=1, source_target_pairs={{0,4},{4,0},{1,5},{5,1},{2,6},{6,2},{3,7},{7,3},{8,12},{12,8},{9,1... | collective-permute-start | bytes 2949128 | tf_op jit(solution)/shard_map/ppermute | solution.py:465
  130.1 24.1 %collective-permute-start.11 = (bf16[160,1536]{1,0:T(8,128)(2,1)}, bf16[160,1536]{1,0:T(8,128)(2,1)}, u32[]{:S(2)}, u32[]{:S(2)}) collective-permute-start(bf16[160,1536]{1,0:T(8,128)(2,1)} %slice.434), channel_id=1, source_target_pairs={{0,8},{16,24},{1,9},{17,25},{2,10},{18,26},{3,11},{19,27},{4,12},{... | collective-permute-start | bytes 1474568 | tf_op jit(solution)/shard_map/ppermute | solution.py:461
  159.4 30.2 %collective-permute-start.18 = (bf16[96,2560]{1,0:T(8,128)(2,1)}, bf16[96,2560]{1,0:T(8,128)(2,1)S(1)}, u32[]{:S(2)}, u32[]{:S(2)}) collective-permute-start(bf16[96,2560]{1,0:T(8,128)(2,1)} %slice.354), channel_id=1, source_target_pairs={{0,4},{4,0},{1,5},{5,1},{2,6},{6,2},{3,7},{7,3},{8,12},{12,8},{9,1... | collective-permute-start | bytes 1474568 | tf_op jit(solution)/shard_map/ppermute | solution.py:465
  159.9 29.7 %collective-permute-start.17 = (bf16[96,2560]{1,0:T(8,128)(2,1)}, bf16[96,2560]{1,0:T(8,128)(2,1)}, u32[]{:S(2)}, u32[]{:S(2)}) collective-permute-start(bf16[96,2560]{1,0:T(8,128)(2,1)} %slice.353), channel_id=1, source_target_pairs={{0,2},{2,0},{1,3},{3,1},{4,6},{6,4},{5,7},{7,5},{8,10},{10,8},{9,1... | collective-permute-start | bytes 1474568 | tf_op jit(solution)/shard_map/ppermute | solution.py:465
  194.9 331.1 %reduce-scatter.5.cloned.1.call-start = ((), (), s32[]{:S(2)}) async-start(), calls=%async_computation.8 | async-start | bytes 7372800 | tf_op jit(solution)/shard_map/reduce_scatter | solution.py:551
  195.4 28.5 %collective-permute-start.33 = (bf16[192,2560]{1,0:T(8,128)(2,1)}, bf16[192,2560]{1,0:T(8,128)(2,1)S(1)}, u32[]{:S(2)}, u32[]{:S(2)}) collective-permute-start(bf16[192,2560]{1,0:T(8,128)(2,1)} %param.25), channel_id=1, source_target_pairs={{0,1},{1,0},{2,3},{3,2},{4,5},{5,4},{6,7},{7,6},{8,9},{9,8},{10,11... | collective-permute-start | bytes 2949128 | tf_op jit(solution)/shard_map/ppermute | solution.py:465
  197.3 52.6 %collective-permute-start.35 = (bf16[192,2560]{1,0:T(8,128)(2,1)}, bf16[192,2560]{1,0:T(8,128)(2,1)S(1)}, u32[]{:S(2)}, u32[]{:S(2)}) collective-permute-start(bf16[192,2560]{1,0:T(8,128)(2,1)} %collective-permute-done.16), channel_id=1, source_target_pairs={{0,1},{1,0},{2,3},{3,2},{4,5},{5,4},{6,7},{7,6},{8,9},{9,8},{10,11... | collective-permute-start | bytes 2949128 | tf_op jit(solution)/shard_map/ppermute | solution.py:465
  197.4 26.6 %collective-permute-start.34 = (bf16[192,2560]{1,0:T(8,128)(2,1)}, bf16[192,2560]{1,0:T(8,128)(2,1)S(1)}, u32[]{:S(2)}, u32[]{:S(2)}) collective-permute-start(bf16[192,2560]{1,0:T(8,128)(2,1)} %collective-permute-done.15), channel_id=1, source_target_pairs={{0,1},{1,0},{2,3},{3,2},{4,5},{5,4},{6,7},{7,6},{8,9},{9,8},{10,11... | collective-permute-start | bytes 2949128 | tf_op jit(solution)/shard_map/ppermute | solution.py:465
  223.9 26.0 %collective-permute-start.36 = (bf16[96,2560]{1,0:T(8,128)(2,1)}, bf16[96,2560]{1,0:T(8,128)(2,1)S(1)}, u32[]{:S(2)}, u32[]{:S(2)}) collective-permute-start(bf16[96,2560]{1,0:T(8,128)(2,1)} %collective-permute-done.17), channel_id=1, source_target_pairs={{0,1},{1,0},{2,3},{3,2},{4,5},{5,4},{6,7},{7,6},{8,9},{9,8},{10,11... | collective-permute-start | bytes 1474568 | tf_op jit(solution)/shard_map/ppermute | solution.py:465
  224.1 25.9 %collective-permute-start.37 = (bf16[96,2560]{1,0:T(8,128)(2,1)S(1)}, bf16[96,2560]{1,0:T(8,128)(2,1)S(1)}, u32[]{:S(2)}, u32[]{:S(2)}) collective-permute-start(bf16[96,2560]{1,0:T(8,128)(2,1)S(1)} %collective-permute-done.18), channel_id=1, source_target_pairs={{0,1},{1,0},{2,3},{3,2},{4,5},{5,4},{6,7},{7,6},{8,9},{9,8},{10,11... | collective-permute-start | bytes 1474568 | tf_op jit(solution)/shard_map/ppermute | solution.py:465
  250.1 33.2 %collective-permute-start.28 = (bf16[192,2560]{1,0:T(8,128)(2,1)S(1)}, bf16[192,2560]{1,0:T(8,128)(2,1)S(1)}, u32[]{:S(2)}, u32[]{:S(2)}) collective-permute-start(bf16[192,2560]{1,0:T(8,128)(2,1)S(1)} %get-tuple-element.185), channel_id=1, source_target_pairs={{0,1},{1,0},{2,3},{3,2},{4,5},{5,4},{6,7},{7,6},{8,9},{9,8},{10,11... | collective-permute-start | bytes 2949128 | tf_op jit(solution)/shard_map/ppermute | solution.py:465
  384.0 296.8 %reduce-scatter.7.cloned.1.call-start = ((), (), s32[]{:S(2)}) async-start(), calls=%async_computation.9 | async-start | bytes 9830400 | tf_op jit(solution)/shard_map/reduce_scatter | solution.py:551
  469.6 277.6 %reduce-scatter.9.cloned.1.call-start = ((), (), s32[]{:S(2)}) async-start(), calls=%async_computation.10 | async-start | bytes 3276800 | tf_op jit(solution)/shard_map/reduce_scatter | solution.py:551
  571.8 43.9 %collective-permute-start.53 = (bf16[160,1536]{1,0:T(8,128)(2,1)S(1)}, bf16[160,1536]{1,0:T(8,128)(2,1)S(1)}, u32[]{:S(2)}, u32[]{:S(2)}) collective-permute-start(bf16[160,1536]{1,0:T(8,128)(2,1)S(1)} %slice.578), channel_id=1, source_target_pairs={{8,0},{24,16},{9,1},{25,17},{10,2},{26,18},{11,3},{27,19},{12,4},{... | collective-permute-start | bytes 1474568 | tf_op jit(solution)/shard_map/ppermute | solution.py:461
  633.2 42.9 %collective-permute-start.54 = (bf16[768,2560]{1,0:T(8,128)(2,1)S(1)}, bf16[768,2560]{1,0:T(8,128)(2,1)S(1)}, u32[]{:S(2)}, u32[]{:S(2)}) collective-permute-start(bf16[768,2560]{1,0:T(8,128)(2,1)S(1)} %convolution_convert_fusion), channel_id=1, source_target_pairs={{0,1},{1,0},{2,3},{3,2},{4,5},{5,4},{6,7},{7,6},{8,9},{9,8},{10,11... | collective-permute-start | bytes 11796488 | tf_op jit(solution)/shard_map/ppermute | solution.py:465
  633.7 40.5 %collective-permute-start.63 = (bf16[320,1152]{1,0:T(8,128)(2,1)S(1)}, bf16[320,1152]{1,0:T(8,128)(2,1)S(1)}, u32[]{:S(2)}, u32[]{:S(2)}) collective-permute-start(bf16[320,1152]{1,0:T(8,128)(2,1)S(1)} %broadcast_select_fusion.10), channel_id=1, source_target_pairs={{0,4},{4,0},{1,5},{5,1},{2,6},{6,2},{3,7},{7,3},{8,12},{12,8},{9,1... | collective-permute-start | bytes 2211848 | tf_op jit(solution)/shard_map/ppermute | solution.py:465
  636.9 61.0 %collective-permute-start.59 = (bf16[192,2560]{1,0:T(8,128)(2,1)}, bf16[192,2560]{1,0:T(8,128)(2,1)}, u32[]{:S(2)}, u32[]{:S(2)}) collective-permute-start(bf16[192,2560]{1,0:T(8,128)(2,1)} %get-tuple-element.196), channel_id=1, source_target_pairs={{0,6},{2,4},{4,2},{6,0},{1,7},{3,5},{5,3},{7,1},{8,14},{10,12},{12... | collective-permute-start | bytes 2949128 | tf_op jit(solution)/shard_map/ppermute | solution.py:469
  638.4 60.1 %collective-permute-start.58 = (bf16[192,2560]{1,0:T(8,128)(2,1)}, bf16[192,2560]{1,0:T(8,128)(2,1)}, u32[]{:S(2)}, u32[]{:S(2)}) collective-permute-start(bf16[192,2560]{1,0:T(8,128)(2,1)} %get-tuple-element.197), channel_id=1, source_target_pairs={{0,4},{4,0},{1,5},{5,1},{2,6},{6,2},{3,7},{7,3},{8,12},{12,8},{9,1... | collective-permute-start | bytes 2949128 | tf_op jit(solution)/shard_map/ppermute | solution.py:465
  639.8 58.7 %collective-permute-start.57 = (bf16[192,2560]{1,0:T(8,128)(2,1)}, bf16[192,2560]{1,0:T(8,128)(2,1)}, u32[]{:S(2)}, u32[]{:S(2)}) collective-permute-start(bf16[192,2560]{1,0:T(8,128)(2,1)} %get-tuple-element.198), channel_id=1, source_target_pairs={{0,2},{2,0},{1,3},{3,1},{4,6},{6,4},{5,7},{7,5},{8,10},{10,8},{9,1... | collective-permute-start | bytes 2949128 | tf_op jit(solution)/shard_map/ppermute | solution.py:465
  680.9 106.2 %reduce-scatter.11.cloned.1.call-start = ((), (), s32[]{:S(2)}) async-start(), calls=%async_computation.11 | async-start | bytes 2457600 | tf_op jit(solution)/shard_map/reduce_scatter | solution.py:551
  697.8 28.9 %collective-permute-start.64 = (bf16[320,1536]{1,0:T(8,128)(2,1)S(1)}, bf16[320,1536]{1,0:T(8,128)(2,1)S(1)}, u32[]{:S(2)}, u32[]{:S(2)}) collective-permute-start(bf16[320,1536]{1,0:T(8,128)(2,1)S(1)} %broadcast_select_fusion.2), channel_id=1, source_target_pairs={{0,4},{4,0},{1,5},{5,1},{2,6},{6,2},{3,7},{7,3},{8,12},{12,8},{9,1... | collective-permute-start | bytes 2949128 | tf_op jit(solution)/shard_map/ppermute | solution.py:465
  708.5 33.0 %collective-permute-start.60 = (bf16[192,2560]{1,0:T(8,128)(2,1)}, bf16[192,2560]{1,0:T(8,128)(2,1)}, u32[]{:S(2)}, u32[]{:S(2)}) collective-permute-start(bf16[192,2560]{1,0:T(8,128)(2,1)} %pad_maximum_fusion.8), channel_id=1, source_target_pairs={{0,2},{2,0},{1,3},{3,1},{4,6},{6,4},{5,7},{7,5},{8,10},{10,8},{9,1... | collective-permute-start | bytes 2949128 | tf_op jit(solution)/shard_map/ppermute | solution.py:465
  711.1 36.1 %collective-permute-start.61 = (bf16[192,2560]{1,0:T(8,128)(2,1)}, bf16[192,2560]{1,0:T(8,128)(2,1)}, u32[]{:S(2)}, u32[]{:S(2)}) collective-permute-start(bf16[192,2560]{1,0:T(8,128)(2,1)} %pad_maximum_fusion.9), channel_id=1, source_target_pairs={{0,4},{4,0},{1,5},{5,1},{2,6},{6,2},{3,7},{7,3},{8,12},{12,8},{9,1... | collective-permute-start | bytes 2949128 | tf_op jit(solution)/shard_map/ppermute | solution.py:465
  (115 other events, 1595.6 us)
Sparse Core Ops, SparseCore 0:
  25.1 56.2 all-gather.4
  83.5 42.3 all-gather.6
  128.0 111.4 all-gather.10
  241.5 142.4 all-gather.8
  386.2 102.5 reduce-scatter.4
  491.0 147.2 reduce-scatter.6
  681.0 50.3 reduce-scatter.8
  747.4 39.6 reduce-scatter.10

commit v3 on v2

--- a/solution.py
+++ b/solution.py
@@ -309,6 +309,51 @@
     )(bounds, q_cols, kv_cols, starts, out_cols, logs, grad_cols)
 
 
+TINY = pl.CostEstimate(flops=10**6, bytes_accessed=10**5, transcendentals=0)
+ANY = pl.BlockSpec(memory_space=pl.ANY)
+
+
+def params():
+    return pltpu.CompilerParams(vmem_limit_bytes=VMEM_BYTES)
+
+
+def join_kernel(*refs):
+    *parts, out, whole, sems = refs
+    pairs, first = [], 0
+    for k, part in enumerate(parts):
+        rows = pl.ds(first, part.shape[0])
+        pairs.append(
+            (
+                pltpu.make_async_copy(part, whole.at[rows, :], sems.at[0, k]),
+                pltpu.make_async_copy(whole.at[rows, :], out.at[rows, :], sems.at[1, k]),
+            )
+        )
+        first += part.shape[0]
+    for copy_in, _ in pairs:
+        copy_in.start()
+    for copy_in, copy_out in pairs:
+        copy_in.wait()
+        copy_out.start()
+    for _, copy_out in pairs:
+        copy_out.wait()
+
+
+def join(parts):
+    rows = sum(part.shape[0] for part in parts)
+    return pl.pallas_call(
+        join_kernel,
+        in_specs=[ANY] * len(parts),
+        out_specs=ANY,
+        out_shape=jax.ShapeDtypeStruct((rows, parts[0].shape[1]), parts[0].dtype),
+        scratch_shapes=[
+            pltpu.VMEM((rows, parts[0].shape[1]), parts[0].dtype),
+            pltpu.SemaphoreType.DMA((2, len(parts))),
+        ],
+        compiler_params=params(),
+        cost_estimate=TINY,
+    )(*parts)
+
+
 def project_kernel(x_ref, gain_ref, weight_ref, h_ref, out_ref):
     x = x_ref[...].astype(F32)
     inverse = lax.rsqrt(jnp.mean(x * x, axis=-1, keepdims=True) + eps)
@@ -341,106 +386,107 @@
     )(x_all, gain_row, weights)
 
 
-def hidden_kernel(h_ref, cot_ref, weight_ref, out_ref):
+def narrow_kernel(a_ref, weight_ref, out_ref):
+    out_ref[...] = dot(a_ref[...], weight_ref[...], 1, 0).astype(out_ref.dtype)
+
+
+def whole(array):
+    return pl.BlockSpec(array.shape, lambda i: (0, 0), pipeline_mode=pl.Buffered(1))
+
+
+def narrow(a, weight, rows=256):
+    count, model = a.shape
+    return pl.pallas_call(
+        narrow_kernel,
+        grid=(count // rows,),
+        in_specs=[pl.BlockSpec((rows, model), lambda i: (i, 0)), whole(weight)],
+        out_specs=pl.BlockSpec((rows, weight.shape[1]), lambda i: (i, 0)),
+        out_shape=jax.ShapeDtypeStruct((count, weight.shape[1]), WIDE),
+        compiler_params=params(),
+        cost_estimate=TINY,
+    )(a, weight)
+
+
+def units_kernel(has_prior, h_ref, cot_ref, weight_ref, *refs):
+    *prior, acts_ref, back_ref, out_ref = refs
     width = weight_ref.shape[1] // 3
-    gate = dot(h_ref[...], weight_ref[:, width : 2 * width], 1, 0)
-    up = dot(h_ref[...], weight_ref[:, 2 * width :], 1, 0)
-    grad = dot(cot_ref[...], weight_ref[:, :width], 1, 0)
+    down_w, gate_w, up_w = [weight_ref[:, k * width : (k + 1) * width] for k in range(3)]
+    gate = dot(h_ref[...], gate_w, 1, 0)
+    up = dot(h_ref[...], up_w, 1, 0)
+    grad = dot(cot_ref[...], down_w, 1, 0)
     sigma = 1.0 / (1.0 + jnp.exp(-gate))
     silu = gate * sigma
-    out_ref[:, :width] = (silu * up).astype(WIDE)
-    out_ref[:, width : 2 * width] = (grad * up * sigma * (1.0 + gate * (1.0 - sigma))).astype(WIDE)
-    out_ref[:, 2 * width :] = (grad * silu).astype(WIDE)
-
-
-def hidden_units(h_two, cot, weights, rows=256):
+    hidden = (silu * up).astype(WIDE)
+    grad_gate = (grad * up * sigma * (1.0 + gate * (1.0 - sigma))).astype(WIDE)
+    grad_up = (grad * silu).astype(WIDE)
+    acts_ref[:, :width] = hidden
+    acts_ref[:, width : 2 * width] = grad_gate
+    acts_ref[:, 2 * width :] = grad_up
+    back = dot(grad_gate, gate_w, 1, 1) + dot(grad_up, up_w, 1, 1)
+    out = dot(hidden, down_w, 1, 1)
+    if has_prior:
+        back, out = back + prior[0][...].astype(F32), out + prior[1][...].astype(F32)
+    back_ref[...] = back.astype(WIDE)
+    out_ref[...] = out.astype(WIDE)
+
+
+def hidden_units(h_two, cot, weights, first, count, prior=(), rows=256):
+    model, width = h_two.shape[1], weights.shape[1]
+    at = first // rows
+    block = lambda n: pl.BlockSpec((rows, n), lambda i: (i, 0))
+    shape = lambda n: jax.ShapeDtypeStruct((count, n), WIDE)
+    return pl.pallas_call(
+        functools.partial(units_kernel, bool(prior)),
+        grid=(count // rows,),
+        in_specs=[pl.BlockSpec((rows, model), lambda i: (i + at, 0))] * 2
+        + [whole(weights)]
+        + [block(model)] * len(prior),
+        out_specs=[block(width), block(model), block(model)],
+        out_shape=[shape(width), shape(model), shape(model)],
+        compiler_params=params(),
+        cost_estimate=TINY,
+    )(h_two, cot, weights, *prior)
+
+
+def unit_grads_kernel(h_ref, cot_ref, mine_ref, other_ref, out_ref):
+    half, width = mine_ref.shape[0], mine_ref.shape[1] // 3
+    for a_ref, columns in ((cot_ref, slice(0, width)), (h_ref, slice(width, 3 * width))):
+        out_ref[:, columns] = (
+            dot(a_ref[:half, :], mine_ref[:, columns], 0, 0)
+            + dot(a_ref[half:, :], other_ref[:, columns], 0, 0)
+        ).astype(WIDE)
+
+
+def unit_grads(h_two, cot, mine, other, rows=256):
     count, model = h_two.shape
-    return pl.pallas_call(
-        hidden_kernel,
-        grid=(count // rows,),
-        in_specs=[
-            pl.BlockSpec((rows, model), lambda i: (i, 0)),
-            pl.BlockSpec((rows, model), lambda i: (i, 0)),
-            pl.BlockSpec(weights.shape, lambda i: (0, 0), pipeline_mode=pl.Buffered(1)),
-        ],
-        out_specs=pl.BlockSpec((rows, weights.shape[1]), lambda i: (i, 0)),
-        out_shape=jax.ShapeDtypeStruct((count, weights.shape[1]), WIDE),
-        compiler_params=pltpu.CompilerParams(vmem_limit_bytes=VMEM_BYTES),
-        cost_estimate=pl.CostEstimate(flops=10**6, bytes_accessed=10**5, transcendentals=0),
-    )(h_two, cot, weights)
-
-
-def rows_kernel(spans, has_prior, *refs):
-    out_ref = refs[-1]
-    total = refs[-2][...].astype(F32) if has_prior else None
-    for k, (lo, hi) in enumerate(spans):
-        part = dot(refs[2 * k][:, lo:hi], refs[2 * k + 1][:, lo:hi], 1, 1)
-        total = part if total is None else total + part
-    out_ref[...] = total.astype(out_ref.dtype)
-
-
-def row_products(pairs, spans, first, count, prior=None, rows=256):
-    model = pairs[0][1].shape[0]
-    at = first // rows
-    operands, specs = [], []
-    for a, b in pairs:
-        operands += [a, b]
-        specs += [
-            pl.BlockSpec((rows, a.shape[1]), lambda i: (i + at, 0)),
-            pl.BlockSpec(b.shape, lambda i: (0, 0), pipeline_mode=pl.Buffered(1)),
-        ]
-    if prior is not None:
-        operands.append(prior)
-        specs.append(pl.BlockSpec((rows, model), lambda i: (i, 0)))
-    return pl.pallas_call(
-        functools.partial(rows_kernel, spans, prior is not None),
-        grid=(count // rows,),
-        in_specs=specs,
-        out_specs=pl.BlockSpec((rows, model), lambda i: (i, 0)),
-        out_shape=jax.ShapeDtypeStruct((count, model), WIDE),
-        compiler_params=pltpu.CompilerParams(vmem_limit_bytes=VMEM_BYTES),
-        cost_estimate=pl.CostEstimate(flops=10**6, bytes_accessed=10**5, transcendentals=0),
-    )(*operands)
-
-
-def grads_kernel(spans, *refs):
-    out_ref = refs[-1]
-    for k, (lo, hi, at) in enumerate(spans):
-        out_ref[:, at : at + hi - lo] = dot(refs[2 * k][...], refs[2 * k + 1][:, lo:hi], 0, 0).astype(
-            WIDE
-        )
-    end = max(at + hi - lo for lo, hi, at in spans)
-    if end < out_ref.shape[1]:
-        out_ref[:, end:] = jnp.zeros((out_ref.shape[0], out_ref.shape[1] - end), WIDE)
-
-
-def column_products(pairs, spans, width, rows=256):
-    count, model = pairs[0][0].shape
-    operands, specs = [], []
-    for a, b in pairs:
-        operands += [a, b]
-        specs += [
-            pl.BlockSpec((count, rows), lambda i: (0, i)),
-            pl.BlockSpec(b.shape, lambda i: (0, 0), pipeline_mode=pl.Buffered(1)),
-        ]
-    return pl.pallas_call(
-        functools.partial(grads_kernel, spans),
+    width = mine.shape[1]
+    return pl.pallas_call(
+        unit_grads_kernel,
         grid=(model // rows,),
-        in_specs=specs,
+        in_specs=[pl.BlockSpec((count, rows), lambda i: (0, i))] * 2 + [whole(mine), whole(other)],
         out_specs=pl.BlockSpec((rows, width), lambda i: (i, 0)),
         out_shape=jax.ShapeDtypeStruct((model, width), WIDE),
-        compiler_params=pltpu.CompilerParams(vmem_limit_bytes=VMEM_BYTES),
-        cost_estimate=pl.CostEstimate(flops=10**6, bytes_accessed=10**5, transcendentals=0),
-    )(*operands)
-
-
-def hidden_grads(h_two, cot, acts):
-    width = acts.shape[1] // 3
-    return column_products(
-        [(cot, acts), (h_two, acts)],
-        [(0, width, 0), (width, 3 * width, width)],
-        3 * width,
-    )
+        compiler_params=params(),
+        cost_estimate=TINY,
+    )(h_two, cot, mine, other)
+
+
+def grads_kernel(a_ref, b_ref, out_ref):
+    out_ref[...] = dot(a_ref[...], b_ref[...], 0, 0).astype(WIDE)
+
+
+def weight_grads(a, b, rows=256):
+    count, model = a.shape
+    width = b.shape[1]
+    return pl.pallas_call(
+        grads_kernel,
+        grid=(model // rows,),
+        in_specs=[pl.BlockSpec((count, rows), lambda i: (0, i)), whole(b)],
+        out_specs=pl.BlockSpec((rows, width), lambda i: (i, 0)),
+        out_shape=jax.ShapeDtypeStruct((model, width), WIDE),
+        compiler_params=params(),
+        cost_estimate=TINY,
+    )(a, b)
 
 
 def tied(value, *others):
@@ -479,18 +525,19 @@
 
 
 def plane_join(*mine):
-    return jnp.concatenate(list(mine) + [over(part, "c") for part in mine], axis=0)
-
-
-def core_sum(own, term, prior=None):
-    half = 4 * own
-    got = over(term(half, half).astype(WIDE), "c")
-    mine = term(0, half)
-    return (mine.astype(F32) + got.astype(F32)).astype(WIDE)
-
-
-def product(a, b):
-    return lambda first, count: dot(a[first : first + count], b, 1, 1)
+    return join(list(mine) + [over(part, "c") for part in mine])
+
+
+def added_pair(one, two):
+    return (one.astype(F32) + two.astype(F32)).astype(WIDE)
+
+
+def landed(values, *flights):
+    held = [getattr(holder, field) for holder, field in flights]
+    values, held = lax.optimization_barrier((values, held))
+    for (holder, field), value in zip(flights, held):
+        setattr(holder, field, value)
+    return values
 
 
 def plane_sum_one(total):
@@ -535,12 +582,18 @@
     return both_rows(keep, over(give, "y"), first_y)
 
 
-def unshare_columns(block, first_y):
-    half = block.shape[0] // 2
-    keep = jnp.where(first_y, block[:half], block[half:])
-    give = jnp.where(first_y, block[half:], block[:half])
-    got = over(give, "y")
-    return jnp.where(first_y, keep, got), jnp.where(first_y, got, keep)
+class Unshare:
+    def __init__(self, block, first_y):
+        half = block.shape[0] // 2
+        self.first_y = first_y
+        self.keep = jnp.where(first_y, block[:half], block[half:])
+        self.got = over(jnp.where(first_y, block[half:], block[:half]), "y")
+
+    def both(self):
+        return (
+            jnp.where(self.first_y, self.keep, self.got),
+            jnp.where(self.first_y, self.got, self.keep),
+        )
 
 
 def gather_z(block):
@@ -577,7 +630,7 @@
     cotangent,
 ):
     own = inputs.shape[0]
-    count = 8 * own
+    half, count = 4 * own, 8 * own
     length = segments.shape[0] // SEQS
     reach = (DOC_MOST - 2) // count + 1
     period = lax.axis_size("z")
@@ -611,12 +664,12 @@
     triple = lambda cut: jnp.concatenate(
         [padded(halves(w)[i][:, cut]) for i in range(2) for w in (w_d, w_g, w_u)], axis=1
     )
-    x_parts = over(inputs, "x"), over(tied(inputs, near_a), "y")
-    x_parts += plane_step_two(*x_parts)
-    x_all = plane_join(inputs, *x_parts)
-    cot_parts = plane_step_one(tied(cotangent, *x_parts))
-    near_o = share_columns(w_o, first_y, *x_parts)
-    near_c = [share_columns(triple(cut), first_y, *x_parts) for cut in chunks]
+    x_one = over(inputs, "x"), over(tied(inputs, near_a), "y")
+    x_two = plane_step_two(*x_one)
+    x_all = plane_join(inputs, *x_one, *x_two)
+    cot_one = plane_step_one(tied(cotangent, *x_two))
+    near_o = share_columns(w_o, first_y, *x_two)
+    near_c = [share_columns(triple(cut), first_y, *x_two) for cut in chunks]
     full_a, full_o = gather_z(near_a), gather_z(near_o)
     full_c = [gather_z(near) for near in near_c]
     first_gain = nq + 2 * nk
@@ -652,17 +705,17 @@
     q_cols, kv_own = turned[: GROUP * HD], turned[GROUP * HD :]
     far_kv = [shifted(kv_own, distance, period) for distance in range(reach, 0, -1)]
     kv_cols = jnp.concatenate(far_kv + [kv_own], axis=1)
-    kv_cols, full_o, *near_all = together(kv_cols, full_o, *near_c, *cot_parts)
-    cot_parts = near_all[len(near_c) :]
-    cot_far = plane_step_two(*cot_parts)
+    kv_cols, full_o, cot_one, _ = lax.optimization_barrier((kv_cols, full_o, cot_one, near_c))
+    cot_two = plane_step_two(*cot_one)
     out_cols, logs = attend(q_cols, kv_cols, starts, bounds)
-    out_cols, *cot_far = together(out_cols, *cot_far)
+    out_cols, *cot_two = together(out_cols, *cot_two)
     attended = to_rows(out_cols, index, cos_tab, sin_tab, 0, GROUP, GROUP * HD)
-    grad_mix = plane_join(cotangent, *cot_parts, *cot_far)
+    grad_mix = plane_join(cotangent, *cot_one, *cot_two)
     input_f32 = inputs.astype(F32)
     inverse_one = lax.rsqrt(jnp.mean(input_f32 * input_f32, axis=-1, keepdims=True) + eps)
     normed_one = input_f32 * inverse_one
-    mid_total = core_sum(own, product(attended, full_o))
+    mid_got = over(dot(attended[half:], full_o, 1, 1).astype(WIDE), "c")
+    mid_total = (dot(attended[:half], full_o, 1, 1) + mid_got.astype(F32)).astype(WIDE)
     mid_far = plane_sum_one(mid_total)
     mid_near = plane_sum_two(mid_total, *mid_far)
     x_mid = input_f32 + added(mid_total, *mid_near)
@@ -670,61 +723,55 @@
     inverse_two = lax.rsqrt(jnp.mean(x_mid * x_mid, axis=-1, keepdims=True) + eps)
     normed_two = x_mid * inverse_two
     h_own = (normed_two * gain_second).astype(WIDE)
-    h_parts = plane_step_one(h_own)
-    h_parts += plane_step_two(*h_parts)
-    h_two, grad_mix = together(plane_join(h_own, *h_parts), grad_mix)
-    half = 4 * own
-    acts = [hidden_units(h_two, grad_mix, full_c[0])]
-    width = [full.shape[1] // 3 for full in full_c]
-    later = lambda k: (width[k], 3 * width[k])
-    back_other = row_products([(acts[0], full_c[0])], [later(0)], half, half)
-    back_mine = row_products([(acts[0], full_c[0])], [later(0)], 0, half)
-    grads = [hidden_grads(h_two, grad_mix, acts[0])]
-    full_c[1], back_mine, back_other, *grads = together(full_c[1], back_mine, back_other, *grads)
-    sums = [sum_z(grads[0])]
-    acts.append(hidden_units(h_two, grad_mix, full_c[1]))
-    back_other = row_products([(acts[1], full_c[1])], [later(1)], half, half, back_other)
-    got = over(back_other, "c")
-    back_mine = row_products([(acts[1], full_c[1])], [later(1)], 0, half, back_mine)
-    back_total = (back_mine.astype(F32) + got.astype(F32)).astype(WIDE)
+    h_step = plane_step_one(h_own)
+    h_two = plane_join(h_own, *h_step, *plane_step_two(*h_step))
+    h_two, grad_mix = together(h_two, grad_mix)
+    other_1 = hidden_units(h_two, grad_mix, full_c[0], half, half)
+    mine_1 = hidden_units(h_two, grad_mix, full_c[0], 0, half)
+    term_1 = unit_grads(h_two, grad_mix, mine_1[0], other_1[0])
+    full_c[1], other_1, mine_1, term_1 = lax.optimization_barrier(
+        (full_c[1], other_1, mine_1, term_1)
+    )
+    sums = [sum_z(term_1)]
+    acts_other, back_other, out_other = hidden_units(
+        h_two, grad_mix, full_c[1], half, half, other_1[1:]
+    )
+    back_got, out_got = over(back_other, "c"), over(out_other, "c")
+    acts_mine, back_mine, out_mine = hidden_units(h_two, grad_mix, full_c[1], 0, half, mine_1[1:])
+    back_total = added_pair(back_mine, back_got)
     back_far = plane_sum_one(back_total)
-    grads.append(hidden_grads(h_two, grad_mix, acts[1]))
+    term_2 = unit_grads(h_two, grad_mix, acts_mine, acts_other)
     back_near = plane_sum_two(back_total, *back_far)
-    *back_near, grads[1] = together(*back_near, grads[1])
-    sums.append(sum_z(grads[1]))
+    *back_near, term_2 = together(*back_near, term_2)
+    sums.append(sum_z(term_2))
     grad_h_two = added(back_total, *back_near)
     grad_mid = cotangent.astype(F32) + norm_back(grad_h_two, normed_two, inverse_two, gain_second)
     branch_own = grad_mid.astype(WIDE)
-    branch_parts = plane_step_one(branch_own)
-    acts_later = [tied(part, branch_own) for part in acts]
-    hidden_pairs = list(zip(acts_later, full_c))
-    out_other = row_products(hidden_pairs, [(0, w) for w in width], half, half)
-    *branch_parts, out_other = together(*branch_parts, out_other)
-    out_got = over(out_other, "c")
-    branch_far = plane_step_two(*branch_parts)
-    hidden_pairs = [(tied(part, *branch_parts), full) for part, full in zip(acts, full_c)]
-    out_mine = row_products(hidden_pairs, [(0, w) for w in width], 0, half)
-    *branch_far, out_mine, out_got = together(*branch_far, out_mine, out_got)
-    out_total = (out_mine.astype(F32) + out_got.astype(F32)).astype(WIDE)
-    grad_branch = plane_join(branch_own, *branch_parts, *branch_far)
+    branch_one = plane_step_one(branch_own)
+    branch_two = plane_step_two(*branch_one)
+    out_total = added_pair(out_mine, out_got)
+    grad_branch = plane_join(branch_own, *branch_one, *branch_two)
     grad_branch, out_total, sums[0] = together(grad_branch, out_total, sums[0])
 
-    grad_attended = dot(grad_branch, full_o, 1, 0).astype(WIDE)
+    grad_attended = narrow(grad_branch, full_o)
     grad_cols = to_columns(grad_attended, index, cos_tab, sin_tab, 0, GROUP)
-    out_total, sums[0] = together(out_total, sums[0], grad_cols)[:2]
+    grad_cols, out_total, sums[0] = together(grad_cols, out_total, sums[0])
     out_sends = [
         over(out_total[own : 2 * own], "x"),
         over(out_total[2 * own : 3 * own], "y"),
         across(out_total[3 * own :]),
     ]
-    owned = [unshare_columns(sums[0], first_y)]
     dq_cols, dkv_cols = attend_back(q_cols, kv_cols, starts, bounds, out_cols, logs, grad_cols)
+    dkv_cols, *out_sends = together(dkv_cols, *out_sends)
+    output = (x_mid + added(out_total, *out_sends)).astype(WIDE)
+    owned = [Unshare(tied(sums[0], dkv_cols), first_y)]
     dkv_own = dkv_cols[:, reach * count :]
     for distance in range(1, reach + 1):
         first = (reach - distance) * count
         dkv_own = dkv_own + shifted(
             dkv_cols[:, first : first + count].astype(WIDE), -distance, period
         ).astype(F32)
+    dkv_own = landed(dkv_own, (owned[0], "got"))
     grad_qkv = to_rows(
         jnp.concatenate([dq_cols, dkv_own], axis=0),
         index,
@@ -734,26 +781,29 @@
         GROUP + 2,
         full_a.shape[1],
     )
-    qkv_part = column_products([(h_one, grad_qkv)], [(0, full_a.shape[1], 0)], full_a.shape[1])
+    qkv_part = weight_grads(h_one, grad_qkv)
     grad_qkv, qkv_part = together(grad_qkv, qkv_part)
-    one_total = core_sum(own, product(grad_qkv, full_a))
+    one_got = over(dot(grad_qkv[half:], full_a, 1, 1).astype(WIDE), "c")
+    one_total = (dot(grad_qkv[:half], full_a, 1, 1) + one_got.astype(F32)).astype(WIDE)
     one_total, qkv_part, sums[1] = together(one_total, qkv_part, sums[1])
     qkv_grad = sum_z(qkv_part)
+    owned.append(Unshare(sums[1], first_y))
     one_far = plane_sum_one(one_total)
-    out_part = column_products([(grad_branch, tied(attended, qkv_part))], [(0, nq, 0)], nq)
-    *one_far, to_x, to_y, to_xy = together(*one_far, *out_sends)
-    out_sends = to_x, to_y, to_xy
-    output = (x_mid + added(out_total, *out_sends)).astype(WIDE)
+    out_term = weight_grads(grad_branch, tied(attended, qkv_part))
+    *one_far, out_term = together(*one_far, out_term)
     one_near = plane_sum_two(one_total, *one_far)
-    *one_near, qkv_grad, out_part = together(*one_near, qkv_grad, out_part)
-    out_grad = sum_z(out_part)
+    *one_near, qkv_grad, out_term = together(*one_near, qkv_grad, out_term)
+    out_grad = sum_z(out_term)
+    owned_o = Unshare(out_grad, first_y)
     grad_h_one = added(one_total, *one_near)
     input_grad = (grad_mid + norm_back(grad_h_one, normed_one, inverse_one, gain_first)).astype(
         WIDE
     )
 
-    owned.append(unshare_columns(sums[1], first_y))
+    input_grad, out_term = landed((input_grad, out_term), (owned[0], "got"), (owned[1], "got"))
+    owned = [part.both() for part in owned]
     kept = [CHUNK, nf - CHUNK]
+    width = [full.shape[1] // 3 for full in full_c]
 
     def unit_columns(k):
         return jnp.concatenate(
@@ -766,10 +816,10 @@
         ).astype(F32)
 
     down_out, gate_out, up_out = unit_columns(0).T, unit_columns(1), unit_columns(2)
-    one, two = unshare_columns(qkv_grad, first_y)
+    one, two = Unshare(qkv_grad, first_y).both()
     pick = lambda a, b: jnp.concatenate([one[:, a:b], two[:, a:b]], axis=1).astype(F32)
     q_out, k_out, v_out = pick(0, nq), pick(nq, nq + nk), pick(nq + nk, nq + 2 * nk)
-    o_out = jnp.concatenate(unshare_columns(out_grad, first_y), axis=1).T.astype(F32)
+    o_out = jnp.concatenate(owned_o.both(), axis=1).T.astype(F32)
 
     def row_sums(weight, grad):
         return jnp.sum(weight.astype(F32) * grad, axis=1)

time: 812 us -> 769 us (0.947)
  local copies, waits for them, and re-layouts: 76.3 us -> 52.8 us
  waiting for transfers between devices: 334 us -> 314 us
  Pallas kernels: 218 us -> 234 us
    unnamed x180 -> x166, local copies, waits for them, and re-layouts: 41.6 us -> 22.6 us
    pallas_call x12 -> x13, Pallas kernels: 145 us -> 161 us  [the longest x4 75.5 us: hidden_units(): pl.pallas_call(functools.partial(units_kernel, bool(prior)), grid=(count...]
    reduce_scatter x4, waiting for transfers between devices: 19.8 us -> 4.39 us  [sum_z(): lax.psum_scatter(block.astype(WIDE), 'z', scatter_dimension=0, tiled=True)]
    all_gather x4, waiting for transfers between devices: 47.9 us -> 34.4 us  [gather_z(): return lax.all_gather(block, 'z', axis=0, tiled=True)]
    dot_general x5 -> x4, matrix products: 24.6 us -> 17.8 us  [dot(): lax.dot_general(a, b, (((ca,), (cb,)), ((), ())), preferred_element_type=...]
  transfers between devices with their start and end apart: 76 -> 76, of which waited for: 32 -> 37; matrix products, arithmetic and copies ran while one was open for 20% -> 14% of each run, Pallas kernels for 27% -> 31%
where the time goes in v3:
time: 769 us; the launch traced here: 763 us
  waiting for transfers between devices  314 us (41%)
  Pallas kernels  234 us (30%)
  other arithmetic  66.9 us (9%)
  starting transfers between devices  62.3 us (8%)
  local copies, waits for them, and re-layouts  52.8 us (7%)
  matrix products  17.8 us (2%)
  between operations  16.1 us (2%)
    ppermute x62, waiting for transfers between devices, over(): return lax.ppermute(block, axis, SWAP)  227 us
    pallas_call x4, Pallas kernels, hidden_units(): pl.pallas_call(functools.partial(units_kernel, bool(prior)), grid=(count...  75.5 us
    ppermute x62, starting transfers between devices, over(): return lax.ppermute(block, axis, SWAP)  52.2 us
    ppermute x2, waiting for transfers between devices, shifted(): return lax.ppermute(block, 'z', route)  45.5 us
    all_gather x4, waiting for transfers between devices, gather_z(): return lax.all_gather(block, 'z', axis=0, tiled=True)  34.4 us
    pallas_call x2, Pallas kernels, unit_grads(): pl.pallas_call(unit_grads_kernel, grid=(model // rows,), in_specs=[pl.Blo...  34 us
    pallas_call x1, Pallas kernels, attend_back(): pl.pallas_call(functools.partial(attend_back_kernel, span - count), grid_...  31.7 us
    pallas_call x1, Pallas kernels, attend(): pl.pallas_call(functools.partial(attend_kernel, span - count), grid_spec=...  27.3 us
  transfers between devices with their start and end apart: 76, of which 37 were waited for; matrix products, arithmetic and copies ran while one was open for 14% of the time, Pallas kernels for 31%

profile of v3, /device:TPU:0, one launch (start us, length us, event | category | flops | bytes accessed | tf_op | source)
XLA Modules:
  0.0 763.5 jit_solution(333458356792100019)
XLA Ops:
  16.1 7.7 %collective-permute-done.1 = bf16[320,512]{1,0:T(8,128)(2,1)S(1)} collective-permute-done((bf16[320,512]{1,0:T(8,128)(2,1)S(1)}, bf16[320,512]{1,0:T(8,128)(2,1)S(1)}, u32[]{:S(2)}, u32[]{:S(2)}) %collective-permute-start.1) | collective-permute-done | bytes 327712 | tf_op jit(solution)/shard_map/ppermute | solution.py:511
  28.3 19.7 %collective-permute-done.refs_1_ = bf16[192,2560]{1,0:T(8,128)(2,1)S(1)} collective-permute-done((bf16[192,2560]{1,0:T(8,128)(2,1)S(1)}, bf16[192,2560]{1,0:T(8,128)(2,1)S(1)}, u32[]{:S(2)}, u32[]{:S(2)}) %collective-permute-start) | collective-permute-done | bytes 983072 | tf_op jit(solution)/shard_map/ppermute | solution.py:511
  52.3 7.5 collective-permute-done.4.refs_4_
  76.0 13.5 %collective-permute-done.15 = bf16[320,1152]{1,0:T(8,128)(2,1)S(1)} collective-permute-done((bf16[320,1152]{1,0:T(8,128)(2,1)S(1)}, bf16[320,1152]{1,0:T(8,128)(2,1)S(1)}, u32[]{:S(2)}, u32[]{:S(2)}) %collective-permute-start.15) | collective-permute-done | bytes 737312 | tf_op jit(solution)/shard_map/ppermute | solution.py:511
  114.2 9.2 %shard_map.213 = (bf16[1536,2560]{1,0:T(8,128)(2,1)}, f32[1536,512]{1,0:T(8,128)S(1)}) custom-call(bf16[1536,2560]{1,0:T(8,128)(2,1)} %shard_map.212.x_ref, f32[1,2560]{1,0:T(1,128)S(1)} %broadcast_in_dim_squeeze.2.gain_ref, bf16[2560,512]{1,0:T(8,128)(2,1)S(1)} %copy-done.5), custom_call_target="tpu_custom_call" | custom-call | flops 1000000 | bytes 100000 | tf_op jit(solution)/shard_map/pallas_call | solution.py:368
  133.5 11.5 %collective-permute-done.11 = bf16[160,1536]{1,0:T(8,128)(2,1)} collective-permute-done((bf16[160,1536]{1,0:T(8,128)(2,1)}, bf16[160,1536]{1,0:T(8,128)(2,1)}, u32[]{:S(2)}, u32[]{:S(2)}) %collective-permute-start.11) | collective-permute-done | bytes 491552 | tf_op jit(solution)/shard_map/ppermute | solution.py:507
  154.9 27.3 %shard_map.215 = (bf16[320,1536]{1,0:T(8,128)(2,1)S(1)}, f32[8,1536]{1,0:T(8,128)S(1)}) custom-call(s32[4,6]{1,0:T(4,128)S(1)} %pad_add_fusion.bounds_ref, bf16[320,1536]{1,0:T(8,128)(2,1)S(1)} %slice.433.q_ref, bf16[160,3072]{1,0:T(8,128)(2,1)S(1)} %pad_maximum_fusion.3.kv_ref, s32[1,1536]{1,0:T(1,128)S(1)} %broadcast_in_dim.2.start_ref), custom_call_target="tpu_custom_call" | custom-call | flops 1000000 | bytes 100000 | tf_op jit(solution)/shard_map/pallas_call | solution.py:167
  187.6 7.0 collective-permute-done.19
  201.7 11.6 %collective-permute-done.22 = bf16[96,2560]{1,0:T(8,128)(2,1)S(1)} collective-permute-done((bf16[96,2560]{1,0:T(8,128)(2,1)S(1)}, bf16[96,2560]{1,0:T(8,128)(2,1)S(1)}, u32[]{:S(2)}, u32[]{:S(2)}) %collective-permute-start.22) | collective-permute-done | bytes 491552 | tf_op jit(solution)/shard_map/ppermute | solution.py:511
  216.0 20.9 %collective-permute-done.23 = bf16[192,2560]{1,0:T(8,128)(2,1)S(1)} collective-permute-done((bf16[192,2560]{1,0:T(8,128)(2,1)S(1)}, bf16[192,2560]{1,0:T(8,128)(2,1)S(1)}, u32[]{:S(2)}, u32[]{:S(2)}) %collective-permute-start.23) | collective-permute-done | bytes 983072 | tf_op jit(solution)/shard_map/ppermute | solution.py:511
  242.7 18.8 %collective-permute-done.25.refs_2_ = bf16[192,2560]{1,0:T(8,128)(2,1)S(1)} collective-permute-done((bf16[192,2560]{1,0:T(8,128)(2,1)S(1)}, bf16[192,2560]{1,0:T(8,128)(2,1)S(1)}, u32[]{:S(2)}, u32[]{:S(2)}) %collective-permute-start.25) | collective-permute-done | bytes 983072 | tf_op jit(solution)/shard_map/ppermute | solution.py:511
  266.9 9.9 %collective-permute-done.26.refs_3_ = bf16[96,2560]{1,0:T(8,128)(2,1)S(1)} collective-permute-done((bf16[96,2560]{1,0:T(8,128)(2,1)S(1)}, bf16[96,2560]{1,0:T(8,128)(2,1)S(1)}, u32[]{:S(2)}, u32[]{:S(2)}) %collective-permute-start.26) | collective-permute-done | bytes 491552 | tf_op jit(solution)/shard_map/ppermute | solution.py:511
  289.7 17.8 %shard_map.220 = (bf16[768,1152]{1,0:T(8,128)(2,1)S(1)}, bf16[768,2560]{1,0:T(8,128)(2,1)S(1)}, bf16[768,2560]{1,0:T(8,128)(2,1)}) custom-call(bf16[1536,2560]{1,0:T(8,128)(2,1)} %shard_map.217.h_ref, bf16[1536,2560]{1,0:T(8,128)(2,1)} %shard_map.218.cot_ref, bf16[2560,1152]{1,0:T(8,128)(2,1)} %all-gather.11.cloned.1.call-done.weight_ref), custom_call_target="tpu_custom_call" | custom-call | flops 1000000 | bytes 100000 | tf_op jit(solution)/shard_map/pallas_call | solution.py:438
  309.5 17.8 %shard_map.219 = (bf16[768,1152]{1,0:T(8,128)(2,1)S(1)}, bf16[768,2560]{1,0:T(8,128)(2,1)S(1)}, bf16[768,2560]{1,0:T(8,128)(2,1)}) custom-call(bf16[1536,2560]{1,0:T(8,128)(2,1)} %shard_map.217.h_ref, bf16[1536,2560]{1,0:T(8,128)(2,1)} %shard_map.218.cot_ref, bf16[2560,1152]{1,0:T(8,128)(2,1)} %all-gather.11.cloned.1.call-done.weight_ref), custom_call_target="tpu_custom_call" | custom-call | flops 1000000 | bytes 100000 | tf_op jit(solution)/shard_map/pallas_call | solution.py:438
  329.2 16.3 %shard_map.221 = bf16[2560,1152]{1,0:T(8,128)(2,1)} custom-call(bf16[1536,2560]{1,0:T(8,128)(2,1)} %shard_map.217.h_ref, bf16[1536,2560]{1,0:T(8,128)(2,1)} %shard_map.218.cot_ref, bf16[768,1152]{1,0:T(8,128)(2,1)S(1)} %get-tuple-element.100.mine_ref, bf16[768,1152]{1,0:T(8,128)(2,1)S(1)} %get-tuple-element.97.other_ref), custom_call_target="tpu_custom_call" | custom-call | flops 1000000 | bytes 100000 | tf_op jit(solution)/shard_map/pallas_call | solution.py:463
  345.5 34.3 %all-gather.9.cloned.1.call-done.weight_ref = bf16[2560,1536]{1,0:T(8,128)(2,1)} async-done(((bf16[640,1536]{1,0:T(8,128)(2,1)}), bf16[2560,1536]{1,0:T(8,128)(2,1)}) %all-gather.9.cloned.1.call-update) | async-done | bytes 7864336 | tf_op jit(solution)/shard_map/all_gather | solution.py:600
  379.9 19.9 %shard_map.223 = (bf16[768,1536]{1,0:T(8,128)(2,1)S(1)}, bf16[768,2560]{1,0:T(8,128)(2,1)}, bf16[768,2560]{1,0:T(8,128)(2,1)}) custom-call(bf16[1536,2560]{1,0:T(8,128)(2,1)} %shard_map.217.h_ref, bf16[1536,2560]{1,0:T(8,128)(2,1)} %shard_map.218.cot_ref, bf16[2560,1536]{1,0:T(8,128)(2,1)} %all-gather.9.cloned.1.call-done.weight_ref, ...), custom_call_target="tpu_custom_call" | custom-call | flops 1000000 | bytes 100000 | tf_op jit(solution)/shard_map/pallas_call | solution.py:438
  399.8 20.0 %shard_map.222 = (bf16[768,1536]{1,0:T(8,128)(2,1)S(1)}, bf16[768,2560]{1,0:T(8,128)(2,1)}, bf16[768,2560]{1,0:T(8,128)(2,1)}) custom-call(bf16[1536,2560]{1,0:T(8,128)(2,1)} %shard_map.217.h_ref, bf16[1536,2560]{1,0:T(8,128)(2,1)} %shard_map.218.cot_ref, bf16[2560,1536]{1,0:T(8,128)(2,1)} %all-gather.9.cloned.1.call-done.weight_ref, ...), custom_call_target="tpu_custom_call" | custom-call | flops 1000000 | bytes 100000 | tf_op jit(solution)/shard_map/pallas_call | solution.py:438
  429.3 10.7 %collective-permute-done.41 = bf16[96,2560]{1,0:T(8,128)(2,1)S(1)} collective-permute-done((bf16[96,2560]{1,0:T(8,128)(2,1)S(1)}, bf16[96,2560]{1,0:T(8,128)(2,1)S(1)}, u32[]{:S(2)}, u32[]{:S(2)}) %collective-permute-start.41) | collective-permute-done | bytes 491552 | tf_op jit(solution)/shard_map/ppermute | solution.py:511
  445.5 17.7 %shard_map.224 = bf16[2560,1536]{1,0:T(8,128)(2,1)} custom-call(bf16[1536,2560]{1,0:T(8,128)(2,1)} %shard_map.217.h_ref, bf16[1536,2560]{1,0:T(8,128)(2,1)} %shard_map.218.cot_ref, bf16[768,1536]{1,0:T(8,128)(2,1)S(1)} %get-tuple-element.110.mine_ref, bf16[768,1536]{1,0:T(8,128)(2,1)S(1)} %get-tuple-element.111.other_ref), custom_call_target="tpu_custom_call" | custom-call | flops 1000000 | bytes 100000 | tf_op jit(solution)/shard_map/pallas_call | solution.py:463
  478.0 21.0 %collective-permute-done.44.refs_2_ = bf16[192,2560]{1,0:T(8,128)(2,1)S(1)} collective-permute-done((bf16[192,2560]{1,0:T(8,128)(2,1)S(1)}, bf16[192,2560]{1,0:T(8,128)(2,1)S(1)}, u32[]{:S(2)}, u32[]{:S(2)}) %collective-permute-start.44) | collective-permute-done | bytes 983072 | tf_op jit(solution)/shard_map/ppermute | solution.py:511
  502.7 9.2 %collective-permute-done.45.refs_3_ = bf16[96,2560]{1,0:T(8,128)(2,1)S(1)} collective-permute-done((bf16[96,2560]{1,0:T(8,128)(2,1)S(1)}, bf16[96,2560]{1,0:T(8,128)(2,1)S(1)}, u32[]{:S(2)}, u32[]{:S(2)}) %collective-permute-start.45) | collective-permute-done | bytes 491552 | tf_op jit(solution)/shard_map/ppermute | solution.py:511
  524.7 7.8 %shard_map.226.rows_ref = bf16[1536,320]{1,0:T(8,128)(2,1)S(1)} custom-call(bf16[1536,2560]{1,0:T(8,128)(2,1)} %shard_map.225.a_ref, bf16[2560,320]{1,0:T(8,128)(2,1)S(1)} %copy-done.17), custom_call_target="tpu_custom_call" | custom-call | flops 1000000 | bytes 100000 | tf_op jit(solution)/shard_map/pallas_call | solution.py:399
  537.2 31.7 %shard_map.228 = (f32[320,1536]{1,0:T(8,128)S(1)}, f32[160,3072]{1,0:T(8,128)}) custom-call(s32[4,6]{1,0:T(4,128)S(1)} %pad_add_fusion.bounds_ref, bf16[320,1536]{1,0:T(8,128)(2,1)S(1)} %slice.433.q_ref, bf16[160,3072]{1,0:T(8,128)(2,1)S(1)} %pad_maximum_fusion.3.kv_ref, s32[1,1536]{1,0:T(1,128)S(1)} %broadcast_in_dim.2.start_ref, ...), custom_call_target="tpu_custom_call" | custom-call | flops 1000000 | bytes 100000 | tf_op jit(solution)/shard_map/pallas_call | solution.py:277
  568.9 10.9 %collective-permute-done.54 = bf16[192,2560]{1,0:T(8,128)(2,1)S(1)} collective-permute-done((bf16[192,2560]{1,0:T(8,128)(2,1)S(1)}, bf16[192,2560]{1,0:T(8,128)(2,1)S(1)}, u32[]{:S(2)}, u32[]{:S(2)}) %collective-permute-start.54) | collective-permute-done | bytes 983072 | tf_op jit(solution)/shard_map/ppermute | solution.py:511
  584.9 34.1 %collective-permute-done.56 = bf16[160,1536]{1,0:T(8,128)(2,1)S(1)} collective-permute-done((bf16[160,1536]{1,0:T(8,128)(2,1)S(1)}, bf16[160,1536]{1,0:T(8,128)(2,1)S(1)}, u32[]{:S(2)}, u32[]{:S(2)}) %collective-permute-start.56) | collective-permute-done | bytes 491552 | tf_op jit(solution)/shard_map/ppermute | solution.py:507
  621.3 9.5 %shard_map.230 = bf16[2560,512]{1,0:T(8,128)(2,1)S(1)} custom-call(bf16[1536,2560]{1,0:T(8,128)(2,1)} %get-tuple-element.132.a_ref, bf16[1536,512]{1,0:T(8,128)(2,1)S(1)} %shard_map.229.b_ref), custom_call_target="tpu_custom_call" | custom-call | flops 1000000 | bytes 100000 | tf_op jit(solution)/shard_map/pallas_call | solution.py:481
  636.9 6.5 collective-permute-done.58
  653.2 10.6 %shard_map.231 = bf16[2560,320]{1,0:T(8,128)(2,1)} custom-call(bf16[1536,2560]{1,0:T(8,128)(2,1)} %shard_map.225.a_ref, bf16[1536,320]{1,0:T(8,128)(2,1)S(1)} %copy-done.4), custom_call_target="tpu_custom_call" | custom-call | flops 1000000 | bytes 100000 | tf_op jit(solution)/shard_map/pallas_call | solution.py:481
  674.7 15.4 %collective-permute-done.61 = bf16[192,2560]{1,0:T(8,128)(2,1)} collective-permute-done((bf16[192,2560]{1,0:T(8,128)(2,1)S(1)}, bf16[192,2560]{1,0:T(8,128)(2,1)}, u32[]{:S(2)}, u32[]{:S(2)}) %collective-permute-start.61) | collective-permute-done | bytes 983072 | tf_op jit(solution)/shard_map/ppermute | solution.py:511
  704.5 8.0 %collective-permute-done.63 = bf16[320,1536]{1,0:T(8,128)(2,1)} collective-permute-done((bf16[320,1536]{1,0:T(8,128)(2,1)}, bf16[320,1536]{1,0:T(8,128)(2,1)}, u32[]{:S(2)}, u32[]{:S(2)}) %collective-permute-start.63) | collective-permute-done | bytes 983072 | tf_op jit(solution)/shard_map/ppermute | solution.py:511
  747.7 6.3 collective-permute-done.67
  (445 shorter events, 257.2 us)
Async XLA Ops:
  7.2 104.4 %all-gather.5.cloned.1.call-start = ((), (), s32[]{:S(2)}) async-start(), calls=%async_computation.4 | async-start | bytes 3276800 | tf_op jit(solution)/shard_map/all_gather | solution.py:600
  24.9 121.3 %all-gather.7.cloned.1.call-start = ((), (), s32[]{:S(2)}) async-start(), calls=%async_computation.5 | async-start | bytes 2457600 | tf_op jit(solution)/shard_map/all_gather | solution.py:600
  25.0 23.0 %collective-permute-start = (bf16[192,2560]{1,0:T(8,128)(2,1)S(1)}, bf16[192,2560]{1,0:T(8,128)(2,1)S(1)}, u32[]{:S(2)}, u32[]{:S(2)}) collective-permute-start(bf16[192,2560]{1,0:T(8,128)(2,1)S(1)} %copy-done), channel_id=1, source_target_pairs={{0,2},{2,0},{1,3},{3,1},{4,6},{6,4},{5,7},{7,5},{8,10},{10,8},{9,1... | collective-permute-start | bytes 2949128 | tf_op jit(solution)/shard_map/ppermute | solution.py:511
  26.8 22.8 %collective-permute-start.2 = (bf16[192,2560]{1,0:T(8,128)(2,1)S(1)}, bf16[192,2560]{1,0:T(8,128)(2,1)S(1)}, u32[]{:S(2)}, u32[]{:S(2)}) collective-permute-start(bf16[192,2560]{1,0:T(8,128)(2,1)S(1)} %copy-done), channel_id=1, source_target_pairs={{0,4},{4,0},{1,5},{5,1},{2,6},{6,2},{3,7},{7,3},{8,12},{12,8},{9,1... | collective-permute-start | bytes 2949128 | tf_op jit(solution)/shard_map/ppermute | solution.py:511
  68.9 220.8 %all-gather.11.cloned.1.call-start = ((), (), s32[]{:S(2)}) async-start(), calls=%async_computation.7 | async-start | bytes 7372800 | tf_op jit(solution)/shard_map/all_gather | solution.py:600
  91.2 288.6 %all-gather.9.cloned.1.call-start = ((), (), s32[]{:S(2)}) async-start(), calls=%async_computation.6 | async-start | bytes 9830400 | tf_op jit(solution)/shard_map/all_gather | solution.py:600
  100.5 29.9 %collective-permute-start.16 = (bf16[320,1536]{1,0:T(8,128)(2,1)}, bf16[320,1536]{1,0:T(8,128)(2,1)}, u32[]{:S(2)}, u32[]{:S(2)}) collective-permute-start(bf16[320,1536]{1,0:T(8,128)(2,1)} %broadcast_select_fusion.6), channel_id=1, source_target_pairs={{0,4},{4,0},{1,5},{5,1},{2,6},{6,2},{3,7},{7,3},{8,12},{12,8},{9,1... | collective-permute-start | bytes 2949128 | tf_op jit(solution)/shard_map/ppermute | solution.py:511
  102.7 43.5 %collective-permute-start.14 = (bf16[192,2560]{1,0:T(8,128)(2,1)S(1)}, bf16[192,2560]{1,0:T(8,128)(2,1)}, u32[]{:S(2)}, u32[]{:S(2)}) collective-permute-start(bf16[192,2560]{1,0:T(8,128)(2,1)S(1)} %copy-done.11), channel_id=1, source_target_pairs={{0,4},{4,0},{1,5},{5,1},{2,6},{6,2},{3,7},{7,3},{8,12},{12,8},{9,1... | collective-permute-start | bytes 2949128 | tf_op jit(solution)/shard_map/ppermute | solution.py:511
  103.6 42.6 %collective-permute-start.13 = (bf16[192,2560]{1,0:T(8,128)(2,1)S(1)}, bf16[192,2560]{1,0:T(8,128)(2,1)}, u32[]{:S(2)}, u32[]{:S(2)}) collective-permute-start(bf16[192,2560]{1,0:T(8,128)(2,1)S(1)} %copy-done.11), channel_id=1, source_target_pairs={{0,2},{2,0},{1,3},{3,1},{4,6},{6,4},{5,7},{7,5},{8,10},{10,8},{9,1... | collective-permute-start | bytes 2949128 | tf_op jit(solution)/shard_map/ppermute | solution.py:511
  149.9 32.3 %collective-permute-start.18 = (bf16[96,2560]{1,0:T(8,128)(2,1)}, bf16[96,2560]{1,0:T(8,128)(2,1)}, u32[]{:S(2)}, u32[]{:S(2)}) collective-permute-start(bf16[96,2560]{1,0:T(8,128)(2,1)} %slice.354), channel_id=1, source_target_pairs={{0,4},{4,0},{1,5},{5,1},{2,6},{6,2},{3,7},{7,3},{8,12},{12,8},{9,1... | collective-permute-start | bytes 1474568 | tf_op jit(solution)/shard_map/ppermute | solution.py:511
  151.1 31.2 %collective-permute-start.17 = (bf16[96,2560]{1,0:T(8,128)(2,1)}, bf16[96,2560]{1,0:T(8,128)(2,1)}, u32[]{:S(2)}, u32[]{:S(2)}) collective-permute-start(bf16[96,2560]{1,0:T(8,128)(2,1)} %slice.353), channel_id=1, source_target_pairs={{0,2},{2,0},{1,3},{3,1},{4,6},{6,4},{5,7},{7,5},{8,10},{10,8},{9,1... | collective-permute-start | bytes 1474568 | tf_op jit(solution)/shard_map/ppermute | solution.py:511
  187.5 335.6 %reduce-scatter.5.cloned.1.call-start = ((), (), s32[]{:S(2)}) async-start(), calls=%async_computation.8 | async-start | bytes 7372800 | tf_op jit(solution)/shard_map/reduce_scatter | solution.py:604
  214.1 22.8 %collective-permute-start.23 = (bf16[192,2560]{1,0:T(8,128)(2,1)S(1)}, bf16[192,2560]{1,0:T(8,128)(2,1)S(1)}, u32[]{:S(2)}, u32[]{:S(2)}) collective-permute-start(bf16[192,2560]{1,0:T(8,128)(2,1)S(1)} %pad_maximum_fusion.5), channel_id=1, source_target_pairs={{0,4},{4,0},{1,5},{5,1},{2,6},{6,2},{3,7},{7,3},{8,12},{12,8},{9,1... | collective-permute-start | bytes 2949128 | tf_op jit(solution)/shard_map/ppermute | solution.py:511
  215.1 22.5 %collective-permute-start.21 = (bf16[192,2560]{1,0:T(8,128)(2,1)S(1)}, bf16[192,2560]{1,0:T(8,128)(2,1)S(1)}, u32[]{:S(2)}, u32[]{:S(2)}) collective-permute-start(bf16[192,2560]{1,0:T(8,128)(2,1)S(1)} %pad_maximum_fusion.4), channel_id=1, source_target_pairs={{0,2},{2,0},{1,3},{3,1},{4,6},{6,4},{5,7},{7,5},{8,10},{10,8},{9,1... | collective-permute-start | bytes 2949128 | tf_op jit(solution)/shard_map/ppermute | solution.py:511
  242.2 23.7 %collective-permute-start.35 = (bf16[192,2560]{1,0:T(8,128)(2,1)}, bf16[192,2560]{1,0:T(8,128)(2,1)S(1)}, u32[]{:S(2)}, u32[]{:S(2)}) collective-permute-start(bf16[192,2560]{1,0:T(8,128)(2,1)} %collective-permute-done.14.refs_2_), channel_id=1, source_target_pairs={{0,1},{1,0},{2,3},{3,2},{4,5},{5,4},{6,7},{7,6},{8,9},{9,8},{10,11... | collective-permute-start | bytes 2949128 | tf_op jit(solution)/shard_map/ppermute | solution.py:511
  242.7 23.2 %collective-permute-start.34 = (bf16[192,2560]{1,0:T(8,128)(2,1)}, bf16[192,2560]{1,0:T(8,128)(2,1)S(1)}, u32[]{:S(2)}, u32[]{:S(2)}) collective-permute-start(bf16[192,2560]{1,0:T(8,128)(2,1)} %collective-permute-done.13.refs_1_), channel_id=1, source_target_pairs={{0,1},{1,0},{2,3},{3,2},{4,5},{5,4},{6,7},{7,6},{8,9},{9,8},{10,11... | collective-permute-start | bytes 2949128 | tf_op jit(solution)/shard_map/ppermute | solution.py:511
  379.8 267.8 %reduce-scatter.7.cloned.1.call-start = ((), (), s32[]{:S(2)}) async-start(), calls=%async_computation.9 | async-start | bytes 9830400 | tf_op jit(solution)/shard_map/reduce_scatter | solution.py:604
  442.4 23.5 %collective-permute-start.40 = (bf16[192,2560]{1,0:T(8,128)(2,1)}, bf16[192,2560]{1,0:T(8,128)(2,1)}, u32[]{:S(2)}, u32[]{:S(2)}) collective-permute-start(bf16[192,2560]{1,0:T(8,128)(2,1)} %pad_maximum_fusion.6), channel_id=1, source_target_pairs={{0,2},{2,0},{1,3},{3,1},{4,6},{6,4},{5,7},{7,5},{8,10},{10,8},{9,1... | collective-permute-start | bytes 2949128 | tf_op jit(solution)/shard_map/ppermute | solution.py:511
  444.0 23.2 %collective-permute-start.42 = (bf16[192,2560]{1,0:T(8,128)(2,1)}, bf16[192,2560]{1,0:T(8,128)(2,1)}, u32[]{:S(2)}, u32[]{:S(2)}) collective-permute-start(bf16[192,2560]{1,0:T(8,128)(2,1)} %pad_maximum_fusion.7), channel_id=1, source_target_pairs={{0,4},{4,0},{1,5},{5,1},{2,6},{6,2},{3,7},{7,3},{8,12},{12,8},{9,1... | collective-permute-start | bytes 2949128 | tf_op jit(solution)/shard_map/ppermute | solution.py:511
  467.3 230.7 %reduce-scatter.9.cloned.1.call-start = ((), (), s32[]{:S(2)}) async-start(), calls=%async_computation.10 | async-start | bytes 3276800 | tf_op jit(solution)/shard_map/reduce_scatter | solution.py:604
  467.6 35.1 %collective-permute-start.52 = (bf16[768,2560]{1,0:T(8,128)(2,1)}, bf16[768,2560]{1,0:T(8,128)(2,1)S(1)}, u32[]{:S(2)}, u32[]{:S(2)}) collective-permute-start(bf16[768,2560]{1,0:T(8,128)(2,1)} %get-tuple-element.115), channel_id=1, source_target_pairs={{0,1},{1,0},{2,3},{3,2},{4,5},{5,4},{6,7},{7,6},{8,9},{9,8},{10,11... | collective-permute-start | bytes 11796488 | tf_op jit(solution)/shard_map/ppermute | solution.py:511
  475.1 23.9 %collective-permute-start.44 = (bf16[192,2560]{1,0:T(8,128)(2,1)S(1)}, bf16[192,2560]{1,0:T(8,128)(2,1)S(1)}, u32[]{:S(2)}, u32[]{:S(2)}) collective-permute-start(bf16[192,2560]{1,0:T(8,128)(2,1)S(1)} %get-tuple-element.194.refs_0_), channel_id=1, source_target_pairs={{0,4},{4,0},{1,5},{5,1},{2,6},{6,2},{3,7},{7,3},{8,12},{12,8},{9,1... | collective-permute-start | bytes 2949128 | tf_op jit(solution)/shard_map/ppermute | solution.py:511
  476.6 24.0 %collective-permute-start.43 = (bf16[192,2560]{1,0:T(8,128)(2,1)S(1)}, bf16[192,2560]{1,0:T(8,128)(2,1)S(1)}, u32[]{:S(2)}, u32[]{:S(2)}) collective-permute-start(bf16[192,2560]{1,0:T(8,128)(2,1)S(1)} %get-tuple-element.194.refs_0_), channel_id=1, source_target_pairs={{0,2},{2,0},{1,3},{3,1},{4,6},{6,4},{5,7},{7,5},{8,10},{10,8},{9,1... | collective-permute-start | bytes 2949128 | tf_op jit(solution)/shard_map/ppermute | solution.py:511
  533.6 35.3 %collective-permute-start.55 = (bf16[192,2560]{1,0:T(8,128)(2,1)S(1)}, bf16[192,2560]{1,0:T(8,128)(2,1)S(1)}, u32[]{:S(2)}, u32[]{:S(2)}) collective-permute-start(bf16[192,2560]{1,0:T(8,128)(2,1)S(1)} %get-tuple-element.206), channel_id=1, source_target_pairs={{0,6},{2,4},{4,2},{6,0},{1,7},{3,5},{5,3},{7,1},{8,14},{10,12},{12... | collective-permute-start | bytes 2949128 | tf_op jit(solution)/shard_map/ppermute | solution.py:515
  535.2 44.6 %collective-permute-start.54 = (bf16[192,2560]{1,0:T(8,128)(2,1)S(1)}, bf16[192,2560]{1,0:T(8,128)(2,1)S(1)}, u32[]{:S(2)}, u32[]{:S(2)}) collective-permute-start(bf16[192,2560]{1,0:T(8,128)(2,1)S(1)} %get-tuple-element.207), channel_id=1, source_target_pairs={{0,4},{4,0},{1,5},{5,1},{2,6},{6,2},{3,7},{7,3},{8,12},{12,8},{9,1... | collective-permute-start | bytes 2949128 | tf_op jit(solution)/shard_map/ppermute | solution.py:511
  536.2 43.7 %collective-permute-start.53 = (bf16[192,2560]{1,0:T(8,128)(2,1)S(1)}, bf16[192,2560]{1,0:T(8,128)(2,1)S(1)}, u32[]{:S(2)}, u32[]{:S(2)}) collective-permute-start(bf16[192,2560]{1,0:T(8,128)(2,1)S(1)} %get-tuple-element.208), channel_id=1, source_target_pairs={{0,2},{2,0},{1,3},{3,1},{4,6},{6,4},{5,7},{7,5},{8,10},{10,8},{9,1... | collective-permute-start | bytes 2949128 | tf_op jit(solution)/shard_map/ppermute | solution.py:511
  581.8 37.1 %collective-permute-start.56 = (bf16[160,1536]{1,0:T(8,128)(2,1)S(1)}, bf16[160,1536]{1,0:T(8,128)(2,1)S(1)}, u32[]{:S(2)}, u32[]{:S(2)}) collective-permute-start(bf16[160,1536]{1,0:T(8,128)(2,1)S(1)} %slice.580), channel_id=1, source_target_pairs={{8,0},{24,16},{9,1},{25,17},{10,2},{26,18},{11,3},{27,19},{12,4},{... | collective-permute-start | bytes 1474568 | tf_op jit(solution)/shard_map/ppermute | solution.py:507
  583.4 35.7 %collective-permute-start.57 = (bf16[320,1152]{1,0:T(8,128)(2,1)S(1)}, bf16[320,1152]{1,0:T(8,128)(2,1)S(1)}, u32[]{:S(2)}, u32[]{:S(2)}) collective-permute-start(bf16[320,1152]{1,0:T(8,128)(2,1)S(1)} %broadcast_select_fusion.11), channel_id=1, source_target_pairs={{0,4},{4,0},{1,5},{5,1},{2,6},{6,2},{3,7},{7,3},{8,12},{12,8},{9,1... | collective-permute-start | bytes 2211848 | tf_op jit(solution)/shard_map/ppermute | solution.py:511
  647.7 96.9 %reduce-scatter.11.cloned.1.call-start = ((), (), s32[]{:S(2)}) async-start(), calls=%async_computation.11 | async-start | bytes 2457600 | tf_op jit(solution)/shard_map/reduce_scatter | solution.py:604
  667.2 23.0 %collective-permute-start.61 = (bf16[192,2560]{1,0:T(8,128)(2,1)S(1)}, bf16[192,2560]{1,0:T(8,128)(2,1)}, u32[]{:S(2)}, u32[]{:S(2)}) collective-permute-start(bf16[192,2560]{1,0:T(8,128)(2,1)S(1)} %pad_maximum_fusion.8), channel_id=1, source_target_pairs={{0,2},{2,0},{1,3},{3,1},{4,6},{6,4},{5,7},{7,5},{8,10},{10,8},{9,1... | collective-permute-start | bytes 2949128 | tf_op jit(solution)/shard_map/ppermute | solution.py:511
  668.8 24.9 %collective-permute-start.62 = (bf16[192,2560]{1,0:T(8,128)(2,1)S(1)}, bf16[192,2560]{1,0:T(8,128)(2,1)}, u32[]{:S(2)}, u32[]{:S(2)}) collective-permute-start(bf16[192,2560]{1,0:T(8,128)(2,1)S(1)} %pad_maximum_fusion.9), channel_id=1, source_target_pairs={{0,4},{4,0},{1,5},{5,1},{2,6},{6,2},{3,7},{7,3},{8,12},{12,8},{9,1... | collective-permute-start | bytes 2949128 | tf_op jit(solution)/shard_map/ppermute | solution.py:511
  673.2 39.3 %collective-permute-start.63 = (bf16[320,1536]{1,0:T(8,128)(2,1)}, bf16[320,1536]{1,0:T(8,128)(2,1)}, u32[]{:S(2)}, u32[]{:S(2)}) collective-permute-start(bf16[320,1536]{1,0:T(8,128)(2,1)} %broadcast_select_fusion.3), channel_id=1, source_target_pairs={{0,4},{4,0},{1,5},{5,1},{2,6},{6,2},{3,7},{7,3},{8,12},{12,8},{9,1... | collective-permute-start | bytes 2949128 | tf_op jit(solution)/shard_map/ppermute | solution.py:511
  (125 other events, 1131.2 us)
Sparse Core Ops, SparseCore 0:
  25.1 56.2 all-gather.4
  83.5 42.3 all-gather.6
  128.0 107.7 all-gather.10
  237.8 141.9 all-gather.8
  382.0 102.5 reduce-scatter.4
  486.7 147.2 reduce-scatter.6
  647.8 50.1 reduce-scatter.8
  700.3 41.1 reduce-scatter.10

commit v4 on v3

--- a/solution.py
+++ b/solution.py
@@ -116,7 +116,9 @@
     return (places >= starts) & (places <= own_places)
 
 
-def attend_kernel(span_before, bounds_ref, q_ref, kv_ref, start_ref, out_ref, log_ref, k_rows, acc):
+def attend_kernel(places, bounds_ref, q_ref, kv_ref, start_ref, *refs):
+    first_query, first_key = places
+    *prior, out_ref, log_ref, k_rows, acc = refs
     step = pl.program_id(0)
     span = kv_ref.shape[1]
 
@@ -128,11 +130,15 @@
             )
 
     starts = start_ref[0:1, :]
-    own_places = span_before + step * BQ + lax.broadcasted_iota(jnp.int32, (1, BQ), 1)
-    acc[...] = jnp.zeros_like(acc)
+    own_places = first_query + step * BQ + lax.broadcasted_iota(jnp.int32, (1, BQ), 1)
+    if prior:
+        for h in range(GROUP):
+            acc[h] = prior[0][h * HD : (h + 1) * HD, :]
+    else:
+        acc[...] = jnp.zeros_like(acc)
 
     def one(masked, block, carry):
-        first = pl.multiple_of(block * KB, KB)
+        first = pl.multiple_of(block * KB - first_key, KB)
         keys = k_rows[pl.ds(first, KB), :]
         values = kv_ref[HD : 2 * HD, pl.ds(first, KB)]
         if masked:
@@ -152,64 +158,48 @@
         return tuple(fresh)
 
     carry = (jnp.full((1, BQ), LOW, F32), jnp.zeros((1, BQ), F32)) * GROUP
+    if prior:
+        carry = sum(((prior[1][h : h + 1, :], jnp.ones((1, BQ), F32)) for h in range(GROUP)), ())
     lo, full_lo, full_hi, hi = [bounds_ref[k, step] for k in range(4)]
     carry = lax.fori_loop(lo, full_lo, functools.partial(one, True), carry)
     carry = lax.fori_loop(full_lo, full_hi, functools.partial(one, False), carry)
     carry = lax.fori_loop(full_hi, hi, functools.partial(one, True), carry)
     for h in range(GROUP):
         top, total = carry[2 * h], carry[2 * h + 1]
-        out_ref[h * HD : (h + 1) * HD, :] = (acc[h] / total).astype(WIDE)
+        out_ref[h * HD : (h + 1) * HD, :] = (acc[h] / total).astype(out_ref.dtype)
         log_ref[h : h + 1, :] = top + jnp.log2(total)
 
 
-def attend(q_cols, kv_cols, starts, bounds):
+def attend(q_cols, kv_cols, starts, bounds, places, prior, out_type):
     count, span = q_cols.shape[1], kv_cols.shape[1]
+    wide_block = pl.BlockSpec((GROUP * HD, BQ), lambda i, s: (0, i))
+    log_block = pl.BlockSpec((8, BQ), lambda i, s: (0, i))
     return pl.pallas_call(
-        functools.partial(attend_kernel, span - count),
+        functools.partial(attend_kernel, places),
         grid_spec=pltpu.PrefetchScalarGridSpec(
             num_scalar_prefetch=1,
             grid=(count // BQ,),
             in_specs=[
-                pl.BlockSpec((GROUP * HD, BQ), lambda i, s: (0, i)),
+                wide_block,
                 pl.BlockSpec((2 * HD, span), lambda i, s: (0, 0)),
                 pl.BlockSpec((1, BQ), lambda i, s: (0, i)),
-            ],
-            out_specs=[
-                pl.BlockSpec((GROUP * HD, BQ), lambda i, s: (0, i)),
-                pl.BlockSpec((8, BQ), lambda i, s: (0, i)),
-            ],
+            ]
+            + [wide_block, log_block][: len(prior)],
+            out_specs=[wide_block, log_block],
             scratch_shapes=[pltpu.VMEM((span, HD), WIDE), pltpu.VMEM((GROUP, HD, BQ), F32)],
         ),
         out_shape=[
-            jax.ShapeDtypeStruct((GROUP * HD, count), WIDE),
+            jax.ShapeDtypeStruct((GROUP * HD, count), out_type),
             jax.ShapeDtypeStruct((8, count), F32),
         ],
         compiler_params=pltpu.CompilerParams(vmem_limit_bytes=VMEM_BYTES),
         cost_estimate=pl.CostEstimate(flops=10**6, bytes_accessed=10**5, transcendentals=0),
-    )(bounds, q_cols, kv_cols, starts)
-
-
-def attend_back_kernel(
-    span_before,
-    bounds_ref,
-    q_ref,
-    kv_ref,
-    start_ref,
-    out_ref,
-    log_ref,
-    grad_ref,
-    dq_ref,
-    dkv_ref,
-    k_rows,
-    v_rows,
-    q_rows,
-    g_rows,
-    dk,
-    dv,
-    probs_all,
-    grads_all,
-    dq,
-):
+    )(bounds, q_cols, kv_cols, starts, *prior)
+
+
+def attend_back_kernel(places, bounds_ref, q_ref, kv_ref, start_ref, out_ref, log_ref, grad_ref, *refs):
+    first_query, first_key = places
+    *prior, dq_ref, dkv_ref, k_rows, v_rows, q_rows, g_rows, dk, dv, probs_all, grads_all, dq = refs
     step = pl.program_id(0)
     span = kv_ref.shape[1]
 
@@ -223,7 +213,7 @@
         dv[...] = jnp.zeros_like(dv)
 
     starts = start_ref[0:1, :]
-    own_places = span_before + step * BQ + lax.broadcasted_iota(jnp.int32, (1, BQ), 1)
+    own_places = first_query + step * BQ + lax.broadcasted_iota(jnp.int32, (1, BQ), 1)
     dq[...] = jnp.zeros_like(dq)
     deltas = []
     for h in range(GROUP):
@@ -234,7 +224,7 @@
         deltas.append(jnp.sum(g_f32 * out_ref[part, :].astype(F32), axis=0, keepdims=True))
 
     def one(masked, block, carry):
-        first = pl.multiple_of(block * KB, KB)
+        first = pl.multiple_of(block * KB - first_key, KB)
         rows = pl.ds(first, KB)
         keys, values = k_rows[rows, :], v_rows[rows, :]
         key_cols = kv_ref[0:HD, rows]
@@ -261,7 +251,8 @@
     lax.fori_loop(full_lo, full_hi, functools.partial(one, False), 0)
     lax.fori_loop(full_hi, hi, functools.partial(one, True), 0)
     for h in range(GROUP):
-        dq_ref[h * HD : (h + 1) * HD, :] = dq[h] * SCORE_SCALE
+        part = slice(h * HD, (h + 1) * HD)
+        dq_ref[part, :] = dq[h] * SCORE_SCALE + (prior[0][part, :] if prior else 0.0)
 
     @pl.when(step == pl.num_programs(0) - 1)
     def _():
@@ -271,11 +262,11 @@
             dkv_ref[HD : 2 * HD, lanes] = dv[lanes, :].T
 
 
-def attend_back(q_cols, kv_cols, starts, bounds, out_cols, logs, grad_cols):
+def attend_back(q_cols, kv_cols, starts, bounds, places, out_cols, logs, grad_cols, prior=()):
     count, span = q_cols.shape[1], kv_cols.shape[1]
     wide_block = pl.BlockSpec((GROUP * HD, BQ), lambda i, s: (0, i))
     return pl.pallas_call(
-        functools.partial(attend_back_kernel, span - count),
+        functools.partial(attend_back_kernel, places),
         grid_spec=pltpu.PrefetchScalarGridSpec(
             num_scalar_prefetch=1,
             grid=(count // BQ,),
@@ -286,7 +277,8 @@
                 wide_block,
                 pl.BlockSpec((8, BQ), lambda i, s: (0, i)),
                 wide_block,
-            ],
+            ]
+            + [wide_block] * len(prior),
             out_specs=[wide_block, pl.BlockSpec((2 * HD, span), lambda i, s: (0, 0))],
             scratch_shapes=[
                 pltpu.VMEM((span, HD), WIDE),
@@ -306,7 +298,7 @@
         ],
         compiler_params=pltpu.CompilerParams(vmem_limit_bytes=VMEM_BYTES),
         cost_estimate=pl.CostEstimate(flops=10**6, bytes_accessed=10**5, transcendentals=0),
-    )(bounds, q_cols, kv_cols, starts, out_cols, logs, grad_cols)
+    )(bounds, q_cols, kv_cols, starts, out_cols, logs, grad_cols, *prior)
 
 
 TINY = pl.CostEstimate(flops=10**6, bytes_accessed=10**5, transcendentals=0)
@@ -594,6 +586,36 @@
             jnp.where(self.first_y, self.keep, self.got),
             jnp.where(self.first_y, self.got, self.keep),
         )
+
+
+class SpreadGather:
+    def __init__(self, block, first_y):
+        self.rows, self.first_y = block.shape[0], first_y
+        whole = gather_z(block)
+        half = whole.shape[1] // 2
+        self.keep = jnp.where(first_y, whole[:, :half], whole[:, half:])
+        self.got = over(jnp.where(first_y, whole[:, half:], whole[:, :half]), "y")
+
+    def total(self):
+        count, width = self.keep.shape[0] // self.rows, self.keep.shape[1]
+        sides = [
+            jnp.where(self.first_y, a, b).reshape(count, self.rows, width)
+            for a, b in ((self.keep, self.got), (self.got, self.keep))
+        ]
+        return jnp.concatenate(sides, axis=1).reshape(2 * count * self.rows, width)
+
+
+def spread_sum(term, rows, first_y):
+    blocks = term.reshape(-1, 2, rows, term.shape[1])
+    pick = lambda a, b: jnp.where(first_y, a, b).reshape(-1, term.shape[1])
+    keep = pick(blocks[:, 0], blocks[:, 1])
+    got = over(pick(blocks[:, 1], blocks[:, 0]), "y")
+    both = jnp.where(
+        first_y,
+        jnp.concatenate([keep, got], axis=1),
+        jnp.concatenate([got, keep], axis=1),
+    )
+    return both
 
 
 def gather_z(block):
@@ -650,6 +672,11 @@
     rows_w = w_q.shape[0]
     halves = lambda w: (w[:, : w.shape[1] // 2], w[:, w.shape[1] // 2 :])
     gain_pair = jnp.stack([gain_attn, gain_mlp] * 2, 1).astype(WIDE)
+    chunks = (slice(0, CHUNK), slice(CHUNK, nf))
+    triple = lambda cut: jnp.concatenate(
+        [padded(halves(w)[i][:, cut]) for i in range(2) for w in (w_d, w_g, w_u)], axis=1
+    )
+    flow_o = SpreadGather(w_o, first_y)
     near_a = share_columns(
         jnp.concatenate(
             [
@@ -660,18 +687,12 @@
         ),
         first_y,
     )
-    chunks = (slice(0, CHUNK), slice(CHUNK, nf))
-    triple = lambda cut: jnp.concatenate(
-        [padded(halves(w)[i][:, cut]) for i in range(2) for w in (w_d, w_g, w_u)], axis=1
-    )
+    full_a = gather_z(near_a)
     x_one = over(inputs, "x"), over(tied(inputs, near_a), "y")
     x_two = plane_step_two(*x_one)
     x_all = plane_join(inputs, *x_one, *x_two)
-    cot_one = plane_step_one(tied(cotangent, *x_two))
-    near_o = share_columns(w_o, first_y, *x_two)
-    near_c = [share_columns(triple(cut), first_y, *x_two) for cut in chunks]
-    full_a, full_o = gather_z(near_a), gather_z(near_o)
-    full_c = [gather_z(near) for near in near_c]
+    near_c = [share_columns(triple(chunks[0]), first_y, x_all)]
+    full_c = [gather_z(near_c[0])]
     first_gain = nq + 2 * nk
     gains = full_a[:, first_gain : first_gain + 2].astype(F32)
     gain_first, gain_second = gains[:, 0], gains[:, 1]
@@ -698,26 +719,40 @@
     full_lo = jnp.clip((starts[first_rows + BQ - 1] + KB - 1) // KB, lo, hi)
     full_hi = jnp.clip((reach * count + first_rows + 1) // KB, full_lo, hi)
     bounds = jnp.stack([lo, full_lo, full_hi, hi])
+    own_key = reach * count
+    own_bounds = jnp.maximum(bounds, own_key // KB)
+    far_bounds = jnp.minimum(bounds, own_key // KB)
     starts = starts[None, :]
 
     h_one, qkv = project(x_all, gain_first[None, :], full_a)
+    near_c.append(share_columns(triple(chunks[1]), first_y, qkv))
+    full_c.append(gather_z(near_c[1]))
     turned = to_columns(qkv, index, cos_tab, sin_tab, GROUP + 1, GROUP + 2)
     q_cols, kv_own = turned[: GROUP * HD], turned[GROUP * HD :]
     far_kv = [shifted(kv_own, distance, period) for distance in range(reach, 0, -1)]
-    kv_cols = jnp.concatenate(far_kv + [kv_own], axis=1)
-    kv_cols, full_o, cot_one, _ = lax.optimization_barrier((kv_cols, full_o, cot_one, near_c))
+    far_kv = [shifted(kv_own, distance, period) for distance in range(reach, 0, -1)]
+    kv_own = landed(kv_own, (flow_o, "got"))
+    cot_one = plane_step_one(tied(cotangent, kv_own))
+    own_part = attend(q_cols, kv_own, starts, own_bounds, (own_key, own_key), (), F32)
+    own_part, far_kv, near_0 = lax.optimization_barrier((own_part, far_kv, near_c[0]))
+    if reach:
+        far_kv = jnp.concatenate(far_kv, axis=1)
+        out_cols, logs = attend(q_cols, far_kv, starts, far_bounds, (own_key, 0), own_part, WIDE)
+    else:
+        out_cols, logs = own_part[0].astype(WIDE), own_part[1]
+    out_cols, cot_one, _ = lax.optimization_barrier((out_cols, cot_one, near_c[1]))
     cot_two = plane_step_two(*cot_one)
-    out_cols, logs = attend(q_cols, kv_cols, starts, bounds)
-    out_cols, *cot_two = together(out_cols, *cot_two)
+    full_o = flow_o.total()
     attended = to_rows(out_cols, index, cos_tab, sin_tab, 0, GROUP, GROUP * HD)
-    grad_mix = plane_join(cotangent, *cot_one, *cot_two)
     input_f32 = inputs.astype(F32)
     inverse_one = lax.rsqrt(jnp.mean(input_f32 * input_f32, axis=-1, keepdims=True) + eps)
     normed_one = input_f32 * inverse_one
     mid_got = over(dot(attended[half:], full_o, 1, 1).astype(WIDE), "c")
     mid_total = (dot(attended[:half], full_o, 1, 1) + mid_got.astype(F32)).astype(WIDE)
+    mid_total, *cot_two = together(mid_total, *cot_two)
     mid_far = plane_sum_one(mid_total)
     mid_near = plane_sum_two(mid_total, *mid_far)
+    grad_mix = plane_join(cotangent, *cot_one, *cot_two)
     x_mid = input_f32 + added(mid_total, *mid_near)
 
     inverse_two = lax.rsqrt(jnp.mean(x_mid * x_mid, axis=-1, keepdims=True) + eps)
@@ -761,17 +796,29 @@
         over(out_total[2 * own : 3 * own], "y"),
         across(out_total[3 * own :]),
     ]
-    dq_cols, dkv_cols = attend_back(q_cols, kv_cols, starts, bounds, out_cols, logs, grad_cols)
-    dkv_cols, *out_sends = together(dkv_cols, *out_sends)
+    back = functools.partial(attend_back, q_cols)
+    prior, far_got = (), []
+    if reach:
+        dq_far, dkv_far = back(
+            far_kv, starts, far_bounds, (own_key, 0), out_cols, logs, grad_cols
+        )
+        prior = (dq_far,)
+        far_got = [
+            shifted(
+                dkv_far[:, (reach - d) * count : (reach - d + 1) * count].astype(WIDE), -d, period
+            )
+            for d in range(1, reach + 1)
+        ]
+    dq_cols, dkv_cols = back(
+        kv_own, starts, own_bounds, (own_key, own_key), out_cols, logs, grad_cols, prior
+    )
+    dkv_cols, out_sends, far_got = lax.optimization_barrier((dkv_cols, out_sends, far_got))
     output = (x_mid + added(out_total, *out_sends)).astype(WIDE)
     owned = [Unshare(tied(sums[0], dkv_cols), first_y)]
-    dkv_own = dkv_cols[:, reach * count :]
-    for distance in range(1, reach + 1):
-        first = (reach - distance) * count
-        dkv_own = dkv_own + shifted(
-            dkv_cols[:, first : first + count].astype(WIDE), -distance, period
-        ).astype(F32)
-    dkv_own = landed(dkv_own, (owned[0], "got"))
+    dkv_own = sum((part.astype(F32) for part in far_got), dkv_cols)
+    out_term = weight_grads(grad_branch, tied(attended, dkv_cols))
+    dkv_own, out_term = landed((dkv_own, out_term), (owned[0], "got"))
+    out_term = spread_sum(out_term, w_o.shape[0], first_y)
     grad_qkv = to_rows(
         jnp.concatenate([dq_cols, dkv_own], axis=0),
         index,
@@ -782,25 +829,24 @@
         full_a.shape[1],
     )
     qkv_part = weight_grads(h_one, grad_qkv)
-    grad_qkv, qkv_part = together(grad_qkv, qkv_part)
+    grad_qkv, qkv_part, out_term = together(grad_qkv, qkv_part, out_term)
     one_got = over(dot(grad_qkv[half:], full_a, 1, 1).astype(WIDE), "c")
     one_total = (dot(grad_qkv[:half], full_a, 1, 1) + one_got.astype(F32)).astype(WIDE)
     one_total, qkv_part, sums[1] = together(one_total, qkv_part, sums[1])
     qkv_grad = sum_z(qkv_part)
     owned.append(Unshare(sums[1], first_y))
     one_far = plane_sum_one(one_total)
-    out_term = weight_grads(grad_branch, tied(attended, qkv_part))
-    *one_far, out_term = together(*one_far, out_term)
+    one_far = landed(one_far, (owned[1], "got"))
     one_near = plane_sum_two(one_total, *one_far)
-    *one_near, qkv_grad, out_term = together(*one_near, qkv_grad, out_term)
-    out_grad = sum_z(out_term)
-    owned_o = Unshare(out_grad, first_y)
+    out_grad = sum_z(tied(out_term, qkv_grad))
+    owned_a = Unshare(qkv_grad, first_y)
+    *one_near, qkv_grad = together(*one_near, qkv_grad)
     grad_h_one = added(one_total, *one_near)
     input_grad = (grad_mid + norm_back(grad_h_one, normed_one, inverse_one, gain_first)).astype(
         WIDE
     )
 
-    input_grad, out_term = landed((input_grad, out_term), (owned[0], "got"), (owned[1], "got"))
+    input_grad = landed(input_grad, (owned_a, "got"))
     owned = [part.both() for part in owned]
     kept = [CHUNK, nf - CHUNK]
     width = [full.shape[1] // 3 for full in full_c]
@@ -816,10 +862,9 @@
         ).astype(F32)
 
     down_out, gate_out, up_out = unit_columns(0).T, unit_columns(1), unit_columns(2)
-    one, two = Unshare(qkv_grad, first_y).both()
+    one, two = owned_a.both()
     pick = lambda a, b: jnp.concatenate([one[:, a:b], two[:, a:b]], axis=1).astype(F32)
     q_out, k_out, v_out = pick(0, nq), pick(nq, nq + nk), pick(nq + nk, nq + 2 * nk)
-    o_out = jnp.concatenate(owned_o.both(), axis=1).T.astype(F32)
 
     def row_sums(weight, grad):
         return jnp.sum(weight.astype(F32) * grad, axis=1)
@@ -831,7 +876,9 @@
         ]
     )
     gain_sums = gain_sums + lax.ppermute(gain_sums, "x", SWAP)
+    gain_sums, out_grad = together(gain_sums, out_grad)
     gain_sums = gain_sums + lax.ppermute(gain_sums, "c", SWAP)
+    o_out = out_grad.T.astype(F32)
     gain_one_out = gain_sums[0] / gain_attn.astype(WIDE).astype(F32)
     gain_two_out = gain_sums[1] / gain_mlp.astype(WIDE).astype(F32)
     return (

time: 769 us -> 750 us (0.975)
  waiting for transfers between devices: 314 us -> 287 us
    ppermute x2, waiting for transfers between devices: 45.5 us -> 15.8 us  [shifted(): return lax.ppermute(block, 'z', route)]
    unnamed x8 -> x9, waiting for transfers between devices: 0.13 us -> 18.7 us
    ppermute x62, waiting for transfers between devices: 227 us -> 214 us  [over(): return lax.ppermute(block, axis, SWAP)]
    select_n x1 -> x4, other arithmetic: 0.01 us -> 8.47 us  [the longest x1 3.44 us: spread_sum(): jnp.where(first_y, jnp.concatenate([keep, got], axis=1), jnp.concatenate(...]
    pallas_call x2 -> x4, Pallas kernels: 59.1 us -> 65 us  [the longest x2 36.3 us: attend_back(): pl.pallas_call(functools.partial(attend_back_kernel, places), grid_spec=p...]
    unnamed x166 -> x170, local copies, waits for them, and re-layouts: 22.6 us -> 24.6 us
  transfers between devices with their start and end apart: 76 -> 76, of which waited for: 37 -> 34; matrix products, arithmetic and copies ran while one was open for 14% -> 16% of each run, Pallas kernels for 31% -> 32%
where the time goes in v4:
time: 750 us; the launch traced here: 743 us
  waiting for transfers between devices  287 us (38%)
  Pallas kernels  238 us (32%)
  other arithmetic  71.3 us (10%)
  starting transfers between devices  58.3 us (8%)
  local copies, waits for them, and re-layouts  57.1 us (8%)
  between operations  15.9 us (2%)
  matrix products  15.6 us (2%)
    ppermute x62, waiting for transfers between devices, over(): return lax.ppermute(block, axis, SWAP)  214 us
    pallas_call x4, Pallas kernels, hidden_units(): pl.pallas_call(functools.partial(units_kernel, bool(prior)), grid=(count...  75.5 us
    ppermute x62, starting transfers between devices, over(): return lax.ppermute(block, axis, SWAP)  50.7 us
    all_gather x4, waiting for transfers between devices, gather_z(): return lax.all_gather(block, 'z', axis=0, tiled=True)  36.9 us
    pallas_call x2, Pallas kernels, attend_back(): pl.pallas_call(functools.partial(attend_back_kernel, places), grid_spec=p...  36.3 us
    pallas_call x2, Pallas kernels, unit_grads(): pl.pallas_call(unit_grads_kernel, grid=(model // rows,), in_specs=[pl.Blo...  34 us
    pallas_call x2, Pallas kernels, attend(): pl.pallas_call(functools.partial(attend_kernel, places), grid_spec=pltpu....  28.7 us
    unnamed x170, local copies, waits for them, and re-layouts  24.6 us
  transfers between devices with their start and end apart: 76, of which 34 were waited for; matrix products, arithmetic and copies ran while one was open for 16% of the time, Pallas kernels for 32%

profile of v4, /device:TPU:0, one launch (start us, length us, event | category | flops | bytes accessed | tf_op | source)
XLA Modules:
  0.0 742.9 jit_solution(17706742757898532362)
XLA Ops:
  15.3 7.7 %collective-permute-done.1 = bf16[320,512]{1,0:T(8,128)(2,1)S(1)} collective-permute-done((bf16[320,512]{1,0:T(8,128)(2,1)S(1)}, bf16[320,512]{1,0:T(8,128)(2,1)S(1)}, u32[]{:S(2)}, u32[]{:S(2)}) %collective-permute-start.1) | collective-permute-done | bytes 327712 | tf_op jit(solution)/shard_map/ppermute | solution.py:503
  27.4 19.7 %collective-permute-done.refs_1_ = bf16[192,2560]{1,0:T(8,128)(2,1)S(1)} collective-permute-done((bf16[192,2560]{1,0:T(8,128)(2,1)S(1)}, bf16[192,2560]{1,0:T(8,128)(2,1)S(1)}, u32[]{:S(2)}, u32[]{:S(2)}) %collective-permute-start) | collective-permute-done | bytes 983072 | tf_op jit(solution)/shard_map/ppermute | solution.py:503
  65.2 5.8 shard_map.212.x_ref
  71.7 17.9 %collective-permute-done.13 = bf16[320,1152]{1,0:T(8,128)(2,1)S(1)} collective-permute-done((bf16[320,1152]{1,0:T(8,128)(2,1)S(1)}, bf16[320,1152]{1,0:T(8,128)(2,1)S(1)}, u32[]{:S(2)}, u32[]{:S(2)}) %collective-permute-start.13) | collective-permute-done | bytes 737312 | tf_op jit(solution)/shard_map/ppermute | solution.py:503
  109.5 9.6 %shard_map.213 = (bf16[1536,2560]{1,0:T(8,128)(2,1)}, f32[1536,512]{1,0:T(8,128)S(1)}) custom-call(bf16[1536,2560]{1,0:T(8,128)(2,1)} %shard_map.212.x_ref, f32[1,2560]{1,0:T(1,128)S(1)} %broadcast_in_dim_squeeze.2.gain_ref, bf16[2560,512]{1,0:T(8,128)(2,1)S(1)} %copy-done.11), custom_call_target="tpu_custom_call" | custom-call | flops 1000000 | bytes 100000 | tf_op jit(solution)/shard_map/pallas_call | solution.py:360
  133.7 27.2 %shard_map.215 = (f32[320,1536]{1,0:T(8,128)S(1)}, f32[8,1536]{1,0:T(8,128)S(1)}) custom-call(s32[4,6]{1,0:T(4,128)S(1)} %get-tuple-element.316.bounds_ref, bf16[320,1536]{1,0:T(8,128)(2,1)S(1)} %slice.424.q_ref, bf16[160,1536]{1,0:T(8,128)(2,1)S(1)} %slice.425.kv_ref, s32[1,1536]{1,0:T(1,128)S(1)} %broadcast_in_dim.2.start_ref), custom_call_target="tpu_custom_call" | custom-call | flops 1000000 | bytes 100000 | tf_op jit(solution)/shard_map/pallas_call | solution.py:177
  180.3 4.9 add_convert_fusion.3
  192.0 11.3 %collective-permute-done.22 = bf16[96,2560]{1,0:T(8,128)(2,1)S(1)} collective-permute-done((bf16[96,2560]{1,0:T(8,128)(2,1)S(1)}, bf16[96,2560]{1,0:T(8,128)(2,1)S(1)}, u32[]{:S(2)}, u32[]{:S(2)}) %collective-permute-start.22) | collective-permute-done | bytes 491552 | tf_op jit(solution)/shard_map/ppermute | solution.py:503
  206.3 19.7 %collective-permute-done.23 = bf16[192,2560]{1,0:T(8,128)(2,1)S(1)} collective-permute-done((bf16[192,2560]{1,0:T(8,128)(2,1)S(1)}, bf16[192,2560]{1,0:T(8,128)(2,1)S(1)}, u32[]{:S(2)}, u32[]{:S(2)}) %collective-permute-start.23) | collective-permute-done | bytes 983072 | tf_op jit(solution)/shard_map/ppermute | solution.py:503
  232.3 17.7 %collective-permute-done.25.refs_2_ = bf16[192,2560]{1,0:T(8,128)(2,1)S(1)} collective-permute-done((bf16[192,2560]{1,0:T(8,128)(2,1)S(1)}, bf16[192,2560]{1,0:T(8,128)(2,1)S(1)}, u32[]{:S(2)}, u32[]{:S(2)}) %collective-permute-start.25) | collective-permute-done | bytes 983072 | tf_op jit(solution)/shard_map/ppermute | solution.py:503
  254.4 10.5 %collective-permute-done.26.refs_3_ = bf16[96,2560]{1,0:T(8,128)(2,1)S(1)} collective-permute-done((bf16[96,2560]{1,0:T(8,128)(2,1)S(1)}, bf16[96,2560]{1,0:T(8,128)(2,1)S(1)}, u32[]{:S(2)}, u32[]{:S(2)}) %collective-permute-start.26) | collective-permute-done | bytes 491552 | tf_op jit(solution)/shard_map/ppermute | solution.py:503
  266.0 5.4 shard_map.219.cot_ref
  271.4 5.8 shard_map.218.h_ref
  277.2 17.8 %shard_map.221 = (bf16[768,1152]{1,0:T(8,128)(2,1)S(1)}, bf16[768,2560]{1,0:T(8,128)(2,1)S(1)}, bf16[768,2560]{1,0:T(8,128)(2,1)}) custom-call(bf16[1536,2560]{1,0:T(8,128)(2,1)} %shard_map.218.h_ref, bf16[1536,2560]{1,0:T(8,128)(2,1)} %shard_map.219.cot_ref, bf16[2560,1152]{1,0:T(8,128)(2,1)} %all-gather.11.cloned.1.call-done.weight_ref), custom_call_target="tpu_custom_call" | custom-call | flops 1000000 | bytes 100000 | tf_op jit(solution)/shard_map/pallas_call | solution.py:430
  296.9 17.8 %shard_map.220 = (bf16[768,1152]{1,0:T(8,128)(2,1)S(1)}, bf16[768,2560]{1,0:T(8,128)(2,1)S(1)}, bf16[768,2560]{1,0:T(8,128)(2,1)}) custom-call(bf16[1536,2560]{1,0:T(8,128)(2,1)} %shard_map.218.h_ref, bf16[1536,2560]{1,0:T(8,128)(2,1)} %shard_map.219.cot_ref, bf16[2560,1152]{1,0:T(8,128)(2,1)} %all-gather.11.cloned.1.call-done.weight_ref), custom_call_target="tpu_custom_call" | custom-call | flops 1000000 | bytes 100000 | tf_op jit(solution)/shard_map/pallas_call | solution.py:430
  316.7 16.3 %shard_map.222 = bf16[2560,1152]{1,0:T(8,128)(2,1)} custom-call(bf16[1536,2560]{1,0:T(8,128)(2,1)} %shard_map.218.h_ref, bf16[1536,2560]{1,0:T(8,128)(2,1)} %shard_map.219.cot_ref, bf16[768,1152]{1,0:T(8,128)(2,1)S(1)} %get-tuple-element.115.mine_ref, bf16[768,1152]{1,0:T(8,128)(2,1)S(1)} %get-tuple-element.112.other_ref), custom_call_target="tpu_custom_call" | custom-call | flops 1000000 | bytes 100000 | tf_op jit(solution)/shard_map/pallas_call | solution.py:455
  333.0 34.5 %all-gather.9.cloned.1.call-done.weight_ref = bf16[2560,1536]{1,0:T(8,128)(2,1)} async-done(((bf16[640,1536]{1,0:T(8,128)(2,1)}), bf16[2560,1536]{1,0:T(8,128)(2,1)}) %all-gather.9.cloned.1.call-update) | async-done | bytes 7864336 | tf_op jit(solution)/shard_map/all_gather | solution.py:622
  367.6 19.9 %shard_map.224 = (bf16[768,1536]{1,0:T(8,128)(2,1)S(1)}, bf16[768,2560]{1,0:T(8,128)(2,1)}, bf16[768,2560]{1,0:T(8,128)(2,1)}) custom-call(bf16[1536,2560]{1,0:T(8,128)(2,1)} %shard_map.218.h_ref, bf16[1536,2560]{1,0:T(8,128)(2,1)} %shard_map.219.cot_ref, bf16[2560,1536]{1,0:T(8,128)(2,1)} %all-gather.9.cloned.1.call-done.weight_ref, ...), custom_call_target="tpu_custom_call" | custom-call | flops 1000000 | bytes 100000 | tf_op jit(solution)/shard_map/pallas_call | solution.py:430
  387.5 20.0 %shard_map.223 = (bf16[768,1536]{1,0:T(8,128)(2,1)S(1)}, bf16[768,2560]{1,0:T(8,128)(2,1)}, bf16[768,2560]{1,0:T(8,128)(2,1)}) custom-call(bf16[1536,2560]{1,0:T(8,128)(2,1)} %shard_map.218.h_ref, bf16[1536,2560]{1,0:T(8,128)(2,1)} %shard_map.219.cot_ref, bf16[2560,1536]{1,0:T(8,128)(2,1)} %all-gather.9.cloned.1.call-done.weight_ref, ...), custom_call_target="tpu_custom_call" | custom-call | flops 1000000 | bytes 100000 | tf_op jit(solution)/shard_map/pallas_call | solution.py:430
  413.9 10.6 %collective-permute-done.41 = bf16[96,2560]{1,0:T(8,128)(2,1)S(1)} collective-permute-done((bf16[96,2560]{1,0:T(8,128)(2,1)S(1)}, bf16[96,2560]{1,0:T(8,128)(2,1)S(1)}, u32[]{:S(2)}, u32[]{:S(2)}) %collective-permute-start.41) | collective-permute-done | bytes 491552 | tf_op jit(solution)/shard_map/ppermute | solution.py:503
  430.0 17.7 %shard_map.225 = bf16[2560,1536]{1,0:T(8,128)(2,1)} custom-call(bf16[1536,2560]{1,0:T(8,128)(2,1)} %shard_map.218.h_ref, bf16[1536,2560]{1,0:T(8,128)(2,1)} %shard_map.219.cot_ref, bf16[768,1536]{1,0:T(8,128)(2,1)S(1)} %get-tuple-element.125.mine_ref, bf16[768,1536]{1,0:T(8,128)(2,1)S(1)} %get-tuple-element.126.other_ref), custom_call_target="tpu_custom_call" | custom-call | flops 1000000 | bytes 100000 | tf_op jit(solution)/shard_map/pallas_call | solution.py:455
  462.6 21.2 %collective-permute-done.44.refs_2_ = bf16[192,2560]{1,0:T(8,128)(2,1)S(1)} collective-permute-done((bf16[192,2560]{1,0:T(8,128)(2,1)S(1)}, bf16[192,2560]{1,0:T(8,128)(2,1)S(1)}, u32[]{:S(2)}, u32[]{:S(2)}) %collective-permute-start.44) | collective-permute-done | bytes 983072 | tf_op jit(solution)/shard_map/ppermute | solution.py:503
  487.4 9.3 %collective-permute-done.45.refs_3_ = bf16[96,2560]{1,0:T(8,128)(2,1)S(1)} collective-permute-done((bf16[96,2560]{1,0:T(8,128)(2,1)S(1)}, bf16[96,2560]{1,0:T(8,128)(2,1)S(1)}, u32[]{:S(2)}, u32[]{:S(2)}) %collective-permute-start.45) | collective-permute-done | bytes 491552 | tf_op jit(solution)/shard_map/ppermute | solution.py:503
  502.2 5.8 shard_map.226.a_ref
  509.6 7.7 %shard_map.227.rows_ref = bf16[1536,320]{1,0:T(8,128)(2,1)S(1)} custom-call(bf16[1536,2560]{1,0:T(8,128)(2,1)} %shard_map.226.a_ref, bf16[2560,320]{1,0:T(8,128)(2,1)S(1)} %bitcast.47), custom_call_target="tpu_custom_call" | custom-call | flops 1000000 | bytes 100000 | tf_op jit(solution)/shard_map/pallas_call | solution.py:391
  528.6 31.5 %shard_map.230 = (f32[320,1536]{1,0:T(8,128)}, f32[160,1536]{1,0:T(8,128)S(1)}) custom-call(s32[4,6]{1,0:T(4,128)S(1)} %get-tuple-element.316.bounds_ref, bf16[320,1536]{1,0:T(8,128)(2,1)S(1)} %slice.424.q_ref, bf16[160,1536]{1,0:T(8,128)(2,1)S(1)} %copy-done.10, s32[1,1536]{1,0:T(1,128)S(1)} %broadcast_in_dim.2.start_ref, ...), custom_call_target="tpu_custom_call" | custom-call | flops 1000000 | bytes 100000 | tf_op jit(solution)/shard_map/pallas_call | solution.py:268
  560.1 15.8 %collective-permute-done.56 = bf16[160,1536]{1,0:T(8,128)(2,1)S(1)} collective-permute-done((bf16[160,1536]{1,0:T(8,128)(2,1)S(1)}, bf16[160,1536]{1,0:T(8,128)(2,1)S(1)}, u32[]{:S(2)}, u32[]{:S(2)}) %collective-permute-start.56) | collective-permute-done | bytes 491552 | tf_op jit(solution)/shard_map/ppermute | solution.py:499
  578.3 9.6 %shard_map.231 = bf16[2560,320]{1,0:T(8,128)(2,1)S(1)} custom-call(bf16[1536,2560]{1,0:T(8,128)(2,1)} %shard_map.226.a_ref, bf16[1536,320]{1,0:T(8,128)(2,1)S(1)} %copy-done.8), custom_call_target="tpu_custom_call" | custom-call | flops 1000000 | bytes 100000 | tf_op jit(solution)/shard_map/pallas_call | solution.py:473
  588.0 7.4 %collective-permute-done.57 = bf16[320,1152]{1,0:T(8,128)(2,1)S(1)} collective-permute-done((bf16[320,1152]{1,0:T(8,128)(2,1)S(1)}, bf16[320,1152]{1,0:T(8,128)(2,1)S(1)}, u32[]{:S(2)}, u32[]{:S(2)}) %collective-permute-start.57) | collective-permute-done | bytes 737312 | tf_op jit(solution)/shard_map/ppermute | solution.py:503
  604.5 9.6 %shard_map.233 = bf16[2560,512]{1,0:T(8,128)(2,1)S(1)} custom-call(bf16[1536,2560]{1,0:T(8,128)(2,1)} %get-tuple-element.151.a_ref, bf16[1536,512]{1,0:T(8,128)(2,1)S(1)} %shard_map.232.b_ref), custom_call_target="tpu_custom_call" | custom-call | flops 1000000 | bytes 100000 | tf_op jit(solution)/shard_map/pallas_call | solution.py:473
  644.2 27.4 %collective-permute-done.61 = bf16[96,2560]{1,0:T(8,128)(2,1)S(1)} collective-permute-done((bf16[96,2560]{1,0:T(8,128)(2,1)S(1)}, bf16[96,2560]{1,0:T(8,128)(2,1)S(1)}, u32[]{:S(2)}, u32[]{:S(2)}) %collective-permute-start.61) | collective-permute-done | bytes 491552 | tf_op jit(solution)/shard_map/ppermute | solution.py:503
  713.5 18.5 %reduce-scatter.13.cloned.1.call-done = bf16[320,640]{1,0:T(8,128)(2,1)} async-done(((bf16[1280,640]{1,0:T(8,128)(2,1)}), bf16[320,640]{1,0:T(8,128)(2,1)}) %reduce-scatter.13.cloned.1.call-update) | async-done | bytes 409616
  (454 shorter events, 245.3 us)
Async XLA Ops:
  7.2 92.8 %all-gather.7.cloned.1.call-start = ((), (), s32[]{:S(2)}) async-start(), calls=%async_computation.5 | async-start | bytes 2048000 | tf_op jit(solution)/shard_map/all_gather | solution.py:622
  9.3 97.6 %all-gather.5.cloned.1.call-start = ((), (), s32[]{:S(2)}) async-start(), calls=%async_computation.4 | async-start | bytes 3276800 | tf_op jit(solution)/shard_map/all_gather | solution.py:622
  24.1 253.1 %all-gather.11.cloned.1.call-start = ((), (), s32[]{:S(2)}) async-start(), calls=%async_computation.7 | async-start | bytes 7372800 | tf_op jit(solution)/shard_map/all_gather | solution.py:622
  24.1 23.0 %collective-permute-start = (bf16[192,2560]{1,0:T(8,128)(2,1)S(1)}, bf16[192,2560]{1,0:T(8,128)(2,1)S(1)}, u32[]{:S(2)}, u32[]{:S(2)}) collective-permute-start(bf16[192,2560]{1,0:T(8,128)(2,1)S(1)} %copy-done), channel_id=1, source_target_pairs={{0,2},{2,0},{1,3},{3,1},{4,6},{6,4},{5,7},{7,5},{8,10},{10,8},{9,1... | collective-permute-start | bytes 2949128 | tf_op jit(solution)/shard_map/ppermute | solution.py:503
  25.9 22.8 %collective-permute-start.2 = (bf16[192,2560]{1,0:T(8,128)(2,1)S(1)}, bf16[192,2560]{1,0:T(8,128)(2,1)S(1)}, u32[]{:S(2)}, u32[]{:S(2)}) collective-permute-start(bf16[192,2560]{1,0:T(8,128)(2,1)S(1)} %copy-done), channel_id=1, source_target_pairs={{0,4},{4,0},{1,5},{5,1},{2,6},{6,2},{3,7},{7,3},{8,12},{12,8},{9,1... | collective-permute-start | bytes 2949128 | tf_op jit(solution)/shard_map/ppermute | solution.py:503
  27.4 35.3 %collective-permute-start.5 = (bf16[192,2560]{1,0:T(8,128)(2,1)S(1)}, bf16[192,2560]{1,0:T(8,128)(2,1)S(1)}, u32[]{:S(2)}, u32[]{:S(2)}) collective-permute-start(bf16[192,2560]{1,0:T(8,128)(2,1)S(1)} %copy-done), channel_id=1, source_target_pairs={{0,1},{1,0},{2,3},{3,2},{4,5},{5,4},{6,7},{7,6},{8,9},{9,8},{10,11... | collective-permute-start | bytes 2949128 | tf_op jit(solution)/shard_map/ppermute | solution.py:503
  91.2 276.3 %all-gather.9.cloned.1.call-start = ((), (), s32[]{:S(2)}) async-start(), calls=%async_computation.6 | async-start | bytes 9830400 | tf_op jit(solution)/shard_map/all_gather | solution.py:622
  103.2 22.6 %collective-permute-start.11 = (bf16[1280,320]{0,1:T(8,128)(2,1)}, bf16[1280,320]{0,1:T(8,128)(2,1)S(1)}, u32[]{:S(2)}, u32[]{:S(2)}) collective-permute-start(bf16[1280,320]{0,1:T(8,128)(2,1)} %copy.70), channel_id=1, source_target_pairs={{0,4},{4,0},{1,5},{5,1},{2,6},{6,2},{3,7},{7,3},{8,12},{12,8},{9,1... | collective-permute-start | bytes 2457608 | tf_op jit(solution)/shard_map/ppermute | solution.py:503
  119.1 45.2 %collective-permute-start.16 = (bf16[320,1536]{1,0:T(8,128)(2,1)}, bf16[320,1536]{1,0:T(8,128)(2,1)}, u32[]{:S(2)}, u32[]{:S(2)}) collective-permute-start(bf16[320,1536]{1,0:T(8,128)(2,1)} %broadcast_select_fusion.8), channel_id=1, source_target_pairs={{0,4},{4,0},{1,5},{5,1},{2,6},{6,2},{3,7},{7,3},{8,12},{12,8},{9,1... | collective-permute-start | bytes 2949128 | tf_op jit(solution)/shard_map/ppermute | solution.py:503
  124.1 36.9 %collective-permute-start.12 = (bf16[160,1536]{1,0:T(8,128)(2,1)S(1)}, bf16[160,1536]{1,0:T(8,128)(2,1)S(1)}, u32[]{:S(2)}, u32[]{:S(2)}) collective-permute-start(bf16[160,1536]{1,0:T(8,128)(2,1)S(1)} %slice.425.kv_ref), channel_id=1, source_target_pairs={{0,8},{16,24},{1,9},{17,25},{2,10},{18,26},{3,11},{19,27},{4,12},{... | collective-permute-start | bytes 1474568 | tf_op jit(solution)/shard_map/ppermute | solution.py:499
  125.8 41.6 %collective-permute-start.15 = (bf16[192,2560]{1,0:T(8,128)(2,1)}, bf16[192,2560]{1,0:T(8,128)(2,1)}, u32[]{:S(2)}, u32[]{:S(2)}) collective-permute-start(bf16[192,2560]{1,0:T(8,128)(2,1)} %refs_0_.3), channel_id=1, source_target_pairs={{0,4},{4,0},{1,5},{5,1},{2,6},{6,2},{3,7},{7,3},{8,12},{12,8},{9,1... | collective-permute-start | bytes 2949128 | tf_op jit(solution)/shard_map/ppermute | solution.py:503
  126.7 40.7 %collective-permute-start.14 = (bf16[192,2560]{1,0:T(8,128)(2,1)}, bf16[192,2560]{1,0:T(8,128)(2,1)}, u32[]{:S(2)}, u32[]{:S(2)}) collective-permute-start(bf16[192,2560]{1,0:T(8,128)(2,1)} %refs_0_.3), channel_id=1, source_target_pairs={{0,2},{2,0},{1,3},{3,1},{4,6},{6,4},{5,7},{7,5},{8,10},{10,8},{9,1... | collective-permute-start | bytes 2949128 | tf_op jit(solution)/shard_map/ppermute | solution.py:503
  173.2 334.9 %reduce-scatter.7.cloned.1.call-start = ((), (), s32[]{:S(2)}) async-start(), calls=%async_computation.8 | async-start | bytes 7372800 | tf_op jit(solution)/shard_map/reduce_scatter | solution.py:626
  203.8 22.2 %collective-permute-start.23 = (bf16[192,2560]{1,0:T(8,128)(2,1)S(1)}, bf16[192,2560]{1,0:T(8,128)(2,1)S(1)}, u32[]{:S(2)}, u32[]{:S(2)}) collective-permute-start(bf16[192,2560]{1,0:T(8,128)(2,1)S(1)} %pad_maximum_fusion.5), channel_id=1, source_target_pairs={{0,4},{4,0},{1,5},{5,1},{2,6},{6,2},{3,7},{7,3},{8,12},{12,8},{9,1... | collective-permute-start | bytes 2949128 | tf_op jit(solution)/shard_map/ppermute | solution.py:503
  204.7 21.9 %collective-permute-start.21 = (bf16[192,2560]{1,0:T(8,128)(2,1)S(1)}, bf16[192,2560]{1,0:T(8,128)(2,1)S(1)}, u32[]{:S(2)}, u32[]{:S(2)}) collective-permute-start(bf16[192,2560]{1,0:T(8,128)(2,1)S(1)} %pad_maximum_fusion.4), channel_id=1, source_target_pairs={{0,2},{2,0},{1,3},{3,1},{4,6},{6,4},{5,7},{7,5},{8,10},{10,8},{9,1... | collective-permute-start | bytes 2949128 | tf_op jit(solution)/shard_map/ppermute | solution.py:503
  367.5 268.0 %reduce-scatter.9.cloned.1.call-start = ((), (), s32[]{:S(2)}) async-start(), calls=%async_computation.9 | async-start | bytes 9830400 | tf_op jit(solution)/shard_map/reduce_scatter | solution.py:626
  426.9 23.4 %collective-permute-start.40 = (bf16[192,2560]{1,0:T(8,128)(2,1)}, bf16[192,2560]{1,0:T(8,128)(2,1)}, u32[]{:S(2)}, u32[]{:S(2)}) collective-permute-start(bf16[192,2560]{1,0:T(8,128)(2,1)} %pad_maximum_fusion.6), channel_id=1, source_target_pairs={{0,2},{2,0},{1,3},{3,1},{4,6},{6,4},{5,7},{7,5},{8,10},{10,8},{9,1... | collective-permute-start | bytes 2949128 | tf_op jit(solution)/shard_map/ppermute | solution.py:503
  428.5 23.2 %collective-permute-start.42 = (bf16[192,2560]{1,0:T(8,128)(2,1)}, bf16[192,2560]{1,0:T(8,128)(2,1)}, u32[]{:S(2)}, u32[]{:S(2)}) collective-permute-start(bf16[192,2560]{1,0:T(8,128)(2,1)} %pad_maximum_fusion.7), channel_id=1, source_target_pairs={{0,4},{4,0},{1,5},{5,1},{2,6},{6,2},{3,7},{7,3},{8,12},{12,8},{9,1... | collective-permute-start | bytes 2949128 | tf_op jit(solution)/shard_map/ppermute | solution.py:503
  451.7 245.3 %reduce-scatter.11.cloned.1.call-start = ((), (), s32[]{:S(2)}) async-start(), calls=%async_computation.10 | async-start | bytes 3276800 | tf_op jit(solution)/shard_map/reduce_scatter | solution.py:626
  452.0 35.4 %collective-permute-start.52 = (bf16[768,2560]{1,0:T(8,128)(2,1)}, bf16[768,2560]{1,0:T(8,128)(2,1)S(1)}, u32[]{:S(2)}, u32[]{:S(2)}) collective-permute-start(bf16[768,2560]{1,0:T(8,128)(2,1)} %get-tuple-element.130), channel_id=1, source_target_pairs={{0,1},{1,0},{2,3},{3,2},{4,5},{5,4},{6,7},{7,6},{8,9},{9,8},{10,11... | collective-permute-start | bytes 11796488 | tf_op jit(solution)/shard_map/ppermute | solution.py:503
  459.7 24.1 %collective-permute-start.44 = (bf16[192,2560]{1,0:T(8,128)(2,1)S(1)}, bf16[192,2560]{1,0:T(8,128)(2,1)S(1)}, u32[]{:S(2)}, u32[]{:S(2)}) collective-permute-start(bf16[192,2560]{1,0:T(8,128)(2,1)S(1)} %get-tuple-element.236.refs_0_), channel_id=1, source_target_pairs={{0,4},{4,0},{1,5},{5,1},{2,6},{6,2},{3,7},{7,3},{8,12},{12,8},{9,1... | collective-permute-start | bytes 2949128 | tf_op jit(solution)/shard_map/ppermute | solution.py:503
  461.1 24.2 %collective-permute-start.43 = (bf16[192,2560]{1,0:T(8,128)(2,1)S(1)}, bf16[192,2560]{1,0:T(8,128)(2,1)S(1)}, u32[]{:S(2)}, u32[]{:S(2)}) collective-permute-start(bf16[192,2560]{1,0:T(8,128)(2,1)S(1)} %get-tuple-element.236.refs_0_), channel_id=1, source_target_pairs={{0,2},{2,0},{1,3},{3,1},{4,6},{6,4},{5,7},{7,5},{8,10},{10,8},{9,1... | collective-permute-start | bytes 2949128 | tf_op jit(solution)/shard_map/ppermute | solution.py:503
  518.5 57.4 %collective-permute-start.55 = (bf16[192,2560]{1,0:T(8,128)(2,1)S(1)}, bf16[192,2560]{1,0:T(8,128)(2,1)S(1)}, u32[]{:S(2)}, u32[]{:S(2)}) collective-permute-start(bf16[192,2560]{1,0:T(8,128)(2,1)S(1)} %get-tuple-element.248), channel_id=1, source_target_pairs={{0,6},{2,4},{4,2},{6,0},{1,7},{3,5},{5,3},{7,1},{8,14},{10,12},{12... | collective-permute-start | bytes 2949128 | tf_op jit(solution)/shard_map/ppermute | solution.py:507
  520.2 55.7 %collective-permute-start.54 = (bf16[192,2560]{1,0:T(8,128)(2,1)S(1)}, bf16[192,2560]{1,0:T(8,128)(2,1)S(1)}, u32[]{:S(2)}, u32[]{:S(2)}) collective-permute-start(bf16[192,2560]{1,0:T(8,128)(2,1)S(1)} %get-tuple-element.249), channel_id=1, source_target_pairs={{0,4},{4,0},{1,5},{5,1},{2,6},{6,2},{3,7},{7,3},{8,12},{12,8},{9,1... | collective-permute-start | bytes 2949128 | tf_op jit(solution)/shard_map/ppermute | solution.py:503
  521.1 54.8 %collective-permute-start.53 = (bf16[192,2560]{1,0:T(8,128)(2,1)S(1)}, bf16[192,2560]{1,0:T(8,128)(2,1)S(1)}, u32[]{:S(2)}, u32[]{:S(2)}) collective-permute-start(bf16[192,2560]{1,0:T(8,128)(2,1)S(1)} %get-tuple-element.250), channel_id=1, source_target_pairs={{0,2},{2,0},{1,3},{3,1},{4,6},{6,4},{5,7},{7,5},{8,10},{10,8},{9,1... | collective-permute-start | bytes 2949128 | tf_op jit(solution)/shard_map/ppermute | solution.py:503
  526.9 49.0 %collective-permute-start.56 = (bf16[160,1536]{1,0:T(8,128)(2,1)S(1)}, bf16[160,1536]{1,0:T(8,128)(2,1)S(1)}, u32[]{:S(2)}, u32[]{:S(2)}) collective-permute-start(bf16[160,1536]{1,0:T(8,128)(2,1)S(1)} %convert_element_type.297), channel_id=1, source_target_pairs={{8,0},{24,16},{9,1},{25,17},{10,2},{26,18},{11,3},{27,19},{12,4},{... | collective-permute-start | bytes 1474568 | tf_op jit(solution)/shard_map/ppermute | solution.py:499
  635.6 96.5 %reduce-scatter.13.cloned.1.call-start = ((), (), s32[]{:S(2)}) async-start(), calls=%async_computation.11 | async-start | bytes 2048000
  637.2 34.4 %collective-permute-start.62 = (bf16[320,1536]{1,0:T(8,128)(2,1)S(1)}, bf16[320,1536]{1,0:T(8,128)(2,1)S(1)}, u32[]{:S(2)}, u32[]{:S(2)}) collective-permute-start(bf16[320,1536]{1,0:T(8,128)(2,1)S(1)} %broadcast_select_fusion.5), channel_id=1, source_target_pairs={{0,4},{4,0},{1,5},{5,1},{2,6},{6,2},{3,7},{7,3},{8,12},{12,8},{9,1... | collective-permute-start | bytes 2949128 | tf_op jit(solution)/shard_map/ppermute | solution.py:503
  640.7 30.9 %collective-permute-start.61 = (bf16[96,2560]{1,0:T(8,128)(2,1)S(1)}, bf16[96,2560]{1,0:T(8,128)(2,1)S(1)}, u32[]{:S(2)}, u32[]{:S(2)}) collective-permute-start(bf16[96,2560]{1,0:T(8,128)(2,1)S(1)} %get-tuple-element.245), channel_id=1, source_target_pairs={{0,4},{4,0},{1,5},{5,1},{2,6},{6,2},{3,7},{7,3},{8,12},{12,8},{9,1... | collective-permute-start | bytes 1474568 | tf_op jit(solution)/shard_map/ppermute | solution.py:503
  641.0 30.6 %collective-permute-start.60 = (bf16[96,2560]{1,0:T(8,128)(2,1)S(1)}, bf16[96,2560]{1,0:T(8,128)(2,1)S(1)}, u32[]{:S(2)}, u32[]{:S(2)}) collective-permute-start(bf16[96,2560]{1,0:T(8,128)(2,1)S(1)} %get-tuple-element.246), channel_id=1, source_target_pairs={{0,2},{2,0},{1,3},{3,1},{4,6},{6,4},{5,7},{7,5},{8,10},{10,8},{9,1... | collective-permute-start | bytes 1474568 | tf_op jit(solution)/shard_map/ppermute | solution.py:503
  674.1 25.8 %collective-permute-start.63 = (bf16[192,2560]{1,0:T(8,128)(2,1)}, bf16[192,2560]{1,0:T(8,128)(2,1)}, u32[]{:S(2)}, u32[]{:S(2)}) collective-permute-start(bf16[192,2560]{1,0:T(8,128)(2,1)} %pad_maximum_fusion.8), channel_id=1, source_target_pairs={{0,2},{2,0},{1,3},{3,1},{4,6},{6,4},{5,7},{7,5},{8,10},{10,8},{9,1... | collective-permute-start | bytes 2949128 | tf_op jit(solution)/shard_map/ppermute | solution.py:503
  676.6 23.3 %collective-permute-start.64 = (bf16[192,2560]{1,0:T(8,128)(2,1)}, bf16[192,2560]{1,0:T(8,128)(2,1)}, u32[]{:S(2)}, u32[]{:S(2)}) collective-permute-start(bf16[192,2560]{1,0:T(8,128)(2,1)} %pad_maximum_fusion.9), channel_id=1, source_target_pairs={{0,4},{4,0},{1,5},{5,1},{2,6},{6,2},{3,7},{7,3},{8,12},{12,8},{9,1... | collective-permute-start | bytes 2949128 | tf_op jit(solution)/shard_map/ppermute | solution.py:503
  (126 other events, 1129.7 us)
Sparse Core Ops, SparseCore 0:
  10.2 40.8 all-gather.6
  53.2 53.6 all-gather.4
  108.5 113.8 all-gather.10
  224.4 143.0 all-gather.8
  369.7 103.5 reduce-scatter.6
  475.5 147.2 reduce-scatter.8
  635.7 50.2 reduce-scatter.10
  699.4 32.6 reduce-scatter.12

commit v5 on v4

--- a/solution.py
+++ b/solution.py
@@ -786,11 +786,12 @@
     branch_two = plane_step_two(*branch_one)
     out_total = added_pair(out_mine, out_got)
     grad_branch = plane_join(branch_own, *branch_one, *branch_two)
-    grad_branch, out_total, sums[0] = together(grad_branch, out_total, sums[0])
+    owned = [Unshare(tied(sums[0], *branch_two), first_y)]
+    grad_branch, out_total = together(grad_branch, out_total)
 
     grad_attended = narrow(grad_branch, full_o)
     grad_cols = to_columns(grad_attended, index, cos_tab, sin_tab, 0, GROUP)
-    grad_cols, out_total, sums[0] = together(grad_cols, out_total, sums[0])
+    grad_cols, out_total = landed((grad_cols, out_total), (owned[0], "got"))
     out_sends = [
         over(out_total[own : 2 * own], "x"),
         over(out_total[2 * own : 3 * own], "y"),
@@ -809,16 +810,15 @@
             )
             for d in range(1, reach + 1)
         ]
+    out_term = weight_grads(grad_branch, tied(attended, *prior))
+    kv_own, out_term = together(kv_own, out_term)
     dq_cols, dkv_cols = back(
         kv_own, starts, own_bounds, (own_key, own_key), out_cols, logs, grad_cols, prior
     )
     dkv_cols, out_sends, far_got = lax.optimization_barrier((dkv_cols, out_sends, far_got))
     output = (x_mid + added(out_total, *out_sends)).astype(WIDE)
-    owned = [Unshare(tied(sums[0], dkv_cols), first_y)]
     dkv_own = sum((part.astype(F32) for part in far_got), dkv_cols)
-    out_term = weight_grads(grad_branch, tied(attended, dkv_cols))
-    dkv_own, out_term = landed((dkv_own, out_term), (owned[0], "got"))
-    out_term = spread_sum(out_term, w_o.shape[0], first_y)
+    out_term = spread_sum(tied(out_term, dkv_cols), w_o.shape[0], first_y)
     grad_qkv = to_rows(
         jnp.concatenate([dq_cols, dkv_own], axis=0),
         index,

time: 750 us -> 743 us (level)
  waiting for transfers between devices: 287 us -> 278 us
    unnamed x170 -> x160, local copies, waits for them, and re-layouts: 24.6 us -> 21.1 us
  transfers between devices with their start and end apart: 76 -> 76, of which waited for: 34 -> 32; matrix products, arithmetic and copies ran while one was open for 16% -> 17% of each run, Pallas kernels for 32% -> 33%
where the time goes in v5:
time: 743 us; the launch traced here: 737 us
  waiting for transfers between devices  278 us (37%)
  Pallas kernels  240 us (32%)
  other arithmetic  74.1 us (10%)
  starting transfers between devices  56.8 us (8%)
  local copies, waits for them, and re-layouts  55.8 us (8%)
  between operations  15.9 us (2%)
  matrix products  15.6 us (2%)
    ppermute x62, waiting for transfers between devices, over(): return lax.ppermute(block, axis, SWAP)  210 us
    pallas_call x4, Pallas kernels, hidden_units(): pl.pallas_call(functools.partial(units_kernel, bool(prior)), grid=(count...  75.5 us
    ppermute x62, starting transfers between devices, over(): return lax.ppermute(block, axis, SWAP)  49.3 us
    all_gather x4, waiting for transfers between devices, gather_z(): return lax.all_gather(block, 'z', axis=0, tiled=True)  38.3 us
    pallas_call x2, Pallas kernels, attend_back(): pl.pallas_call(functools.partial(attend_back_kernel, places), grid_spec=p...  36.3 us
    pallas_call x2, Pallas kernels, unit_grads(): pl.pallas_call(unit_grads_kernel, grid=(model // rows,), in_specs=[pl.Blo...  34 us
    pallas_call x2, Pallas kernels, attend(): pl.pallas_call(functools.partial(attend_kernel, places), grid_spec=pltpu....  28.8 us
    pallas_call x4, Pallas kernels, join(): pl.pallas_call(join_kernel, in_specs=[ANY] * len(parts), out_specs=ANY, o...  24.6 us
  transfers between devices with their start and end apart: 76, of which 32 were waited for; matrix products, arithmetic and copies ran while one was open for 17% of the time, Pallas kernels for 33%

profile of v5, /device:TPU:0, one launch (start us, length us, event | category | flops | bytes accessed | tf_op | source)
XLA Modules:
  0.0 736.7 jit_solution(9902979611501034361)
XLA Ops:
  15.3 7.7 %collective-permute-done.1 = bf16[320,512]{1,0:T(8,128)(2,1)S(1)} collective-permute-done((bf16[320,512]{1,0:T(8,128)(2,1)S(1)}, bf16[320,512]{1,0:T(8,128)(2,1)S(1)}, u32[]{:S(2)}, u32[]{:S(2)}) %collective-permute-start.1) | collective-permute-done | bytes 327712 | tf_op jit(solution)/shard_map/ppermute | solution.py:503
  27.4 19.7 %collective-permute-done.refs_1_ = bf16[192,2560]{1,0:T(8,128)(2,1)S(1)} collective-permute-done((bf16[192,2560]{1,0:T(8,128)(2,1)S(1)}, bf16[192,2560]{1,0:T(8,128)(2,1)S(1)}, u32[]{:S(2)}, u32[]{:S(2)}) %collective-permute-start) | collective-permute-done | bytes 983072 | tf_op jit(solution)/shard_map/ppermute | solution.py:503
  65.2 5.8 shard_map.212.x_ref
  71.7 17.9 %collective-permute-done.13 = bf16[320,1152]{1,0:T(8,128)(2,1)S(1)} collective-permute-done((bf16[320,1152]{1,0:T(8,128)(2,1)S(1)}, bf16[320,1152]{1,0:T(8,128)(2,1)S(1)}, u32[]{:S(2)}, u32[]{:S(2)}) %collective-permute-start.13) | collective-permute-done | bytes 737312 | tf_op jit(solution)/shard_map/ppermute | solution.py:503
  109.5 9.6 %shard_map.213 = (bf16[1536,2560]{1,0:T(8,128)(2,1)}, f32[1536,512]{1,0:T(8,128)S(1)}) custom-call(bf16[1536,2560]{1,0:T(8,128)(2,1)} %shard_map.212.x_ref, f32[1,2560]{1,0:T(1,128)S(1)} %broadcast_in_dim_squeeze.2.gain_ref, bf16[2560,512]{1,0:T(8,128)(2,1)S(1)} %copy-done.11), custom_call_target="tpu_custom_call" | custom-call | flops 1000000 | bytes 100000 | tf_op jit(solution)/shard_map/pallas_call | solution.py:360
  133.7 27.2 %shard_map.215 = (f32[320,1536]{1,0:T(8,128)S(1)}, f32[8,1536]{1,0:T(8,128)S(1)}) custom-call(s32[4,6]{1,0:T(4,128)S(1)} %get-tuple-element.314.bounds_ref, bf16[320,1536]{1,0:T(8,128)(2,1)S(1)} %slice.424.q_ref, bf16[160,1536]{1,0:T(8,128)(2,1)S(1)} %slice.425.kv_ref, s32[1,1536]{1,0:T(1,128)S(1)} %broadcast_in_dim.2.start_ref), custom_call_target="tpu_custom_call" | custom-call | flops 1000000 | bytes 100000 | tf_op jit(solution)/shard_map/pallas_call | solution.py:177
  180.2 4.9 add_convert_fusion.3
  191.9 11.3 %collective-permute-done.22 = bf16[96,2560]{1,0:T(8,128)(2,1)S(1)} collective-permute-done((bf16[96,2560]{1,0:T(8,128)(2,1)S(1)}, bf16[96,2560]{1,0:T(8,128)(2,1)S(1)}, u32[]{:S(2)}, u32[]{:S(2)}) %collective-permute-start.22) | collective-permute-done | bytes 491552 | tf_op jit(solution)/shard_map/ppermute | solution.py:503
  206.2 19.7 %collective-permute-done.23 = bf16[192,2560]{1,0:T(8,128)(2,1)S(1)} collective-permute-done((bf16[192,2560]{1,0:T(8,128)(2,1)S(1)}, bf16[192,2560]{1,0:T(8,128)(2,1)S(1)}, u32[]{:S(2)}, u32[]{:S(2)}) %collective-permute-start.23) | collective-permute-done | bytes 983072 | tf_op jit(solution)/shard_map/ppermute | solution.py:503
  232.2 17.7 %collective-permute-done.25.refs_2_ = bf16[192,2560]{1,0:T(8,128)(2,1)S(1)} collective-permute-done((bf16[192,2560]{1,0:T(8,128)(2,1)S(1)}, bf16[192,2560]{1,0:T(8,128)(2,1)S(1)}, u32[]{:S(2)}, u32[]{:S(2)}) %collective-permute-start.25) | collective-permute-done | bytes 983072 | tf_op jit(solution)/shard_map/ppermute | solution.py:503
  254.3 10.5 %collective-permute-done.26.refs_3_ = bf16[96,2560]{1,0:T(8,128)(2,1)S(1)} collective-permute-done((bf16[96,2560]{1,0:T(8,128)(2,1)S(1)}, bf16[96,2560]{1,0:T(8,128)(2,1)S(1)}, u32[]{:S(2)}, u32[]{:S(2)}) %collective-permute-start.26) | collective-permute-done | bytes 491552 | tf_op jit(solution)/shard_map/ppermute | solution.py:503
  265.9 5.3 shard_map.219.cot_ref
  271.3 5.8 shard_map.218.h_ref
  277.1 17.8 %shard_map.221 = (bf16[768,1152]{1,0:T(8,128)(2,1)S(1)}, bf16[768,2560]{1,0:T(8,128)(2,1)S(1)}, bf16[768,2560]{1,0:T(8,128)(2,1)}) custom-call(bf16[1536,2560]{1,0:T(8,128)(2,1)} %shard_map.218.h_ref, bf16[1536,2560]{1,0:T(8,128)(2,1)} %shard_map.219.cot_ref, bf16[2560,1152]{1,0:T(8,128)(2,1)} %all-gather.11.cloned.1.call-done.weight_ref), custom_call_target="tpu_custom_call" | custom-call | flops 1000000 | bytes 100000 | tf_op jit(solution)/shard_map/pallas_call | solution.py:430
  296.8 17.8 %shard_map.220 = (bf16[768,1152]{1,0:T(8,128)(2,1)S(1)}, bf16[768,2560]{1,0:T(8,128)(2,1)S(1)}, bf16[768,2560]{1,0:T(8,128)(2,1)}) custom-call(bf16[1536,2560]{1,0:T(8,128)(2,1)} %shard_map.218.h_ref, bf16[1536,2560]{1,0:T(8,128)(2,1)} %shard_map.219.cot_ref, bf16[2560,1152]{1,0:T(8,128)(2,1)} %all-gather.11.cloned.1.call-done.weight_ref), custom_call_target="tpu_custom_call" | custom-call | flops 1000000 | bytes 100000 | tf_op jit(solution)/shard_map/pallas_call | solution.py:430
  316.6 16.3 %shard_map.222 = bf16[2560,1152]{1,0:T(8,128)(2,1)} custom-call(bf16[1536,2560]{1,0:T(8,128)(2,1)} %shard_map.218.h_ref, bf16[1536,2560]{1,0:T(8,128)(2,1)} %shard_map.219.cot_ref, bf16[768,1152]{1,0:T(8,128)(2,1)S(1)} %get-tuple-element.114.mine_ref, bf16[768,1152]{1,0:T(8,128)(2,1)S(1)} %get-tuple-element.111.other_ref), custom_call_target="tpu_custom_call" | custom-call | flops 1000000 | bytes 100000 | tf_op jit(solution)/shard_map/pallas_call | solution.py:455
  332.8 34.7 %all-gather.9.cloned.1.call-done.weight_ref = bf16[2560,1536]{1,0:T(8,128)(2,1)} async-done(((bf16[640,1536]{1,0:T(8,128)(2,1)}), bf16[2560,1536]{1,0:T(8,128)(2,1)}) %all-gather.9.cloned.1.call-update) | async-done | bytes 7864336 | tf_op jit(solution)/shard_map/all_gather | solution.py:622
  367.6 19.9 %shard_map.224 = (bf16[768,1536]{1,0:T(8,128)(2,1)S(1)}, bf16[768,2560]{1,0:T(8,128)(2,1)}, bf16[768,2560]{1,0:T(8,128)(2,1)}) custom-call(bf16[1536,2560]{1,0:T(8,128)(2,1)} %shard_map.218.h_ref, bf16[1536,2560]{1,0:T(8,128)(2,1)} %shard_map.219.cot_ref, bf16[2560,1536]{1,0:T(8,128)(2,1)} %all-gather.9.cloned.1.call-done.weight_ref, ...), custom_call_target="tpu_custom_call" | custom-call | flops 1000000 | bytes 100000 | tf_op jit(solution)/shard_map/pallas_call | solution.py:430
  387.5 20.0 %shard_map.223 = (bf16[768,1536]{1,0:T(8,128)(2,1)S(1)}, bf16[768,2560]{1,0:T(8,128)(2,1)}, bf16[768,2560]{1,0:T(8,128)(2,1)}) custom-call(bf16[1536,2560]{1,0:T(8,128)(2,1)} %shard_map.218.h_ref, bf16[1536,2560]{1,0:T(8,128)(2,1)} %shard_map.219.cot_ref, bf16[2560,1536]{1,0:T(8,128)(2,1)} %all-gather.9.cloned.1.call-done.weight_ref, ...), custom_call_target="tpu_custom_call" | custom-call | flops 1000000 | bytes 100000 | tf_op jit(solution)/shard_map/pallas_call | solution.py:430
  413.9 10.7 %collective-permute-done.41 = bf16[96,2560]{1,0:T(8,128)(2,1)S(1)} collective-permute-done((bf16[96,2560]{1,0:T(8,128)(2,1)S(1)}, bf16[96,2560]{1,0:T(8,128)(2,1)S(1)}, u32[]{:S(2)}, u32[]{:S(2)}) %collective-permute-start.41) | collective-permute-done | bytes 491552 | tf_op jit(solution)/shard_map/ppermute | solution.py:503
  430.0 17.7 %shard_map.225 = bf16[2560,1536]{1,0:T(8,128)(2,1)} custom-call(bf16[1536,2560]{1,0:T(8,128)(2,1)} %shard_map.218.h_ref, bf16[1536,2560]{1,0:T(8,128)(2,1)} %shard_map.219.cot_ref, bf16[768,1536]{1,0:T(8,128)(2,1)S(1)} %get-tuple-element.124.mine_ref, bf16[768,1536]{1,0:T(8,128)(2,1)S(1)} %get-tuple-element.125.other_ref), custom_call_target="tpu_custom_call" | custom-call | flops 1000000 | bytes 100000 | tf_op jit(solution)/shard_map/pallas_call | solution.py:455
  462.9 21.4 %collective-permute-done.44.refs_2_ = bf16[192,2560]{1,0:T(8,128)(2,1)} collective-permute-done((bf16[192,2560]{1,0:T(8,128)(2,1)}, bf16[192,2560]{1,0:T(8,128)(2,1)}, u32[]{:S(2)}, u32[]{:S(2)}) %collective-permute-start.44) | collective-permute-done | bytes 983072 | tf_op jit(solution)/shard_map/ppermute | solution.py:503
  490.0 8.2 %collective-permute-done.45.refs_3_ = bf16[96,2560]{1,0:T(8,128)(2,1)} collective-permute-done((bf16[96,2560]{1,0:T(8,128)(2,1)S(1)}, bf16[96,2560]{1,0:T(8,128)(2,1)}, u32[]{:S(2)}, u32[]{:S(2)}) %collective-permute-start.45) | collective-permute-done | bytes 491552 | tf_op jit(solution)/shard_map/ppermute | solution.py:503
  508.6 7.7 %shard_map.226.a_ref = bf16[1536,2560]{1,0:T(8,128)(2,1)} custom-call(bf16[192,2560]{1,0:T(8,128)(2,1)} %get-tuple-element.234.refs_0_, bf16[192,2560]{1,0:T(8,128)(2,1)} %collective-permute-done.43.refs_1_, bf16[192,2560]{1,0:T(8,128)(2,1)} %collective-permute-done.44.refs_2_, bf16[96,2560]{1,0:T(8,128)(2,1)} %collective-permute-done.45.refs_3_, ...), custom_call_target="tpu_custom_call" | custom-call | flops 1000000 | bytes 100000 | tf_op jit(solution)/shard_map/pallas_call | solution.py:335
  516.3 7.6 %shard_map.227.rows_ref = bf16[1536,320]{1,0:T(8,128)(2,1)S(1)} custom-call(bf16[1536,2560]{1,0:T(8,128)(2,1)} %shard_map.226.a_ref, bf16[2560,320]{1,0:T(8,128)(2,1)S(1)} %bitcast.47), custom_call_target="tpu_custom_call" | custom-call | flops 1000000 | bytes 100000 | tf_op jit(solution)/shard_map/pallas_call | solution.py:391
  536.4 9.7 %shard_map.230 = bf16[2560,320]{1,0:T(8,128)(2,1)S(1)} custom-call(bf16[1536,2560]{1,0:T(8,128)(2,1)} %shard_map.226.a_ref, bf16[1536,320]{1,0:T(8,128)(2,1)S(1)} %copy-done.8), custom_call_target="tpu_custom_call" | custom-call | flops 1000000 | bytes 100000 | tf_op jit(solution)/shard_map/pallas_call | solution.py:473
  546.1 31.5 %shard_map.231 = (f32[320,1536]{1,0:T(8,128)}, f32[160,1536]{1,0:T(8,128)S(1)}) custom-call(s32[4,6]{1,0:T(4,128)S(1)} %get-tuple-element.314.bounds_ref, bf16[320,1536]{1,0:T(8,128)(2,1)S(1)} %slice.424.q_ref, bf16[160,1536]{1,0:T(8,128)(2,1)S(1)} %copy-done.10, s32[1,1536]{1,0:T(1,128)S(1)} %broadcast_in_dim.2.start_ref, ...), custom_call_target="tpu_custom_call" | custom-call | flops 1000000 | bytes 100000 | tf_op jit(solution)/shard_map/pallas_call | solution.py:268
  577.6 9.4 %collective-permute-done.57 = bf16[160,1536]{1,0:T(8,128)(2,1)S(1)} collective-permute-done((bf16[160,1536]{1,0:T(8,128)(2,1)S(1)}, bf16[160,1536]{1,0:T(8,128)(2,1)S(1)}, u32[]{:S(2)}, u32[]{:S(2)}) %collective-permute-start.57) | collective-permute-done | bytes 491552 | tf_op jit(solution)/shard_map/ppermute | solution.py:499
  596.3 9.6 %shard_map.233 = bf16[2560,512]{1,0:T(8,128)(2,1)S(1)} custom-call(bf16[1536,2560]{1,0:T(8,128)(2,1)} %get-tuple-element.148.a_ref, bf16[1536,512]{1,0:T(8,128)(2,1)S(1)} %shard_map.232.b_ref), custom_call_target="tpu_custom_call" | custom-call | flops 1000000 | bytes 100000 | tf_op jit(solution)/shard_map/pallas_call | solution.py:473
  607.4 5.0 collective-permute-done.58
  637.7 27.7 %collective-permute-done.61 = bf16[96,2560]{1,0:T(8,128)(2,1)S(1)} collective-permute-done((bf16[96,2560]{1,0:T(8,128)(2,1)S(1)}, bf16[96,2560]{1,0:T(8,128)(2,1)S(1)}, u32[]{:S(2)}, u32[]{:S(2)}) %collective-permute-start.61) | collective-permute-done | bytes 491552 | tf_op jit(solution)/shard_map/ppermute | solution.py:503
  705.1 20.7 %reduce-scatter.13.cloned.1.call-done = bf16[320,640]{1,0:T(8,128)(2,1)} async-done(((bf16[1280,640]{1,0:T(8,128)(2,1)}), bf16[320,640]{1,0:T(8,128)(2,1)}) %reduce-scatter.13.cloned.1.call-update) | async-done | bytes 409616
  (444 shorter events, 244.3 us)
Async XLA Ops:
  7.2 91.6 %all-gather.7.cloned.1.call-start = ((), (), s32[]{:S(2)}) async-start(), calls=%async_computation.5 | async-start | bytes 2048000 | tf_op jit(solution)/shard_map/all_gather | solution.py:622
  9.3 97.6 %all-gather.5.cloned.1.call-start = ((), (), s32[]{:S(2)}) async-start(), calls=%async_computation.4 | async-start | bytes 3276800 | tf_op jit(solution)/shard_map/all_gather | solution.py:622
  24.1 253.0 %all-gather.11.cloned.1.call-start = ((), (), s32[]{:S(2)}) async-start(), calls=%async_computation.7 | async-start | bytes 7372800 | tf_op jit(solution)/shard_map/all_gather | solution.py:622
  24.1 23.0 %collective-permute-start = (bf16[192,2560]{1,0:T(8,128)(2,1)S(1)}, bf16[192,2560]{1,0:T(8,128)(2,1)S(1)}, u32[]{:S(2)}, u32[]{:S(2)}) collective-permute-start(bf16[192,2560]{1,0:T(8,128)(2,1)S(1)} %copy-done), channel_id=1, source_target_pairs={{0,2},{2,0},{1,3},{3,1},{4,6},{6,4},{5,7},{7,5},{8,10},{10,8},{9,1... | collective-permute-start | bytes 2949128 | tf_op jit(solution)/shard_map/ppermute | solution.py:503
  25.9 22.8 %collective-permute-start.2 = (bf16[192,2560]{1,0:T(8,128)(2,1)S(1)}, bf16[192,2560]{1,0:T(8,128)(2,1)S(1)}, u32[]{:S(2)}, u32[]{:S(2)}) collective-permute-start(bf16[192,2560]{1,0:T(8,128)(2,1)S(1)} %copy-done), channel_id=1, source_target_pairs={{0,4},{4,0},{1,5},{5,1},{2,6},{6,2},{3,7},{7,3},{8,12},{12,8},{9,1... | collective-permute-start | bytes 2949128 | tf_op jit(solution)/shard_map/ppermute | solution.py:503
  27.4 35.3 %collective-permute-start.5 = (bf16[192,2560]{1,0:T(8,128)(2,1)S(1)}, bf16[192,2560]{1,0:T(8,128)(2,1)S(1)}, u32[]{:S(2)}, u32[]{:S(2)}) collective-permute-start(bf16[192,2560]{1,0:T(8,128)(2,1)S(1)} %copy-done), channel_id=1, source_target_pairs={{0,1},{1,0},{2,3},{3,2},{4,5},{5,4},{6,7},{7,6},{8,9},{9,8},{10,11... | collective-permute-start | bytes 2949128 | tf_op jit(solution)/shard_map/ppermute | solution.py:503
  91.3 276.2 %all-gather.9.cloned.1.call-start = ((), (), s32[]{:S(2)}) async-start(), calls=%async_computation.6 | async-start | bytes 9830400 | tf_op jit(solution)/shard_map/all_gather | solution.py:622
  101.9 23.8 %collective-permute-start.11 = (bf16[1280,320]{0,1:T(8,128)(2,1)}, bf16[1280,320]{0,1:T(8,128)(2,1)S(1)}, u32[]{:S(2)}, u32[]{:S(2)}) collective-permute-start(bf16[1280,320]{0,1:T(8,128)(2,1)} %copy.70), channel_id=1, source_target_pairs={{0,4},{4,0},{1,5},{5,1},{2,6},{6,2},{3,7},{7,3},{8,12},{12,8},{9,1... | collective-permute-start | bytes 2457608 | tf_op jit(solution)/shard_map/ppermute | solution.py:503
  119.1 45.2 %collective-permute-start.16 = (bf16[320,1536]{1,0:T(8,128)(2,1)}, bf16[320,1536]{1,0:T(8,128)(2,1)}, u32[]{:S(2)}, u32[]{:S(2)}) collective-permute-start(bf16[320,1536]{1,0:T(8,128)(2,1)} %broadcast_select_fusion.8), channel_id=1, source_target_pairs={{0,4},{4,0},{1,5},{5,1},{2,6},{6,2},{3,7},{7,3},{8,12},{12,8},{9,1... | collective-permute-start | bytes 2949128 | tf_op jit(solution)/shard_map/ppermute | solution.py:503
  124.1 36.9 %collective-permute-start.12 = (bf16[160,1536]{1,0:T(8,128)(2,1)S(1)}, bf16[160,1536]{1,0:T(8,128)(2,1)S(1)}, u32[]{:S(2)}, u32[]{:S(2)}) collective-permute-start(bf16[160,1536]{1,0:T(8,128)(2,1)S(1)} %slice.425.kv_ref), channel_id=1, source_target_pairs={{0,8},{16,24},{1,9},{17,25},{2,10},{18,26},{3,11},{19,27},{4,12},{... | collective-permute-start | bytes 1474568 | tf_op jit(solution)/shard_map/ppermute | solution.py:499
  125.8 41.6 %collective-permute-start.15 = (bf16[192,2560]{1,0:T(8,128)(2,1)}, bf16[192,2560]{1,0:T(8,128)(2,1)}, u32[]{:S(2)}, u32[]{:S(2)}) collective-permute-start(bf16[192,2560]{1,0:T(8,128)(2,1)} %refs_0_.3), channel_id=1, source_target_pairs={{0,4},{4,0},{1,5},{5,1},{2,6},{6,2},{3,7},{7,3},{8,12},{12,8},{9,1... | collective-permute-start | bytes 2949128 | tf_op jit(solution)/shard_map/ppermute | solution.py:503
  126.7 40.7 %collective-permute-start.14 = (bf16[192,2560]{1,0:T(8,128)(2,1)}, bf16[192,2560]{1,0:T(8,128)(2,1)}, u32[]{:S(2)}, u32[]{:S(2)}) collective-permute-start(bf16[192,2560]{1,0:T(8,128)(2,1)} %refs_0_.3), channel_id=1, source_target_pairs={{0,2},{2,0},{1,3},{3,1},{4,6},{6,4},{5,7},{7,5},{8,10},{10,8},{9,1... | collective-permute-start | bytes 2949128 | tf_op jit(solution)/shard_map/ppermute | solution.py:503
  173.1 327.4 %reduce-scatter.7.cloned.1.call-start = ((), (), s32[]{:S(2)}) async-start(), calls=%async_computation.8 | async-start | bytes 7372800 | tf_op jit(solution)/shard_map/reduce_scatter | solution.py:626
  203.7 22.2 %collective-permute-start.23 = (bf16[192,2560]{1,0:T(8,128)(2,1)S(1)}, bf16[192,2560]{1,0:T(8,128)(2,1)S(1)}, u32[]{:S(2)}, u32[]{:S(2)}) collective-permute-start(bf16[192,2560]{1,0:T(8,128)(2,1)S(1)} %pad_maximum_fusion.5), channel_id=1, source_target_pairs={{0,4},{4,0},{1,5},{5,1},{2,6},{6,2},{3,7},{7,3},{8,12},{12,8},{9,1... | collective-permute-start | bytes 2949128 | tf_op jit(solution)/shard_map/ppermute | solution.py:503
  367.5 261.7 %reduce-scatter.9.cloned.1.call-start = ((), (), s32[]{:S(2)}) async-start(), calls=%async_computation.9 | async-start | bytes 9830400 | tf_op jit(solution)/shard_map/reduce_scatter | solution.py:626
  427.0 23.5 %collective-permute-start.40 = (bf16[192,2560]{1,0:T(8,128)(2,1)}, bf16[192,2560]{1,0:T(8,128)(2,1)}, u32[]{:S(2)}, u32[]{:S(2)}) collective-permute-start(bf16[192,2560]{1,0:T(8,128)(2,1)} %pad_maximum_fusion.6), channel_id=1, source_target_pairs={{0,2},{2,0},{1,3},{3,1},{4,6},{6,4},{5,7},{7,5},{8,10},{10,8},{9,1... | collective-permute-start | bytes 2949128 | tf_op jit(solution)/shard_map/ppermute | solution.py:503
  428.5 23.2 %collective-permute-start.42 = (bf16[192,2560]{1,0:T(8,128)(2,1)}, bf16[192,2560]{1,0:T(8,128)(2,1)}, u32[]{:S(2)}, u32[]{:S(2)}) collective-permute-start(bf16[192,2560]{1,0:T(8,128)(2,1)} %pad_maximum_fusion.7), channel_id=1, source_target_pairs={{0,4},{4,0},{1,5},{5,1},{2,6},{6,2},{3,7},{7,3},{8,12},{12,8},{9,1... | collective-permute-start | bytes 2949128 | tf_op jit(solution)/shard_map/ppermute | solution.py:503
  451.8 236.3 %reduce-scatter.11.cloned.1.call-start = ((), (), s32[]{:S(2)}) async-start(), calls=%async_computation.10 | async-start | bytes 3276800 | tf_op jit(solution)/shard_map/reduce_scatter | solution.py:626
  452.1 49.9 %collective-permute-start.52 = (bf16[768,2560]{1,0:T(8,128)(2,1)}, bf16[768,2560]{1,0:T(8,128)(2,1)}, u32[]{:S(2)}, u32[]{:S(2)}) collective-permute-start(bf16[768,2560]{1,0:T(8,128)(2,1)} %get-tuple-element.129), channel_id=1, source_target_pairs={{0,1},{1,0},{2,3},{3,2},{4,5},{5,4},{6,7},{7,6},{8,9},{9,8},{10,11... | collective-permute-start | bytes 11796488 | tf_op jit(solution)/shard_map/ppermute | solution.py:503
  460.0 24.3 %collective-permute-start.44 = (bf16[192,2560]{1,0:T(8,128)(2,1)}, bf16[192,2560]{1,0:T(8,128)(2,1)}, u32[]{:S(2)}, u32[]{:S(2)}) collective-permute-start(bf16[192,2560]{1,0:T(8,128)(2,1)} %get-tuple-element.234.refs_0_), channel_id=1, source_target_pairs={{0,4},{4,0},{1,5},{5,1},{2,6},{6,2},{3,7},{7,3},{8,12},{12,8},{9,1... | collective-permute-start | bytes 2949128 | tf_op jit(solution)/shard_map/ppermute | solution.py:503
  461.5 25.4 %collective-permute-start.43 = (bf16[192,2560]{1,0:T(8,128)(2,1)}, bf16[192,2560]{1,0:T(8,128)(2,1)}, u32[]{:S(2)}, u32[]{:S(2)}) collective-permute-start(bf16[192,2560]{1,0:T(8,128)(2,1)} %get-tuple-element.234.refs_0_), channel_id=1, source_target_pairs={{0,2},{2,0},{1,3},{3,1},{4,6},{6,4},{5,7},{7,5},{8,10},{10,8},{9,1... | collective-permute-start | bytes 2949128 | tf_op jit(solution)/shard_map/ppermute | solution.py:503
  502.5 22.3 %collective-permute-start.53 = (bf16[320,1152]{1,0:T(8,128)(2,1)S(1)}, bf16[320,1152]{1,0:T(8,128)(2,1)}, u32[]{:S(2)}, u32[]{:S(2)}) collective-permute-start(bf16[320,1152]{1,0:T(8,128)(2,1)S(1)} %broadcast_select_fusion.17), channel_id=1, source_target_pairs={{0,4},{4,0},{1,5},{5,1},{2,6},{6,2},{3,7},{7,3},{8,12},{12,8},{9,1... | collective-permute-start | bytes 2211848 | tf_op jit(solution)/shard_map/ppermute | solution.py:503
  526.3 60.7 %collective-permute-start.56 = (bf16[192,2560]{1,0:T(8,128)(2,1)}, bf16[192,2560]{1,0:T(8,128)(2,1)S(1)}, u32[]{:S(2)}, u32[]{:S(2)}) collective-permute-start(bf16[192,2560]{1,0:T(8,128)(2,1)} %get-tuple-element.246), channel_id=1, source_target_pairs={{0,6},{2,4},{4,2},{6,0},{1,7},{3,5},{5,3},{7,1},{8,14},{10,12},{12... | collective-permute-start | bytes 2949128 | tf_op jit(solution)/shard_map/ppermute | solution.py:507
  526.7 60.3 %collective-permute-start.55 = (bf16[192,2560]{1,0:T(8,128)(2,1)}, bf16[192,2560]{1,0:T(8,128)(2,1)S(1)}, u32[]{:S(2)}, u32[]{:S(2)}) collective-permute-start(bf16[192,2560]{1,0:T(8,128)(2,1)} %get-tuple-element.247), channel_id=1, source_target_pairs={{0,4},{4,0},{1,5},{5,1},{2,6},{6,2},{3,7},{7,3},{8,12},{12,8},{9,1... | collective-permute-start | bytes 2949128 | tf_op jit(solution)/shard_map/ppermute | solution.py:503
  528.2 58.8 %collective-permute-start.54 = (bf16[192,2560]{1,0:T(8,128)(2,1)S(1)}, bf16[192,2560]{1,0:T(8,128)(2,1)S(1)}, u32[]{:S(2)}, u32[]{:S(2)}) collective-permute-start(bf16[192,2560]{1,0:T(8,128)(2,1)S(1)} %get-tuple-element.248), channel_id=1, source_target_pairs={{0,2},{2,0},{1,3},{3,1},{4,6},{6,4},{5,7},{7,5},{8,10},{10,8},{9,1... | collective-permute-start | bytes 2949128 | tf_op jit(solution)/shard_map/ppermute | solution.py:503
  534.7 52.3 %collective-permute-start.57 = (bf16[160,1536]{1,0:T(8,128)(2,1)S(1)}, bf16[160,1536]{1,0:T(8,128)(2,1)S(1)}, u32[]{:S(2)}, u32[]{:S(2)}) collective-permute-start(bf16[160,1536]{1,0:T(8,128)(2,1)S(1)} %convert_element_type.297), channel_id=1, source_target_pairs={{8,0},{24,16},{9,1},{25,17},{10,2},{26,18},{11,3},{27,19},{12,4},{... | collective-permute-start | bytes 1474568 | tf_op jit(solution)/shard_map/ppermute | solution.py:499
  629.3 96.5 %reduce-scatter.13.cloned.1.call-start = ((), (), s32[]{:S(2)}) async-start(), calls=%async_computation.11 | async-start | bytes 2048000
  631.0 34.4 %collective-permute-start.62 = (bf16[320,1536]{1,0:T(8,128)(2,1)S(1)}, bf16[320,1536]{1,0:T(8,128)(2,1)S(1)}, u32[]{:S(2)}, u32[]{:S(2)}) collective-permute-start(bf16[320,1536]{1,0:T(8,128)(2,1)S(1)} %broadcast_select_fusion.5), channel_id=1, source_target_pairs={{0,4},{4,0},{1,5},{5,1},{2,6},{6,2},{3,7},{7,3},{8,12},{12,8},{9,1... | collective-permute-start | bytes 2949128 | tf_op jit(solution)/shard_map/ppermute | solution.py:503
  633.5 31.9 %collective-permute-start.61 = (bf16[96,2560]{1,0:T(8,128)(2,1)S(1)}, bf16[96,2560]{1,0:T(8,128)(2,1)S(1)}, u32[]{:S(2)}, u32[]{:S(2)}) collective-permute-start(bf16[96,2560]{1,0:T(8,128)(2,1)S(1)} %get-tuple-element.243), channel_id=1, source_target_pairs={{0,4},{4,0},{1,5},{5,1},{2,6},{6,2},{3,7},{7,3},{8,12},{12,8},{9,1... | collective-permute-start | bytes 1474568 | tf_op jit(solution)/shard_map/ppermute | solution.py:503
  634.9 30.5 %collective-permute-start.60 = (bf16[96,2560]{1,0:T(8,128)(2,1)S(1)}, bf16[96,2560]{1,0:T(8,128)(2,1)S(1)}, u32[]{:S(2)}, u32[]{:S(2)}) collective-permute-start(bf16[96,2560]{1,0:T(8,128)(2,1)S(1)} %get-tuple-element.244), channel_id=1, source_target_pairs={{0,2},{2,0},{1,3},{3,1},{4,6},{6,4},{5,7},{7,5},{8,10},{10,8},{9,1... | collective-permute-start | bytes 1474568 | tf_op jit(solution)/shard_map/ppermute | solution.py:503
  667.8 24.4 %collective-permute-start.63 = (bf16[192,2560]{1,0:T(8,128)(2,1)}, bf16[192,2560]{1,0:T(8,128)(2,1)}, u32[]{:S(2)}, u32[]{:S(2)}) collective-permute-start(bf16[192,2560]{1,0:T(8,128)(2,1)} %pad_maximum_fusion.8), channel_id=1, source_target_pairs={{0,2},{2,0},{1,3},{3,1},{4,6},{6,4},{5,7},{7,5},{8,10},{10,8},{9,1... | collective-permute-start | bytes 2949128 | tf_op jit(solution)/shard_map/ppermute | solution.py:503
  668.8 23.4 %collective-permute-start.64 = (bf16[192,2560]{1,0:T(8,128)(2,1)}, bf16[192,2560]{1,0:T(8,128)(2,1)}, u32[]{:S(2)}, u32[]{:S(2)}) collective-permute-start(bf16[192,2560]{1,0:T(8,128)(2,1)} %pad_maximum_fusion.9), channel_id=1, source_target_pairs={{0,4},{4,0},{1,5},{5,1},{2,6},{6,2},{3,7},{7,3},{8,12},{12,8},{9,1... | collective-permute-start | bytes 2949128 | tf_op jit(solution)/shard_map/ppermute | solution.py:503
  (121 other events, 1046.2 us)
Sparse Core Ops, SparseCore 0:
  10.2 40.8 all-gather.6
  53.2 53.6 all-gather.4
  108.5 113.8 all-gather.10
  224.4 143.0 all-gather.8
  369.7 102.5 reduce-scatter.6
  474.5 147.2 reduce-scatter.8
  629.4 48.1 reduce-scatter.10
  690.5 35.2 reduce-scatter.12

commit v6 on v5

--- a/solution.py
+++ b/solution.py
@@ -463,6 +463,19 @@
     )(h_two, cot, mine, other)
 
 
+def as_f32_kernel(a_ref, out_ref):
+    out_ref[...] = a_ref[...].astype(F32)
+
+
+def as_f32(a):
+    return pl.pallas_call(
+        as_f32_kernel,
+        out_shape=jax.ShapeDtypeStruct(a.shape, F32),
+        compiler_params=pltpu.CompilerParams(vmem_limit_bytes=VMEM_BYTES // 2),
+        cost_estimate=pl.CostEstimate(flops=3 * 10**10, bytes_accessed=10**5, transcendentals=0),
+    )(a)
+
+
 def grads_kernel(a_ref, b_ref, out_ref):
     out_ref[...] = dot(a_ref[...], b_ref[...], 0, 0).astype(WIDE)
 
@@ -831,8 +844,8 @@
     qkv_part = weight_grads(h_one, grad_qkv)
     grad_qkv, qkv_part, out_term = together(grad_qkv, qkv_part, out_term)
     one_got = over(dot(grad_qkv[half:], full_a, 1, 1).astype(WIDE), "c")
+    qkv_part, sums[1], one_got = together(qkv_part, sums[1], one_got)
     one_total = (dot(grad_qkv[:half], full_a, 1, 1) + one_got.astype(F32)).astype(WIDE)
-    one_total, qkv_part, sums[1] = together(one_total, qkv_part, sums[1])
     qkv_grad = sum_z(qkv_part)
     owned.append(Unshare(sums[1], first_y))
     one_far = plane_sum_one(one_total)
@@ -876,9 +889,9 @@
         ]
     )
     gain_sums = gain_sums + lax.ppermute(gain_sums, "x", SWAP)
+    gain_sums = gain_sums + lax.ppermute(gain_sums, "c", SWAP)
     gain_sums, out_grad = together(gain_sums, out_grad)
-    gain_sums = gain_sums + lax.ppermute(gain_sums, "c", SWAP)
-    o_out = out_grad.T.astype(F32)
+    o_out = as_f32(out_grad).T
     gain_one_out = gain_sums[0] / gain_attn.astype(WIDE).astype(F32)
     gain_two_out = gain_sums[1] / gain_mlp.astype(WIDE).astype(F32)
     return (

time: 743 us -> 738 us (level)
    unnamed x9 -> x8, waiting for transfers between devices: 20.8 us -> 0.13 us
    reduce_scatter x3 -> x4, waiting for transfers between devices: 0.01 us -> 12 us  [sum_z(): lax.psum_scatter(block.astype(WIDE), 'z', scatter_dimension=0, tiled=True)]
  transfers between devices with their start and end apart: 76 -> 76, of which waited for: 32 -> 34; matrix products, arithmetic and copies ran while one was open for 17% -> 17% of each run, Pallas kernels for 33% -> 33%
where the time goes in v6:
time: 738 us; the launch traced here: 729 us
  waiting for transfers between devices  272 us (37%)
  Pallas kernels  241 us (33%)
  other arithmetic  74.2 us (10%)
  starting transfers between devices  57.6 us (8%)
  local copies, waits for them, and re-layouts  50.5 us (7%)
  matrix products  18.1 us (2%)
  between operations  15.9 us (2%)
    ppermute x62, waiting for transfers between devices, over(): return lax.ppermute(block, axis, SWAP)  210 us
    pallas_call x4, Pallas kernels, hidden_units(): pl.pallas_call(functools.partial(units_kernel, bool(prior)), grid=(count...  75.5 us
    ppermute x62, starting transfers between devices, over(): return lax.ppermute(block, axis, SWAP)  51.3 us
    all_gather x4, waiting for transfers between devices, gather_z(): return lax.all_gather(block, 'z', axis=0, tiled=True)  38.2 us
    pallas_call x2, Pallas kernels, attend_back(): pl.pallas_call(functools.partial(attend_back_kernel, places), grid_spec=p...  36.3 us
    pallas_call x2, Pallas kernels, unit_grads(): pl.pallas_call(unit_grads_kernel, grid=(model // rows,), in_specs=[pl.Blo...  34 us
    pallas_call x2, Pallas kernels, attend(): pl.pallas_call(functools.partial(attend_kernel, places), grid_spec=pltpu....  28.8 us
    pallas_call x4, Pallas kernels, join(): pl.pallas_call(join_kernel, in_specs=[ANY] * len(parts), out_specs=ANY, o...  24.7 us
  transfers between devices with their start and end apart: 76, of which 34 were waited for; matrix products, arithmetic and copies ran while one was open for 17% of the time, Pallas kernels for 33%

profile of v6, /device:TPU:0, one launch (start us, length us, event | category | flops | bytes accessed | tf_op | source)
XLA Modules:
  0.0 729.0 jit_solution(6012586802486675755)
XLA Ops:
  15.3 7.7 %collective-permute-done.1 = bf16[320,512]{1,0:T(8,128)(2,1)S(1)} collective-permute-done((bf16[320,512]{1,0:T(8,128)(2,1)S(1)}, bf16[320,512]{1,0:T(8,128)(2,1)S(1)}, u32[]{:S(2)}, u32[]{:S(2)}) %collective-permute-start.1) | collective-permute-done | bytes 327712 | tf_op jit(solution)/shard_map/ppermute | solution.py:516
  27.4 19.7 %collective-permute-done.refs_1_ = bf16[192,2560]{1,0:T(8,128)(2,1)S(1)} collective-permute-done((bf16[192,2560]{1,0:T(8,128)(2,1)S(1)}, bf16[192,2560]{1,0:T(8,128)(2,1)S(1)}, u32[]{:S(2)}, u32[]{:S(2)}) %collective-permute-start) | collective-permute-done | bytes 983072 | tf_op jit(solution)/shard_map/ppermute | solution.py:516
  65.2 5.8 shard_map.212.x_ref
  71.7 17.9 %collective-permute-done.13 = bf16[320,1152]{1,0:T(8,128)(2,1)S(1)} collective-permute-done((bf16[320,1152]{1,0:T(8,128)(2,1)S(1)}, bf16[320,1152]{1,0:T(8,128)(2,1)S(1)}, u32[]{:S(2)}, u32[]{:S(2)}) %collective-permute-start.13) | collective-permute-done | bytes 737312 | tf_op jit(solution)/shard_map/ppermute | solution.py:516
  109.5 9.6 %shard_map.213 = (bf16[1536,2560]{1,0:T(8,128)(2,1)}, f32[1536,512]{1,0:T(8,128)S(1)}) custom-call(bf16[1536,2560]{1,0:T(8,128)(2,1)} %shard_map.212.x_ref, f32[1,2560]{1,0:T(1,128)S(1)} %broadcast_in_dim_squeeze.2.gain_ref, bf16[2560,512]{1,0:T(8,128)(2,1)S(1)} %copy-done.11), custom_call_target="tpu_custom_call" | custom-call | flops 1000000 | bytes 100000 | tf_op jit(solution)/shard_map/pallas_call | solution.py:360
  133.7 27.2 %shard_map.215 = (f32[320,1536]{1,0:T(8,128)S(1)}, f32[8,1536]{1,0:T(8,128)S(1)}) custom-call(s32[4,6]{1,0:T(4,128)S(1)} %get-tuple-element.314.bounds_ref, bf16[320,1536]{1,0:T(8,128)(2,1)S(1)} %slice.424.q_ref, bf16[160,1536]{1,0:T(8,128)(2,1)S(1)} %slice.425.kv_ref, s32[1,1536]{1,0:T(1,128)S(1)} %broadcast_in_dim.2.start_ref), custom_call_target="tpu_custom_call" | custom-call | flops 1000000 | bytes 100000 | tf_op jit(solution)/shard_map/pallas_call | solution.py:177
  180.2 4.9 add_convert_fusion.3
  191.9 11.3 %collective-permute-done.22 = bf16[96,2560]{1,0:T(8,128)(2,1)S(1)} collective-permute-done((bf16[96,2560]{1,0:T(8,128)(2,1)S(1)}, bf16[96,2560]{1,0:T(8,128)(2,1)S(1)}, u32[]{:S(2)}, u32[]{:S(2)}) %collective-permute-start.22) | collective-permute-done | bytes 491552 | tf_op jit(solution)/shard_map/ppermute | solution.py:516
  206.2 19.7 %collective-permute-done.23 = bf16[192,2560]{1,0:T(8,128)(2,1)S(1)} collective-permute-done((bf16[192,2560]{1,0:T(8,128)(2,1)S(1)}, bf16[192,2560]{1,0:T(8,128)(2,1)S(1)}, u32[]{:S(2)}, u32[]{:S(2)}) %collective-permute-start.23) | collective-permute-done | bytes 983072 | tf_op jit(solution)/shard_map/ppermute | solution.py:516
  232.2 17.7 %collective-permute-done.25.refs_2_ = bf16[192,2560]{1,0:T(8,128)(2,1)S(1)} collective-permute-done((bf16[192,2560]{1,0:T(8,128)(2,1)S(1)}, bf16[192,2560]{1,0:T(8,128)(2,1)S(1)}, u32[]{:S(2)}, u32[]{:S(2)}) %collective-permute-start.25) | collective-permute-done | bytes 983072 | tf_op jit(solution)/shard_map/ppermute | solution.py:516
  254.3 10.5 %collective-permute-done.26.refs_3_ = bf16[96,2560]{1,0:T(8,128)(2,1)S(1)} collective-permute-done((bf16[96,2560]{1,0:T(8,128)(2,1)S(1)}, bf16[96,2560]{1,0:T(8,128)(2,1)S(1)}, u32[]{:S(2)}, u32[]{:S(2)}) %collective-permute-start.26) | collective-permute-done | bytes 491552 | tf_op jit(solution)/shard_map/ppermute | solution.py:516
  265.9 5.4 shard_map.219.cot_ref
  271.3 5.8 shard_map.218.h_ref
  277.1 17.8 %shard_map.221 = (bf16[768,1152]{1,0:T(8,128)(2,1)S(1)}, bf16[768,2560]{1,0:T(8,128)(2,1)S(1)}, bf16[768,2560]{1,0:T(8,128)(2,1)}) custom-call(bf16[1536,2560]{1,0:T(8,128)(2,1)} %shard_map.218.h_ref, bf16[1536,2560]{1,0:T(8,128)(2,1)} %shard_map.219.cot_ref, bf16[2560,1152]{1,0:T(8,128)(2,1)} %all-gather.11.cloned.1.call-done.weight_ref), custom_call_target="tpu_custom_call" | custom-call | flops 1000000 | bytes 100000 | tf_op jit(solution)/shard_map/pallas_call | solution.py:430
  296.9 17.8 %shard_map.220 = (bf16[768,1152]{1,0:T(8,128)(2,1)S(1)}, bf16[768,2560]{1,0:T(8,128)(2,1)S(1)}, bf16[768,2560]{1,0:T(8,128)(2,1)}) custom-call(bf16[1536,2560]{1,0:T(8,128)(2,1)} %shard_map.218.h_ref, bf16[1536,2560]{1,0:T(8,128)(2,1)} %shard_map.219.cot_ref, bf16[2560,1152]{1,0:T(8,128)(2,1)} %all-gather.11.cloned.1.call-done.weight_ref), custom_call_target="tpu_custom_call" | custom-call | flops 1000000 | bytes 100000 | tf_op jit(solution)/shard_map/pallas_call | solution.py:430
  316.6 16.3 %shard_map.222 = bf16[2560,1152]{1,0:T(8,128)(2,1)} custom-call(bf16[1536,2560]{1,0:T(8,128)(2,1)} %shard_map.218.h_ref, bf16[1536,2560]{1,0:T(8,128)(2,1)} %shard_map.219.cot_ref, bf16[768,1152]{1,0:T(8,128)(2,1)S(1)} %get-tuple-element.114.mine_ref, bf16[768,1152]{1,0:T(8,128)(2,1)S(1)} %get-tuple-element.111.other_ref), custom_call_target="tpu_custom_call" | custom-call | flops 1000000 | bytes 100000 | tf_op jit(solution)/shard_map/pallas_call | solution.py:455
  332.9 34.6 %all-gather.9.cloned.1.call-done.weight_ref = bf16[2560,1536]{1,0:T(8,128)(2,1)} async-done(((bf16[640,1536]{1,0:T(8,128)(2,1)}), bf16[2560,1536]{1,0:T(8,128)(2,1)}) %all-gather.9.cloned.1.call-update) | async-done | bytes 7864336 | tf_op jit(solution)/shard_map/all_gather | solution.py:635
  367.6 19.9 %shard_map.224 = (bf16[768,1536]{1,0:T(8,128)(2,1)S(1)}, bf16[768,2560]{1,0:T(8,128)(2,1)}, bf16[768,2560]{1,0:T(8,128)(2,1)}) custom-call(bf16[1536,2560]{1,0:T(8,128)(2,1)} %shard_map.218.h_ref, bf16[1536,2560]{1,0:T(8,128)(2,1)} %shard_map.219.cot_ref, bf16[2560,1536]{1,0:T(8,128)(2,1)} %all-gather.9.cloned.1.call-done.weight_ref, ...), custom_call_target="tpu_custom_call" | custom-call | flops 1000000 | bytes 100000 | tf_op jit(solution)/shard_map/pallas_call | solution.py:430
  387.5 20.0 %shard_map.223 = (bf16[768,1536]{1,0:T(8,128)(2,1)S(1)}, bf16[768,2560]{1,0:T(8,128)(2,1)}, bf16[768,2560]{1,0:T(8,128)(2,1)}) custom-call(bf16[1536,2560]{1,0:T(8,128)(2,1)} %shard_map.218.h_ref, bf16[1536,2560]{1,0:T(8,128)(2,1)} %shard_map.219.cot_ref, bf16[2560,1536]{1,0:T(8,128)(2,1)} %all-gather.9.cloned.1.call-done.weight_ref, ...), custom_call_target="tpu_custom_call" | custom-call | flops 1000000 | bytes 100000 | tf_op jit(solution)/shard_map/pallas_call | solution.py:430
  413.9 10.7 %collective-permute-done.41 = bf16[96,2560]{1,0:T(8,128)(2,1)S(1)} collective-permute-done((bf16[96,2560]{1,0:T(8,128)(2,1)S(1)}, bf16[96,2560]{1,0:T(8,128)(2,1)S(1)}, u32[]{:S(2)}, u32[]{:S(2)}) %collective-permute-start.41) | collective-permute-done | bytes 491552 | tf_op jit(solution)/shard_map/ppermute | solution.py:516
  430.0 17.7 %shard_map.225 = bf16[2560,1536]{1,0:T(8,128)(2,1)} custom-call(bf16[1536,2560]{1,0:T(8,128)(2,1)} %shard_map.218.h_ref, bf16[1536,2560]{1,0:T(8,128)(2,1)} %shard_map.219.cot_ref, bf16[768,1536]{1,0:T(8,128)(2,1)S(1)} %get-tuple-element.124.mine_ref, bf16[768,1536]{1,0:T(8,128)(2,1)S(1)} %get-tuple-element.125.other_ref), custom_call_target="tpu_custom_call" | custom-call | flops 1000000 | bytes 100000 | tf_op jit(solution)/shard_map/pallas_call | solution.py:455
  462.9 21.4 %collective-permute-done.44.refs_2_ = bf16[192,2560]{1,0:T(8,128)(2,1)} collective-permute-done((bf16[192,2560]{1,0:T(8,128)(2,1)}, bf16[192,2560]{1,0:T(8,128)(2,1)}, u32[]{:S(2)}, u32[]{:S(2)}) %collective-permute-start.44) | collective-permute-done | bytes 983072 | tf_op jit(solution)/shard_map/ppermute | solution.py:516
  490.0 8.2 %collective-permute-done.45.refs_3_ = bf16[96,2560]{1,0:T(8,128)(2,1)} collective-permute-done((bf16[96,2560]{1,0:T(8,128)(2,1)S(1)}, bf16[96,2560]{1,0:T(8,128)(2,1)}, u32[]{:S(2)}, u32[]{:S(2)}) %collective-permute-start.45) | collective-permute-done | bytes 491552 | tf_op jit(solution)/shard_map/ppermute | solution.py:516
  508.6 7.7 %shard_map.226.a_ref = bf16[1536,2560]{1,0:T(8,128)(2,1)} custom-call(bf16[192,2560]{1,0:T(8,128)(2,1)} %get-tuple-element.234.refs_0_, bf16[192,2560]{1,0:T(8,128)(2,1)} %collective-permute-done.43.refs_1_, bf16[192,2560]{1,0:T(8,128)(2,1)} %collective-permute-done.44.refs_2_, bf16[96,2560]{1,0:T(8,128)(2,1)} %collective-permute-done.45.refs_3_, ...), custom_call_target="tpu_custom_call" | custom-call | flops 1000000 | bytes 100000 | tf_op jit(solution)/shard_map/pallas_call | solution.py:335
  516.3 7.6 %shard_map.227.rows_ref = bf16[1536,320]{1,0:T(8,128)(2,1)S(1)} custom-call(bf16[1536,2560]{1,0:T(8,128)(2,1)} %shard_map.226.a_ref, bf16[2560,320]{1,0:T(8,128)(2,1)S(1)} %bitcast.57), custom_call_target="tpu_custom_call" | custom-call | flops 1000000 | bytes 100000 | tf_op jit(solution)/shard_map/pallas_call | solution.py:391
  536.4 9.7 %shard_map.230 = bf16[2560,320]{1,0:T(8,128)(2,1)S(1)} custom-call(bf16[1536,2560]{1,0:T(8,128)(2,1)} %shard_map.226.a_ref, bf16[1536,320]{1,0:T(8,128)(2,1)S(1)} %copy-done.8), custom_call_target="tpu_custom_call" | custom-call | flops 1000000 | bytes 100000 | tf_op jit(solution)/shard_map/pallas_call | solution.py:486
  546.1 31.5 %shard_map.231 = (f32[320,1536]{1,0:T(8,128)}, f32[160,1536]{1,0:T(8,128)S(1)}) custom-call(s32[4,6]{1,0:T(4,128)S(1)} %get-tuple-element.314.bounds_ref, bf16[320,1536]{1,0:T(8,128)(2,1)S(1)} %slice.424.q_ref, bf16[160,1536]{1,0:T(8,128)(2,1)S(1)} %copy-done.10, s32[1,1536]{1,0:T(1,128)S(1)} %broadcast_in_dim.2.start_ref, ...), custom_call_target="tpu_custom_call" | custom-call | flops 1000000 | bytes 100000 | tf_op jit(solution)/shard_map/pallas_call | solution.py:268
  577.6 7.8 %collective-permute-done.57 = bf16[160,1536]{1,0:T(8,128)(2,1)S(1)} collective-permute-done((bf16[160,1536]{1,0:T(8,128)(2,1)S(1)}, bf16[160,1536]{1,0:T(8,128)(2,1)S(1)}, u32[]{:S(2)}, u32[]{:S(2)}) %collective-permute-start.57) | collective-permute-done | bytes 491552 | tf_op jit(solution)/shard_map/ppermute | solution.py:512
  591.9 9.6 %shard_map.233 = bf16[2560,512]{1,0:T(8,128)(2,1)S(1)} custom-call(bf16[1536,2560]{1,0:T(8,128)(2,1)} %get-tuple-element.148.a_ref, bf16[1536,512]{1,0:T(8,128)(2,1)S(1)} %shard_map.232.b_ref), custom_call_target="tpu_custom_call" | custom-call | flops 1000000 | bytes 100000 | tf_op jit(solution)/shard_map/pallas_call | solution.py:486
  603.1 6.4 collective-permute-done.58
  641.2 22.6 %collective-permute-done.61 = bf16[96,2560]{1,0:T(8,128)(2,1)S(1)} collective-permute-done((bf16[96,2560]{1,0:T(8,128)(2,1)S(1)}, bf16[96,2560]{1,0:T(8,128)(2,1)S(1)}, u32[]{:S(2)}, u32[]{:S(2)}) %collective-permute-start.61) | collective-permute-done | bytes 491552 | tf_op jit(solution)/shard_map/ppermute | solution.py:516
  706.8 12.0 %reduce-scatter.11.cloned.1.call-done.a_ref = bf16[320,640]{1,0:T(8,128)(2,1)} async-done(((bf16[1280,640]{1,0:T(8,128)(2,1)}), bf16[320,640]{1,0:T(8,128)(2,1)}) %reduce-scatter.11.cloned.1.call-update) | async-done | bytes 409616 | tf_op jit(solution)/shard_map/reduce_scatter | solution.py:639
  (443 shorter events, 250.5 us)
Async XLA Ops:
  7.2 91.6 %all-gather.7.cloned.1.call-start = ((), (), s32[]{:S(2)}) async-start(), calls=%async_computation.5 | async-start | bytes 2048000 | tf_op jit(solution)/shard_map/all_gather | solution.py:635
  9.3 97.6 %all-gather.5.cloned.1.call-start = ((), (), s32[]{:S(2)}) async-start(), calls=%async_computation.4 | async-start | bytes 3276800 | tf_op jit(solution)/shard_map/all_gather | solution.py:635
  24.1 253.0 %all-gather.11.cloned.1.call-start = ((), (), s32[]{:S(2)}) async-start(), calls=%async_computation.7 | async-start | bytes 7372800 | tf_op jit(solution)/shard_map/all_gather | solution.py:635
  24.1 23.0 %collective-permute-start = (bf16[192,2560]{1,0:T(8,128)(2,1)S(1)}, bf16[192,2560]{1,0:T(8,128)(2,1)S(1)}, u32[]{:S(2)}, u32[]{:S(2)}) collective-permute-start(bf16[192,2560]{1,0:T(8,128)(2,1)S(1)} %copy-done), channel_id=1, source_target_pairs={{0,2},{2,0},{1,3},{3,1},{4,6},{6,4},{5,7},{7,5},{8,10},{10,8},{9,1... | collective-permute-start | bytes 2949128 | tf_op jit(solution)/shard_map/ppermute | solution.py:516
  25.9 22.8 %collective-permute-start.2 = (bf16[192,2560]{1,0:T(8,128)(2,1)S(1)}, bf16[192,2560]{1,0:T(8,128)(2,1)S(1)}, u32[]{:S(2)}, u32[]{:S(2)}) collective-permute-start(bf16[192,2560]{1,0:T(8,128)(2,1)S(1)} %copy-done), channel_id=1, source_target_pairs={{0,4},{4,0},{1,5},{5,1},{2,6},{6,2},{3,7},{7,3},{8,12},{12,8},{9,1... | collective-permute-start | bytes 2949128 | tf_op jit(solution)/shard_map/ppermute | solution.py:516
  27.4 35.3 %collective-permute-start.5 = (bf16[192,2560]{1,0:T(8,128)(2,1)S(1)}, bf16[192,2560]{1,0:T(8,128)(2,1)S(1)}, u32[]{:S(2)}, u32[]{:S(2)}) collective-permute-start(bf16[192,2560]{1,0:T(8,128)(2,1)S(1)} %copy-done), channel_id=1, source_target_pairs={{0,1},{1,0},{2,3},{3,2},{4,5},{5,4},{6,7},{7,6},{8,9},{9,8},{10,11... | collective-permute-start | bytes 2949128 | tf_op jit(solution)/shard_map/ppermute | solution.py:516
  91.3 276.2 %all-gather.9.cloned.1.call-start = ((), (), s32[]{:S(2)}) async-start(), calls=%async_computation.6 | async-start | bytes 9830400 | tf_op jit(solution)/shard_map/all_gather | solution.py:635
  101.9 23.8 %collective-permute-start.11 = (bf16[1280,320]{0,1:T(8,128)(2,1)}, bf16[1280,320]{0,1:T(8,128)(2,1)S(1)}, u32[]{:S(2)}, u32[]{:S(2)}) collective-permute-start(bf16[1280,320]{0,1:T(8,128)(2,1)} %copy.78), channel_id=1, source_target_pairs={{0,4},{4,0},{1,5},{5,1},{2,6},{6,2},{3,7},{7,3},{8,12},{12,8},{9,1... | collective-permute-start | bytes 2457608 | tf_op jit(solution)/shard_map/ppermute | solution.py:516
  119.1 45.2 %collective-permute-start.16 = (bf16[320,1536]{1,0:T(8,128)(2,1)}, bf16[320,1536]{1,0:T(8,128)(2,1)}, u32[]{:S(2)}, u32[]{:S(2)}) collective-permute-start(bf16[320,1536]{1,0:T(8,128)(2,1)} %broadcast_select_fusion.8), channel_id=1, source_target_pairs={{0,4},{4,0},{1,5},{5,1},{2,6},{6,2},{3,7},{7,3},{8,12},{12,8},{9,1... | collective-permute-start | bytes 2949128 | tf_op jit(solution)/shard_map/ppermute | solution.py:516
  124.1 36.9 %collective-permute-start.12 = (bf16[160,1536]{1,0:T(8,128)(2,1)S(1)}, bf16[160,1536]{1,0:T(8,128)(2,1)S(1)}, u32[]{:S(2)}, u32[]{:S(2)}) collective-permute-start(bf16[160,1536]{1,0:T(8,128)(2,1)S(1)} %slice.425.kv_ref), channel_id=1, source_target_pairs={{0,8},{16,24},{1,9},{17,25},{2,10},{18,26},{3,11},{19,27},{4,12},{... | collective-permute-start | bytes 1474568 | tf_op jit(solution)/shard_map/ppermute | solution.py:512
  125.8 41.6 %collective-permute-start.15 = (bf16[192,2560]{1,0:T(8,128)(2,1)}, bf16[192,2560]{1,0:T(8,128)(2,1)}, u32[]{:S(2)}, u32[]{:S(2)}) collective-permute-start(bf16[192,2560]{1,0:T(8,128)(2,1)} %refs_0_.3), channel_id=1, source_target_pairs={{0,4},{4,0},{1,5},{5,1},{2,6},{6,2},{3,7},{7,3},{8,12},{12,8},{9,1... | collective-permute-start | bytes 2949128 | tf_op jit(solution)/shard_map/ppermute | solution.py:516
  126.7 40.7 %collective-permute-start.14 = (bf16[192,2560]{1,0:T(8,128)(2,1)}, bf16[192,2560]{1,0:T(8,128)(2,1)}, u32[]{:S(2)}, u32[]{:S(2)}) collective-permute-start(bf16[192,2560]{1,0:T(8,128)(2,1)} %refs_0_.3), channel_id=1, source_target_pairs={{0,2},{2,0},{1,3},{3,1},{4,6},{6,4},{5,7},{7,5},{8,10},{10,8},{9,1... | collective-permute-start | bytes 2949128 | tf_op jit(solution)/shard_map/ppermute | solution.py:516
  173.1 327.4 %reduce-scatter.5.cloned.1.call-start = ((), (), s32[]{:S(2)}) async-start(), calls=%async_computation.8 | async-start | bytes 7372800 | tf_op jit(solution)/shard_map/reduce_scatter | solution.py:639
  203.7 22.2 %collective-permute-start.23 = (bf16[192,2560]{1,0:T(8,128)(2,1)S(1)}, bf16[192,2560]{1,0:T(8,128)(2,1)S(1)}, u32[]{:S(2)}, u32[]{:S(2)}) collective-permute-start(bf16[192,2560]{1,0:T(8,128)(2,1)S(1)} %pad_maximum_fusion.5), channel_id=1, source_target_pairs={{0,4},{4,0},{1,5},{5,1},{2,6},{6,2},{3,7},{7,3},{8,12},{12,8},{9,1... | collective-permute-start | bytes 2949128 | tf_op jit(solution)/shard_map/ppermute | solution.py:516
  367.5 259.8 %reduce-scatter.7.cloned.1.call-start = ((), (), s32[]{:S(2)}) async-start(), calls=%async_computation.9 | async-start | bytes 9830400 | tf_op jit(solution)/shard_map/reduce_scatter | solution.py:639
  427.0 23.5 %collective-permute-start.40 = (bf16[192,2560]{1,0:T(8,128)(2,1)}, bf16[192,2560]{1,0:T(8,128)(2,1)}, u32[]{:S(2)}, u32[]{:S(2)}) collective-permute-start(bf16[192,2560]{1,0:T(8,128)(2,1)} %pad_maximum_fusion.6), channel_id=1, source_target_pairs={{0,2},{2,0},{1,3},{3,1},{4,6},{6,4},{5,7},{7,5},{8,10},{10,8},{9,1... | collective-permute-start | bytes 2949128 | tf_op jit(solution)/shard_map/ppermute | solution.py:516
  428.5 23.2 %collective-permute-start.42 = (bf16[192,2560]{1,0:T(8,128)(2,1)}, bf16[192,2560]{1,0:T(8,128)(2,1)}, u32[]{:S(2)}, u32[]{:S(2)}) collective-permute-start(bf16[192,2560]{1,0:T(8,128)(2,1)} %pad_maximum_fusion.7), channel_id=1, source_target_pairs={{0,4},{4,0},{1,5},{5,1},{2,6},{6,2},{3,7},{7,3},{8,12},{12,8},{9,1... | collective-permute-start | bytes 2949128 | tf_op jit(solution)/shard_map/ppermute | solution.py:516
  451.8 232.9 %reduce-scatter.9.cloned.1.call-start = ((), (), s32[]{:S(2)}) async-start(), calls=%async_computation.10 | async-start | bytes 3276800 | tf_op jit(solution)/shard_map/reduce_scatter | solution.py:639
  452.1 49.9 %collective-permute-start.52 = (bf16[768,2560]{1,0:T(8,128)(2,1)}, bf16[768,2560]{1,0:T(8,128)(2,1)}, u32[]{:S(2)}, u32[]{:S(2)}) collective-permute-start(bf16[768,2560]{1,0:T(8,128)(2,1)} %get-tuple-element.129), channel_id=1, source_target_pairs={{0,1},{1,0},{2,3},{3,2},{4,5},{5,4},{6,7},{7,6},{8,9},{9,8},{10,11... | collective-permute-start | bytes 11796488 | tf_op jit(solution)/shard_map/ppermute | solution.py:516
  460.0 24.3 %collective-permute-start.44 = (bf16[192,2560]{1,0:T(8,128)(2,1)}, bf16[192,2560]{1,0:T(8,128)(2,1)}, u32[]{:S(2)}, u32[]{:S(2)}) collective-permute-start(bf16[192,2560]{1,0:T(8,128)(2,1)} %get-tuple-element.234.refs_0_), channel_id=1, source_target_pairs={{0,4},{4,0},{1,5},{5,1},{2,6},{6,2},{3,7},{7,3},{8,12},{12,8},{9,1... | collective-permute-start | bytes 2949128 | tf_op jit(solution)/shard_map/ppermute | solution.py:516
  461.5 25.4 %collective-permute-start.43 = (bf16[192,2560]{1,0:T(8,128)(2,1)}, bf16[192,2560]{1,0:T(8,128)(2,1)}, u32[]{:S(2)}, u32[]{:S(2)}) collective-permute-start(bf16[192,2560]{1,0:T(8,128)(2,1)} %get-tuple-element.234.refs_0_), channel_id=1, source_target_pairs={{0,2},{2,0},{1,3},{3,1},{4,6},{6,4},{5,7},{7,5},{8,10},{10,8},{9,1... | collective-permute-start | bytes 2949128 | tf_op jit(solution)/shard_map/ppermute | solution.py:516
  502.5 22.4 %collective-permute-start.53 = (bf16[320,1152]{1,0:T(8,128)(2,1)S(1)}, bf16[320,1152]{1,0:T(8,128)(2,1)}, u32[]{:S(2)}, u32[]{:S(2)}) collective-permute-start(bf16[320,1152]{1,0:T(8,128)(2,1)S(1)} %broadcast_select_fusion.17), channel_id=1, source_target_pairs={{0,4},{4,0},{1,5},{5,1},{2,6},{6,2},{3,7},{7,3},{8,12},{12,8},{9,1... | collective-permute-start | bytes 2211848 | tf_op jit(solution)/shard_map/ppermute | solution.py:516
  526.4 59.1 %collective-permute-start.56 = (bf16[192,2560]{1,0:T(8,128)(2,1)}, bf16[192,2560]{1,0:T(8,128)(2,1)S(1)}, u32[]{:S(2)}, u32[]{:S(2)}) collective-permute-start(bf16[192,2560]{1,0:T(8,128)(2,1)} %get-tuple-element.246), channel_id=1, source_target_pairs={{0,6},{2,4},{4,2},{6,0},{1,7},{3,5},{5,3},{7,1},{8,14},{10,12},{12... | collective-permute-start | bytes 2949128 | tf_op jit(solution)/shard_map/ppermute | solution.py:520
  526.7 58.8 %collective-permute-start.55 = (bf16[192,2560]{1,0:T(8,128)(2,1)}, bf16[192,2560]{1,0:T(8,128)(2,1)S(1)}, u32[]{:S(2)}, u32[]{:S(2)}) collective-permute-start(bf16[192,2560]{1,0:T(8,128)(2,1)} %get-tuple-element.247), channel_id=1, source_target_pairs={{0,4},{4,0},{1,5},{5,1},{2,6},{6,2},{3,7},{7,3},{8,12},{12,8},{9,1... | collective-permute-start | bytes 2949128 | tf_op jit(solution)/shard_map/ppermute | solution.py:516
  528.2 57.2 %collective-permute-start.54 = (bf16[192,2560]{1,0:T(8,128)(2,1)S(1)}, bf16[192,2560]{1,0:T(8,128)(2,1)S(1)}, u32[]{:S(2)}, u32[]{:S(2)}) collective-permute-start(bf16[192,2560]{1,0:T(8,128)(2,1)S(1)} %get-tuple-element.248), channel_id=1, source_target_pairs={{0,2},{2,0},{1,3},{3,1},{4,6},{6,4},{5,7},{7,5},{8,10},{10,8},{9,1... | collective-permute-start | bytes 2949128 | tf_op jit(solution)/shard_map/ppermute | solution.py:516
  534.7 50.8 %collective-permute-start.57 = (bf16[160,1536]{1,0:T(8,128)(2,1)S(1)}, bf16[160,1536]{1,0:T(8,128)(2,1)S(1)}, u32[]{:S(2)}, u32[]{:S(2)}) collective-permute-start(bf16[160,1536]{1,0:T(8,128)(2,1)S(1)} %convert_element_type.291), channel_id=1, source_target_pairs={{8,0},{24,16},{9,1},{25,17},{10,2},{26,18},{11,3},{27,19},{12,4},{... | collective-permute-start | bytes 1474568 | tf_op jit(solution)/shard_map/ppermute | solution.py:512
  627.4 91.4 %reduce-scatter.11.cloned.1.call-start = ((), (), s32[]{:S(2)}) async-start(), calls=%async_computation.11 | async-start | bytes 2048000 | tf_op jit(solution)/shard_map/reduce_scatter | solution.py:639
  629.4 34.4 %collective-permute-start.62 = (bf16[320,1536]{1,0:T(8,128)(2,1)S(1)}, bf16[320,1536]{1,0:T(8,128)(2,1)S(1)}, u32[]{:S(2)}, u32[]{:S(2)}) collective-permute-start(bf16[320,1536]{1,0:T(8,128)(2,1)S(1)} %broadcast_select_fusion.5), channel_id=1, source_target_pairs={{0,4},{4,0},{1,5},{5,1},{2,6},{6,2},{3,7},{7,3},{8,12},{12,8},{9,1... | collective-permute-start | bytes 2949128 | tf_op jit(solution)/shard_map/ppermute | solution.py:516
  635.1 28.7 %collective-permute-start.61 = (bf16[96,2560]{1,0:T(8,128)(2,1)S(1)}, bf16[96,2560]{1,0:T(8,128)(2,1)S(1)}, u32[]{:S(2)}, u32[]{:S(2)}) collective-permute-start(bf16[96,2560]{1,0:T(8,128)(2,1)S(1)} %get-tuple-element.243), channel_id=1, source_target_pairs={{0,4},{4,0},{1,5},{5,1},{2,6},{6,2},{3,7},{7,3},{8,12},{12,8},{9,1... | collective-permute-start | bytes 1474568 | tf_op jit(solution)/shard_map/ppermute | solution.py:516
  636.8 27.0 %collective-permute-start.60 = (bf16[96,2560]{1,0:T(8,128)(2,1)S(1)}, bf16[96,2560]{1,0:T(8,128)(2,1)S(1)}, u32[]{:S(2)}, u32[]{:S(2)}) collective-permute-start(bf16[96,2560]{1,0:T(8,128)(2,1)S(1)} %get-tuple-element.244), channel_id=1, source_target_pairs={{0,2},{2,0},{1,3},{3,1},{4,6},{6,4},{5,7},{7,5},{8,10},{10,8},{9,1... | collective-permute-start | bytes 1474568 | tf_op jit(solution)/shard_map/ppermute | solution.py:516
  665.1 23.4 %collective-permute-start.63 = (bf16[192,2560]{1,0:T(8,128)(2,1)}, bf16[192,2560]{1,0:T(8,128)(2,1)}, u32[]{:S(2)}, u32[]{:S(2)}) collective-permute-start(bf16[192,2560]{1,0:T(8,128)(2,1)} %pad_maximum_fusion.8), channel_id=1, source_target_pairs={{0,2},{2,0},{1,3},{3,1},{4,6},{6,4},{5,7},{7,5},{8,10},{10,8},{9,1... | collective-permute-start | bytes 2949128 | tf_op jit(solution)/shard_map/ppermute | solution.py:516
  667.5 25.0 %collective-permute-start.64 = (bf16[192,2560]{1,0:T(8,128)(2,1)}, bf16[192,2560]{1,0:T(8,128)(2,1)}, u32[]{:S(2)}, u32[]{:S(2)}) collective-permute-start(bf16[192,2560]{1,0:T(8,128)(2,1)} %pad_maximum_fusion.9), channel_id=1, source_target_pairs={{0,4},{4,0},{1,5},{5,1},{2,6},{6,2},{3,7},{7,3},{8,12},{12,8},{9,1... | collective-permute-start | bytes 2949128 | tf_op jit(solution)/shard_map/ppermute | solution.py:516
  (122 other events, 1073.4 us)
Sparse Core Ops, SparseCore 0:
  10.2 40.8 all-gather.6
  53.2 53.6 all-gather.4
  108.5 113.8 all-gather.10
  224.4 143.0 all-gather.8
  369.7 102.5 reduce-scatter.4
  474.5 147.2 reduce-scatter.6
  627.5 49.2 reduce-scatter.8
  684.9 33.8 reduce-scatter.10

commit v7 on v6

--- a/solution.py
+++ b/solution.py
@@ -472,7 +472,7 @@
         as_f32_kernel,
         out_shape=jax.ShapeDtypeStruct(a.shape, F32),
         compiler_params=pltpu.CompilerParams(vmem_limit_bytes=VMEM_BYTES // 2),
-        cost_estimate=pl.CostEstimate(flops=3 * 10**10, bytes_accessed=10**5, transcendentals=0),
+        cost_estimate=pl.CostEstimate(flops=2 * 10**11, bytes_accessed=10**5, transcendentals=0),
     )(a)
 
 
@@ -766,6 +766,7 @@
     mid_far = plane_sum_one(mid_total)
     mid_near = plane_sum_two(mid_total, *mid_far)
     grad_mix = plane_join(cotangent, *cot_one, *cot_two)
+    *mid_near, grad_mix = together(*mid_near, grad_mix)
     x_mid = input_f32 + added(mid_total, *mid_near)
 
     inverse_two = lax.rsqrt(jnp.mean(x_mid * x_mid, axis=-1, keepdims=True) + eps)
@@ -851,7 +852,8 @@
     one_far = plane_sum_one(one_total)
     one_far = landed(one_far, (owned[1], "got"))
     one_near = plane_sum_two(one_total, *one_far)
-    out_grad = sum_z(tied(out_term, qkv_grad))
+    qkv_raw = qkv_grad
+    out_grad = sum_z(tied(out_term, qkv_raw))
     owned_a = Unshare(qkv_grad, first_y)
     *one_near, qkv_grad = together(*one_near, qkv_grad)
     grad_h_one = added(one_total, *one_near)
@@ -860,6 +862,8 @@
     )
 
     input_grad = landed(input_grad, (owned_a, "got"))
+    for part in owned:
+        part.keep, part.got, _ = lax.optimization_barrier((part.keep, part.got, qkv_raw))
     owned = [part.both() for part in owned]
     kept = [CHUNK, nf - CHUNK]
     width = [full.shape[1] // 3 for full in full_c]

time: 738 us -> 744 us (level)
  other arithmetic: 74.2 us -> 82.5 us
    unnamed x160 -> x158, local copies, waits for them, and re-layouts: 19.8 us -> 20.3 us
  transfers between devices with their start and end apart: 76 -> 76, of which waited for: 34 -> 37; matrix products, arithmetic and copies ran while one was open for 17% -> 17% of each run, Pallas kernels for 33% -> 33%
where the time goes in v7:
time: 744 us; the launch traced here: 737 us
  waiting for transfers between devices  272 us (37%)
  Pallas kernels  241 us (32%)
  other arithmetic  82.5 us (11%)
  starting transfers between devices  58.7 us (8%)
  local copies, waits for them, and re-layouts  54.2 us (7%)
  between operations  15.8 us (2%)
  matrix products  13.1 us (2%)
    ppermute x62, waiting for transfers between devices, over(): return lax.ppermute(block, axis, SWAP)  209 us
    pallas_call x4, Pallas kernels, hidden_units(): pl.pallas_call(functools.partial(units_kernel, bool(prior)), grid=(count...  75.4 us
    ppermute x62, starting transfers between devices, over(): return lax.ppermute(block, axis, SWAP)  52.6 us
    all_gather x4, waiting for transfers between devices, gather_z(): return lax.all_gather(block, 'z', axis=0, tiled=True)  44.6 us
    pallas_call x2, Pallas kernels, attend_back(): pl.pallas_call(functools.partial(attend_back_kernel, places), grid_spec=p...  36.3 us
    pallas_call x2, Pallas kernels, unit_grads(): pl.pallas_call(unit_grads_kernel, grid=(model // rows,), in_specs=[pl.Blo...  34 us
    pallas_call x2, Pallas kernels, attend(): pl.pallas_call(functools.partial(attend_kernel, places), grid_spec=pltpu....  28.8 us
    pallas_call x4, Pallas kernels, join(): pl.pallas_call(join_kernel, in_specs=[ANY] * len(parts), out_specs=ANY, o...  24.5 us
  transfers between devices with their start and end apart: 76, of which 37 were waited for; matrix products, arithmetic and copies ran while one was open for 17% of the time, Pallas kernels for 33%

profile of v7, /device:TPU:0, one launch (start us, length us, event | category | flops | bytes accessed | tf_op | source)
XLA Modules:
  0.0 736.7 jit_solution(5647586076469738957)
XLA Ops:
  15.3 7.7 %collective-permute-done.1 = bf16[320,512]{1,0:T(8,128)(2,1)S(1)} collective-permute-done((bf16[320,512]{1,0:T(8,128)(2,1)S(1)}, bf16[320,512]{1,0:T(8,128)(2,1)S(1)}, u32[]{:S(2)}, u32[]{:S(2)}) %collective-permute-start.1) | collective-permute-done | bytes 327712 | tf_op jit(solution)/shard_map/ppermute | solution.py:516
  27.4 19.7 %collective-permute-done.refs_1_ = bf16[192,2560]{1,0:T(8,128)(2,1)S(1)} collective-permute-done((bf16[192,2560]{1,0:T(8,128)(2,1)S(1)}, bf16[192,2560]{1,0:T(8,128)(2,1)S(1)}, u32[]{:S(2)}, u32[]{:S(2)}) %collective-permute-start) | collective-permute-done | bytes 983072 | tf_op jit(solution)/shard_map/ppermute | solution.py:516
  65.2 5.8 shard_map.212.x_ref
  71.7 17.9 %collective-permute-done.13 = bf16[320,1152]{1,0:T(8,128)(2,1)S(1)} collective-permute-done((bf16[320,1152]{1,0:T(8,128)(2,1)S(1)}, bf16[320,1152]{1,0:T(8,128)(2,1)S(1)}, u32[]{:S(2)}, u32[]{:S(2)}) %collective-permute-start.13) | collective-permute-done | bytes 737312 | tf_op jit(solution)/shard_map/ppermute | solution.py:516
  109.5 9.6 %shard_map.213 = (bf16[1536,2560]{1,0:T(8,128)(2,1)}, f32[1536,512]{1,0:T(8,128)S(1)}) custom-call(bf16[1536,2560]{1,0:T(8,128)(2,1)} %shard_map.212.x_ref, f32[1,2560]{1,0:T(1,128)S(1)} %broadcast_in_dim_squeeze.2.gain_ref, bf16[2560,512]{1,0:T(8,128)(2,1)S(1)} %copy-done.10), custom_call_target="tpu_custom_call" | custom-call | flops 1000000 | bytes 100000 | tf_op jit(solution)/shard_map/pallas_call | solution.py:360
  133.7 27.2 %shard_map.215 = (f32[320,1536]{1,0:T(8,128)S(1)}, f32[8,1536]{1,0:T(8,128)S(1)}) custom-call(s32[4,6]{1,0:T(4,128)S(1)} %get-tuple-element.332.bounds_ref, bf16[320,1536]{1,0:T(8,128)(2,1)S(1)} %slice.424.q_ref, bf16[160,1536]{1,0:T(8,128)(2,1)S(1)} %slice.425.kv_ref, s32[1,1536]{1,0:T(1,128)S(1)} %broadcast_in_dim.2.start_ref), custom_call_target="tpu_custom_call" | custom-call | flops 1000000 | bytes 100000 | tf_op jit(solution)/shard_map/pallas_call | solution.py:177
  180.4 6.7 collective-permute-done.19.refs_4_
  190.2 10.8 %collective-permute-done.22 = bf16[96,2560]{1,0:T(8,128)(2,1)S(1)} collective-permute-done((bf16[96,2560]{1,0:T(8,128)(2,1)S(1)}, bf16[96,2560]{1,0:T(8,128)(2,1)S(1)}, u32[]{:S(2)}, u32[]{:S(2)}) %collective-permute-start.22) | collective-permute-done | bytes 491552 | tf_op jit(solution)/shard_map/ppermute | solution.py:516
  213.6 11.2 %collective-permute-done.21 = bf16[192,2560]{1,0:T(8,128)(2,1)S(1)} collective-permute-done((bf16[192,2560]{1,0:T(8,128)(2,1)}, bf16[192,2560]{1,0:T(8,128)(2,1)S(1)}, u32[]{:S(2)}, u32[]{:S(2)}) %collective-permute-start.21) | collective-permute-done | bytes 983072 | tf_op jit(solution)/shard_map/ppermute | solution.py:516
  230.8 19.9 %collective-permute-done.30.refs_2_ = bf16[192,2560]{1,0:T(8,128)(2,1)S(1)} collective-permute-done((bf16[192,2560]{1,0:T(8,128)(2,1)S(1)}, bf16[192,2560]{1,0:T(8,128)(2,1)S(1)}, u32[]{:S(2)}, u32[]{:S(2)}) %collective-permute-start.30) | collective-permute-done | bytes 983072 | tf_op jit(solution)/shard_map/ppermute | solution.py:516
  254.4 6.9 collective-permute-done.31.refs_3_
  265.1 5.7 shard_map.219.h_ref
  270.9 17.8 %shard_map.221 = (bf16[768,1152]{1,0:T(8,128)(2,1)S(1)}, bf16[768,2560]{1,0:T(8,128)(2,1)S(1)}, bf16[768,2560]{1,0:T(8,128)(2,1)}) custom-call(bf16[1536,2560]{1,0:T(8,128)(2,1)} %shard_map.219.h_ref, bf16[1536,2560]{1,0:T(8,128)(2,1)} %shard_map.218.cot_ref, bf16[2560,1152]{1,0:T(8,128)(2,1)} %all-gather.11.cloned.1.call-done.weight_ref), custom_call_target="tpu_custom_call" | custom-call | flops 1000000 | bytes 100000 | tf_op jit(solution)/shard_map/pallas_call | solution.py:430
  290.6 17.8 %shard_map.220 = (bf16[768,1152]{1,0:T(8,128)(2,1)S(1)}, bf16[768,2560]{1,0:T(8,128)(2,1)S(1)}, bf16[768,2560]{1,0:T(8,128)(2,1)}) custom-call(bf16[1536,2560]{1,0:T(8,128)(2,1)} %shard_map.219.h_ref, bf16[1536,2560]{1,0:T(8,128)(2,1)} %shard_map.218.cot_ref, bf16[2560,1152]{1,0:T(8,128)(2,1)} %all-gather.11.cloned.1.call-done.weight_ref), custom_call_target="tpu_custom_call" | custom-call | flops 1000000 | bytes 100000 | tf_op jit(solution)/shard_map/pallas_call | solution.py:430
  310.3 16.3 %shard_map.222 = bf16[2560,1152]{1,0:T(8,128)(2,1)} custom-call(bf16[1536,2560]{1,0:T(8,128)(2,1)} %shard_map.219.h_ref, bf16[1536,2560]{1,0:T(8,128)(2,1)} %shard_map.218.cot_ref, bf16[768,1152]{1,0:T(8,128)(2,1)S(1)} %get-tuple-element.124.mine_ref, bf16[768,1152]{1,0:T(8,128)(2,1)S(1)} %get-tuple-element.121.other_ref), custom_call_target="tpu_custom_call" | custom-call | flops 1000000 | bytes 100000 | tf_op jit(solution)/shard_map/pallas_call | solution.py:455
  326.5 41.0 %all-gather.9.cloned.1.call-done.weight_ref = bf16[2560,1536]{1,0:T(8,128)(2,1)} async-done(((bf16[640,1536]{1,0:T(8,128)(2,1)}), bf16[2560,1536]{1,0:T(8,128)(2,1)}) %all-gather.9.cloned.1.call-update) | async-done | bytes 7864336 | tf_op jit(solution)/shard_map/all_gather | solution.py:635
  367.6 19.9 %shard_map.224 = (bf16[768,1536]{1,0:T(8,128)(2,1)S(1)}, bf16[768,2560]{1,0:T(8,128)(2,1)}, bf16[768,2560]{1,0:T(8,128)(2,1)}) custom-call(bf16[1536,2560]{1,0:T(8,128)(2,1)} %shard_map.219.h_ref, bf16[1536,2560]{1,0:T(8,128)(2,1)} %shard_map.218.cot_ref, bf16[2560,1536]{1,0:T(8,128)(2,1)} %all-gather.9.cloned.1.call-done.weight_ref, ...), custom_call_target="tpu_custom_call" | custom-call | flops 1000000 | bytes 100000 | tf_op jit(solution)/shard_map/pallas_call | solution.py:430
  387.5 20.0 %shard_map.223 = (bf16[768,1536]{1,0:T(8,128)(2,1)S(1)}, bf16[768,2560]{1,0:T(8,128)(2,1)}, bf16[768,2560]{1,0:T(8,128)(2,1)}) custom-call(bf16[1536,2560]{1,0:T(8,128)(2,1)} %shard_map.219.h_ref, bf16[1536,2560]{1,0:T(8,128)(2,1)} %shard_map.218.cot_ref, bf16[2560,1536]{1,0:T(8,128)(2,1)} %all-gather.9.cloned.1.call-done.weight_ref, ...), custom_call_target="tpu_custom_call" | custom-call | flops 1000000 | bytes 100000 | tf_op jit(solution)/shard_map/pallas_call | solution.py:430
  413.9 10.7 %collective-permute-done.41 = bf16[96,2560]{1,0:T(8,128)(2,1)S(1)} collective-permute-done((bf16[96,2560]{1,0:T(8,128)(2,1)S(1)}, bf16[96,2560]{1,0:T(8,128)(2,1)S(1)}, u32[]{:S(2)}, u32[]{:S(2)}) %collective-permute-start.41) | collective-permute-done | bytes 491552 | tf_op jit(solution)/shard_map/ppermute | solution.py:516
  430.0 17.7 %shard_map.225 = bf16[2560,1536]{1,0:T(8,128)(2,1)} custom-call(bf16[1536,2560]{1,0:T(8,128)(2,1)} %shard_map.219.h_ref, bf16[1536,2560]{1,0:T(8,128)(2,1)} %shard_map.218.cot_ref, bf16[768,1536]{1,0:T(8,128)(2,1)S(1)} %get-tuple-element.134.mine_ref, bf16[768,1536]{1,0:T(8,128)(2,1)S(1)} %get-tuple-element.135.other_ref), custom_call_target="tpu_custom_call" | custom-call | flops 1000000 | bytes 100000 | tf_op jit(solution)/shard_map/pallas_call | solution.py:455
  463.0 21.4 %collective-permute-done.44.refs_2_ = bf16[192,2560]{1,0:T(8,128)(2,1)} collective-permute-done((bf16[192,2560]{1,0:T(8,128)(2,1)}, bf16[192,2560]{1,0:T(8,128)(2,1)}, u32[]{:S(2)}, u32[]{:S(2)}) %collective-permute-start.44) | collective-permute-done | bytes 983072 | tf_op jit(solution)/shard_map/ppermute | solution.py:516
  490.0 8.2 %collective-permute-done.45.refs_3_ = bf16[96,2560]{1,0:T(8,128)(2,1)} collective-permute-done((bf16[96,2560]{1,0:T(8,128)(2,1)S(1)}, bf16[96,2560]{1,0:T(8,128)(2,1)}, u32[]{:S(2)}, u32[]{:S(2)}) %collective-permute-start.45) | collective-permute-done | bytes 491552 | tf_op jit(solution)/shard_map/ppermute | solution.py:516
  509.4 7.7 %shard_map.226.a_ref = bf16[1536,2560]{1,0:T(8,128)(2,1)} custom-call(bf16[192,2560]{1,0:T(8,128)(2,1)} %get-tuple-element.248.refs_0_, bf16[192,2560]{1,0:T(8,128)(2,1)} %collective-permute-done.43.refs_1_, bf16[192,2560]{1,0:T(8,128)(2,1)} %collective-permute-done.44.refs_2_, bf16[96,2560]{1,0:T(8,128)(2,1)} %collective-permute-done.45.refs_3_, ...), custom_call_target="tpu_custom_call" | custom-call | flops 1000000 | bytes 100000 | tf_op jit(solution)/shard_map/pallas_call | solution.py:335
  517.1 7.6 %shard_map.227.rows_ref = bf16[1536,320]{1,0:T(8,128)(2,1)S(1)} custom-call(bf16[1536,2560]{1,0:T(8,128)(2,1)} %shard_map.226.a_ref, bf16[2560,320]{1,0:T(8,128)(2,1)S(1)} %bitcast.57), custom_call_target="tpu_custom_call" | custom-call | flops 1000000 | bytes 100000 | tf_op jit(solution)/shard_map/pallas_call | solution.py:391
  537.2 9.7 %shard_map.230 = bf16[2560,320]{1,0:T(8,128)(2,1)S(1)} custom-call(bf16[1536,2560]{1,0:T(8,128)(2,1)} %shard_map.226.a_ref, bf16[1536,320]{1,0:T(8,128)(2,1)S(1)} %copy-done.7), custom_call_target="tpu_custom_call" | custom-call | flops 1000000 | bytes 100000 | tf_op jit(solution)/shard_map/pallas_call | solution.py:486
  546.9 31.5 %shard_map.231 = (f32[320,1536]{1,0:T(8,128)}, f32[160,1536]{1,0:T(8,128)S(1)}) custom-call(s32[4,6]{1,0:T(4,128)S(1)} %get-tuple-element.332.bounds_ref, bf16[320,1536]{1,0:T(8,128)(2,1)S(1)} %slice.424.q_ref, bf16[160,1536]{1,0:T(8,128)(2,1)S(1)} %copy-done.9, s32[1,1536]{1,0:T(1,128)S(1)} %broadcast_in_dim.2.start_ref, ...), custom_call_target="tpu_custom_call" | custom-call | flops 1000000 | bytes 100000 | tf_op jit(solution)/shard_map/pallas_call | solution.py:268
  578.4 7.1 collective-permute-done.57
  592.9 9.6 %shard_map.233 = bf16[2560,512]{1,0:T(8,128)(2,1)S(1)} custom-call(bf16[1536,2560]{1,0:T(8,128)(2,1)} %get-tuple-element.158.a_ref, bf16[1536,512]{1,0:T(8,128)(2,1)S(1)} %shard_map.232.b_ref), custom_call_target="tpu_custom_call" | custom-call | flops 1000000 | bytes 100000 | tf_op jit(solution)/shard_map/pallas_call | solution.py:486
  604.0 5.5 collective-permute-done.58
  620.4 6.9 collective-permute-done.59
  642.7 22.0 %collective-permute-done.61 = bf16[96,2560]{1,0:T(8,128)(2,1)S(1)} collective-permute-done((bf16[96,2560]{1,0:T(8,128)(2,1)S(1)}, bf16[96,2560]{1,0:T(8,128)(2,1)S(1)}, u32[]{:S(2)}, u32[]{:S(2)}) %collective-permute-start.61) | collective-permute-done | bytes 491552 | tf_op jit(solution)/shard_map/ppermute | solution.py:516
  669.6 7.9 %reduce-scatter.9.cloned.1.call-done = bf16[640,512]{1,0:T(8,128)(2,1)} async-done(((bf16[2560,512]{1,0:T(8,128)(2,1)}), bf16[640,512]{1,0:T(8,128)(2,1)}) %reduce-scatter.9.cloned.1.call-update) | async-done | bytes 655376 | tf_op jit(solution)/shard_map/reduce_scatter | solution.py:639
  (441 shorter events, 265.6 us)
Async XLA Ops:
  7.2 91.6 %all-gather.7.cloned.1.call-start = ((), (), s32[]{:S(2)}) async-start(), calls=%async_computation.5 | async-start | bytes 2048000 | tf_op jit(solution)/shard_map/all_gather | solution.py:635
  9.3 97.6 %all-gather.5.cloned.1.call-start = ((), (), s32[]{:S(2)}) async-start(), calls=%async_computation.4 | async-start | bytes 3276800 | tf_op jit(solution)/shard_map/all_gather | solution.py:635
  24.1 246.8 %all-gather.11.cloned.1.call-start = ((), (), s32[]{:S(2)}) async-start(), calls=%async_computation.7 | async-start | bytes 7372800 | tf_op jit(solution)/shard_map/all_gather | solution.py:635
  24.1 23.0 %collective-permute-start = (bf16[192,2560]{1,0:T(8,128)(2,1)S(1)}, bf16[192,2560]{1,0:T(8,128)(2,1)S(1)}, u32[]{:S(2)}, u32[]{:S(2)}) collective-permute-start(bf16[192,2560]{1,0:T(8,128)(2,1)S(1)} %copy-done), channel_id=1, source_target_pairs={{0,2},{2,0},{1,3},{3,1},{4,6},{6,4},{5,7},{7,5},{8,10},{10,8},{9,1... | collective-permute-start | bytes 2949128 | tf_op jit(solution)/shard_map/ppermute | solution.py:516
  25.9 22.8 %collective-permute-start.2 = (bf16[192,2560]{1,0:T(8,128)(2,1)S(1)}, bf16[192,2560]{1,0:T(8,128)(2,1)S(1)}, u32[]{:S(2)}, u32[]{:S(2)}) collective-permute-start(bf16[192,2560]{1,0:T(8,128)(2,1)S(1)} %copy-done), channel_id=1, source_target_pairs={{0,4},{4,0},{1,5},{5,1},{2,6},{6,2},{3,7},{7,3},{8,12},{12,8},{9,1... | collective-permute-start | bytes 2949128 | tf_op jit(solution)/shard_map/ppermute | solution.py:516
  27.4 35.3 %collective-permute-start.5 = (bf16[192,2560]{1,0:T(8,128)(2,1)S(1)}, bf16[192,2560]{1,0:T(8,128)(2,1)S(1)}, u32[]{:S(2)}, u32[]{:S(2)}) collective-permute-start(bf16[192,2560]{1,0:T(8,128)(2,1)S(1)} %copy-done), channel_id=1, source_target_pairs={{0,1},{1,0},{2,3},{3,2},{4,5},{5,4},{6,7},{7,6},{8,9},{9,8},{10,11... | collective-permute-start | bytes 2949128 | tf_op jit(solution)/shard_map/ppermute | solution.py:516
  91.3 276.2 %all-gather.9.cloned.1.call-start = ((), (), s32[]{:S(2)}) async-start(), calls=%async_computation.6 | async-start | bytes 9830400 | tf_op jit(solution)/shard_map/all_gather | solution.py:635
  102.0 23.8 %collective-permute-start.11 = (bf16[1280,320]{0,1:T(8,128)(2,1)}, bf16[1280,320]{0,1:T(8,128)(2,1)S(1)}, u32[]{:S(2)}, u32[]{:S(2)}) collective-permute-start(bf16[1280,320]{0,1:T(8,128)(2,1)} %copy.78), channel_id=1, source_target_pairs={{0,4},{4,0},{1,5},{5,1},{2,6},{6,2},{3,7},{7,3},{8,12},{12,8},{9,1... | collective-permute-start | bytes 2457608 | tf_op jit(solution)/shard_map/ppermute | solution.py:516
  119.1 45.2 %collective-permute-start.16 = (bf16[320,1536]{1,0:T(8,128)(2,1)}, bf16[320,1536]{1,0:T(8,128)(2,1)}, u32[]{:S(2)}, u32[]{:S(2)}) collective-permute-start(bf16[320,1536]{1,0:T(8,128)(2,1)} %broadcast_select_fusion.8), channel_id=1, source_target_pairs={{0,4},{4,0},{1,5},{5,1},{2,6},{6,2},{3,7},{7,3},{8,12},{12,8},{9,1... | collective-permute-start | bytes 2949128 | tf_op jit(solution)/shard_map/ppermute | solution.py:516
  124.1 36.9 %collective-permute-start.12 = (bf16[160,1536]{1,0:T(8,128)(2,1)S(1)}, bf16[160,1536]{1,0:T(8,128)(2,1)S(1)}, u32[]{:S(2)}, u32[]{:S(2)}) collective-permute-start(bf16[160,1536]{1,0:T(8,128)(2,1)S(1)} %slice.425.kv_ref), channel_id=1, source_target_pairs={{0,8},{16,24},{1,9},{17,25},{2,10},{18,26},{3,11},{19,27},{4,12},{... | collective-permute-start | bytes 1474568 | tf_op jit(solution)/shard_map/ppermute | solution.py:512
  125.8 41.7 %collective-permute-start.15 = (bf16[192,2560]{1,0:T(8,128)(2,1)}, bf16[192,2560]{1,0:T(8,128)(2,1)}, u32[]{:S(2)}, u32[]{:S(2)}) collective-permute-start(bf16[192,2560]{1,0:T(8,128)(2,1)} %refs_0_.3), channel_id=1, source_target_pairs={{0,4},{4,0},{1,5},{5,1},{2,6},{6,2},{3,7},{7,3},{8,12},{12,8},{9,1... | collective-permute-start | bytes 2949128 | tf_op jit(solution)/shard_map/ppermute | solution.py:516
  126.7 40.8 %collective-permute-start.14 = (bf16[192,2560]{1,0:T(8,128)(2,1)}, bf16[192,2560]{1,0:T(8,128)(2,1)}, u32[]{:S(2)}, u32[]{:S(2)}) collective-permute-start(bf16[192,2560]{1,0:T(8,128)(2,1)} %refs_0_.3), channel_id=1, source_target_pairs={{0,2},{2,0},{1,3},{3,1},{4,6},{6,4},{5,7},{7,5},{8,10},{10,8},{9,1... | collective-permute-start | bytes 2949128 | tf_op jit(solution)/shard_map/ppermute | solution.py:516
  167.4 333.1 %reduce-scatter.5.cloned.1.call-start = ((), (), s32[]{:S(2)}) async-start(), calls=%async_computation.8 | async-start | bytes 7372800 | tf_op jit(solution)/shard_map/reduce_scatter | solution.py:639
  230.8 31.1 %collective-permute-start.33 = (bf16[192,2560]{1,0:T(8,128)(2,1)S(1)}, bf16[192,2560]{1,0:T(8,128)(2,1)S(1)}, u32[]{:S(2)}, u32[]{:S(2)}) collective-permute-start(bf16[192,2560]{1,0:T(8,128)(2,1)S(1)} %multiply_convert_fusion.refs_0_), channel_id=1, source_target_pairs={{0,1},{1,0},{2,3},{3,2},{4,5},{5,4},{6,7},{7,6},{8,9},{9,8},{10,11... | collective-permute-start | bytes 2949128 | tf_op jit(solution)/shard_map/ppermute | solution.py:516
  367.5 259.7 %reduce-scatter.7.cloned.1.call-start = ((), (), s32[]{:S(2)}) async-start(), calls=%async_computation.9 | async-start | bytes 9830400 | tf_op jit(solution)/shard_map/reduce_scatter | solution.py:639
  427.0 23.5 %collective-permute-start.40 = (bf16[192,2560]{1,0:T(8,128)(2,1)}, bf16[192,2560]{1,0:T(8,128)(2,1)}, u32[]{:S(2)}, u32[]{:S(2)}) collective-permute-start(bf16[192,2560]{1,0:T(8,128)(2,1)} %pad_maximum_fusion.6), channel_id=1, source_target_pairs={{0,2},{2,0},{1,3},{3,1},{4,6},{6,4},{5,7},{7,5},{8,10},{10,8},{9,1... | collective-permute-start | bytes 2949128 | tf_op jit(solution)/shard_map/ppermute | solution.py:516
  428.5 23.2 %collective-permute-start.42 = (bf16[192,2560]{1,0:T(8,128)(2,1)}, bf16[192,2560]{1,0:T(8,128)(2,1)}, u32[]{:S(2)}, u32[]{:S(2)}) collective-permute-start(bf16[192,2560]{1,0:T(8,128)(2,1)} %pad_maximum_fusion.7), channel_id=1, source_target_pairs={{0,4},{4,0},{1,5},{5,1},{2,6},{6,2},{3,7},{7,3},{8,12},{12,8},{9,1... | collective-permute-start | bytes 2949128 | tf_op jit(solution)/shard_map/ppermute | solution.py:516
  451.8 225.7 %reduce-scatter.9.cloned.1.call-start = ((), (), s32[]{:S(2)}) async-start(), calls=%async_computation.10 | async-start | bytes 3276800 | tf_op jit(solution)/shard_map/reduce_scatter | solution.py:639
  452.1 50.8 %collective-permute-start.52 = (bf16[768,2560]{1,0:T(8,128)(2,1)}, bf16[768,2560]{1,0:T(8,128)(2,1)}, u32[]{:S(2)}, u32[]{:S(2)}) collective-permute-start(bf16[768,2560]{1,0:T(8,128)(2,1)} %get-tuple-element.139), channel_id=1, source_target_pairs={{0,1},{1,0},{2,3},{3,2},{4,5},{5,4},{6,7},{7,6},{8,9},{9,8},{10,11... | collective-permute-start | bytes 11796488 | tf_op jit(solution)/shard_map/ppermute | solution.py:516
  460.0 24.3 %collective-permute-start.44 = (bf16[192,2560]{1,0:T(8,128)(2,1)}, bf16[192,2560]{1,0:T(8,128)(2,1)}, u32[]{:S(2)}, u32[]{:S(2)}) collective-permute-start(bf16[192,2560]{1,0:T(8,128)(2,1)} %get-tuple-element.248.refs_0_), channel_id=1, source_target_pairs={{0,4},{4,0},{1,5},{5,1},{2,6},{6,2},{3,7},{7,3},{8,12},{12,8},{9,1... | collective-permute-start | bytes 2949128 | tf_op jit(solution)/shard_map/ppermute | solution.py:516
  461.5 25.4 %collective-permute-start.43 = (bf16[192,2560]{1,0:T(8,128)(2,1)}, bf16[192,2560]{1,0:T(8,128)(2,1)}, u32[]{:S(2)}, u32[]{:S(2)}) collective-permute-start(bf16[192,2560]{1,0:T(8,128)(2,1)} %get-tuple-element.248.refs_0_), channel_id=1, source_target_pairs={{0,2},{2,0},{1,3},{3,1},{4,6},{6,4},{5,7},{7,5},{8,10},{10,8},{9,1... | collective-permute-start | bytes 2949128 | tf_op jit(solution)/shard_map/ppermute | solution.py:516
  527.1 58.3 %collective-permute-start.56 = (bf16[192,2560]{1,0:T(8,128)(2,1)}, bf16[192,2560]{1,0:T(8,128)(2,1)S(1)}, u32[]{:S(2)}, u32[]{:S(2)}) collective-permute-start(bf16[192,2560]{1,0:T(8,128)(2,1)} %get-tuple-element.260), channel_id=1, source_target_pairs={{0,6},{2,4},{4,2},{6,0},{1,7},{3,5},{5,3},{7,1},{8,14},{10,12},{12... | collective-permute-start | bytes 2949128 | tf_op jit(solution)/shard_map/ppermute | solution.py:520
  527.6 57.9 %collective-permute-start.55 = (bf16[192,2560]{1,0:T(8,128)(2,1)}, bf16[192,2560]{1,0:T(8,128)(2,1)S(1)}, u32[]{:S(2)}, u32[]{:S(2)}) collective-permute-start(bf16[192,2560]{1,0:T(8,128)(2,1)} %get-tuple-element.261), channel_id=1, source_target_pairs={{0,4},{4,0},{1,5},{5,1},{2,6},{6,2},{3,7},{7,3},{8,12},{12,8},{9,1... | collective-permute-start | bytes 2949128 | tf_op jit(solution)/shard_map/ppermute | solution.py:516
  529.2 56.2 %collective-permute-start.54 = (bf16[192,2560]{1,0:T(8,128)(2,1)S(1)}, bf16[192,2560]{1,0:T(8,128)(2,1)S(1)}, u32[]{:S(2)}, u32[]{:S(2)}) collective-permute-start(bf16[192,2560]{1,0:T(8,128)(2,1)S(1)} %get-tuple-element.262), channel_id=1, source_target_pairs={{0,2},{2,0},{1,3},{3,1},{4,6},{6,4},{5,7},{7,5},{8,10},{10,8},{9,1... | collective-permute-start | bytes 2949128 | tf_op jit(solution)/shard_map/ppermute | solution.py:516
  535.5 50.0 %collective-permute-start.57 = (bf16[160,1536]{1,0:T(8,128)(2,1)S(1)}, bf16[160,1536]{1,0:T(8,128)(2,1)S(1)}, u32[]{:S(2)}, u32[]{:S(2)}) collective-permute-start(bf16[160,1536]{1,0:T(8,128)(2,1)S(1)} %convert_element_type.291), channel_id=1, source_target_pairs={{8,0},{24,16},{9,1},{25,17},{10,2},{26,18},{11,3},{27,19},{12,4},{... | collective-permute-start | bytes 1474568 | tf_op jit(solution)/shard_map/ppermute | solution.py:512
  627.3 99.2 %reduce-scatter.11.cloned.1.call-start = ((), (), s32[]{:S(2)}) async-start(), calls=%async_computation.11 | async-start | bytes 2048000 | tf_op jit(solution)/shard_map/reduce_scatter | solution.py:639
  630.3 34.3 %collective-permute-start.62 = (bf16[320,1536]{1,0:T(8,128)(2,1)S(1)}, bf16[320,1536]{1,0:T(8,128)(2,1)S(1)}, u32[]{:S(2)}, u32[]{:S(2)}) collective-permute-start(bf16[320,1536]{1,0:T(8,128)(2,1)S(1)} %get-tuple-element.284), channel_id=1, source_target_pairs={{0,4},{4,0},{1,5},{5,1},{2,6},{6,2},{3,7},{7,3},{8,12},{12,8},{9,1... | collective-permute-start | bytes 2949128 | tf_op jit(solution)/shard_map/ppermute | solution.py:516
  636.5 28.1 %collective-permute-start.61 = (bf16[96,2560]{1,0:T(8,128)(2,1)S(1)}, bf16[96,2560]{1,0:T(8,128)(2,1)S(1)}, u32[]{:S(2)}, u32[]{:S(2)}) collective-permute-start(bf16[96,2560]{1,0:T(8,128)(2,1)S(1)} %get-tuple-element.257), channel_id=1, source_target_pairs={{0,4},{4,0},{1,5},{5,1},{2,6},{6,2},{3,7},{7,3},{8,12},{12,8},{9,1... | collective-permute-start | bytes 1474568 | tf_op jit(solution)/shard_map/ppermute | solution.py:516
  637.5 27.1 %collective-permute-start.60 = (bf16[96,2560]{1,0:T(8,128)(2,1)S(1)}, bf16[96,2560]{1,0:T(8,128)(2,1)S(1)}, u32[]{:S(2)}, u32[]{:S(2)}) collective-permute-start(bf16[96,2560]{1,0:T(8,128)(2,1)S(1)} %get-tuple-element.258), channel_id=1, source_target_pairs={{0,2},{2,0},{1,3},{3,1},{4,6},{6,4},{5,7},{7,5},{8,10},{10,8},{9,1... | collective-permute-start | bytes 1474568 | tf_op jit(solution)/shard_map/ppermute | solution.py:516
  665.9 23.3 %collective-permute-start.63 = (bf16[192,2560]{1,0:T(8,128)(2,1)}, bf16[192,2560]{1,0:T(8,128)(2,1)S(1)}, u32[]{:S(2)}, u32[]{:S(2)}) collective-permute-start(bf16[192,2560]{1,0:T(8,128)(2,1)} %pad_maximum_fusion.8), channel_id=1, source_target_pairs={{0,2},{2,0},{1,3},{3,1},{4,6},{6,4},{5,7},{7,5},{8,10},{10,8},{9,1... | collective-permute-start | bytes 2949128 | tf_op jit(solution)/shard_map/ppermute | solution.py:516
  668.4 24.9 %collective-permute-start.64 = (bf16[192,2560]{1,0:T(8,128)(2,1)}, bf16[192,2560]{1,0:T(8,128)(2,1)S(1)}, u32[]{:S(2)}, u32[]{:S(2)}) collective-permute-start(bf16[192,2560]{1,0:T(8,128)(2,1)} %pad_maximum_fusion.9), channel_id=1, source_target_pairs={{0,4},{4,0},{1,5},{5,1},{2,6},{6,2},{3,7},{7,3},{8,12},{12,8},{9,1... | collective-permute-start | bytes 2949128 | tf_op jit(solution)/shard_map/ppermute | solution.py:516
  682.7 35.1 %collective-permute-start.65 = (bf16[320,512]{1,0:T(8,128)(2,1)}, bf16[320,512]{1,0:T(8,128)(2,1)}, u32[]{:S(2)}, u32[]{:S(2)}) collective-permute-start(bf16[320,512]{1,0:T(8,128)(2,1)} %broadcast_select_fusion.25), channel_id=1, source_target_pairs={{0,4},{4,0},{1,5},{5,1},{2,6},{6,2},{3,7},{7,3},{8,12},{12,8},{9,1... | collective-permute-start | bytes 983048 | tf_op jit(solution)/shard_map/ppermute | solution.py:516
  (121 other events, 991.9 us)
Sparse Core Ops, SparseCore 0:
  10.2 40.8 all-gather.6
  53.2 53.6 all-gather.4
  108.5 113.8 all-gather.10
  224.4 143.0 all-gather.8
  369.7 102.5 reduce-scatter.4
  474.5 147.2 reduce-scatter.6
  627.4 49.9 reduce-scatter.8
  680.8 35.9 reduce-scatter.10

commit v8 on v6

--- a/solution.py
+++ b/solution.py
@@ -851,7 +851,8 @@
     one_far = plane_sum_one(one_total)
     one_far = landed(one_far, (owned[1], "got"))
     one_near = plane_sum_two(one_total, *one_far)
-    out_grad = sum_z(tied(out_term, qkv_grad))
+    qkv_raw = qkv_grad
+    out_grad = sum_z(tied(out_term, qkv_raw))
     owned_a = Unshare(qkv_grad, first_y)
     *one_near, qkv_grad = together(*one_near, qkv_grad)
     grad_h_one = added(one_total, *one_near)
@@ -864,17 +865,15 @@
     kept = [CHUNK, nf - CHUNK]
     width = [full.shape[1] // 3 for full in full_c]
 
-    def unit_columns(k):
-        return jnp.concatenate(
-            [
-                owned[j][i][:, k * width[j] : k * width[j] + kept[j]]
-                for i in range(2)
-                for j in range(2)
-            ],
-            axis=1,
-        ).astype(F32)
-
-    down_out, gate_out, up_out = unit_columns(0).T, unit_columns(1), unit_columns(2)
+    def unit_columns(k, *after):
+        parts = [
+            owned[j][i][:, k * width[j] : k * width[j] + kept[j]] for i in range(2) for j in range(2)
+        ]
+        if after:
+            parts = lax.optimization_barrier((parts, after))[0]
+        return jnp.concatenate(parts, axis=1).astype(F32)
+
+    down_out, gate_out, up_out = unit_columns(0, qkv_raw).T, unit_columns(1), unit_columns(2)
     one, two = owned_a.both()
     pick = lambda a, b: jnp.concatenate([one[:, a:b], two[:, a:b]], axis=1).astype(F32)
     q_out, k_out, v_out = pick(0, nq), pick(nq, nq + nk), pick(nq + nk, nq + 2 * nk)

time: 738 us -> 733 us (level)
  no operation moved by 1% of the time
where the time goes in v8:
time: 733 us; the launch traced here: 726 us
  waiting for transfers between devices  266 us (36%)
  Pallas kernels  241 us (33%)
  other arithmetic  76.1 us (10%)
  starting transfers between devices  56.5 us (8%)
  local copies, waits for them, and re-layouts  52.8 us (7%)
  matrix products  17.8 us (2%)
  between operations  15.9 us (2%)
    ppermute x62, waiting for transfers between devices, over(): return lax.ppermute(block, axis, SWAP)  211 us
    pallas_call x4, Pallas kernels, hidden_units(): pl.pallas_call(functools.partial(units_kernel, bool(prior)), grid=(count...  75.5 us
    ppermute x62, starting transfers between devices, over(): return lax.ppermute(block, axis, SWAP)  48.9 us
    all_gather x4, waiting for transfers between devices, gather_z(): return lax.all_gather(block, 'z', axis=0, tiled=True)  38.2 us
    pallas_call x2, Pallas kernels, attend_back(): pl.pallas_call(functools.partial(attend_back_kernel, places), grid_spec=p...  36.3 us
    pallas_call x2, Pallas kernels, unit_grads(): pl.pallas_call(unit_grads_kernel, grid=(model // rows,), in_specs=[pl.Blo...  34 us
    pallas_call x2, Pallas kernels, attend(): pl.pallas_call(functools.partial(attend_kernel, places), grid_spec=pltpu....  28.8 us
    pallas_call x4, Pallas kernels, join(): pl.pallas_call(join_kernel, in_specs=[ANY] * len(parts), out_specs=ANY, o...  24.7 us
  transfers between devices with their start and end apart: 76, of which 34 were waited for; matrix products, arithmetic and copies ran while one was open for 17% of the time, Pallas kernels for 33%

profile of v8, /device:TPU:0, one launch (start us, length us, event | category | flops | bytes accessed | tf_op | source)
XLA Modules:
  0.0 726.3 jit_solution(17331937818672389906)
XLA Ops:
  15.3 7.7 %collective-permute-done.1 = bf16[320,512]{1,0:T(8,128)(2,1)S(1)} collective-permute-done((bf16[320,512]{1,0:T(8,128)(2,1)S(1)}, bf16[320,512]{1,0:T(8,128)(2,1)S(1)}, u32[]{:S(2)}, u32[]{:S(2)}) %collective-permute-start.1) | collective-permute-done | bytes 327712 | tf_op jit(solution)/shard_map/ppermute | solution.py:516
  27.4 19.7 %collective-permute-done.refs_1_ = bf16[192,2560]{1,0:T(8,128)(2,1)S(1)} collective-permute-done((bf16[192,2560]{1,0:T(8,128)(2,1)S(1)}, bf16[192,2560]{1,0:T(8,128)(2,1)S(1)}, u32[]{:S(2)}, u32[]{:S(2)}) %collective-permute-start) | collective-permute-done | bytes 983072 | tf_op jit(solution)/shard_map/ppermute | solution.py:516
  65.2 5.8 shard_map.212.x_ref
  71.7 17.9 %collective-permute-done.13 = bf16[320,1152]{1,0:T(8,128)(2,1)S(1)} collective-permute-done((bf16[320,1152]{1,0:T(8,128)(2,1)S(1)}, bf16[320,1152]{1,0:T(8,128)(2,1)S(1)}, u32[]{:S(2)}, u32[]{:S(2)}) %collective-permute-start.13) | collective-permute-done | bytes 737312 | tf_op jit(solution)/shard_map/ppermute | solution.py:516
  109.5 9.6 %shard_map.213 = (bf16[1536,2560]{1,0:T(8,128)(2,1)}, f32[1536,512]{1,0:T(8,128)S(1)}) custom-call(bf16[1536,2560]{1,0:T(8,128)(2,1)} %shard_map.212.x_ref, f32[1,2560]{1,0:T(1,128)S(1)} %broadcast_in_dim_squeeze.2.gain_ref, bf16[2560,512]{1,0:T(8,128)(2,1)S(1)} %copy-done.11), custom_call_target="tpu_custom_call" | custom-call | flops 1000000 | bytes 100000 | tf_op jit(solution)/shard_map/pallas_call | solution.py:360
  133.7 27.2 %shard_map.215 = (f32[320,1536]{1,0:T(8,128)S(1)}, f32[8,1536]{1,0:T(8,128)S(1)}) custom-call(s32[4,6]{1,0:T(4,128)S(1)} %get-tuple-element.322.bounds_ref, bf16[320,1536]{1,0:T(8,128)(2,1)S(1)} %slice.424.q_ref, bf16[160,1536]{1,0:T(8,128)(2,1)S(1)} %slice.425.kv_ref, s32[1,1536]{1,0:T(1,128)S(1)} %broadcast_in_dim.2.start_ref), custom_call_target="tpu_custom_call" | custom-call | flops 1000000 | bytes 100000 | tf_op jit(solution)/shard_map/pallas_call | solution.py:177
  180.2 4.9 add_convert_fusion.3
  191.9 11.3 %collective-permute-done.22 = bf16[96,2560]{1,0:T(8,128)(2,1)S(1)} collective-permute-done((bf16[96,2560]{1,0:T(8,128)(2,1)S(1)}, bf16[96,2560]{1,0:T(8,128)(2,1)S(1)}, u32[]{:S(2)}, u32[]{:S(2)}) %collective-permute-start.22) | collective-permute-done | bytes 491552 | tf_op jit(solution)/shard_map/ppermute | solution.py:516
  206.2 19.7 %collective-permute-done.23 = bf16[192,2560]{1,0:T(8,128)(2,1)S(1)} collective-permute-done((bf16[192,2560]{1,0:T(8,128)(2,1)S(1)}, bf16[192,2560]{1,0:T(8,128)(2,1)S(1)}, u32[]{:S(2)}, u32[]{:S(2)}) %collective-permute-start.23) | collective-permute-done | bytes 983072 | tf_op jit(solution)/shard_map/ppermute | solution.py:516
  232.2 17.7 %collective-permute-done.25.refs_2_ = bf16[192,2560]{1,0:T(8,128)(2,1)S(1)} collective-permute-done((bf16[192,2560]{1,0:T(8,128)(2,1)S(1)}, bf16[192,2560]{1,0:T(8,128)(2,1)S(1)}, u32[]{:S(2)}, u32[]{:S(2)}) %collective-permute-start.25) | collective-permute-done | bytes 983072 | tf_op jit(solution)/shard_map/ppermute | solution.py:516
  254.3 10.5 %collective-permute-done.26.refs_3_ = bf16[96,2560]{1,0:T(8,128)(2,1)S(1)} collective-permute-done((bf16[96,2560]{1,0:T(8,128)(2,1)S(1)}, bf16[96,2560]{1,0:T(8,128)(2,1)S(1)}, u32[]{:S(2)}, u32[]{:S(2)}) %collective-permute-start.26) | collective-permute-done | bytes 491552 | tf_op jit(solution)/shard_map/ppermute | solution.py:516
  265.9 5.4 shard_map.219.cot_ref
  271.3 5.8 shard_map.218.h_ref
  277.1 17.8 %shard_map.221 = (bf16[768,1152]{1,0:T(8,128)(2,1)S(1)}, bf16[768,2560]{1,0:T(8,128)(2,1)S(1)}, bf16[768,2560]{1,0:T(8,128)(2,1)}) custom-call(bf16[1536,2560]{1,0:T(8,128)(2,1)} %shard_map.218.h_ref, bf16[1536,2560]{1,0:T(8,128)(2,1)} %shard_map.219.cot_ref, bf16[2560,1152]{1,0:T(8,128)(2,1)} %all-gather.11.cloned.1.call-done.weight_ref), custom_call_target="tpu_custom_call" | custom-call | flops 1000000 | bytes 100000 | tf_op jit(solution)/shard_map/pallas_call | solution.py:430
  296.9 17.8 %shard_map.220 = (bf16[768,1152]{1,0:T(8,128)(2,1)S(1)}, bf16[768,2560]{1,0:T(8,128)(2,1)S(1)}, bf16[768,2560]{1,0:T(8,128)(2,1)}) custom-call(bf16[1536,2560]{1,0:T(8,128)(2,1)} %shard_map.218.h_ref, bf16[1536,2560]{1,0:T(8,128)(2,1)} %shard_map.219.cot_ref, bf16[2560,1152]{1,0:T(8,128)(2,1)} %all-gather.11.cloned.1.call-done.weight_ref), custom_call_target="tpu_custom_call" | custom-call | flops 1000000 | bytes 100000 | tf_op jit(solution)/shard_map/pallas_call | solution.py:430
  316.6 16.3 %shard_map.222 = bf16[2560,1152]{1,0:T(8,128)(2,1)} custom-call(bf16[1536,2560]{1,0:T(8,128)(2,1)} %shard_map.218.h_ref, bf16[1536,2560]{1,0:T(8,128)(2,1)} %shard_map.219.cot_ref, bf16[768,1152]{1,0:T(8,128)(2,1)S(1)} %get-tuple-element.118.mine_ref, bf16[768,1152]{1,0:T(8,128)(2,1)S(1)} %get-tuple-element.115.other_ref), custom_call_target="tpu_custom_call" | custom-call | flops 1000000 | bytes 100000 | tf_op jit(solution)/shard_map/pallas_call | solution.py:455
  332.9 34.6 %all-gather.9.cloned.1.call-done.weight_ref = bf16[2560,1536]{1,0:T(8,128)(2,1)} async-done(((bf16[640,1536]{1,0:T(8,128)(2,1)}), bf16[2560,1536]{1,0:T(8,128)(2,1)}) %all-gather.9.cloned.1.call-update) | async-done | bytes 7864336 | tf_op jit(solution)/shard_map/all_gather | solution.py:635
  367.6 19.9 %shard_map.224 = (bf16[768,1536]{1,0:T(8,128)(2,1)S(1)}, bf16[768,2560]{1,0:T(8,128)(2,1)}, bf16[768,2560]{1,0:T(8,128)(2,1)}) custom-call(bf16[1536,2560]{1,0:T(8,128)(2,1)} %shard_map.218.h_ref, bf16[1536,2560]{1,0:T(8,128)(2,1)} %shard_map.219.cot_ref, bf16[2560,1536]{1,0:T(8,128)(2,1)} %all-gather.9.cloned.1.call-done.weight_ref, ...), custom_call_target="tpu_custom_call" | custom-call | flops 1000000 | bytes 100000 | tf_op jit(solution)/shard_map/pallas_call | solution.py:430
  387.5 20.0 %shard_map.223 = (bf16[768,1536]{1,0:T(8,128)(2,1)S(1)}, bf16[768,2560]{1,0:T(8,128)(2,1)}, bf16[768,2560]{1,0:T(8,128)(2,1)}) custom-call(bf16[1536,2560]{1,0:T(8,128)(2,1)} %shard_map.218.h_ref, bf16[1536,2560]{1,0:T(8,128)(2,1)} %shard_map.219.cot_ref, bf16[2560,1536]{1,0:T(8,128)(2,1)} %all-gather.9.cloned.1.call-done.weight_ref, ...), custom_call_target="tpu_custom_call" | custom-call | flops 1000000 | bytes 100000 | tf_op jit(solution)/shard_map/pallas_call | solution.py:430
  413.9 10.7 %collective-permute-done.41 = bf16[96,2560]{1,0:T(8,128)(2,1)S(1)} collective-permute-done((bf16[96,2560]{1,0:T(8,128)(2,1)S(1)}, bf16[96,2560]{1,0:T(8,128)(2,1)S(1)}, u32[]{:S(2)}, u32[]{:S(2)}) %collective-permute-start.41) | collective-permute-done | bytes 491552 | tf_op jit(solution)/shard_map/ppermute | solution.py:516
  430.0 17.7 %shard_map.225 = bf16[2560,1536]{1,0:T(8,128)(2,1)} custom-call(bf16[1536,2560]{1,0:T(8,128)(2,1)} %shard_map.218.h_ref, bf16[1536,2560]{1,0:T(8,128)(2,1)} %shard_map.219.cot_ref, bf16[768,1536]{1,0:T(8,128)(2,1)S(1)} %get-tuple-element.128.mine_ref, bf16[768,1536]{1,0:T(8,128)(2,1)S(1)} %get-tuple-element.129.other_ref), custom_call_target="tpu_custom_call" | custom-call | flops 1000000 | bytes 100000 | tf_op jit(solution)/shard_map/pallas_call | solution.py:455
  462.9 21.4 %collective-permute-done.44.refs_2_ = bf16[192,2560]{1,0:T(8,128)(2,1)} collective-permute-done((bf16[192,2560]{1,0:T(8,128)(2,1)}, bf16[192,2560]{1,0:T(8,128)(2,1)}, u32[]{:S(2)}, u32[]{:S(2)}) %collective-permute-start.44) | collective-permute-done | bytes 983072 | tf_op jit(solution)/shard_map/ppermute | solution.py:516
  490.0 8.2 %collective-permute-done.45.refs_3_ = bf16[96,2560]{1,0:T(8,128)(2,1)} collective-permute-done((bf16[96,2560]{1,0:T(8,128)(2,1)S(1)}, bf16[96,2560]{1,0:T(8,128)(2,1)}, u32[]{:S(2)}, u32[]{:S(2)}) %collective-permute-start.45) | collective-permute-done | bytes 491552 | tf_op jit(solution)/shard_map/ppermute | solution.py:516
  508.6 7.7 %shard_map.226.a_ref = bf16[1536,2560]{1,0:T(8,128)(2,1)} custom-call(bf16[192,2560]{1,0:T(8,128)(2,1)} %get-tuple-element.242.refs_0_, bf16[192,2560]{1,0:T(8,128)(2,1)} %collective-permute-done.43.refs_1_, bf16[192,2560]{1,0:T(8,128)(2,1)} %collective-permute-done.44.refs_2_, bf16[96,2560]{1,0:T(8,128)(2,1)} %collective-permute-done.45.refs_3_, ...), custom_call_target="tpu_custom_call" | custom-call | flops 1000000 | bytes 100000 | tf_op jit(solution)/shard_map/pallas_call | solution.py:335
  516.3 7.6 %shard_map.227.rows_ref = bf16[1536,320]{1,0:T(8,128)(2,1)S(1)} custom-call(bf16[1536,2560]{1,0:T(8,128)(2,1)} %shard_map.226.a_ref, bf16[2560,320]{1,0:T(8,128)(2,1)S(1)} %bitcast.57), custom_call_target="tpu_custom_call" | custom-call | flops 1000000 | bytes 100000 | tf_op jit(solution)/shard_map/pallas_call | solution.py:391
  529.8 4.8 shard_map.229
  536.4 9.7 %shard_map.230 = bf16[2560,320]{1,0:T(8,128)(2,1)S(1)} custom-call(bf16[1536,2560]{1,0:T(8,128)(2,1)} %shard_map.226.a_ref, bf16[1536,320]{1,0:T(8,128)(2,1)S(1)} %copy-done.8), custom_call_target="tpu_custom_call" | custom-call | flops 1000000 | bytes 100000 | tf_op jit(solution)/shard_map/pallas_call | solution.py:486
  546.1 31.5 %shard_map.231 = (f32[320,1536]{1,0:T(8,128)}, f32[160,1536]{1,0:T(8,128)S(1)}) custom-call(s32[4,6]{1,0:T(4,128)S(1)} %get-tuple-element.322.bounds_ref, bf16[320,1536]{1,0:T(8,128)(2,1)S(1)} %slice.424.q_ref, bf16[160,1536]{1,0:T(8,128)(2,1)S(1)} %copy-done.10, s32[1,1536]{1,0:T(1,128)S(1)} %broadcast_in_dim.2.start_ref, ...), custom_call_target="tpu_custom_call" | custom-call | flops 1000000 | bytes 100000 | tf_op jit(solution)/shard_map/pallas_call | solution.py:268
  577.6 10.1 %collective-permute-done.57 = bf16[160,1536]{1,0:T(8,128)(2,1)S(1)} collective-permute-done((bf16[160,1536]{1,0:T(8,128)(2,1)S(1)}, bf16[160,1536]{1,0:T(8,128)(2,1)S(1)}, u32[]{:S(2)}, u32[]{:S(2)}) %collective-permute-start.57) | collective-permute-done | bytes 491552 | tf_op jit(solution)/shard_map/ppermute | solution.py:512
  594.2 9.6 %shard_map.233 = bf16[2560,512]{1,0:T(8,128)(2,1)S(1)} custom-call(bf16[1536,2560]{1,0:T(8,128)(2,1)} %get-tuple-element.152.a_ref, bf16[1536,512]{1,0:T(8,128)(2,1)S(1)} %shard_map.232.b_ref), custom_call_target="tpu_custom_call" | custom-call | flops 1000000 | bytes 100000 | tf_op jit(solution)/shard_map/pallas_call | solution.py:486
  641.4 22.9 %collective-permute-done.61 = bf16[96,2560]{1,0:T(8,128)(2,1)S(1)} collective-permute-done((bf16[96,2560]{1,0:T(8,128)(2,1)S(1)}, bf16[96,2560]{1,0:T(8,128)(2,1)S(1)}, u32[]{:S(2)}, u32[]{:S(2)}) %collective-permute-start.61) | collective-permute-done | bytes 491552 | tf_op jit(solution)/shard_map/ppermute | solution.py:516
  711.3 4.8 reduce-scatter.11.cloned.1.call-done.a_ref
  (443 shorter events, 254.2 us)
Async XLA Ops:
  7.2 91.6 %all-gather.7.cloned.1.call-start = ((), (), s32[]{:S(2)}) async-start(), calls=%async_computation.5 | async-start | bytes 2048000 | tf_op jit(solution)/shard_map/all_gather | solution.py:635
  9.3 97.6 %all-gather.5.cloned.1.call-start = ((), (), s32[]{:S(2)}) async-start(), calls=%async_computation.4 | async-start | bytes 3276800 | tf_op jit(solution)/shard_map/all_gather | solution.py:635
  24.1 253.0 %all-gather.11.cloned.1.call-start = ((), (), s32[]{:S(2)}) async-start(), calls=%async_computation.7 | async-start | bytes 7372800 | tf_op jit(solution)/shard_map/all_gather | solution.py:635
  24.1 23.0 %collective-permute-start = (bf16[192,2560]{1,0:T(8,128)(2,1)S(1)}, bf16[192,2560]{1,0:T(8,128)(2,1)S(1)}, u32[]{:S(2)}, u32[]{:S(2)}) collective-permute-start(bf16[192,2560]{1,0:T(8,128)(2,1)S(1)} %copy-done), channel_id=1, source_target_pairs={{0,2},{2,0},{1,3},{3,1},{4,6},{6,4},{5,7},{7,5},{8,10},{10,8},{9,1... | collective-permute-start | bytes 2949128 | tf_op jit(solution)/shard_map/ppermute | solution.py:516
  25.9 22.8 %collective-permute-start.2 = (bf16[192,2560]{1,0:T(8,128)(2,1)S(1)}, bf16[192,2560]{1,0:T(8,128)(2,1)S(1)}, u32[]{:S(2)}, u32[]{:S(2)}) collective-permute-start(bf16[192,2560]{1,0:T(8,128)(2,1)S(1)} %copy-done), channel_id=1, source_target_pairs={{0,4},{4,0},{1,5},{5,1},{2,6},{6,2},{3,7},{7,3},{8,12},{12,8},{9,1... | collective-permute-start | bytes 2949128 | tf_op jit(solution)/shard_map/ppermute | solution.py:516
  27.4 35.3 %collective-permute-start.5 = (bf16[192,2560]{1,0:T(8,128)(2,1)S(1)}, bf16[192,2560]{1,0:T(8,128)(2,1)S(1)}, u32[]{:S(2)}, u32[]{:S(2)}) collective-permute-start(bf16[192,2560]{1,0:T(8,128)(2,1)S(1)} %copy-done), channel_id=1, source_target_pairs={{0,1},{1,0},{2,3},{3,2},{4,5},{5,4},{6,7},{7,6},{8,9},{9,8},{10,11... | collective-permute-start | bytes 2949128 | tf_op jit(solution)/shard_map/ppermute | solution.py:516
  91.3 276.2 %all-gather.9.cloned.1.call-start = ((), (), s32[]{:S(2)}) async-start(), calls=%async_computation.6 | async-start | bytes 9830400 | tf_op jit(solution)/shard_map/all_gather | solution.py:635
  101.9 23.8 %collective-permute-start.11 = (bf16[1280,320]{0,1:T(8,128)(2,1)}, bf16[1280,320]{0,1:T(8,128)(2,1)S(1)}, u32[]{:S(2)}, u32[]{:S(2)}) collective-permute-start(bf16[1280,320]{0,1:T(8,128)(2,1)} %copy.78), channel_id=1, source_target_pairs={{0,4},{4,0},{1,5},{5,1},{2,6},{6,2},{3,7},{7,3},{8,12},{12,8},{9,1... | collective-permute-start | bytes 2457608 | tf_op jit(solution)/shard_map/ppermute | solution.py:516
  119.1 45.2 %collective-permute-start.16 = (bf16[320,1536]{1,0:T(8,128)(2,1)}, bf16[320,1536]{1,0:T(8,128)(2,1)}, u32[]{:S(2)}, u32[]{:S(2)}) collective-permute-start(bf16[320,1536]{1,0:T(8,128)(2,1)} %broadcast_select_fusion.8), channel_id=1, source_target_pairs={{0,4},{4,0},{1,5},{5,1},{2,6},{6,2},{3,7},{7,3},{8,12},{12,8},{9,1... | collective-permute-start | bytes 2949128 | tf_op jit(solution)/shard_map/ppermute | solution.py:516
  124.1 36.9 %collective-permute-start.12 = (bf16[160,1536]{1,0:T(8,128)(2,1)S(1)}, bf16[160,1536]{1,0:T(8,128)(2,1)S(1)}, u32[]{:S(2)}, u32[]{:S(2)}) collective-permute-start(bf16[160,1536]{1,0:T(8,128)(2,1)S(1)} %slice.425.kv_ref), channel_id=1, source_target_pairs={{0,8},{16,24},{1,9},{17,25},{2,10},{18,26},{3,11},{19,27},{4,12},{... | collective-permute-start | bytes 1474568 | tf_op jit(solution)/shard_map/ppermute | solution.py:512
  125.8 41.6 %collective-permute-start.15 = (bf16[192,2560]{1,0:T(8,128)(2,1)}, bf16[192,2560]{1,0:T(8,128)(2,1)}, u32[]{:S(2)}, u32[]{:S(2)}) collective-permute-start(bf16[192,2560]{1,0:T(8,128)(2,1)} %refs_0_.3), channel_id=1, source_target_pairs={{0,4},{4,0},{1,5},{5,1},{2,6},{6,2},{3,7},{7,3},{8,12},{12,8},{9,1... | collective-permute-start | bytes 2949128 | tf_op jit(solution)/shard_map/ppermute | solution.py:516
  126.7 40.7 %collective-permute-start.14 = (bf16[192,2560]{1,0:T(8,128)(2,1)}, bf16[192,2560]{1,0:T(8,128)(2,1)}, u32[]{:S(2)}, u32[]{:S(2)}) collective-permute-start(bf16[192,2560]{1,0:T(8,128)(2,1)} %refs_0_.3), channel_id=1, source_target_pairs={{0,2},{2,0},{1,3},{3,1},{4,6},{6,4},{5,7},{7,5},{8,10},{10,8},{9,1... | collective-permute-start | bytes 2949128 | tf_op jit(solution)/shard_map/ppermute | solution.py:516
  173.1 327.4 %reduce-scatter.5.cloned.1.call-start = ((), (), s32[]{:S(2)}) async-start(), calls=%async_computation.8 | async-start | bytes 7372800 | tf_op jit(solution)/shard_map/reduce_scatter | solution.py:639
  203.7 22.2 %collective-permute-start.23 = (bf16[192,2560]{1,0:T(8,128)(2,1)S(1)}, bf16[192,2560]{1,0:T(8,128)(2,1)S(1)}, u32[]{:S(2)}, u32[]{:S(2)}) collective-permute-start(bf16[192,2560]{1,0:T(8,128)(2,1)S(1)} %pad_maximum_fusion.5), channel_id=1, source_target_pairs={{0,4},{4,0},{1,5},{5,1},{2,6},{6,2},{3,7},{7,3},{8,12},{12,8},{9,1... | collective-permute-start | bytes 2949128 | tf_op jit(solution)/shard_map/ppermute | solution.py:516
  367.5 260.3 %reduce-scatter.7.cloned.1.call-start = ((), (), s32[]{:S(2)}) async-start(), calls=%async_computation.9 | async-start | bytes 9830400 | tf_op jit(solution)/shard_map/reduce_scatter | solution.py:639
  427.0 23.5 %collective-permute-start.40 = (bf16[192,2560]{1,0:T(8,128)(2,1)}, bf16[192,2560]{1,0:T(8,128)(2,1)}, u32[]{:S(2)}, u32[]{:S(2)}) collective-permute-start(bf16[192,2560]{1,0:T(8,128)(2,1)} %pad_maximum_fusion.6), channel_id=1, source_target_pairs={{0,2},{2,0},{1,3},{3,1},{4,6},{6,4},{5,7},{7,5},{8,10},{10,8},{9,1... | collective-permute-start | bytes 2949128 | tf_op jit(solution)/shard_map/ppermute | solution.py:516
  428.5 23.2 %collective-permute-start.42 = (bf16[192,2560]{1,0:T(8,128)(2,1)}, bf16[192,2560]{1,0:T(8,128)(2,1)}, u32[]{:S(2)}, u32[]{:S(2)}) collective-permute-start(bf16[192,2560]{1,0:T(8,128)(2,1)} %pad_maximum_fusion.7), channel_id=1, source_target_pairs={{0,4},{4,0},{1,5},{5,1},{2,6},{6,2},{3,7},{7,3},{8,12},{12,8},{9,1... | collective-permute-start | bytes 2949128 | tf_op jit(solution)/shard_map/ppermute | solution.py:516
  451.8 228.9 %reduce-scatter.9.cloned.1.call-start = ((), (), s32[]{:S(2)}) async-start(), calls=%async_computation.10 | async-start | bytes 3276800 | tf_op jit(solution)/shard_map/reduce_scatter | solution.py:639
  452.1 49.9 %collective-permute-start.52 = (bf16[768,2560]{1,0:T(8,128)(2,1)}, bf16[768,2560]{1,0:T(8,128)(2,1)}, u32[]{:S(2)}, u32[]{:S(2)}) collective-permute-start(bf16[768,2560]{1,0:T(8,128)(2,1)} %get-tuple-element.133), channel_id=1, source_target_pairs={{0,1},{1,0},{2,3},{3,2},{4,5},{5,4},{6,7},{7,6},{8,9},{9,8},{10,11... | collective-permute-start | bytes 11796488 | tf_op jit(solution)/shard_map/ppermute | solution.py:516
  460.0 24.3 %collective-permute-start.44 = (bf16[192,2560]{1,0:T(8,128)(2,1)}, bf16[192,2560]{1,0:T(8,128)(2,1)}, u32[]{:S(2)}, u32[]{:S(2)}) collective-permute-start(bf16[192,2560]{1,0:T(8,128)(2,1)} %get-tuple-element.242.refs_0_), channel_id=1, source_target_pairs={{0,4},{4,0},{1,5},{5,1},{2,6},{6,2},{3,7},{7,3},{8,12},{12,8},{9,1... | collective-permute-start | bytes 2949128 | tf_op jit(solution)/shard_map/ppermute | solution.py:516
  461.5 25.4 %collective-permute-start.43 = (bf16[192,2560]{1,0:T(8,128)(2,1)}, bf16[192,2560]{1,0:T(8,128)(2,1)}, u32[]{:S(2)}, u32[]{:S(2)}) collective-permute-start(bf16[192,2560]{1,0:T(8,128)(2,1)} %get-tuple-element.242.refs_0_), channel_id=1, source_target_pairs={{0,2},{2,0},{1,3},{3,1},{4,6},{6,4},{5,7},{7,5},{8,10},{10,8},{9,1... | collective-permute-start | bytes 2949128 | tf_op jit(solution)/shard_map/ppermute | solution.py:516
  502.5 22.4 %collective-permute-start.53 = (bf16[320,1152]{1,0:T(8,128)(2,1)S(1)}, bf16[320,1152]{1,0:T(8,128)(2,1)}, u32[]{:S(2)}, u32[]{:S(2)}) collective-permute-start(bf16[320,1152]{1,0:T(8,128)(2,1)S(1)} %broadcast_select_fusion.17), channel_id=1, source_target_pairs={{0,4},{4,0},{1,5},{5,1},{2,6},{6,2},{3,7},{7,3},{8,12},{12,8},{9,1... | collective-permute-start | bytes 2211848 | tf_op jit(solution)/shard_map/ppermute | solution.py:516
  526.4 61.4 %collective-permute-start.56 = (bf16[192,2560]{1,0:T(8,128)(2,1)}, bf16[192,2560]{1,0:T(8,128)(2,1)S(1)}, u32[]{:S(2)}, u32[]{:S(2)}) collective-permute-start(bf16[192,2560]{1,0:T(8,128)(2,1)} %get-tuple-element.254), channel_id=1, source_target_pairs={{0,6},{2,4},{4,2},{6,0},{1,7},{3,5},{5,3},{7,1},{8,14},{10,12},{12... | collective-permute-start | bytes 2949128 | tf_op jit(solution)/shard_map/ppermute | solution.py:520
  526.7 61.0 %collective-permute-start.55 = (bf16[192,2560]{1,0:T(8,128)(2,1)}, bf16[192,2560]{1,0:T(8,128)(2,1)S(1)}, u32[]{:S(2)}, u32[]{:S(2)}) collective-permute-start(bf16[192,2560]{1,0:T(8,128)(2,1)} %get-tuple-element.255), channel_id=1, source_target_pairs={{0,4},{4,0},{1,5},{5,1},{2,6},{6,2},{3,7},{7,3},{8,12},{12,8},{9,1... | collective-permute-start | bytes 2949128 | tf_op jit(solution)/shard_map/ppermute | solution.py:516
  528.2 59.5 %collective-permute-start.54 = (bf16[192,2560]{1,0:T(8,128)(2,1)S(1)}, bf16[192,2560]{1,0:T(8,128)(2,1)S(1)}, u32[]{:S(2)}, u32[]{:S(2)}) collective-permute-start(bf16[192,2560]{1,0:T(8,128)(2,1)S(1)} %get-tuple-element.256), channel_id=1, source_target_pairs={{0,2},{2,0},{1,3},{3,1},{4,6},{6,4},{5,7},{7,5},{8,10},{10,8},{9,1... | collective-permute-start | bytes 2949128 | tf_op jit(solution)/shard_map/ppermute | solution.py:516
  534.7 53.0 %collective-permute-start.57 = (bf16[160,1536]{1,0:T(8,128)(2,1)S(1)}, bf16[160,1536]{1,0:T(8,128)(2,1)S(1)}, u32[]{:S(2)}, u32[]{:S(2)}) collective-permute-start(bf16[160,1536]{1,0:T(8,128)(2,1)S(1)} %convert_element_type.291), channel_id=1, source_target_pairs={{8,0},{24,16},{9,1},{25,17},{10,2},{26,18},{11,3},{27,19},{12,4},{... | collective-permute-start | bytes 1474568 | tf_op jit(solution)/shard_map/ppermute | solution.py:512
  627.9 88.3 %reduce-scatter.11.cloned.1.call-start = ((), (), s32[]{:S(2)}) async-start(), calls=%async_computation.11 | async-start | bytes 2048000 | tf_op jit(solution)/shard_map/reduce_scatter | solution.py:639
  629.9 34.4 %collective-permute-start.62 = (bf16[320,1536]{1,0:T(8,128)(2,1)S(1)}, bf16[320,1536]{1,0:T(8,128)(2,1)S(1)}, u32[]{:S(2)}, u32[]{:S(2)}) collective-permute-start(bf16[320,1536]{1,0:T(8,128)(2,1)S(1)} %broadcast_select_fusion.5), channel_id=1, source_target_pairs={{0,4},{4,0},{1,5},{5,1},{2,6},{6,2},{3,7},{7,3},{8,12},{12,8},{9,1... | collective-permute-start | bytes 2949128 | tf_op jit(solution)/shard_map/ppermute | solution.py:516
  635.2 29.0 %collective-permute-start.61 = (bf16[96,2560]{1,0:T(8,128)(2,1)S(1)}, bf16[96,2560]{1,0:T(8,128)(2,1)S(1)}, u32[]{:S(2)}, u32[]{:S(2)}) collective-permute-start(bf16[96,2560]{1,0:T(8,128)(2,1)S(1)} %get-tuple-element.251), channel_id=1, source_target_pairs={{0,4},{4,0},{1,5},{5,1},{2,6},{6,2},{3,7},{7,3},{8,12},{12,8},{9,1... | collective-permute-start | bytes 1474568 | tf_op jit(solution)/shard_map/ppermute | solution.py:516
  637.0 27.3 %collective-permute-start.60 = (bf16[96,2560]{1,0:T(8,128)(2,1)S(1)}, bf16[96,2560]{1,0:T(8,128)(2,1)S(1)}, u32[]{:S(2)}, u32[]{:S(2)}) collective-permute-start(bf16[96,2560]{1,0:T(8,128)(2,1)S(1)} %get-tuple-element.252), channel_id=1, source_target_pairs={{0,2},{2,0},{1,3},{3,1},{4,6},{6,4},{5,7},{7,5},{8,10},{10,8},{9,1... | collective-permute-start | bytes 1474568 | tf_op jit(solution)/shard_map/ppermute | solution.py:516
  665.5 23.4 %collective-permute-start.63 = (bf16[192,2560]{1,0:T(8,128)(2,1)}, bf16[192,2560]{1,0:T(8,128)(2,1)}, u32[]{:S(2)}, u32[]{:S(2)}) collective-permute-start(bf16[192,2560]{1,0:T(8,128)(2,1)} %pad_maximum_fusion.8), channel_id=1, source_target_pairs={{0,2},{2,0},{1,3},{3,1},{4,6},{6,4},{5,7},{7,5},{8,10},{10,8},{9,1... | collective-permute-start | bytes 2949128 | tf_op jit(solution)/shard_map/ppermute | solution.py:516
  666.5 25.0 %collective-permute-start.64 = (bf16[192,2560]{1,0:T(8,128)(2,1)}, bf16[192,2560]{1,0:T(8,128)(2,1)}, u32[]{:S(2)}, u32[]{:S(2)}) collective-permute-start(bf16[192,2560]{1,0:T(8,128)(2,1)} %pad_maximum_fusion.9), channel_id=1, source_target_pairs={{0,4},{4,0},{1,5},{5,1},{2,6},{6,2},{3,7},{7,3},{8,12},{12,8},{9,1... | collective-permute-start | bytes 2949128 | tf_op jit(solution)/shard_map/ppermute | solution.py:516
  (122 other events, 1073.1 us)
Sparse Core Ops, SparseCore 0:
  10.2 40.8 all-gather.6
  53.2 53.6 all-gather.4
  108.5 113.8 all-gather.10
  224.4 143.0 all-gather.8
  369.7 102.5 reduce-scatter.4
  474.5 147.2 reduce-scatter.6
  628.0 48.5 reduce-scatter.8
  680.9 35.2 reduce-scatter.10
